TPU v7x, 32 devices: a whole 2x2x4 slice. The times are simulated.
32 devices in a mesh: group: 2 (over y), row: 4 (over z), col: 2 (over x), rep: 2 (over core).
Axes of the slice: x: 2, y: 2, z: 4, core: 2. Of those that a mesh axis runs over, the one named last changes fastest.
Arguments:
- matrix: float32 [192, 7, 64, 64], P(('group', 'row', 'col'), None, 'rep'), parts along dimension 0, as said below
- pattern: int32 [192, 7], P('group'), parts along dimension 0, may hold values from 0 to 1, as said below
Outputs:
- square: float32 [192, 7, 64, 64], P(('group', 'row', 'col'), None, 'rep'), parts along dimension 0
- sign_next: float32 [192, 7, 64, 64], P(('group', 'row', 'col'), None, 'rep'), parts along dimension 0
There are 2 independent parts, one for each index of `group`. A program takes and returns all parts, laid end to end along the dimension named above; each array names one. Nothing has to cross between parts.
Inputs may be any that keep to these rules, and one draw needn't show every extreme that they name: symmetric: pattern[a, k] equals pattern[(a + k - 3) mod 96, 6 - k]; ones at k = 3; from distances between block positions. Symmetric as a whole matrix; zero in the blocks whose pattern flag is 0.
All inputs are finite; a program needn't handle non-finite values.
Results may differ from a plain program's by a relative error of at most 0.0001.
Values sent between devices are 32-bit elements; how exact they have to be, the bound alone decides.
No kernel may reach another device: no remote copies, remote signals or barrier semaphores. Data moves between devices by JAX's collectives and lax.ppermute only.
A program may use at most 64 MiB of HBM per device.

v0:
```python
import jax
import jax.numpy as jnp
from jax import lax
from jax.sharding import PartitionSpec as P

REACH = 3


def with_halo(block, sides, width):
    for axis, dim in sides:
        count = lax.axis_size(axis)
        forward = [(i, i + 1) for i in range(count - 1)]
        forward.append((count - 1, 0))
        backward = [(target, source) for source, target in forward]
        low = lax.ppermute(
            lax.slice_in_dim(block, block.shape[dim] - width, None, axis=dim), axis, forward
        )
        high = lax.ppermute(lax.slice_in_dim(block, 0, width, axis=dim), axis, backward)
        block = jnp.concatenate([low, block, high], axis=dim)
    return block


def band_product(factor, others, reach):
    count = factor.shape[0]
    span = factor.shape[1]
    columns = []
    for target in range(span):
        total = None
        for offset in range(span):
            source_col = target - offset + reach
            if source_col >= 0 and source_col < span:
                piece = jnp.einsum(
                    "rij,rjl->ril",
                    factor[:, offset],
                    others[offset : offset + count, source_col],
                    precision=lax.Precision.HIGHEST,
                    preferred_element_type=jnp.float32,
                )
                total = piece if total is None else total + piece
        columns.append(total)
    return jnp.stack(columns, axis=1)


def shards(matrix, pattern):
    count = matrix.shape[0]
    first = lax.axis_index(("row", "col")) * count
    full = lax.all_gather(matrix, "rep", axis=2, tiled=True)
    own_flags = lax.dynamic_slice_in_dim(pattern, first, count, 0).astype(jnp.float32)[
        :, :, None, None
    ]
    widened = with_halo(full, ((("row", "col"), 0),), REACH)
    square = own_flags * band_product(matrix, widened, REACH)
    square_full = lax.all_gather(square, "rep", axis=2, tiled=True)
    square_wide = with_halo(square_full, ((("row", "col"), 0),), REACH)
    second = own_flags * band_product(matrix, square_wide, REACH)
    sign_next = 1.5 * matrix - 0.5 * second
    return (square, sign_next)


def solution(mesh):
    in_specs = (P(("group", "row", "col"), None, "rep", None), P("group", None))
    out_specs = (
        P(("group", "row", "col"), None, "rep", None),
        P(("group", "row", "col"), None, "rep", None),
    )
    return jax.shard_map(shards, mesh=mesh, in_specs=in_specs, out_specs=out_specs, check_vma=False)
```

profile of v0, /device:TPU:0, one launch (start us, length us, event | category | flops | bytes accessed | tf_op | source)
XLA Modules:
  0.0 149.7 jit_solution(2142546111176185318)
XLA Ops:
  7.2 2.6 %copy.4 = f32[12,7,32,64]{3,2,0,1:T(8,128)} copy(f32[12,7,32,64]{3,2,1,0:T(8,128)} %param.2) | data formatting | bytes 1376256 | tf_op args[0]
  9.9 14.5 %all-gather.3.cloned.1.call-done = f32[12,7,64,64]{3,2,0,1:T(8,128)} async-done(((f32[12,7,32,64]{3,2,0,1:T(8,128)}), f32[12,7,64,64]{3,2,0,1:T(8,128)}) %all-gather.3.cloned.1.call-update) | async-done | bytes 1376272 | tf_op jit(solution)/shard_map/all_gather | solution.py:47
  24.4 1.5 %fusion.78 = (f32[3,7,64,64]{3,2,0,1:T(8,128)S(1)}, f32[3,7,64,64]{3,2,0,1:T(8,128)S(1)}) fusion(f32[12,7,64,64]{3,2,0,1:T(8,128)} %all-gather.3.cloned.1.call-done), kind=kLoop, calls=%fused_computation.223 | loop fusion | bytes 1376256 | tf_op jit(solution)/shard_map/slice | solution.py:18
  25.9 1.8 %collective-permute-start = (f32[3,7,64,64]{3,2,0,1:T(8,128)S(1)}, f32[3,7,64,64]{3,2,0,1:T(8,128)S(1)}, u32[]{:S(2)}, u32[]{:S(2)}) collective-permute-start(f32[3,7,64,64]{3,2,0,1:T(8,128)S(1)} %get-tuple-element.9), channel_id=1, source_target_pairs={{0,2},{2,4},{4,6},{6,8},{8,10},{10,12},{12,14},{14,0},{1,3},{3,5},... | collective-permute-start | bytes 1032200 | tf_op jit(solution)/shard_map/ppermute | solution.py:15
  27.8 3.0 %collective-permute-start.1 = (f32[3,7,64,64]{3,2,0,1:T(8,128)S(1)}, f32[3,7,64,64]{3,2,0,1:T(8,128)S(1)}, u32[]{:S(2)}, u32[]{:S(2)}) collective-permute-start(f32[3,7,64,64]{3,2,0,1:T(8,128)S(1)} %get-tuple-element.8), channel_id=1, source_target_pairs={{2,0},{4,2},{6,4},{8,6},{10,8},{12,10},{14,12},{0,14},{3,1},{5,3},... | collective-permute-start | bytes 1032200 | tf_op jit(solution)/shard_map/ppermute | solution.py:18
  30.8 1.5 fusion.71
  32.3 25.4 %collective-permute-done = f32[3,7,64,64]{3,2,0,1:T(8,128)S(1)} collective-permute-done((f32[3,7,64,64]{3,2,0,1:T(8,128)S(1)}, f32[3,7,64,64]{3,2,0,1:T(8,128)S(1)}, u32[]{:S(2)}, u32[]{:S(2)}) %collective-permute-start) | collective-permute-done | bytes 344096 | tf_op jit(solution)/shard_map/ppermute | solution.py:15
  57.7 0.8 constant_dynamic-update-slice_fusion.3
  58.5 0.5 fusion.72
  61.8 0.5 convolution_add_fusion.23
  62.3 0.5 fusion.27
  62.8 0.5 fusion.26
  63.3 0.5 convolution_add_fusion.27
  63.7 0.5 fusion.34
  64.2 0.5 convolution_add_fusion.25
  64.7 0.5 fusion.33
  65.2 0.5 fusion.32
  65.6 0.5 convolution_add_fusion.30
  66.1 0.5 fusion.39
  66.6 0.5 convolution_add_fusion.28
  67.0 0.5 fusion.38
  67.5 0.5 convolution_add_fusion.33
  68.0 0.5 fusion.43
  68.4 0.5 convolution_add_fusion.36
  68.9 0.5 fusion.46
  69.4 0.5 convolution_add_fusion.22
  69.9 0.6 fusion.22
  70.5 0.5 fusion.21
  71.0 0.5 fusion.17
  71.4 0.5 fusion.16
  71.9 0.5 convolution_add_fusion.31
  72.4 0.5 fusion.45
  72.9 0.5 fusion.42
  73.3 0.5 fusion.37
  73.8 0.5 fusion.31
  74.3 0.5 fusion.25
  74.7 0.5 fusion.20
  75.2 0.5 fusion.15
  75.7 1.2 broadcast_multiply_fusion
  76.9 1.3 copy-done.3
  78.3 1.2 copy.13
  79.4 11.1 %all-gather.5.cloned.1.call-done = f32[12,7,64,64]{3,2,0,1:T(8,128)} async-done(((f32[12,7,32,64]{3,2,0,1:T(8,128)}), f32[12,7,64,64]{3,2,0,1:T(8,128)}) %all-gather.5.cloned.1.call-update) | async-done | bytes 1376272 | tf_op jit(solution)/shard_map/all_gather | solution.py:53
  90.6 1.5 %fusion.77 = (f32[3,7,64,64]{3,2,0,1:T(8,128)S(1)}, f32[3,7,64,64]{3,2,0,1:T(8,128)S(1)}) fusion(f32[12,7,64,64]{3,2,0,1:T(8,128)} %all-gather.5.cloned.1.call-done), kind=kLoop, calls=%fused_computation.222 | loop fusion | bytes 1376256 | tf_op jit(solution)/shard_map/slice | solution.py:18
  92.1 1.8 %collective-permute-start.2 = (f32[3,7,64,64]{3,2,0,1:T(8,128)S(1)}, f32[3,7,64,64]{3,2,0,1:T(8,128)S(1)}, u32[]{:S(2)}, u32[]{:S(2)}) collective-permute-start(f32[3,7,64,64]{3,2,0,1:T(8,128)S(1)} %get-tuple-element.5), channel_id=1, source_target_pairs={{0,2},{2,4},{4,6},{6,8},{8,10},{10,12},{12,14},{14,0},{1,3},{3,5},... | collective-permute-start | bytes 1032200 | tf_op jit(solution)/shard_map/ppermute | solution.py:15
  93.9 3.0 %collective-permute-start.3 = (f32[3,7,64,64]{3,2,0,1:T(8,128)S(1)}, f32[3,7,64,64]{3,2,0,1:T(8,128)S(1)}, u32[]{:S(2)}, u32[]{:S(2)}) collective-permute-start(f32[3,7,64,64]{3,2,0,1:T(8,128)S(1)} %get-tuple-element.4), channel_id=1, source_target_pairs={{2,0},{4,2},{6,4},{8,6},{10,8},{12,10},{14,12},{0,14},{3,1},{5,3},... | collective-permute-start | bytes 1032200 | tf_op jit(solution)/shard_map/ppermute | solution.py:18
  97.8 26.0 %collective-permute-done.2 = f32[3,7,64,64]{3,2,0,1:T(8,128)S(1)} collective-permute-done((f32[3,7,64,64]{3,2,0,1:T(8,128)S(1)}, f32[3,7,64,64]{3,2,0,1:T(8,128)S(1)}, u32[]{:S(2)}, u32[]{:S(2)}) %collective-permute-start.2) | collective-permute-done | bytes 344096 | tf_op jit(solution)/shard_map/ppermute | solution.py:15
  123.9 0.8 constant_dynamic-update-slice_fusion.7
  124.7 0.5 fusion.63
  127.1 0.5 fusion.67
  130.8 0.5 convolution_add_fusion.1
  131.3 0.5 convolution_add_fusion.3
  131.8 0.5 convolution_add_fusion.6
  132.2 0.5 convolution_add_fusion.10
  132.7 0.5 convolution_add_fusion.9
  133.2 0.5 convolution_add_fusion.14
  133.6 0.5 convolution_add_fusion.13
  136.0 0.7 convolution_add_fusion.16
  137.2 0.5 fusion.10
  138.1 0.5 fusion.8
  139.0 0.5 fusion.49
  140.0 0.5 fusion.52
  140.5 0.5 fusion.55
  140.9 0.5 fusion.2
  141.7 1.2 copy.14
  (48 shorter events, 13.1 us)
Async XLA Ops:
  7.2 17.2 %all-gather.3.cloned.1.call-start = ((), (), s32[]{:S(2)}) async-start(), calls=%async_computation | async-start | bytes 4128768 | tf_op jit(solution)/shard_map/all_gather | solution.py:47
  9.8 80.8 %all-gather.5.cloned.1.call-start = ((), (), s32[]{:S(2)}) async-start(), calls=%async_computation.1 | async-start | bytes 4128768 | tf_op jit(solution)/shard_map/all_gather | solution.py:53
  9.8 17.9 %copy-start.4 = (s32[96,7]{0,1:T(8,128)S(1)}, s32[96,7]{0,1:T(8,128)}, u32[]{:S(2)}) copy-start(s32[96,7]{0,1:T(8,128)} %param.3) | copy-start | bytes 8068
  9.9 20.9 %copy-start = (f32[12,7,32,64]{3,2,1,0:T(8,128)S(1)}, f32[12,7,32,64]{3,2,1,0:T(8,128)}, u32[]{:S(2)}) copy-start(f32[12,7,32,64]{3,2,1,0:T(8,128)} %param.2) | copy-start | bytes 2064388
  24.4 33.3 %copy-start.1 = (f32[12,7,64,64]{3,2,0,1:T(8,128)S(1)}, f32[12,7,64,64]{3,2,0,1:T(8,128)}, u32[]{:S(2)}) copy-start(f32[12,7,64,64]{3,2,0,1:T(8,128)} %all-gather.3.cloned.1.call-done) | copy-start | bytes 4128772
  25.9 31.7 %collective-permute-start = (f32[3,7,64,64]{3,2,0,1:T(8,128)S(1)}, f32[3,7,64,64]{3,2,0,1:T(8,128)S(1)}, u32[]{:S(2)}, u32[]{:S(2)}) collective-permute-start(f32[3,7,64,64]{3,2,0,1:T(8,128)S(1)} %get-tuple-element.9), channel_id=1, source_target_pairs={{0,2},{2,4},{4,6},{6,8},{8,10},{10,12},{12,14},{14,0},{1,3},{3,5},... | collective-permute-start | bytes 1032200 | tf_op jit(solution)/shard_map/ppermute | solution.py:15
  27.8 34.4 %collective-permute-start.1 = (f32[3,7,64,64]{3,2,0,1:T(8,128)S(1)}, f32[3,7,64,64]{3,2,0,1:T(8,128)S(1)}, u32[]{:S(2)}, u32[]{:S(2)}) collective-permute-start(f32[3,7,64,64]{3,2,0,1:T(8,128)S(1)} %get-tuple-element.8), channel_id=1, source_target_pairs={{2,0},{4,2},{6,4},{8,6},{10,8},{12,10},{14,12},{0,14},{3,1},{5,3},... | collective-permute-start | bytes 1032200 | tf_op jit(solution)/shard_map/ppermute | solution.py:18
  76.9 1.3 copy-start.3
  90.6 6.3 %copy-start.2 = (f32[12,7,64,64]{3,2,0,1:T(8,128)S(1)}, f32[12,7,64,64]{3,2,0,1:T(8,128)}, u32[]{:S(2)}) copy-start(f32[12,7,64,64]{3,2,0,1:T(8,128)} %all-gather.5.cloned.1.call-done) | copy-start | bytes 4128772
  92.1 31.7 %collective-permute-start.2 = (f32[3,7,64,64]{3,2,0,1:T(8,128)S(1)}, f32[3,7,64,64]{3,2,0,1:T(8,128)S(1)}, u32[]{:S(2)}, u32[]{:S(2)}) collective-permute-start(f32[3,7,64,64]{3,2,0,1:T(8,128)S(1)} %get-tuple-element.5), channel_id=1, source_target_pairs={{0,2},{2,4},{4,6},{6,8},{8,10},{10,12},{12,14},{14,0},{1,3},{3,5},... | collective-permute-start | bytes 1032200 | tf_op jit(solution)/shard_map/ppermute | solution.py:15
  93.9 33.1 %collective-permute-start.3 = (f32[3,7,64,64]{3,2,0,1:T(8,128)S(1)}, f32[3,7,64,64]{3,2,0,1:T(8,128)S(1)}, u32[]{:S(2)}, u32[]{:S(2)}) collective-permute-start(f32[3,7,64,64]{3,2,0,1:T(8,128)S(1)} %get-tuple-element.4), channel_id=1, source_target_pairs={{2,0},{4,2},{6,4},{8,6},{10,8},{12,10},{14,12},{0,14},{3,1},{5,3},... | collective-permute-start | bytes 1032200 | tf_op jit(solution)/shard_map/ppermute | solution.py:18
Sparse Core Ops, SparseCore 0:
  10.1 14.2 all-gather.2
  77.1 13.4 all-gather.4
where the time goes:
time: 150 us
  waiting for transfers between devices  77 us (51%)
  matrix products  35.6 us (24%)
  between operations  14.7 us (10%)
  local copies, waits for them, and re-layouts  11.1 us (7%)
  starting transfers between devices  9.63 us (6%)
  other arithmetic  1.57 us (1%)
    ppermute x2, waiting for transfers between devices, with_halo(): lax.ppermute(lax.slice_in_dim(block, block.shape[dim] - width, None, axis...  51.3 us
    dot_general x74, matrix products, band_product(): jnp.einsum('rij,rjl->ril', factor[:, offset], others[offset:offset + coun...  35.6 us
    all_gather x1, waiting for transfers between devices, shards(): full = lax.all_gather(matrix, 'rep', axis=2, tiled=True)  14.5 us
    all_gather x1, waiting for transfers between devices, shards(): square_full = lax.all_gather(square, 'rep', axis=2, tiled=True)  11.1 us
    unnamed x17, local copies, waits for them, and re-layouts  7.92 us
    ppermute x2, starting transfers between devices, with_halo(): lax.ppermute(lax.slice_in_dim(block, 0, width, axis=dim), axis, backward)  5.99 us
    ppermute x2, starting transfers between devices, with_halo(): lax.ppermute(lax.slice_in_dim(block, block.shape[dim] - width, None, axis...  3.56 us
    slice x2, local copies, waits for them, and re-layouts, with_halo(): lax.slice_in_dim(block, 0, width, axis=dim)  3.09 us
  transfers between devices with their start and end apart: 6, of which 4 were waited for; matrix products, arithmetic and copies ran while one was open for 8% of the time, Pallas kernels for 0%

commit v1 on v0

v1 whole, which is shorter than its diff:
```python
import functools

import jax
import jax.numpy as jnp
from jax import lax
from jax.experimental import pallas as pl
from jax.experimental.pallas import tpu as pltpu
from jax.sharding import PartitionSpec as P

REACH = 3
SPAN = 7
BS = 64
HALF = 32
GROUP = 4
WIDE = GROUP * BS
BF = jnp.bfloat16
F32 = jnp.float32
LIMIT = 40 * 1024 * 1024


def split(x):
    hi = x.astype(BF)
    return hi, (x - hi.astype(F32)).astype(BF)


def dot3(a, b, transposed):
    dims = (((1,), (1 if transposed else 0,)), ((), ()))
    one = functools.partial(lax.dot_general, dimension_numbers=dims, preferred_element_type=F32)
    return one(a[0], b[0]) + (one(a[0], b[1]) + one(a[1], b[0]))


def flag_row(pat, row, places):
    lane = lax.broadcasted_iota(jnp.int32, (1, WIDE), 1)
    line = jnp.zeros((1, WIDE), F32)
    for place, k in places:
        value = pat[k, row].astype(F32)
        line = jnp.where((lane >= place * BS) & (lane < (place + 1) * BS), value, line)
    return line


def edge_kernel(top, bottom, to_left, to_right):
    for s in range(REACH):
        rows = slice(s * HALF, (s + 1) * HALF)
        for t in range(2):
            lanes = slice(t * 2 * BS, (t + 1) * 2 * BS)
            to_left[rows, lanes] = jnp.concatenate(
                [top[s, REACH + 2 * t], top[s, REACH + 2 * t + 1]], axis=1
            )
            to_right[rows, lanes] = jnp.concatenate([bottom[s, 2 * t], bottom[s, 2 * t + 1]], axis=1)


def interior_kernel(
    own, other, pat, square, sign, low_a, low_b, low_m, low_p, high_a, high_b, high_m, high_p,
    full, mine, tile, keep, *, axes, half_axis
):
    count = own.shape[0]
    total = pat.shape[1]
    groups = count // GROUP
    first = lax.axis_index(axes) * count
    half = lax.axis_index(half_axis)
    own_at = half * HALF
    other_at = HALF - own_at

    for a in range(count):
        g, s = divmod(a, GROUP)
        for src, at in ((own, own_at), (other, other_at)):
            rows = pl.ds(pl.multiple_of(s * BS + at, HALF), HALF)
            for t in range(3 * GROUP // 2):
                ks = [2 * t + e - s - 1 for e in range(2)]
                lanes = slice(t * 2 * BS, (t + 1) * 2 * BS)
                if all(k < 0 or k >= SPAN for k in ks):
                    parts = (jnp.zeros((HALF, 2 * BS), BF),) * 2
                else:
                    parts = split(
                        jnp.concatenate(
                            [
                                src[a, k] if 0 <= k < SPAN else jnp.zeros((HALF, BS), F32)
                                for k in ks
                            ],
                            axis=1,
                        )
                    )
                for p in range(2):
                    full[p, g, rows, lanes] = parts[p]
                    if src is own:
                        mine[p, g, s * HALF : (s + 1) * HALF, lanes] = parts[p]

    def panel(ref, g, lo, hi, r0=0, r1=None):
        return [ref[p, g, r0:r1, lo * WIDE : hi * WIDE] for p in range(2)]

    def flags(g, s, delta):
        a = g * GROUP + s
        places = [
            (t, t + GROUP * delta - s + REACH)
            for t in range(GROUP)
            if 0 <= t + GROUP * delta - s + REACH < SPAN
        ]
        row = lax.rem(first + a + total, total)
        return flag_row(pat, row, places)

    def masked(g, delta, value):
        return jnp.concatenate(
            [value[s * BS : (s + 1) * BS] * flags(g, s, delta) for s in range(GROUP)], axis=0
        )

    def emit_square(g, delta, value):
        tile[...] = value
        for s in range(GROUP):
            part = tile[pl.ds(pl.multiple_of(s * BS + own_at, HALF), HALF), :]
            for t in range(GROUP):
                k = t + GROUP * delta - s + REACH
                if 0 <= k < SPAN:
                    square[g * GROUP + s, k] = part[:, t * BS : (t + 1) * BS]

    def emit_sign(g, delta, value):
        for s in range(GROUP):
            part = value[s * HALF : (s + 1) * HALF] * (flags(g, s, delta) * 0.5)
            for t in range(GROUP):
                k = t + GROUP * delta - s + REACH
                if 0 <= k < SPAN:
                    a = g * GROUP + s
                    sign[a, k] = 1.5 * own[a, k] - part[:, t * BS : (t + 1) * BS]

    diag = []
    upper = []
    for g in range(groups):
        r = panel(full, g, 0, 3)
        value = masked(g, 0, dot3(r, r, True))
        emit_square(g, 0, value)
        for p, part in enumerate(split(value)):
            keep[p, 2 * g] = part
        if g + 1 < groups:
            value = masked(g, 1, dot3(panel(full, g, 1, 3), panel(full, g + 1, 0, 2), True))
            emit_square(g, 1, value)
            emit_square(g + 1, -1, value.T)
            for p, part in enumerate(split(value)):
                keep[p, 2 * g + 1] = part

    def kept(i):
        return [keep[p, i] for p in range(2)]

    for g in range(groups):
        low = panel(mine, g, 0, 1)
        mid = panel(mine, g, 1, 2)
        high = panel(mine, g, 2, 3)
        centre = dot3(mid, kept(2 * g), True)
        if g > 0:
            centre = centre + dot3(low, kept(2 * g - 1), False)
            emit_sign(g, -1, dot3(low, kept(2 * g - 2), True) + dot3(mid, kept(2 * g - 1), True))
        if g + 1 < groups:
            centre = centre + dot3(high, kept(2 * g + 1), True)
            emit_sign(g, 1, dot3(mid, kept(2 * g + 1), False) + dot3(high, kept(2 * g + 2), True))
        emit_sign(g, 0, centre)
    for s in range(REACH):
        for t in range(REACH - s):
            sign[s, t] = 1.5 * own[s, t]
            sign[count - 1 - s, SPAN - 1 - t] = 1.5 * own[count - 1 - s, SPAN - 1 - t]

    last = groups - 1
    for a_ref, b_ref, m_ref, p_ref, g, part, r0 in (
        (low_a, low_b, low_m, low_p, 0, 0, 0),
        (high_a, high_b, high_m, high_p, last, 2, BS),
    ):
        rows = slice(r0, r0 + REACH * BS)
        out = panel(full, g, part, part + 1)
        turned = [x.astype(F32).T.astype(BF) for x in out]
        a_ref[...] = dot3(turned, turned, True)
        b_ref[...] = dot3(panel(full, g, 1, 2), turned, True)[rows]
        for p in range(2):
            m_ref[p] = out[p][rows]
            p_ref[p, 0] = mine[p, g, r0 // 2 : r0 // 2 + REACH * HALF, part * WIDE : (part + 1) * WIDE]
            p_ref[p, 1] = mine[p, g, r0 // 2 : r0 // 2 + REACH * HALF, WIDE : 2 * WIDE]


def border_kernel(
    low_own, low_other, high_own, high_other, pat, low_a, low_b, low_m, low_p, high_a, high_b,
    high_m, high_p, square_in, sign_in, square_out, sign_out, near, halo, tile, keep, blocks, sems,
    *, axes, half_axis
):
    count = square_in.shape[0]
    total = pat.shape[1]
    first = lax.axis_index(axes) * count
    own_at = lax.axis_index(half_axis) * HALF
    other_at = HALF - own_at
    ends = (0, count - REACH)
    loads = [
        pltpu.make_async_copy(ref.at[pl.ds(ends[side], REACH)], blocks.at[i, side], sems.at[i, side])
        for i, ref in enumerate((square_in, sign_in))
        for side in range(2)
    ]
    for load in loads:
        load.start()

    def put(p, rows, lanes, value):
        for q, part in enumerate(split(value)):
            halo[q, rows, lanes] = part

    def sides(side):
        return (
            (low_own, low_other, low_a, low_b, low_m, low_p)
            if side == 0
            else (high_own, high_other, high_a, high_b, high_m, high_p)
        )

    squares = []
    for side in range(2):
        mine, theirs, a_ref, b_ref, m_ref, p_ref = sides(side)
        for p in range(REACH):
            for src, at in ((mine, own_at), (theirs, other_at)):
                near[side, pl.ds(pl.multiple_of(p * BS + at, HALF), HALF), :] = src[
                    p * HALF : (p + 1) * HALF, :
                ]
        def block(p, c):
            k = c - p + (REACH if side == 0 else 0)
            if 0 <= k <= REACH:
                return near[side, p * BS : (p + 1) * BS, k * BS : (k + 1) * BS]
            k = p - c + (REACH if side == 0 else 0)
            if 0 <= c < REACH and 0 <= k <= REACH:
                return near[side, c * BS : (c + 1) * BS, k * BS : (k + 1) * BS].T
            return jnp.zeros((BS, BS), F32)

        base = -5 if side == 0 else 0
        for p in range(REACH):
            for t in range(4):
                cs = [base + 2 * t, base + 2 * t + 1]
                value = jnp.concatenate([block(p, c) for c in cs], axis=1)
                for q, part in enumerate(split(value)):
                    halo[side, q, p * BS : (p + 1) * BS, t * 2 * BS : (t + 1) * 2 * BS] = part
    for load in loads:
        load.wait()

    lane = lax.broadcasted_iota(jnp.int32, (1, WIDE), 1)
    for side in range(2):
        mine, theirs, a_ref, b_ref, m_ref, p_ref = sides(side)
        shift = 1 if side == 0 else 0
        row0 = shift * BS
        whole = [halo[side, q] for q in range(2)]
        inner = [halo[side, q, :, (WIDE if side == 0 else 0) : (2 * WIDE if side == 0 else WIDE)] for q in range(2)]
        outer_first = first - REACH if side == 0 else first + count
        edge_first = first + ends[side]

        rows = []
        value = dot3(whole, whole, True) + a_ref[row0 : row0 + REACH * BS, row0 : row0 + REACH * BS]
        lane3 = lax.broadcasted_iota(jnp.int32, (1, REACH * BS), 1)
        for p in range(REACH):
            row = lax.rem(outer_first + p + total, total)
            line = jnp.zeros((1, REACH * BS), F32)
            for t in range(REACH):
                f = pat[t - p + REACH, row].astype(F32)
                line = jnp.where((lane3 >= t * BS) & (lane3 < (t + 1) * BS), f, line)
            rows.append(value[p * BS : (p + 1) * BS] * line)
        corner = split(jnp.concatenate(rows, axis=0))

        m = [m_ref[q] for q in range(2)]
        m3 = [x[:, row0 : row0 + REACH * BS] for x in m]
        inner3 = [x[:, row0 : row0 + REACH * BS] for x in inner]
        value = dot3(m3, inner3, True) + b_ref[:, row0 : row0 + REACH * BS]
        rows = []
        lines = []
        for s in range(REACH):
            row = lax.rem(edge_first + s, total)
            line = jnp.zeros((1, REACH * BS), F32)
            for t in range(REACH):
                k = t - s + (0 if side == 0 else 2 * REACH)
                if 0 <= k < SPAN:
                    f = pat[k, row].astype(F32)
                    line = jnp.where((lane3 >= t * BS) & (lane3 < (t + 1) * BS), f, line)
            lines.append(line)
            rows.append(value[s * BS : (s + 1) * BS] * line)
        value = jnp.concatenate(rows, axis=0)
        tile[side] = value
        across = split(value)

        reach_out = [p_ref[q, 0][:, row0 : row0 + REACH * BS] for q in range(2)]
        col0 = 0 if side == 0 else BS
        inside = [p_ref[q, 1][:, col0 : col0 + REACH * BS] for q in range(2)]
        out = dot3(reach_out, corner, True) + dot3(inside, across, False)
        back = dot3(reach_out, across, True)
        for s in range(REACH):
            row = lax.rem(edge_first + s, total)
            part = tile[side, pl.ds(pl.multiple_of(s * BS + own_at, HALF), HALF), :]
            far = out[s * HALF : (s + 1) * HALF] * (lines[s] * 0.5)
            near_line = jnp.zeros((1, REACH * BS), F32)
            for t in range(REACH):
                f = pat[t - s + REACH, row].astype(F32)
                near_line = jnp.where((lane3 >= t * BS) & (lane3 < (t + 1) * BS), f, near_line)
            close = back[s * HALF : (s + 1) * HALF] * (near_line * 0.5)
            for t in range(REACH):
                k = t - s + (0 if side == 0 else 2 * REACH)
                lanes = slice(t * BS, (t + 1) * BS)
                if 0 <= k < SPAN:
                    blocks[0, side, s, k] = part[:, lanes]
                    blocks[1, side, s, k] = blocks[1, side, s, k] - far[:, lanes]
                k = t - s + REACH
                blocks[1, side, s, k] = blocks[1, side, s, k] - close[:, lanes]

    stores = [
        pltpu.make_async_copy(blocks.at[i, side], ref.at[pl.ds(ends[side], REACH)], sems.at[i, side])
        for i, ref in enumerate((square_out, sign_out))
        for side in range(2)
    ]
    for store in stores:
        store.start()
    for store in stores:
        store.wait()


def shards(matrix, pattern, *, axes, half_axis):
    count = matrix.shape[0]
    groups = count // GROUP
    flags = pattern.T
    vmem = pl.BlockSpec(memory_space=pltpu.VMEM)
    smem = pl.BlockSpec(memory_space=pltpu.SMEM)
    anywhere = pl.BlockSpec(memory_space=pl.ANY)
    params = pltpu.CompilerParams(vmem_limit_bytes=LIMIT)

    edge = jax.ShapeDtypeStruct((REACH * HALF, (REACH + 1) * BS), F32)
    ends = count // REACH - 1
    to_left, to_right = pl.pallas_call(
        edge_kernel,
        grid=(1,),
        out_shape=(edge, edge),
        in_specs=[
            pl.BlockSpec((REACH, SPAN, HALF, BS), lambda i: (0, 0, 0, 0)),
            pl.BlockSpec((REACH, SPAN, HALF, BS), lambda i: (ends, 0, 0, 0)),
        ],
        out_specs=[pl.BlockSpec(edge.shape, lambda i: (0, 0))] * 2,
        compiler_params=params,
    )(matrix, matrix)

    size = 1
    for axis in axes:
        size *= lax.axis_size(axis)
    swap = [(0, 1), (1, 0)]
    other = lax.ppermute(matrix, half_axis, swap)
    ring = axes + (half_axis,)

    def around(step, cross):
        return [
            (2 * i + r, 2 * ((i + step) % size) + (1 - r if cross else r))
            for i in range(size)
            for r in range(2)
        ]

    low_own = lax.ppermute(to_right, ring, around(1, False))
    high_own = lax.ppermute(to_left, ring, around(-1, False))
    low_other = lax.ppermute(to_right, ring, around(1, True))
    high_other = lax.ppermute(to_left, ring, around(-1, True))

    names = dict(axes=axes, half_axis=half_axis)
    ends_out = [
        jax.ShapeDtypeStruct((WIDE, WIDE), F32),
        jax.ShapeDtypeStruct((REACH * BS, WIDE), F32),
        jax.ShapeDtypeStruct((2, REACH * BS, WIDE), BF),
        jax.ShapeDtypeStruct((2, 2, REACH * HALF, WIDE), BF),
    ] * 2
    band = jax.ShapeDtypeStruct(matrix.shape, F32)
    square, sign, *inside = pl.pallas_call(
        functools.partial(interior_kernel, **names),
        out_shape=[band, band] + ends_out,
        in_specs=[vmem, vmem, smem],
        out_specs=[vmem] * 10,
        scratch_shapes=[
            pltpu.VMEM((2, groups, WIDE, 3 * WIDE), BF),
            pltpu.VMEM((2, groups, GROUP * HALF, 3 * WIDE), BF),
            pltpu.VMEM((WIDE, WIDE), F32),
            pltpu.VMEM((2, 2 * groups - 1, WIDE, WIDE), BF),
        ],
        compiler_params=params,
        cost_estimate=pl.CostEstimate(
            flops=3 * 2 * 16 * WIDE**3, bytes_accessed=6 * 2**20, transcendentals=0
        ),
    )(matrix, other, flags)

    return tuple(
        pl.pallas_call(
            functools.partial(border_kernel, **names),
            out_shape=(band, band),
            in_specs=[vmem] * 4 + [smem] + [vmem] * 8 + [anywhere] * 2,
            out_specs=[anywhere] * 2,
            scratch_shapes=[
                pltpu.VMEM((2, REACH * BS, WIDE), F32),
                pltpu.VMEM((2, 2, REACH * BS, 2 * WIDE), BF),
                pltpu.VMEM((2, REACH * BS, REACH * BS), F32),
                pltpu.VMEM((8, 128), F32),
                pltpu.VMEM((2, 2, REACH, SPAN, HALF, BS), F32),
                pltpu.SemaphoreType.DMA((2, 2)),
            ],
            input_output_aliases={13: 0, 14: 1},
            compiler_params=params,
            cost_estimate=pl.CostEstimate(
                flops=3 * 2 * 4 * WIDE**3, bytes_accessed=2 * 2**20, transcendentals=0
            ),
        )(low_own, low_other, high_own, high_other, flags, *inside, square, sign)
    )


def solution(mesh):
    band = P(("group", "row", "col"), None, "rep", None)
    return jax.shard_map(
        functools.partial(shards, axes=("row", "col"), half_axis="rep"),
        mesh=mesh,
        in_specs=(band, P("group", None)),
        out_specs=(band, band),
        check_vma=False,
    )
```

time: 150 us -> 22.8 us (0.15)
  waiting for transfers between devices: 77 us -> 1.43 us
  matrix products: 35.6 us -> 0 us
  between operations: 14.7 us -> 0.65 us
  Pallas kernels: 0 us -> 11.2 us
  local copies, waits for them, and re-layouts: 11.1 us -> 1.34 us
  starting transfers between devices: 9.63 us -> 8.02 us
  other arithmetic: 1.57 us -> 0 us
    ppermute x4 -> x5, waiting for transfers between devices: 51.3 us -> 1.43 us  [the longest x1 1.42 us: shards(): high_own = lax.ppermute(to_left, ring, around(-1, False))]
    dot_general x74 -> x0, matrix products: 35.6 us -> none  [band_product(): jnp.einsum('rij,rjl->ril', factor[:, offset], others[offset:offset + coun...]
    all_gather x2 -> x0, waiting for transfers between devices: 25.7 us -> none  [the longest x1 14.5 us: shards(): full = lax.all_gather(matrix, 'rep', axis=2, tiled=True)]
    pallas_call x0 -> x3, Pallas kernels: none -> 11.2 us  [the longest x1 6.42 us: shards(): pl.pallas_call(functools.partial(interior_kernel, **names), out_shape=[ba...]
    unnamed x17 -> x4, local copies, waits for them, and re-layouts: 7.92 us -> 1.34 us
    slice x2 -> x0, local copies, waits for them, and re-layouts: 3.09 us -> none  [with_halo(): lax.slice_in_dim(block, 0, width, axis=dim)]
    ppermute x4 -> x5, starting transfers between devices: 9.55 us -> 8.02 us  [the longest x1 2.65 us: shards(): low_other = lax.ppermute(to_right, ring, around(1, True))]
  transfers between devices with their start and end apart: 6 -> 5, of which waited for: 4 -> 1; matrix products, arithmetic and copies ran while one was open for 8% -> 0% of each run, Pallas kernels for 0% -> 29%
where the time goes in v1:
time: 22.8 us; the launch traced here: 22.6 us
  Pallas kernels  11.2 us (49%)
  starting transfers between devices  8.02 us (35%)
  waiting for transfers between devices  1.43 us (6%)
  local copies, waits for them, and re-layouts  1.34 us (6%)
  between operations  0.65 us (3%)
    pallas_call x1, Pallas kernels, shards(): pl.pallas_call(functools.partial(interior_kernel, **names), out_shape=[ba...  6.42 us
    pallas_call x1, Pallas kernels, shards(): pl.pallas_call(functools.partial(border_kernel, **names), out_shape=(band...  4.65 us
    ppermute x1, starting transfers between devices, shards(): low_other = lax.ppermute(to_right, ring, around(1, True))  2.65 us
    ppermute x1, starting transfers between devices, shards(): high_other = lax.ppermute(to_left, ring, around(-1, True))  2.51 us
    ppermute x1, starting transfers between devices, shards(): low_own = lax.ppermute(to_right, ring, around(1, False))  1.55 us
    ppermute x1, waiting for transfers between devices, shards(): high_own = lax.ppermute(to_left, ring, around(-1, False))  1.42 us
    unnamed x4, local copies, waits for them, and re-layouts  1.34 us
    ppermute x1, starting transfers between devices, shards(): high_own = lax.ppermute(to_left, ring, around(-1, False))  0.79 us
  transfers between devices with their start and end apart: 5, of which 1 were waited for; matrix products, arithmetic and copies ran while one was open for 0% of the time, Pallas kernels for 29%

profile of v1, /device:TPU:0, one launch (start us, length us, event | category | flops | bytes accessed | tf_op | source)
XLA Modules:
  0.0 22.6 jit_solution(16329180565222264556)
XLA Ops:
  0.6 0.5 %collective-permute-start.4 = (f32[12,7,32,64]{3,2,1,0:T(8,128)}, f32[12,7,32,64]{3,2,1,0:T(8,128)S(1)}, u32[]{:S(2)}, u32[]{:S(2)}) collective-permute-start(f32[12,7,32,64]{3,2,1,0:T(8,128)} %own.1), channel_id=1, source_target_pairs={{0,1},{1,0},{2,3},{3,2},{4,5},{5,4},{6,7},{7,6},{8,9},{9,8},{10,11... | collective-permute-start | bytes 2064392 | tf_op jit(solution)/shard_map/ppermute | solution.py:335
  1.1 0.0 copy-start
  1.1 1.3 %copy-done = f32[12,7,32,64]{3,2,1,0:T(8,128)S(1)} copy-done((f32[12,7,32,64]{3,2,1,0:T(8,128)S(1)}, f32[12,7,32,64]{3,2,1,0:T(8,128)}, u32[]{:S(2)}) %copy-start) | copy-done | bytes 688152
  2.5 0.0 copy-start.1
  2.5 0.1 shard_map.41
  2.6 2.7 %collective-permute-start.1 = (f32[96,256]{1,0:T(8,128)S(1)}, f32[96,256]{1,0:T(8,128)S(1)}, u32[]{:S(2)}, u32[]{:S(2)}) collective-permute-start(f32[96,256]{1,0:T(8,128)S(1)} %get-tuple-element.14), channel_id=1, source_target_pairs={{0,3},{1,2},{2,5},{3,4},{4,7},{5,6},{6,9},{7,8},{8,11},{9,10},{10,... | collective-permute-start | bytes 294920 | tf_op jit(solution)/shard_map/ppermute | solution.py:347
  5.3 1.5 %collective-permute-start = (f32[96,256]{1,0:T(8,128)S(1)}, f32[96,256]{1,0:T(8,128)S(1)}, u32[]{:S(2)}, u32[]{:S(2)}) collective-permute-start(f32[96,256]{1,0:T(8,128)S(1)} %get-tuple-element.14), channel_id=1, source_target_pairs={{0,2},{1,3},{2,4},{3,5},{4,6},{5,7},{6,8},{7,9},{8,10},{9,11},{10,... | collective-permute-start | bytes 294920 | tf_op jit(solution)/shard_map/ppermute | solution.py:345
  6.8 2.5 %collective-permute-start.3 = (f32[96,256]{1,0:T(8,128)S(1)}, f32[96,256]{1,0:T(8,128)S(1)}, u32[]{:S(2)}, u32[]{:S(2)}) collective-permute-start(f32[96,256]{1,0:T(8,128)S(1)} %get-tuple-element.15), channel_id=1, source_target_pairs={{0,15},{1,14},{2,1},{3,0},{4,3},{5,2},{6,5},{7,4},{8,7},{9,6},{10,... | collective-permute-start | bytes 294920 | tf_op jit(solution)/shard_map/ppermute | solution.py:348
  9.3 0.8 %collective-permute-start.2 = (f32[96,256]{1,0:T(8,128)S(1)}, f32[96,256]{1,0:T(8,128)S(1)}, u32[]{:S(2)}, u32[]{:S(2)}) collective-permute-start(f32[96,256]{1,0:T(8,128)S(1)} %get-tuple-element.15), channel_id=1, source_target_pairs={{0,14},{1,15},{2,0},{3,1},{4,2},{5,3},{6,4},{7,5},{8,6},{9,7},{10,... | collective-permute-start | bytes 294920 | tf_op jit(solution)/shard_map/ppermute | solution.py:346
  10.1 0.0 collective-permute-done.4.other
  10.1 0.0 copy-done.1
  10.1 6.4 %shard_map.42 = (f32[12,7,32,64]{3,2,1,0:T(8,128)}, f32[12,7,32,64]{3,2,1,0:T(8,128)}, f32[256,256]{1,0:T(8,128)S(1)}, f32[192,256]{1,0:T(8,128)S(1)}, bf16[2,19...) custom-call(f32[12,7,32,64]{3,2,1,0:T(8,128)S(1)} %copy-done, ...), custom_call_target="tpu_custom_call" | custom-call | flops 1610612736 | bytes 6291456 | tf_op jit(solution)/shard_map/pallas_call | solution.py:358
  16.5 0.0 collective-permute-done.1.low_other
  16.5 0.0 collective-permute-done.low_own
  16.5 0.0 collective-permute-done.3.high_other
  16.6 1.4 %collective-permute-done.2.high_own = f32[96,256]{1,0:T(8,128)S(1)} collective-permute-done((f32[96,256]{1,0:T(8,128)S(1)}, f32[96,256]{1,0:T(8,128)S(1)}, u32[]{:S(2)}, u32[]{:S(2)}) %collective-permute-start.2) | collective-permute-done | bytes 98336 | tf_op jit(solution)/shard_map/ppermute | solution.py:346
  18.0 4.6 %shard_map.43 = (f32[12,7,32,64]{3,2,1,0:T(8,128)}, f32[12,7,32,64]{3,2,1,0:T(8,128)}) custom-call(f32[96,256]{1,0:T(8,128)S(1)} %collective-permute-done.low_own, f32[96,256]{1,0:T(8,128)S(1)} %collective-permute-done.1.low_other, f32[96,256]{1,0:T(8,128)S(1)} %collective-permute-done.2.high_own, ...), custom_call_target="tpu_custom_call", output_to_operand_aliasing={{0}: (13, {}), {1}: (14, {})} | custom-call | flops 402653184 | bytes 2097152 | tf_op jit(solution)/shard_map/pallas_call | solution.py:376
Async XLA Ops:
  0.6 9.5 %collective-permute-start.4 = (f32[12,7,32,64]{3,2,1,0:T(8,128)}, f32[12,7,32,64]{3,2,1,0:T(8,128)S(1)}, u32[]{:S(2)}, u32[]{:S(2)}) collective-permute-start(f32[12,7,32,64]{3,2,1,0:T(8,128)} %own.1), channel_id=1, source_target_pairs={{0,1},{1,0},{2,3},{3,2},{4,5},{5,4},{6,7},{7,6},{8,9},{9,8},{10,11... | collective-permute-start | bytes 2064392 | tf_op jit(solution)/shard_map/ppermute | solution.py:335
  1.1 1.3 %copy-start = (f32[12,7,32,64]{3,2,1,0:T(8,128)S(1)}, f32[12,7,32,64]{3,2,1,0:T(8,128)}, u32[]{:S(2)}) copy-start(f32[12,7,32,64]{3,2,1,0:T(8,128)} %own.1) | copy-start | bytes 2064388
  2.5 7.6 %copy-start.1 = (s32[96,7]{0,1:T(8,128)S(1)}, s32[96,7]{0,1:T(8,128)}, u32[]{:S(2)}) copy-start(s32[96,7]{0,1:T(8,128)} %param.3) | copy-start | bytes 8068
  2.6 13.9 %collective-permute-start.1 = (f32[96,256]{1,0:T(8,128)S(1)}, f32[96,256]{1,0:T(8,128)S(1)}, u32[]{:S(2)}, u32[]{:S(2)}) collective-permute-start(f32[96,256]{1,0:T(8,128)S(1)} %get-tuple-element.14), channel_id=1, source_target_pairs={{0,3},{1,2},{2,5},{3,4},{4,7},{5,6},{6,9},{7,8},{8,11},{9,10},{10,... | collective-permute-start | bytes 294920 | tf_op jit(solution)/shard_map/ppermute | solution.py:347
  5.3 11.3 %collective-permute-start = (f32[96,256]{1,0:T(8,128)S(1)}, f32[96,256]{1,0:T(8,128)S(1)}, u32[]{:S(2)}, u32[]{:S(2)}) collective-permute-start(f32[96,256]{1,0:T(8,128)S(1)} %get-tuple-element.14), channel_id=1, source_target_pairs={{0,2},{1,3},{2,4},{3,5},{4,6},{5,7},{6,8},{7,9},{8,10},{9,11},{10,... | collective-permute-start | bytes 294920 | tf_op jit(solution)/shard_map/ppermute | solution.py:345
  6.8 9.7 %collective-permute-start.3 = (f32[96,256]{1,0:T(8,128)S(1)}, f32[96,256]{1,0:T(8,128)S(1)}, u32[]{:S(2)}, u32[]{:S(2)}) collective-permute-start(f32[96,256]{1,0:T(8,128)S(1)} %get-tuple-element.15), channel_id=1, source_target_pairs={{0,15},{1,14},{2,1},{3,0},{4,3},{5,2},{6,5},{7,4},{8,7},{9,6},{10,... | collective-permute-start | bytes 294920 | tf_op jit(solution)/shard_map/ppermute | solution.py:348
  9.3 8.6 %collective-permute-start.2 = (f32[96,256]{1,0:T(8,128)S(1)}, f32[96,256]{1,0:T(8,128)S(1)}, u32[]{:S(2)}, u32[]{:S(2)}) collective-permute-start(f32[96,256]{1,0:T(8,128)S(1)} %get-tuple-element.15), channel_id=1, source_target_pairs={{0,14},{1,15},{2,0},{3,1},{4,2},{5,3},{6,4},{7,5},{8,6},{9,7},{10,... | collective-permute-start | bytes 294920 | tf_op jit(solution)/shard_map/ppermute | solution.py:346

commit v2 on v1

--- a/solution.py
+++ b/solution.py
@@ -38,20 +38,40 @@
     return line
 
 
-def edge_kernel(top, bottom, to_left, to_right):
-    for s in range(REACH):
-        rows = slice(s * HALF, (s + 1) * HALF)
-        for t in range(2):
-            lanes = slice(t * 2 * BS, (t + 1) * 2 * BS)
-            to_left[rows, lanes] = jnp.concatenate(
-                [top[s, REACH + 2 * t], top[s, REACH + 2 * t + 1]], axis=1
+def edge_kernel(matrix, to_left, to_right, blocks, sems):
+    count = matrix.shape[0]
+    loads = [
+        pltpu.make_async_copy(source, blocks.at[i], sems.at[i])
+        for i, source in enumerate(
+            (
+                matrix.at[pl.ds(0, REACH), pl.ds(REACH, REACH + 1)],
+                matrix.at[pl.ds(count - REACH, REACH), pl.ds(0, REACH + 1)],
             )
-            to_right[rows, lanes] = jnp.concatenate([bottom[s, 2 * t], bottom[s, 2 * t + 1]], axis=1)
+        )
+    ]
+    for load in loads:
+        load.start()
+    for i, target in enumerate((to_left, to_right)):
+        loads[i].wait()
+        for s in range(REACH):
+            for t in range(2):
+                target[s * HALF : (s + 1) * HALF, t * 2 * BS : (t + 1) * 2 * BS] = jnp.concatenate(
+                    [blocks[i, s, 2 * t], blocks[i, s, 2 * t + 1]], axis=1
+                )
+
+
+def span_of(a, count, is_square):
+    if a < REACH:
+        return (REACH - a if is_square else 2 * REACH - a), SPAN
+    s = a - (count - REACH)
+    if s >= 0:
+        return 0, (2 * REACH - s if is_square else REACH - s)
+    return 0, SPAN
 
 
 def interior_kernel(
-    own, other, pat, square, sign, low_a, low_b, low_m, low_p, high_a, high_b, high_m, high_p,
-    full, mine, tile, keep, *, axes, half_axis
+    own, other, pat, square_out, sign_out, seed, low_a, low_b, low_m, low_p, high_a, high_b,
+    high_m, high_p, square, sign, full, mine, tile, keep, sems, *, axes, half_axis
 ):
     count = own.shape[0]
     total = pat.shape[1]
@@ -119,10 +139,25 @@
                 k = t + GROUP * delta - s + REACH
                 if 0 <= k < SPAN:
                     a = g * GROUP + s
-                    sign[a, k] = 1.5 * own[a, k] - part[:, t * BS : (t + 1) * BS]
-
-    diag = []
-    upper = []
+                    k0, k1 = span_of(a, count, False)
+                    value_k = 1.5 * own[a, k] - part[:, t * BS : (t + 1) * BS]
+                    if k0 <= k < k1:
+                        sign[a, k] = value_k
+                    else:
+                        side = 0 if a < REACH else 1
+                        seed[side, a - side * (count - REACH), k] = value_k
+
+    stores = []
+
+    def send_rows(g, i, source, target):
+        for a in range(g * GROUP, (g + 1) * GROUP):
+            k0, k1 = span_of(a, count, i == 0)
+            store = pltpu.make_async_copy(
+                source.at[a, pl.ds(k0, k1 - k0)], target.at[a, pl.ds(k0, k1 - k0)], sems.at[i, a]
+            )
+            store.start()
+            stores.append(store)
+
     for g in range(groups):
         r = panel(full, g, 0, 3)
         value = masked(g, 0, dot3(r, r, True))
@@ -135,6 +170,7 @@
             emit_square(g + 1, -1, value.T)
             for p, part in enumerate(split(value)):
                 keep[p, 2 * g + 1] = part
+        send_rows(g, 0, square, square_out)
 
     def kept(i):
         return [keep[p, i] for p in range(2)]
@@ -151,10 +187,12 @@
             centre = centre + dot3(high, kept(2 * g + 1), True)
             emit_sign(g, 1, dot3(mid, kept(2 * g + 1), False) + dot3(high, kept(2 * g + 2), True))
         emit_sign(g, 0, centre)
+        send_rows(g, 1, sign, sign_out)
     for s in range(REACH):
         for t in range(REACH - s):
-            sign[s, t] = 1.5 * own[s, t]
-            sign[count - 1 - s, SPAN - 1 - t] = 1.5 * own[count - 1 - s, SPAN - 1 - t]
+            seed[0, s, t] = 1.5 * own[s, t]
+            k = SPAN - 1 - t
+            seed[1, REACH - 1 - s, k] = 1.5 * own[count - 1 - s, k]
 
     last = groups - 1
     for a_ref, b_ref, m_ref, p_ref, g, part, r0 in (
@@ -165,16 +203,18 @@
         out = panel(full, g, part, part + 1)
         turned = [x.astype(F32).T.astype(BF) for x in out]
         a_ref[...] = dot3(turned, turned, True)
-        b_ref[...] = dot3(panel(full, g, 1, 2), turned, True)[rows]
+        b_ref[...] = dot3(panel(full, g, 1, 2, r0, r0 + REACH * BS), turned, True)
         for p in range(2):
             m_ref[p] = out[p][rows]
             p_ref[p, 0] = mine[p, g, r0 // 2 : r0 // 2 + REACH * HALF, part * WIDE : (part + 1) * WIDE]
             p_ref[p, 1] = mine[p, g, r0 // 2 : r0 // 2 + REACH * HALF, WIDE : 2 * WIDE]
+    for store in stores:
+        store.wait()
 
 
 def border_kernel(
-    low_own, low_other, high_own, high_other, pat, low_a, low_b, low_m, low_p, high_a, high_b,
-    high_m, high_p, square_in, sign_in, square_out, sign_out, near, halo, tile, keep, blocks, sems,
+    low_own, low_other, high_own, high_other, pat, seed, low_a, low_b, low_m, low_p, high_a, high_b,
+    high_m, high_p, square_in, sign_in, square_out, sign_out, near, halo, tile, blocks, sems,
     *, axes, half_axis
 ):
     count = square_in.shape[0]
@@ -183,18 +223,6 @@
     own_at = lax.axis_index(half_axis) * HALF
     other_at = HALF - own_at
     ends = (0, count - REACH)
-    loads = [
-        pltpu.make_async_copy(ref.at[pl.ds(ends[side], REACH)], blocks.at[i, side], sems.at[i, side])
-        for i, ref in enumerate((square_in, sign_in))
-        for side in range(2)
-    ]
-    for load in loads:
-        load.start()
-
-    def put(p, rows, lanes, value):
-        for q, part in enumerate(split(value)):
-            halo[q, rows, lanes] = part
-
     def sides(side):
         return (
             (low_own, low_other, low_a, low_b, low_m, low_p)
@@ -202,7 +230,6 @@
             else (high_own, high_other, high_a, high_b, high_m, high_p)
         )
 
-    squares = []
     for side in range(2):
         mine, theirs, a_ref, b_ref, m_ref, p_ref = sides(side)
         for p in range(REACH):
@@ -226,10 +253,7 @@
                 value = jnp.concatenate([block(p, c) for c in cs], axis=1)
                 for q, part in enumerate(split(value)):
                     halo[side, q, p * BS : (p + 1) * BS, t * 2 * BS : (t + 1) * 2 * BS] = part
-    for load in loads:
-        load.wait()
-
-    lane = lax.broadcasted_iota(jnp.int32, (1, WIDE), 1)
+    stores = []
     for side in range(2):
         mine, theirs, a_ref, b_ref, m_ref, p_ref = sides(side)
         shift = 1 if side == 0 else 0
@@ -290,17 +314,20 @@
                 lanes = slice(t * BS, (t + 1) * BS)
                 if 0 <= k < SPAN:
                     blocks[0, side, s, k] = part[:, lanes]
-                    blocks[1, side, s, k] = blocks[1, side, s, k] - far[:, lanes]
+                    blocks[1, side, s, k] = seed[side, s, k] - far[:, lanes]
                 k = t - s + REACH
-                blocks[1, side, s, k] = blocks[1, side, s, k] - close[:, lanes]
-
-    stores = [
-        pltpu.make_async_copy(blocks.at[i, side], ref.at[pl.ds(ends[side], REACH)], sems.at[i, side])
-        for i, ref in enumerate((square_out, sign_out))
-        for side in range(2)
-    ]
-    for store in stores:
-        store.start()
+                blocks[1, side, s, k] = seed[side, s, k] - close[:, lanes]
+            a = ends[side] + s
+            for i, ref in enumerate((square_out, sign_out)):
+                k0, k1 = span_of(a, count, i == 0)
+                k0, k1 = (0, k0) if side == 0 else (k1, SPAN)
+                store = pltpu.make_async_copy(
+                    blocks.at[i, side, s, pl.ds(k0, k1 - k0)],
+                    ref.at[a, pl.ds(k0, k1 - k0)],
+                    sems.at[i, side, s],
+                )
+                store.start()
+                stores.append(store)
     for store in stores:
         store.wait()
 
@@ -311,41 +338,33 @@
     flags = pattern.T
     vmem = pl.BlockSpec(memory_space=pltpu.VMEM)
     smem = pl.BlockSpec(memory_space=pltpu.SMEM)
-    anywhere = pl.BlockSpec(memory_space=pl.ANY)
+    hbm = pl.BlockSpec(memory_space=pltpu.HBM)
     params = pltpu.CompilerParams(vmem_limit_bytes=LIMIT)
 
     edge = jax.ShapeDtypeStruct((REACH * HALF, (REACH + 1) * BS), F32)
-    ends = count // REACH - 1
     to_left, to_right = pl.pallas_call(
         edge_kernel,
-        grid=(1,),
         out_shape=(edge, edge),
-        in_specs=[
-            pl.BlockSpec((REACH, SPAN, HALF, BS), lambda i: (0, 0, 0, 0)),
-            pl.BlockSpec((REACH, SPAN, HALF, BS), lambda i: (ends, 0, 0, 0)),
+        in_specs=[hbm],
+        out_specs=[vmem] * 2,
+        scratch_shapes=[
+            pltpu.VMEM((2, REACH, REACH + 1, HALF, BS), F32),
+            pltpu.SemaphoreType.DMA((2,)),
         ],
-        out_specs=[pl.BlockSpec(edge.shape, lambda i: (0, 0))] * 2,
         compiler_params=params,
-    )(matrix, matrix)
+    )(matrix)
 
     size = 1
     for axis in axes:
         size *= lax.axis_size(axis)
     swap = [(0, 1), (1, 0)]
     other = lax.ppermute(matrix, half_axis, swap)
-    ring = axes + (half_axis,)
-
-    def around(step, cross):
-        return [
-            (2 * i + r, 2 * ((i + step) % size) + (1 - r if cross else r))
-            for i in range(size)
-            for r in range(2)
-        ]
-
-    low_own = lax.ppermute(to_right, ring, around(1, False))
-    high_own = lax.ppermute(to_left, ring, around(-1, False))
-    low_other = lax.ppermute(to_right, ring, around(1, True))
-    high_other = lax.ppermute(to_left, ring, around(-1, True))
+    forward = [(i, (i + 1) % size) for i in range(size)]
+    backward = [(target, source) for source, target in forward]
+    low_own = lax.ppermute(to_right, axes, forward)
+    high_own = lax.ppermute(to_left, axes, backward)
+    low_other = lax.ppermute(low_own, half_axis, swap)
+    high_other = lax.ppermute(high_own, half_axis, swap)
 
     names = dict(axes=axes, half_axis=half_axis)
     ends_out = [
@@ -355,16 +374,20 @@
         jax.ShapeDtypeStruct((2, 2, REACH * HALF, WIDE), BF),
     ] * 2
     band = jax.ShapeDtypeStruct(matrix.shape, F32)
+    seed = jax.ShapeDtypeStruct((2, REACH, SPAN, HALF, BS), F32)
     square, sign, *inside = pl.pallas_call(
         functools.partial(interior_kernel, **names),
-        out_shape=[band, band] + ends_out,
+        out_shape=[band, band, seed] + ends_out,
         in_specs=[vmem, vmem, smem],
-        out_specs=[vmem] * 10,
+        out_specs=[hbm] * 2 + [vmem] * 9,
         scratch_shapes=[
+            pltpu.VMEM(matrix.shape, F32),
+            pltpu.VMEM(matrix.shape, F32),
             pltpu.VMEM((2, groups, WIDE, 3 * WIDE), BF),
             pltpu.VMEM((2, groups, GROUP * HALF, 3 * WIDE), BF),
             pltpu.VMEM((WIDE, WIDE), F32),
             pltpu.VMEM((2, 2 * groups - 1, WIDE, WIDE), BF),
+            pltpu.SemaphoreType.DMA((2, count)),
         ],
         compiler_params=params,
         cost_estimate=pl.CostEstimate(
@@ -376,17 +399,16 @@
         pl.pallas_call(
             functools.partial(border_kernel, **names),
             out_shape=(band, band),
-            in_specs=[vmem] * 4 + [smem] + [vmem] * 8 + [anywhere] * 2,
-            out_specs=[anywhere] * 2,
+            in_specs=[vmem] * 4 + [smem] + [vmem] * 9 + [hbm] * 2,
+            out_specs=[hbm] * 2,
             scratch_shapes=[
                 pltpu.VMEM((2, REACH * BS, WIDE), F32),
                 pltpu.VMEM((2, 2, REACH * BS, 2 * WIDE), BF),
                 pltpu.VMEM((2, REACH * BS, REACH * BS), F32),
-                pltpu.VMEM((8, 128), F32),
                 pltpu.VMEM((2, 2, REACH, SPAN, HALF, BS), F32),
-                pltpu.SemaphoreType.DMA((2, 2)),
+                pltpu.SemaphoreType.DMA((2, 2, REACH)),
             ],
-            input_output_aliases={13: 0, 14: 1},
+            input_output_aliases={14: 0, 15: 1},
             compiler_params=params,
             cost_estimate=pl.CostEstimate(
                 flops=3 * 2 * 4 * WIDE**3, bytes_accessed=2 * 2**20, transcendentals=0

time: 22.8 us -> 21.9 us (0.961)
  waiting for transfers between devices: 1.43 us -> 3.92 us
  starting transfers between devices: 8.02 us -> 6.27 us
  Pallas kernels: 11.2 us -> 9.58 us
    ppermute x4, waiting for transfers between devices: 1.43 us -> 3.92 us  [the longest x1 3.5 us: shards(): low_own = lax.ppermute(to_right, axes, forward)]
    ppermute x4, starting transfers between devices: 7.5 us -> 5.75 us  [the longest x1 3.1 us: shards(): high_own = lax.ppermute(to_left, axes, backward)]
    pallas_call x1, Pallas kernels: 4.65 us -> 3.27 us  [shards(): pl.pallas_call(functools.partial(border_kernel, **names), out_shape=(band...]
    pallas_call x1, Pallas kernels: 6.42 us -> 5.95 us  [shards(): pl.pallas_call(functools.partial(interior_kernel, **names), out_shape=[ba...]
    pallas_call x1, Pallas kernels: 0.11 us -> 0.36 us  [shards(): pl.pallas_call(edge_kernel, out_shape=(edge, edge), in_specs=[hbm], out_s...]
  transfers between devices with their start and end apart: 5 -> 5, of which waited for: 1 -> 2; matrix products, arithmetic and copies ran while one was open for 0% -> 0% of each run, Pallas kernels for 29% -> 29%
where the time goes in v2:
time: 21.9 us; the launch traced here: 21.8 us
  Pallas kernels  9.58 us (44%)
  starting transfers between devices  6.27 us (29%)
  waiting for transfers between devices  3.92 us (18%)
  local copies, waits for them, and re-layouts  1.34 us (6%)
  between operations  0.67 us (3%)
    pallas_call x1, Pallas kernels, shards(): pl.pallas_call(functools.partial(interior_kernel, **names), out_shape=[ba...  5.95 us
    ppermute x1, waiting for transfers between devices, shards(): low_own = lax.ppermute(to_right, axes, forward)  3.5 us
    pallas_call x1, Pallas kernels, shards(): pl.pallas_call(functools.partial(border_kernel, **names), out_shape=(band...  3.27 us
    ppermute x1, starting transfers between devices, shards(): high_own = lax.ppermute(to_left, axes, backward)  3.1 us
    ppermute x1, starting transfers between devices, shards(): low_own = lax.ppermute(to_right, axes, forward)  2.55 us
    unnamed x4, local copies, waits for them, and re-layouts  1.34 us
    ppermute x1, starting transfers between devices, shards(): other = lax.ppermute(matrix, half_axis, swap)  0.52 us
  transfers between devices with their start and end apart: 5, of which 2 were waited for; matrix products, arithmetic and copies ran while one was open for 0% of the time, Pallas kernels for 29%

profile of v2, /device:TPU:0, one launch (start us, length us, event | category | flops | bytes accessed | tf_op | source)
XLA Modules:
  0.0 21.8 jit_solution(14431824184702471523)
XLA Ops:
  0.6 0.5 %collective-permute-start.4 = (f32[12,7,32,64]{3,2,1,0:T(8,128)}, f32[12,7,32,64]{3,2,1,0:T(8,128)S(1)}, u32[]{:S(2)}, u32[]{:S(2)}) collective-permute-start(f32[12,7,32,64]{3,2,1,0:T(8,128)} %own.1), channel_id=1, source_target_pairs={{0,1},{1,0},{2,3},{3,2},{4,5},{5,4},{6,7},{7,6},{8,9},{9,8},{10,11... | collective-permute-start | bytes 2064392 | tf_op jit(solution)/shard_map/ppermute | solution.py:361
  1.1 0.0 copy-start
  1.1 1.3 %copy-done = f32[12,7,32,64]{3,2,1,0:T(8,128)S(1)} copy-done((f32[12,7,32,64]{3,2,1,0:T(8,128)S(1)}, f32[12,7,32,64]{3,2,1,0:T(8,128)}, u32[]{:S(2)}) %copy-start) | copy-done | bytes 688152
  2.5 0.0 copy-start.1
  2.5 0.4 %shard_map.41 = (f32[96,256]{1,0:T(8,128)S(1)}, f32[96,256]{1,0:T(8,128)S(1)}) custom-call(f32[12,7,32,64]{3,2,1,0:T(8,128)S(1)} %copy-done), custom_call_target="tpu_custom_call" | custom-call | tf_op jit(solution)/shard_map/pallas_call | solution.py:345
  2.9 2.6 %collective-permute-start = (f32[96,256]{1,0:T(8,128)S(1)}, f32[96,256]{1,0:T(8,128)S(1)}, u32[]{:S(2)}, u32[]{:S(2)}) collective-permute-start(f32[96,256]{1,0:T(8,128)S(1)} %get-tuple-element.15), channel_id=1, source_target_pairs={{0,2},{2,4},{4,6},{6,8},{8,10},{10,12},{12,14},{14,0},{1,3},{3,5},... | collective-permute-start | bytes 294920 | tf_op jit(solution)/shard_map/ppermute | solution.py:364
  5.4 3.1 %collective-permute-start.2 = (f32[96,256]{1,0:T(8,128)S(1)}, f32[96,256]{1,0:T(8,128)S(1)}, u32[]{:S(2)}, u32[]{:S(2)}) collective-permute-start(f32[96,256]{1,0:T(8,128)S(1)} %get-tuple-element.16), channel_id=1, source_target_pairs={{2,0},{4,2},{6,4},{8,6},{10,8},{12,10},{14,12},{0,14},{3,1},{5,3},... | collective-permute-start | bytes 294920 | tf_op jit(solution)/shard_map/ppermute | solution.py:365
  8.5 3.5 %collective-permute-done.low_own = f32[96,256]{1,0:T(8,128)S(1)} collective-permute-done((f32[96,256]{1,0:T(8,128)S(1)}, f32[96,256]{1,0:T(8,128)S(1)}, u32[]{:S(2)}, u32[]{:S(2)}) %collective-permute-start) | collective-permute-done | bytes 98336 | tf_op jit(solution)/shard_map/ppermute | solution.py:364
  12.0 0.0 collective-permute-start.1
  12.0 0.4 %collective-permute-done.2.high_own = f32[96,256]{1,0:T(8,128)S(1)} collective-permute-done((f32[96,256]{1,0:T(8,128)S(1)}, f32[96,256]{1,0:T(8,128)S(1)}, u32[]{:S(2)}, u32[]{:S(2)}) %collective-permute-start.2) | collective-permute-done | bytes 98336 | tf_op jit(solution)/shard_map/ppermute | solution.py:365
  12.4 0.1 collective-permute-start.3
  12.5 0.0 collective-permute-done.4.other
  12.5 0.0 copy-done.1
  12.5 5.9 %shard_map.42 = (f32[12,7,32,64]{3,2,1,0:T(8,128)}, f32[12,7,32,64]{3,2,1,0:T(8,128)}, f32[2,3,7,32,64]{4,3,2,1,0:T(8,128)S(1)}, f32[256,256]{1,0:T(8,128)S(1)},...) custom-call(f32[12,7,32,64]{3,2,1,0:T(8,128)S(1)} %copy-done, ...), custom_call_target="tpu_custom_call" | custom-call | flops 1610612736 | bytes 6291456 | tf_op jit(solution)/shard_map/pallas_call | solution.py:378
  18.5 0.0 collective-permute-done.1.low_other
  18.5 0.0 collective-permute-done.3.high_other
  18.5 3.3 %shard_map.43 = (f32[12,7,32,64]{3,2,1,0:T(8,128)}, f32[12,7,32,64]{3,2,1,0:T(8,128)}) custom-call(f32[96,256]{1,0:T(8,128)S(1)} %collective-permute-done.low_own, f32[96,256]{1,0:T(8,128)S(1)} %collective-permute-done.1.low_other, f32[96,256]{1,0:T(8,128)S(1)} %collective-permute-done.2.high_own, ...), custom_call_target="tpu_custom_call", output_to_operand_aliasing={{0}: (14, {}), {1}: (15, {})} | custom-call | flops 402653184 | bytes 2097152 | tf_op jit(solution)/shard_map/pallas_call | solution.py:399
Async XLA Ops:
  0.6 11.9 %collective-permute-start.4 = (f32[12,7,32,64]{3,2,1,0:T(8,128)}, f32[12,7,32,64]{3,2,1,0:T(8,128)S(1)}, u32[]{:S(2)}, u32[]{:S(2)}) collective-permute-start(f32[12,7,32,64]{3,2,1,0:T(8,128)} %own.1), channel_id=1, source_target_pairs={{0,1},{1,0},{2,3},{3,2},{4,5},{5,4},{6,7},{7,6},{8,9},{9,8},{10,11... | collective-permute-start | bytes 2064392 | tf_op jit(solution)/shard_map/ppermute | solution.py:361
  1.1 1.3 %copy-start = (f32[12,7,32,64]{3,2,1,0:T(8,128)S(1)}, f32[12,7,32,64]{3,2,1,0:T(8,128)}, u32[]{:S(2)}) copy-start(f32[12,7,32,64]{3,2,1,0:T(8,128)} %own.1) | copy-start | bytes 2064388
  2.5 10.0 %copy-start.1 = (s32[96,7]{0,1:T(8,128)S(1)}, s32[96,7]{0,1:T(8,128)}, u32[]{:S(2)}) copy-start(s32[96,7]{0,1:T(8,128)} %param.3) | copy-start | bytes 8068
  2.9 9.2 %collective-permute-start = (f32[96,256]{1,0:T(8,128)S(1)}, f32[96,256]{1,0:T(8,128)S(1)}, u32[]{:S(2)}, u32[]{:S(2)}) collective-permute-start(f32[96,256]{1,0:T(8,128)S(1)} %get-tuple-element.15), channel_id=1, source_target_pairs={{0,2},{2,4},{4,6},{6,8},{8,10},{10,12},{12,14},{14,0},{1,3},{3,5},... | collective-permute-start | bytes 294920 | tf_op jit(solution)/shard_map/ppermute | solution.py:364
  5.4 7.0 %collective-permute-start.2 = (f32[96,256]{1,0:T(8,128)S(1)}, f32[96,256]{1,0:T(8,128)S(1)}, u32[]{:S(2)}, u32[]{:S(2)}) collective-permute-start(f32[96,256]{1,0:T(8,128)S(1)} %get-tuple-element.16), channel_id=1, source_target_pairs={{2,0},{4,2},{6,4},{8,6},{10,8},{12,10},{14,12},{0,14},{3,1},{5,3},... | collective-permute-start | bytes 294920 | tf_op jit(solution)/shard_map/ppermute | solution.py:365
  12.0 6.5 %collective-permute-start.1 = (f32[96,256]{1,0:T(8,128)S(1)}, f32[96,256]{1,0:T(8,128)S(1)}, u32[]{:S(2)}, u32[]{:S(2)}) collective-permute-start(f32[96,256]{1,0:T(8,128)S(1)} %collective-permute-done.low_own), channel_id=1, source_target_pairs={{0,1},{1,0},{2,3},{3,2},{4,5},{5,4},{6,7},{7,6},{8,9},{9,8},{10,11... | collective-permute-start | bytes 294920 | tf_op jit(solution)/shard_map/ppermute | solution.py:366
  12.4 6.1 %collective-permute-start.3 = (f32[96,256]{1,0:T(8,128)S(1)}, f32[96,256]{1,0:T(8,128)S(1)}, u32[]{:S(2)}, u32[]{:S(2)}) collective-permute-start(f32[96,256]{1,0:T(8,128)S(1)} %collective-permute-done.2.high_own), channel_id=1, source_target_pairs={{0,1},{1,0},{2,3},{3,2},{4,5},{5,4},{6,7},{7,6},{8,9},{9,8},{10,11... | collective-permute-start | bytes 294920 | tf_op jit(solution)/shard_map/ppermute | solution.py:367

commit v3 on v0

v3 whole, which is shorter than its diff:
```python
import functools

import jax
import jax.numpy as jnp
from jax import lax
from jax.experimental import pallas as pl
from jax.experimental.pallas import tpu as pltpu
from jax.sharding import PartitionSpec as P

REACH = 3
SPAN = 7
BS = 64
HALF = 32
GROUP = 4
WIDE = GROUP * BS
BF = jnp.bfloat16
F32 = jnp.float32
LIMIT = 32 * 1024 * 1024
EDGE_LIMIT = 58 * 1024 * 1024


def split(x):
    hi = x.astype(BF)
    return hi, (x - hi.astype(F32)).astype(BF)


def product(pairs, transposed=False):
    side = 1 if transposed else 0
    left = [x for a, _ in pairs for x in (a[0], a[0], a[1])]
    right = [x for _, b in pairs for x in (b[0], b[1], b[0])]
    return lax.dot_general(
        jnp.concatenate(left, axis=1),
        jnp.concatenate(right, axis=side),
        (((1,), (side,)), ((), ())),
        preferred_element_type=F32,
    )


def turn(x):
    return split((x[0].astype(F32) + x[1].astype(F32)).T)


def flag_line(pat, row, places):
    lane = lax.broadcasted_iota(jnp.int32, (1, WIDE), 1)
    line = jnp.zeros((1, WIDE), F32)
    for place, k in places:
        if 0 <= k < SPAN:
            value = pat[k, row].astype(F32)
            line = jnp.where((lane >= place * BS) & (lane < (place + 1) * BS), value, line)
    return line


def span_of(a, count, is_square):
    if a < REACH:
        return (REACH - a if is_square else 2 * REACH - a), SPAN
    s = a - (count - REACH)
    if s >= 0:
        return 0, (2 * REACH - s if is_square else REACH - s)
    return 0, SPAN


def edge_kernel(matrix, to_left, to_right, blocks, sems):
    count = matrix.shape[0]
    loads = [
        pltpu.make_async_copy(source, blocks.at[i], sems.at[i])
        for i, source in enumerate(
            (
                matrix.at[pl.ds(0, REACH), pl.ds(REACH, REACH + 1)],
                matrix.at[pl.ds(count - REACH, REACH), pl.ds(0, REACH + 1)],
            )
        )
    ]
    for load in loads:
        load.start()
    for i, target in enumerate((to_left, to_right)):
        loads[i].wait()
        for s in range(REACH):
            for t in range(2):
                target[s * HALF : (s + 1) * HALF, t * 2 * BS : (t + 1) * 2 * BS] = jnp.concatenate(
                    [blocks[i, s, 2 * t], blocks[i, s, 2 * t + 1]], axis=1
                )


class Interior:
    def __init__(self, own, pat, full, mine, keep, axes):
        self.own = own
        self.pat = pat
        self.full = full
        self.mine = mine
        self.keep = keep
        self.count = own.shape[0]
        self.groups = self.count // GROUP
        self.first = lax.axis_index(axes) * self.count
        self.lines = {}
        self.stores = []

    def flags(self, g, s, delta):
        if (g, s, delta) not in self.lines:
            row = lax.rem(self.first + g * GROUP + s, self.pat.shape[1])
            places = [(t, t + GROUP * delta - s + REACH) for t in range(GROUP)]
            self.lines[g, s, delta] = flag_line(self.pat, row, places)
        return self.lines[g, s, delta]

    def part(self, g, h, rows=slice(None)):
        at = (h - g + 1) * WIDE
        return [self.full[p, g, rows, at : at + WIDE] for p in range(2)]

    def my_part(self, g, h):
        at = (h - g + 1) * WIDE
        return [self.mine[p, g, :, at : at + WIDE] for p in range(2)]

    def tile(self, g, h):
        return 3 * g + h - g + 1

    def kept(self, g, h):
        return [self.keep[p, self.tile(g, h)] for p in range(2)]

    def second(self, g, sign, seed):
        near = [e for e in (g - 1, g, g + 1) if 0 <= e < self.groups]
        for h in near:
            value = product([(self.my_part(g, e), self.kept(e, h)) for e in near if abs(e - h) <= 1])
            for s in range(GROUP):
                a = g * GROUP + s
                k0, k1 = span_of(a, self.count, False)
                part = value[s * HALF : (s + 1) * HALF] * (self.flags(g, s, h - g) * 0.5)
                for t in range(GROUP):
                    k = t + GROUP * (h - g) - s + REACH
                    if 0 <= k < SPAN:
                        block = 1.5 * self.own[a, k] - part[:, t * BS : (t + 1) * BS]
                        if k0 <= k < k1:
                            sign[a - sign_first(sign, self.count, g), k] = block
                        else:
                            seed[a if a < REACH else a - (self.count - REACH), k] = block

    def far_seed(self, g, seed):
        for s in range(REACH):
            a = s if g == 0 else self.count - REACH + s
            for k in range(0, REACH - s) if g == 0 else range(2 * REACH - s, SPAN):
                seed[s, k] = 1.5 * self.own[a, k]

    def send(self, g, i, source, target, sems):
        for a in range(g * GROUP, (g + 1) * GROUP):
            k0, k1 = span_of(a, self.count, i == 0)
            store = pltpu.make_async_copy(
                source.at[a - sign_first(source, self.count, g), pl.ds(k0, k1 - k0)],
                target.at[a, pl.ds(k0, k1 - k0)],
                sems.at[i, a],
            )
            store.start()
            self.stores.append(store)

    def finish(self):
        for store in self.stores:
            store.wait()


def sign_first(ref, count, g):
    return 0 if ref.shape[0] == count else g * GROUP


def first_kernel(
    own, other, pat, square_out, sign_out, seed, full, mine, keep, square, sign, sems, *, axes,
    half_axis
):
    it = Interior(own, pat, full, mine, keep, axes)
    groups = it.groups
    upper_half = lax.axis_index(half_axis) == 1

    def build(g):
        for s in range(GROUP):
            a = g * GROUP + s
            for t in range(3 * GROUP // 2):
                ks = [2 * t + e - s - 1 for e in range(2)]
                lanes = slice(t * 2 * BS, (t + 1) * 2 * BS)
                rows = slice(s * BS, (s + 1) * BS)
                mine_rows = slice(s * HALF, (s + 1) * HALF)
                if all(k < 0 or k >= SPAN for k in ks):
                    for p in range(2):
                        full[p, g, rows, lanes] = jnp.zeros((BS, 2 * BS), BF)
                        mine[p, g, mine_rows, lanes] = jnp.zeros((HALF, 2 * BS), BF)
                    continue
                two = [
                    jnp.concatenate(
                        [src[a, k] if 0 <= k < SPAN else jnp.zeros((HALF, BS), F32) for k in ks],
                        axis=1,
                    )
                    for src in (own, other)
                ]
                parts = [split(x) for x in two]
                for p in range(2):
                    mine[p, g, mine_rows, lanes] = parts[0][p]
                whole = jnp.concatenate(
                    [
                        jnp.where(upper_half, two[1], two[0]),
                        jnp.where(upper_half, two[0], two[1]),
                    ],
                    axis=0,
                )
                for p, x in enumerate(split(whole)):
                    full[p, g, rows, lanes] = x

    def emit(g, h, value):
        for s in range(GROUP):
            rows = value[s * BS : (s + 1) * BS]
            part = jnp.where(upper_half, rows[HALF:], rows[:HALF])
            for t in range(GROUP):
                k = t + GROUP * (h - g) - s + REACH
                if 0 <= k < SPAN:
                    square[g * GROUP + s, k] = part[:, t * BS : (t + 1) * BS]
        for p, x in enumerate(split(value)):
            keep[p, it.tile(g, h)] = x

    def squares(g, h):
        pairs = []
        for e in (g - 1, g, g + 1):
            if abs(e - h) <= 1:
                inside = 0 <= e < groups
                pairs.append((it.part(g, e), it.part(e, h) if inside else turn(it.part(h, e))))
        value = product(pairs)
        value = jnp.concatenate(
            [value[s * BS : (s + 1) * BS] * it.flags(g, s, h - g) for s in range(GROUP)], axis=0
        )
        emit(g, h, value)
        if h > g:
            emit(h, g, value.T)

    build(0)
    for g in range(groups):
        if g + 1 < groups:
            build(g + 1)
        squares(g, g)
        if g + 1 < groups:
            squares(g, g + 1)
        it.send(g, 0, square, square_out, sems)
        if g > 0:
            it.second(g - 1, sign, seed)
            it.send(g - 1, 1, sign, sign_out, sems)
    it.far_seed(0, seed)
    it.finish()


def last_kernel(
    own, pat, full, mine, keep, sign_in, sign_out, seed, low_a, low_b, low_m, low_p, high_a,
    high_b, high_m, high_p, sign, sems, *, axes
):
    it = Interior(own, pat, full, mine, keep, axes)
    last = it.groups - 1
    it.second(last, sign, seed)
    it.send(last, 1, sign, sign_out, sems)
    it.far_seed(last, seed)
    for a_ref, b_ref, m_ref, p_ref, g, e, r0 in (
        (low_a, low_b, low_m, low_p, 0, -1, 0),
        (high_a, high_b, high_m, high_p, last, last + 1, BS),
    ):
        rows = slice(r0, r0 + REACH * BS)
        mine_rows = slice(r0 // 2, r0 // 2 + REACH * HALF)
        out = it.part(g, e)
        turned = turn(out)
        outer = slice(BS - r0, BS - r0 + REACH * BS)
        a_ref[...] = product([([x[outer] for x in turned], out)])
        b_ref[...] = product([(it.part(g, g, rows), out)])
        for p in range(2):
            m_ref[p] = out[p][rows]
            p_ref[p, 0] = it.my_part(g, e)[p][mine_rows]
            p_ref[p, 1] = it.my_part(g, g)[p][mine_rows]
    it.finish()


def border_kernel(
    low_own, low_other, high_own, high_other, pat, low_seed, low_a, low_b, low_m, low_p, high_seed,
    high_a, high_b, high_m, high_p, square_in, sign_in, square_out, sign_out, halo, blocks, sems,
    *, axes, half_axis
):
    count = square_in.shape[0]
    total = pat.shape[1]
    first = lax.axis_index(axes) * count
    upper_half = lax.axis_index(half_axis) == 1
    ends = (0, count - REACH)
    given = (
        (low_own, low_other, low_seed, low_a, low_b, low_m, low_p),
        (high_own, high_other, high_seed, high_a, high_b, high_m, high_p),
    )
    shift = (1, 0)
    zero = jnp.zeros((BS, WIDE), F32)

    for side in range(2):
        mine, theirs = given[side][:2]
        below = REACH if side == 0 else 0
        lines = []
        for p in range(REACH):
            rows = slice(p * HALF, (p + 1) * HALF)
            lines.append(
                jnp.concatenate(
                    [
                        jnp.where(upper_half, theirs[rows, :], mine[rows, :]),
                        jnp.where(upper_half, mine[rows, :], theirs[rows, :]),
                    ],
                    axis=0,
                )
            )

        def block(p, c):
            k = c - p + below
            if 0 <= k <= REACH:
                return lines[p][:, k * BS : (k + 1) * BS]
            k = p - c + below
            if 0 <= c < REACH and 0 <= k <= REACH:
                return lines[c][:, k * BS : (k + 1) * BS].T
            return jnp.zeros((BS, BS), F32)

        base = -5 if side == 0 else 0
        for p in range(REACH):
            rows = slice((p + shift[side]) * BS, (p + shift[side] + 1) * BS)
            for t in range(4):
                value = jnp.concatenate([block(p, base + 2 * t), block(p, base + 2 * t + 1)], axis=1)
                for q, x in enumerate(split(value)):
                    halo[side, q, rows, t * 2 * BS : (t + 1) * 2 * BS] = x
        rows = slice(0, BS) if side == 0 else slice(REACH * BS, WIDE)
        for q in range(2):
            halo[side, q, rows, :] = jnp.zeros((BS, 2 * WIDE), BF)

    corners = []
    across = []
    far_lines = []
    for side in range(2):
        _, _, _, a_ref, b_ref, m_ref, _ = given[side]
        at = shift[side]
        whole = [halo[side, q] for q in range(2)]
        outer_rows = slice(at * BS, (at + REACH) * BS)
        inner = slice(WIDE, 2 * WIDE) if side == 0 else slice(0, WIDE)
        outer_first = first - REACH if side == 0 else first + count
        edge_first = first + ends[side]

        value = product([([x[outer_rows] for x in whole], whole)], True) + a_ref[...]
        rows = []
        for p in range(REACH):
            row = lax.rem(outer_first + p + total, total)
            line = flag_line(pat, row, [(t + at, t - p + REACH) for t in range(REACH)])
            rows.append(value[p * BS : (p + 1) * BS] * line)
        rows = [zero] + rows if side == 0 else rows + [zero]
        corners.append(split(jnp.concatenate(rows, axis=0)))

        value = product([([m_ref[q] for q in range(2)], [x[:, inner] for x in whole])], True)
        value = value + b_ref[...]
        rows = []
        lines = []
        for s in range(REACH):
            row = lax.rem(edge_first + s, total)
            offset = 0 if side == 0 else 2 * REACH
            line = flag_line(pat, row, [(t + at, t - s + offset) for t in range(REACH)])
            lines.append(line)
            rows.append(value[s * BS : (s + 1) * BS] * line)
            part = jnp.where(upper_half, rows[s][HALF:], rows[s][:HALF])
            for t in range(REACH):
                k = t - s + offset
                if 0 <= k < SPAN:
                    blocks[0, side, s, k] = part[:, (t + at) * BS : (t + at + 1) * BS]
        far_lines.append(lines)
        rows = rows + [zero] if side == 0 else [zero] + rows
        across.append(split(jnp.concatenate(rows, axis=0)))

    stores = []
    for side in range(2):
        seed, p_ref = given[side][2], given[side][6]
        at = shift[side]
        reach_out = [p_ref[q, 0] for q in range(2)]
        inside = [p_ref[q, 1] for q in range(2)]
        out = product([(reach_out, corners[side]), (inside, across[side])])
        back = product([(reach_out, across[side])], True)
        offset = 0 if side == 0 else 2 * REACH
        for s in range(REACH):
            a = ends[side] + s
            row = lax.rem(first + a, total)
            line = flag_line(pat, row, [(t + 1 - at, t - s + REACH) for t in range(REACH)])
            far = out[s * HALF : (s + 1) * HALF] * (far_lines[side][s] * 0.5)
            close = back[s * HALF : (s + 1) * HALF] * (line * 0.5)
            for t in range(REACH):
                k = t - s + offset
                if 0 <= k < SPAN:
                    lanes = slice((t + at) * BS, (t + at + 1) * BS)
                    blocks[1, side, s, k] = seed[s, k] - far[:, lanes]
                k = t - s + REACH
                lanes = slice((t + 1 - at) * BS, (t + 2 - at) * BS)
                blocks[1, side, s, k] = seed[s, k] - close[:, lanes]
            for i, ref in enumerate((square_out, sign_out)):
                k0, k1 = span_of(a, count, i == 0)
                k0, k1 = (0, k0) if side == 0 else (k1, SPAN)
                store = pltpu.make_async_copy(
                    blocks.at[i, side, s, pl.ds(k0, k1 - k0)],
                    ref.at[a, pl.ds(k0, k1 - k0)],
                    sems.at[i, side, s],
                )
                store.start()
                stores.append(store)
    for store in stores:
        store.wait()


def shards(matrix, pattern, *, axes, half_axis):
    count = matrix.shape[0]
    groups = count // GROUP
    flags = pattern.T
    vmem = pl.BlockSpec(memory_space=pltpu.VMEM)
    smem = pl.BlockSpec(memory_space=pltpu.SMEM)
    hbm = pl.BlockSpec(memory_space=pl.ANY)
    params = pltpu.CompilerParams(vmem_limit_bytes=LIMIT)

    edge = jax.ShapeDtypeStruct((REACH * HALF, (REACH + 1) * BS), F32)
    to_left, to_right = pl.pallas_call(
        edge_kernel,
        out_shape=(edge, edge),
        in_specs=[hbm],
        out_specs=[vmem] * 2,
        scratch_shapes=[
            pltpu.VMEM((2, REACH, REACH + 1, HALF, BS), F32),
            pltpu.SemaphoreType.DMA((2,)),
        ],
        compiler_params=pltpu.CompilerParams(vmem_limit_bytes=EDGE_LIMIT),
    )(matrix)

    size = 1
    for axis in axes:
        size *= lax.axis_size(axis)
    swap = [(0, 1), (1, 0)]
    other = lax.ppermute(matrix, half_axis, swap)
    forward = [(i, (i + 1) % size) for i in range(size)]
    backward = [(target, source) for source, target in forward]
    low_own = lax.ppermute(to_right, axes, forward)
    high_own = lax.ppermute(to_left, axes, backward)

    band = jax.ShapeDtypeStruct(matrix.shape, F32)
    seed = jax.ShapeDtypeStruct((REACH, SPAN, HALF, BS), F32)
    full = jax.ShapeDtypeStruct((2, groups, WIDE, 3 * WIDE), BF)
    mine = jax.ShapeDtypeStruct((2, groups, GROUP * HALF, 3 * WIDE), BF)
    keep = jax.ShapeDtypeStruct((2, 3 * groups, WIDE, WIDE), BF)
    square, sign, low_seed, full, mine, keep = pl.pallas_call(
        functools.partial(first_kernel, axes=axes, half_axis=half_axis),
        out_shape=[band, band, seed, full, mine, keep],
        in_specs=[vmem, vmem, smem],
        out_specs=[hbm] * 2 + [vmem] * 4,
        scratch_shapes=[
            pltpu.VMEM(matrix.shape, F32),
            pltpu.VMEM(matrix.shape, F32),
            pltpu.SemaphoreType.DMA((2, count)),
        ],
        compiler_params=params,
        cost_estimate=pl.CostEstimate(
            flops=3 * 2 * 16 * WIDE**3, bytes_accessed=16 * 2**20, transcendentals=0
        ),
    )(matrix, other, flags)

    low_own, high_own, low_seed = lax.optimization_barrier((low_own, high_own, low_seed))
    low_other = lax.ppermute(low_own, half_axis, swap)
    high_other = lax.ppermute(high_own, half_axis, swap)

    ends_out = [
        jax.ShapeDtypeStruct((REACH * BS, WIDE), F32),
        jax.ShapeDtypeStruct((REACH * BS, WIDE), F32),
        jax.ShapeDtypeStruct((2, REACH * BS, WIDE), BF),
        jax.ShapeDtypeStruct((2, 2, REACH * HALF, WIDE), BF),
    ]
    sign, high_seed, *ends = pl.pallas_call(
        functools.partial(last_kernel, axes=axes),
        out_shape=[band, seed] + ends_out * 2,
        in_specs=[vmem, smem] + [vmem] * 3 + [hbm],
        out_specs=[hbm] + [vmem] * 9,
        scratch_shapes=[
            pltpu.VMEM((GROUP, SPAN, HALF, BS), F32),
            pltpu.SemaphoreType.DMA((2, count)),
        ],
        input_output_aliases={5: 0},
        compiler_params=params,
        cost_estimate=pl.CostEstimate(
            flops=3 * 2 * 4 * WIDE**3, bytes_accessed=4 * 2**20, transcendentals=0
        ),
    )(matrix, flags, full, mine, keep, sign)

    return tuple(
        pl.pallas_call(
            functools.partial(border_kernel, axes=axes, half_axis=half_axis),
            out_shape=(band, band),
            in_specs=[vmem] * 4 + [smem] + [vmem] * 10 + [hbm] * 2,
            out_specs=[hbm] * 2,
            scratch_shapes=[
                pltpu.VMEM((2, 2, WIDE, 2 * WIDE), BF),
                pltpu.VMEM((2, 2, REACH, SPAN, HALF, BS), F32),
                pltpu.SemaphoreType.DMA((2, 2, REACH)),
            ],
            input_output_aliases={15: 0, 16: 1},
            compiler_params=params,
            cost_estimate=pl.CostEstimate(
                flops=3 * 2 * 4 * WIDE**3, bytes_accessed=2 * 2**20, transcendentals=0
            ),
        )(
            low_own, low_other, high_own, high_other, flags, low_seed, *ends[:4], high_seed,
            *ends[4:], square, sign,
        )
    )


def solution(mesh):
    band = P(("group", "row", "col"), None, "rep", None)
    return jax.shard_map(
        functools.partial(shards, axes=("row", "col"), half_axis="rep"),
        mesh=mesh,
        in_specs=(band, P("group", None)),
        out_specs=(band, band),
        check_vma=False,
    )
```

time: 150 us -> 18.9 us (0.13)
  waiting for transfers between devices: 77 us -> 0.01 us
  matrix products: 35.6 us -> 0 us
  between operations: 14.7 us -> 0.71 us
  Pallas kernels: 0 us -> 11.2 us
  local copies, waits for them, and re-layouts: 11.1 us -> 0.01 us
  starting transfers between devices: 9.63 us -> 6.84 us
  other arithmetic: 1.57 us -> 0 us
    ppermute x4 -> x5, waiting for transfers between devices: 51.3 us -> 0.01 us  [the longest x1 0.01 us: shards(): other = lax.ppermute(matrix, half_axis, swap)]
    dot_general x74 -> x0, matrix products: 35.6 us -> none  [band_product(): jnp.einsum('rij,rjl->ril', factor[:, offset], others[offset:offset + coun...]
    all_gather x2 -> x0, waiting for transfers between devices: 25.7 us -> none  [the longest x1 14.5 us: shards(): full = lax.all_gather(matrix, 'rep', axis=2, tiled=True)]
    pallas_call x0 -> x4, Pallas kernels: none -> 11.2 us  [the longest x1 4.53 us: shards(): pl.pallas_call(functools.partial(first_kernel, axes=axes, half_axis=half_...]
    unnamed x17 -> x4, local copies, waits for them, and re-layouts: 7.92 us -> 0.01 us
    slice x2 -> x0, local copies, waits for them, and re-layouts: 3.09 us -> none  [with_halo(): lax.slice_in_dim(block, 0, width, axis=dim)]
    ppermute x4 -> x5, starting transfers between devices: 9.55 us -> 6.84 us  [the longest x1 3.1 us: shards(): high_own = lax.ppermute(to_left, axes, backward)]
  transfers between devices with their start and end apart: 6 -> 5, of which waited for: 4 -> 0; matrix products, arithmetic and copies ran while one was open for 8% -> 0% of each run, Pallas kernels for 0% -> 44%
where the time goes in v3:
time: 18.9 us; the launch traced here: 18.8 us
  Pallas kernels  11.2 us (59%)
  starting transfers between devices  6.84 us (36%)
  between operations  0.71 us (4%)
    pallas_call x1, Pallas kernels, shards(): pl.pallas_call(functools.partial(first_kernel, axes=axes, half_axis=half_...  4.53 us
    ppermute x1, starting transfers between devices, shards(): high_own = lax.ppermute(to_left, axes, backward)  3.1 us
    pallas_call x1, Pallas kernels, shards(): pl.pallas_call(functools.partial(border_kernel, axes=axes, half_axis=half...  2.96 us
    ppermute x1, starting transfers between devices, shards(): low_own = lax.ppermute(to_right, axes, forward)  2.64 us
    pallas_call x1, Pallas kernels, shards(): pl.pallas_call(functools.partial(last_kernel, axes=axes), out_shape=[band...  1.97 us
    pallas_call x1, Pallas kernels, shards(): pl.pallas_call(edge_kernel, out_shape=(edge, edge), in_specs=[hbm], out_s...  1.77 us
    ppermute x1, starting transfers between devices, shards(): other = lax.ppermute(matrix, half_axis, swap)  0.52 us
  transfers between devices with their start and end apart: 5, of which 0 were waited for; matrix products, arithmetic and copies ran while one was open for 0% of the time, Pallas kernels for 44%

profile of v3, /device:TPU:0, one launch (start us, length us, event | category | flops | bytes accessed | tf_op | source)
XLA Modules:
  0.0 18.8 jit_solution(13041211574324536754)
XLA Ops:
  0.6 0.0 copy-start
  0.6 0.0 copy-start.1
  0.6 0.5 %collective-permute-start.2 = (f32[12,7,32,64]{3,2,1,0:T(8,128)}, f32[12,7,32,64]{3,2,1,0:T(8,128)S(1)}, u32[]{:S(2)}, u32[]{:S(2)}) collective-permute-start(f32[12,7,32,64]{3,2,1,0:T(8,128)} %own.3), channel_id=1, source_target_pairs={{0,1},{1,0},{2,3},{3,2},{4,5},{5,4},{6,7},{7,6},{8,9},{9,8},{10,11... | collective-permute-start | bytes 2064392 | tf_op jit(solution)/shard_map/ppermute | solution.py:425
  1.2 1.8 %shard_map.41 = (f32[96,256]{1,0:T(8,128)}, f32[96,256]{1,0:T(8,128)}) custom-call(f32[12,7,32,64]{3,2,1,0:T(8,128)} %own.3), custom_call_target="tpu_custom_call" | custom-call | tf_op jit(solution)/shard_map/pallas_call | solution.py:409
  2.9 2.6 %collective-permute-start = (f32[96,256]{1,0:T(8,128)}, f32[96,256]{1,0:T(8,128)S(1)}, u32[]{:S(2)}, u32[]{:S(2)}) collective-permute-start(f32[96,256]{1,0:T(8,128)} %get-tuple-element.23), channel_id=1, source_target_pairs={{0,2},{2,4},{4,6},{6,8},{8,10},{10,12},{12,14},{14,0},{1,3},{3,5},... | collective-permute-start | bytes 294920 | tf_op jit(solution)/shard_map/ppermute | solution.py:428
  5.6 3.1 %collective-permute-start.1 = (f32[96,256]{1,0:T(8,128)}, f32[96,256]{1,0:T(8,128)S(1)}, u32[]{:S(2)}, u32[]{:S(2)}) collective-permute-start(f32[96,256]{1,0:T(8,128)} %get-tuple-element.24), channel_id=1, source_target_pairs={{2,0},{4,2},{6,4},{8,6},{10,8},{12,10},{14,12},{0,14},{3,1},{5,3},... | collective-permute-start | bytes 294920 | tf_op jit(solution)/shard_map/ppermute | solution.py:429
  8.7 0.0 collective-permute-done.2.other
  8.7 0.0 copy-done
  8.7 0.0 copy-done.1
  8.7 4.5 %shard_map.42 = (f32[12,7,32,64]{3,2,1,0:T(8,128)}, f32[12,7,32,64]{3,2,1,0:T(8,128)}, f32[3,7,32,64]{3,2,1,0:T(8,128)S(1)}, bf16[2,3,256,768]{3,2,1,0:T(8,128)(...) custom-call(f32[12,7,32,64]{3,2,1,0:T(8,128)S(1)} %copy-done, ...), custom_call_target="tpu_custom_call" | custom-call | flops 1610612736 | bytes 16777216 | tf_op jit(solution)/shard_map/pallas_call | solution.py:436
  13.2 0.0 collective-permute-done.low_own
  13.2 0.0 collective-permute-done.1.high_own
  13.3 0.2 %collective-permute-start.3 = (f32[96,256]{1,0:T(8,128)S(1)}, f32[96,256]{1,0:T(8,128)S(1)}, u32[]{:S(2)}, u32[]{:S(2)}) collective-permute-start(f32[96,256]{1,0:T(8,128)S(1)} %collective-permute-done.low_own), channel_id=1, source_target_pairs={{0,1},{1,0},{2,3},{3,2},{4,5},{5,4},{6,7},{7,6},{8,9},{9,8},{10,11... | collective-permute-start | bytes 294920 | tf_op jit(solution)/shard_map/ppermute | solution.py:453
  13.5 0.4 %collective-permute-start.4 = (f32[96,256]{1,0:T(8,128)S(1)}, f32[96,256]{1,0:T(8,128)S(1)}, u32[]{:S(2)}, u32[]{:S(2)}) collective-permute-start(f32[96,256]{1,0:T(8,128)S(1)} %collective-permute-done.1.high_own), channel_id=1, source_target_pairs={{0,1},{1,0},{2,3},{3,2},{4,5},{5,4},{6,7},{7,6},{8,9},{9,8},{10,11... | collective-permute-start | bytes 294920 | tf_op jit(solution)/shard_map/ppermute | solution.py:454
  13.8 2.0 %shard_map.43 = (f32[12,7,32,64]{3,2,1,0:T(8,128)}, f32[3,7,32,64]{3,2,1,0:T(8,128)S(1)}, f32[192,256]{1,0:T(8,128)S(1)}, f32[192,256]{1,0:T(8,128)S(1)}, bf16[2...) custom-call(f32[12,7,32,64]{3,2,1,0:T(8,128)S(1)} %copy-done, ...), custom_call_target="tpu_custom_call", output_to_operand_aliasing={{0}: (5, {})} | custom-call | flops 402653184 | bytes 4194304 | tf_op jit(solution)/shard_map/pallas_call | solution.py:462
  15.8 0.0 collective-permute-done.3.low_other
  15.8 0.0 collective-permute-done.4.high_other
  15.8 3.0 %shard_map.44 = (f32[12,7,32,64]{3,2,1,0:T(8,128)}, f32[12,7,32,64]{3,2,1,0:T(8,128)}) custom-call(f32[96,256]{1,0:T(8,128)S(1)} %collective-permute-done.low_own, f32[96,256]{1,0:T(8,128)S(1)} %collective-permute-done.3.low_other, f32[96,256]{1,0:T(8,128)S(1)} %collective-permute-done.1.high_own, ...), custom_call_target="tpu_custom_call", output_to_operand_aliasing={{0}: (15, {}), {1}: (16, {})} | custom-call | flops 402653184 | bytes 2097152 | tf_op jit(solution)/shard_map/pallas_call | solution.py:479
Async XLA Ops:
  0.6 8.1 %copy-start = (f32[12,7,32,64]{3,2,1,0:T(8,128)S(1)}, f32[12,7,32,64]{3,2,1,0:T(8,128)}, u32[]{:S(2)}) copy-start(f32[12,7,32,64]{3,2,1,0:T(8,128)} %own.3) | copy-start | bytes 2064388
  0.6 8.1 %copy-start.1 = (s32[96,7]{0,1:T(8,128)S(1)}, s32[96,7]{0,1:T(8,128)}, u32[]{:S(2)}) copy-start(s32[96,7]{0,1:T(8,128)} %param.3) | copy-start | bytes 8068
  0.6 8.0 %collective-permute-start.2 = (f32[12,7,32,64]{3,2,1,0:T(8,128)}, f32[12,7,32,64]{3,2,1,0:T(8,128)S(1)}, u32[]{:S(2)}, u32[]{:S(2)}) collective-permute-start(f32[12,7,32,64]{3,2,1,0:T(8,128)} %own.3), channel_id=1, source_target_pairs={{0,1},{1,0},{2,3},{3,2},{4,5},{5,4},{6,7},{7,6},{8,9},{9,8},{10,11... | collective-permute-start | bytes 2064392 | tf_op jit(solution)/shard_map/ppermute | solution.py:425
  2.9 10.3 %collective-permute-start = (f32[96,256]{1,0:T(8,128)}, f32[96,256]{1,0:T(8,128)S(1)}, u32[]{:S(2)}, u32[]{:S(2)}) collective-permute-start(f32[96,256]{1,0:T(8,128)} %get-tuple-element.23), channel_id=1, source_target_pairs={{0,2},{2,4},{4,6},{6,8},{8,10},{10,12},{12,14},{14,0},{1,3},{3,5},... | collective-permute-start | bytes 294920 | tf_op jit(solution)/shard_map/ppermute | solution.py:428
  5.6 7.7 %collective-permute-start.1 = (f32[96,256]{1,0:T(8,128)}, f32[96,256]{1,0:T(8,128)S(1)}, u32[]{:S(2)}, u32[]{:S(2)}) collective-permute-start(f32[96,256]{1,0:T(8,128)} %get-tuple-element.24), channel_id=1, source_target_pairs={{2,0},{4,2},{6,4},{8,6},{10,8},{12,10},{14,12},{0,14},{3,1},{5,3},... | collective-permute-start | bytes 294920 | tf_op jit(solution)/shard_map/ppermute | solution.py:429
  13.3 2.6 %collective-permute-start.3 = (f32[96,256]{1,0:T(8,128)S(1)}, f32[96,256]{1,0:T(8,128)S(1)}, u32[]{:S(2)}, u32[]{:S(2)}) collective-permute-start(f32[96,256]{1,0:T(8,128)S(1)} %collective-permute-done.low_own), channel_id=1, source_target_pairs={{0,1},{1,0},{2,3},{3,2},{4,5},{5,4},{6,7},{7,6},{8,9},{9,8},{10,11... | collective-permute-start | bytes 294920 | tf_op jit(solution)/shard_map/ppermute | solution.py:453
  13.5 2.4 %collective-permute-start.4 = (f32[96,256]{1,0:T(8,128)S(1)}, f32[96,256]{1,0:T(8,128)S(1)}, u32[]{:S(2)}, u32[]{:S(2)}) collective-permute-start(f32[96,256]{1,0:T(8,128)S(1)} %collective-permute-done.1.high_own), channel_id=1, source_target_pairs={{0,1},{1,0},{2,3},{3,2},{4,5},{5,4},{6,7},{7,6},{8,9},{9,8},{10,11... | collective-permute-start | bytes 294920 | tf_op jit(solution)/shard_map/ppermute | solution.py:454

commit v4 on v3

--- a/solution.py
+++ b/solution.py
@@ -16,7 +16,6 @@
 BF = jnp.bfloat16
 F32 = jnp.float32
 LIMIT = 32 * 1024 * 1024
-EDGE_LIMIT = 58 * 1024 * 1024
 
 
 def split(x):
@@ -40,14 +39,23 @@
     return split((x[0].astype(F32) + x[1].astype(F32)).T)
 
 
-def flag_line(pat, row, places):
-    lane = lax.broadcasted_iota(jnp.int32, (1, WIDE), 1)
-    line = jnp.zeros((1, WIDE), F32)
-    for place, k in places:
-        if 0 <= k < SPAN:
-            value = pat[k, row].astype(F32)
-            line = jnp.where((lane >= place * BS) & (lane < (place + 1) * BS), value, line)
-    return line
+def write_lines(pat, lines, first, groups):
+    total = pat.shape[1]
+    lane = lax.broadcasted_iota(jnp.int32, (1, 2 * BS), 1)
+    for g in range(-1, groups + 1):
+        for s in range(GROUP):
+            row = lax.rem(first + g * GROUP + s + total, total)
+            for t in range(3 * GROUP // 2):
+                ks = [2 * t + e - s - 1 for e in range(2)]
+                f = [pat[k, row].astype(F32) if 0 <= k < SPAN else F32(0) for k in ks]
+                at = (g + 1) * GROUP + s
+                lines[at : at + 1, t * 2 * BS : (t + 1) * 2 * BS] = jnp.where(lane < BS, f[0], f[1])
+
+
+def line_of(lines, g, s, h):
+    at = (g + 1) * GROUP + s
+    lo = (h - g + 1) * WIDE
+    return lines[at : at + 1, lo : lo + WIDE]
 
 
 def span_of(a, count, is_square):
@@ -59,47 +67,25 @@
     return 0, SPAN
 
 
-def edge_kernel(matrix, to_left, to_right, blocks, sems):
-    count = matrix.shape[0]
-    loads = [
-        pltpu.make_async_copy(source, blocks.at[i], sems.at[i])
-        for i, source in enumerate(
-            (
-                matrix.at[pl.ds(0, REACH), pl.ds(REACH, REACH + 1)],
-                matrix.at[pl.ds(count - REACH, REACH), pl.ds(0, REACH + 1)],
-            )
-        )
-    ]
-    for load in loads:
-        load.start()
-    for i, target in enumerate((to_left, to_right)):
-        loads[i].wait()
+def edge_kernel(top, bottom, to_left, to_right):
+    for source, target in ((top, to_left), (bottom, to_right)):
         for s in range(REACH):
             for t in range(2):
                 target[s * HALF : (s + 1) * HALF, t * 2 * BS : (t + 1) * 2 * BS] = jnp.concatenate(
-                    [blocks[i, s, 2 * t], blocks[i, s, 2 * t + 1]], axis=1
+                    [source[s, 2 * t], source[s, 2 * t + 1]], axis=1
                 )
 
 
 class Interior:
-    def __init__(self, own, pat, full, mine, keep, axes):
+    def __init__(self, own, lines, full, mine, keep):
         self.own = own
-        self.pat = pat
+        self.lines = lines
         self.full = full
         self.mine = mine
         self.keep = keep
         self.count = own.shape[0]
         self.groups = self.count // GROUP
-        self.first = lax.axis_index(axes) * self.count
-        self.lines = {}
         self.stores = []
-
-    def flags(self, g, s, delta):
-        if (g, s, delta) not in self.lines:
-            row = lax.rem(self.first + g * GROUP + s, self.pat.shape[1])
-            places = [(t, t + GROUP * delta - s + REACH) for t in range(GROUP)]
-            self.lines[g, s, delta] = flag_line(self.pat, row, places)
-        return self.lines[g, s, delta]
 
     def part(self, g, h, rows=slice(None)):
         at = (h - g + 1) * WIDE
@@ -122,13 +108,13 @@
             for s in range(GROUP):
                 a = g * GROUP + s
                 k0, k1 = span_of(a, self.count, False)
-                part = value[s * HALF : (s + 1) * HALF] * (self.flags(g, s, h - g) * 0.5)
+                part = value[s * HALF : (s + 1) * HALF] * (line_of(self.lines, g, s, h) * 0.5)
                 for t in range(GROUP):
                     k = t + GROUP * (h - g) - s + REACH
                     if 0 <= k < SPAN:
                         block = 1.5 * self.own[a, k] - part[:, t * BS : (t + 1) * BS]
                         if k0 <= k < k1:
-                            sign[a - sign_first(sign, self.count, g), k] = block
+                            sign[s, k] = block
                         else:
                             seed[a if a < REACH else a - (self.count - REACH), k] = block
 
@@ -139,12 +125,11 @@
                 seed[s, k] = 1.5 * self.own[a, k]
 
     def send(self, g, i, source, target, sems):
-        for a in range(g * GROUP, (g + 1) * GROUP):
+        for s in range(GROUP):
+            a = g * GROUP + s
             k0, k1 = span_of(a, self.count, i == 0)
             store = pltpu.make_async_copy(
-                source.at[a - sign_first(source, self.count, g), pl.ds(k0, k1 - k0)],
-                target.at[a, pl.ds(k0, k1 - k0)],
-                sems.at[i, a],
+                source.at[s, pl.ds(k0, k1 - k0)], target.at[a, pl.ds(k0, k1 - k0)], sems.at[i, a]
             )
             store.start()
             self.stores.append(store)
@@ -154,15 +139,13 @@
             store.wait()
 
 
-def sign_first(ref, count, g):
-    return 0 if ref.shape[0] == count else g * GROUP
-
-
 def first_kernel(
-    own, other, pat, square_out, sign_out, seed, full, mine, keep, square, sign, sems, *, axes,
-    half_axis
+    own, other, pattern, square_out, sign_out, seed, full, mine, keep, lines, square_left, sign_left,
+    pat, square, sign, sems, pat_sem, *, axes, half_axis
 ):
-    it = Interior(own, pat, full, mine, keep, axes)
+    load = pltpu.make_async_copy(pattern, pat, pat_sem)
+    load.start()
+    it = Interior(own, lines, full, mine, keep)
     groups = it.groups
     upper_half = lax.axis_index(half_axis) == 1
 
@@ -186,18 +169,11 @@
                     )
                     for src in (own, other)
                 ]
-                parts = [split(x) for x in two]
-                for p in range(2):
-                    mine[p, g, mine_rows, lanes] = parts[0][p]
-                whole = jnp.concatenate(
-                    [
-                        jnp.where(upper_half, two[1], two[0]),
-                        jnp.where(upper_half, two[0], two[1]),
-                    ],
-                    axis=0,
-                )
-                for p, x in enumerate(split(whole)):
-                    full[p, g, rows, lanes] = x
+                for p, (x, y) in enumerate(zip(*[split(x) for x in two])):
+                    mine[p, g, mine_rows, lanes] = x
+                    full[p, g, rows, lanes] = jnp.concatenate(
+                        [jnp.where(upper_half, y, x), jnp.where(upper_half, x, y)], axis=0
+                    )
 
     def emit(g, h, value):
         for s in range(GROUP):
@@ -206,7 +182,7 @@
             for t in range(GROUP):
                 k = t + GROUP * (h - g) - s + REACH
                 if 0 <= k < SPAN:
-                    square[g * GROUP + s, k] = part[:, t * BS : (t + 1) * BS]
+                    staged[g][s, k] = part[:, t * BS : (t + 1) * BS]
         for p, x in enumerate(split(value)):
             keep[p, it.tile(g, h)] = x
 
@@ -218,33 +194,40 @@
                 pairs.append((it.part(g, e), it.part(e, h) if inside else turn(it.part(h, e))))
         value = product(pairs)
         value = jnp.concatenate(
-            [value[s * BS : (s + 1) * BS] * it.flags(g, s, h - g) for s in range(GROUP)], axis=0
+            [value[s * BS : (s + 1) * BS] * line_of(lines, g, s, h) for s in range(GROUP)], axis=0
         )
         emit(g, h, value)
         if h > g:
             emit(h, g, value.T)
 
+    staged = [square.at[g] for g in range(groups - 1)] + [square_left]
     build(0)
     for g in range(groups):
         if g + 1 < groups:
             build(g + 1)
+        if g == 0:
+            load.wait()
+            write_lines(pat, lines, lax.axis_index(axes) * it.count, groups)
         squares(g, g)
         if g + 1 < groups:
             squares(g, g + 1)
-        it.send(g, 0, square, square_out, sems)
-        if g > 0:
-            it.second(g - 1, sign, seed)
-            it.send(g - 1, 1, sign, sign_out, sems)
+            it.send(g, 0, staged[g], square_out, sems)
+        if 0 < g < groups - 1:
+            it.second(g - 1, sign.at[g - 1], seed)
+            it.send(g - 1, 1, sign.at[g - 1], sign_out, sems)
     it.far_seed(0, seed)
+    it.second(groups - 2, sign_left, seed)
     it.finish()
 
 
 def last_kernel(
-    own, pat, full, mine, keep, sign_in, sign_out, seed, low_a, low_b, low_m, low_p, high_a,
-    high_b, high_m, high_p, sign, sems, *, axes
+    own, lines, full, mine, keep, square_left, sign_left, square_in, sign_in, square_out, sign_out,
+    seed, low_a, low_b, low_m, low_p, high_a, high_b, high_m, high_p, sign, sems
 ):
-    it = Interior(own, pat, full, mine, keep, axes)
+    it = Interior(own, lines, full, mine, keep)
     last = it.groups - 1
+    it.send(last, 0, square_left, square_out, sems)
+    it.send(last - 1, 1, sign_left, sign_out, sems)
     it.second(last, sign, seed)
     it.send(last, 1, sign, sign_out, sems)
     it.far_seed(last, seed)
@@ -267,13 +250,12 @@
 
 
 def border_kernel(
-    low_own, low_other, high_own, high_other, pat, low_seed, low_a, low_b, low_m, low_p, high_seed,
+    low_own, low_other, high_own, high_other, lines, low_seed, low_a, low_b, low_m, low_p, high_seed,
     high_a, high_b, high_m, high_p, square_in, sign_in, square_out, sign_out, halo, blocks, sems,
-    *, axes, half_axis
+    *, half_axis
 ):
     count = square_in.shape[0]
-    total = pat.shape[1]
-    first = lax.axis_index(axes) * count
+    groups = count // GROUP
     upper_half = lax.axis_index(half_axis) == 1
     ends = (0, count - REACH)
     given = (
@@ -286,10 +268,10 @@
     for side in range(2):
         mine, theirs = given[side][:2]
         below = REACH if side == 0 else 0
-        lines = []
+        whole_rows = []
         for p in range(REACH):
             rows = slice(p * HALF, (p + 1) * HALF)
-            lines.append(
+            whole_rows.append(
                 jnp.concatenate(
                     [
                         jnp.where(upper_half, theirs[rows, :], mine[rows, :]),
@@ -302,10 +284,10 @@
         def block(p, c):
             k = c - p + below
             if 0 <= k <= REACH:
-                return lines[p][:, k * BS : (k + 1) * BS]
+                return whole_rows[p][:, k * BS : (k + 1) * BS]
             k = p - c + below
             if 0 <= c < REACH and 0 <= k <= REACH:
-                return lines[c][:, k * BS : (k + 1) * BS].T
+                return whole_rows[c][:, k * BS : (k + 1) * BS].T
             return jnp.zeros((BS, BS), F32)
 
         base = -5 if side == 0 else 0
@@ -321,21 +303,19 @@
 
     corners = []
     across = []
-    far_lines = []
     for side in range(2):
         _, _, _, a_ref, b_ref, m_ref, _ = given[side]
         at = shift[side]
         whole = [halo[side, q] for q in range(2)]
         outer_rows = slice(at * BS, (at + REACH) * BS)
         inner = slice(WIDE, 2 * WIDE) if side == 0 else slice(0, WIDE)
-        outer_first = first - REACH if side == 0 else first + count
-        edge_first = first + ends[side]
+        edge_group, outer_group = ((0, -1), (groups - 1, groups))[side]
+        low_row = 1 - at
 
         value = product([([x[outer_rows] for x in whole], whole)], True) + a_ref[...]
         rows = []
         for p in range(REACH):
-            row = lax.rem(outer_first + p + total, total)
-            line = flag_line(pat, row, [(t + at, t - p + REACH) for t in range(REACH)])
+            line = line_of(lines, outer_group, p + at, outer_group)
             rows.append(value[p * BS : (p + 1) * BS] * line)
         rows = [zero] + rows if side == 0 else rows + [zero]
         corners.append(split(jnp.concatenate(rows, axis=0)))
@@ -343,19 +323,15 @@
         value = product([([m_ref[q] for q in range(2)], [x[:, inner] for x in whole])], True)
         value = value + b_ref[...]
         rows = []
-        lines = []
+        offset = 0 if side == 0 else 2 * REACH
         for s in range(REACH):
-            row = lax.rem(edge_first + s, total)
-            offset = 0 if side == 0 else 2 * REACH
-            line = flag_line(pat, row, [(t + at, t - s + offset) for t in range(REACH)])
-            lines.append(line)
+            line = line_of(lines, edge_group, s + low_row, outer_group)
             rows.append(value[s * BS : (s + 1) * BS] * line)
             part = jnp.where(upper_half, rows[s][HALF:], rows[s][:HALF])
             for t in range(REACH):
                 k = t - s + offset
                 if 0 <= k < SPAN:
                     blocks[0, side, s, k] = part[:, (t + at) * BS : (t + at + 1) * BS]
-        far_lines.append(lines)
         rows = rows + [zero] if side == 0 else [zero] + rows
         across.append(split(jnp.concatenate(rows, axis=0)))
 
@@ -368,11 +344,12 @@
         out = product([(reach_out, corners[side]), (inside, across[side])])
         back = product([(reach_out, across[side])], True)
         offset = 0 if side == 0 else 2 * REACH
+        edge_group, outer_group = ((0, -1), (groups - 1, groups))[side]
         for s in range(REACH):
             a = ends[side] + s
-            row = lax.rem(first + a, total)
-            line = flag_line(pat, row, [(t + 1 - at, t - s + REACH) for t in range(REACH)])
-            far = out[s * HALF : (s + 1) * HALF] * (far_lines[side][s] * 0.5)
+            far_line = line_of(lines, edge_group, s + 1 - at, outer_group)
+            line = line_of(lines, edge_group, s + 1 - at, edge_group)
+            far = out[s * HALF : (s + 1) * HALF] * (far_line * 0.5)
             close = back[s * HALF : (s + 1) * HALF] * (line * 0.5)
             for t in range(REACH):
                 k = t - s + offset
@@ -401,23 +378,22 @@
     groups = count // GROUP
     flags = pattern.T
     vmem = pl.BlockSpec(memory_space=pltpu.VMEM)
-    smem = pl.BlockSpec(memory_space=pltpu.SMEM)
     hbm = pl.BlockSpec(memory_space=pl.ANY)
     params = pltpu.CompilerParams(vmem_limit_bytes=LIMIT)
 
+    top, bottom = matrix[:REACH, REACH:], matrix[count - REACH :, : REACH + 1]
+    matrix, top, bottom = lax.optimization_barrier((matrix, top, bottom))
     edge = jax.ShapeDtypeStruct((REACH * HALF, (REACH + 1) * BS), F32)
     to_left, to_right = pl.pallas_call(
         edge_kernel,
         out_shape=(edge, edge),
-        in_specs=[hbm],
+        in_specs=[vmem] * 2,
         out_specs=[vmem] * 2,
-        scratch_shapes=[
-            pltpu.VMEM((2, REACH, REACH + 1, HALF, BS), F32),
-            pltpu.SemaphoreType.DMA((2,)),
-        ],
-        compiler_params=pltpu.CompilerParams(vmem_limit_bytes=EDGE_LIMIT),
-    )(matrix)
-
+        compiler_params=params,
+        cost_estimate=pl.CostEstimate(
+            flops=1 * 10**9, bytes_accessed=2**20, transcendentals=0
+        ),
+    )(top, bottom)
     size = 1
     for axis in axes:
         size *= lax.axis_size(axis)
@@ -425,23 +401,27 @@
     other = lax.ppermute(matrix, half_axis, swap)
     forward = [(i, (i + 1) % size) for i in range(size)]
     backward = [(target, source) for source, target in forward]
+    high_own = lax.ppermute(to_left, axes, backward)
     low_own = lax.ppermute(to_right, axes, forward)
-    high_own = lax.ppermute(to_left, axes, backward)
 
     band = jax.ShapeDtypeStruct(matrix.shape, F32)
     seed = jax.ShapeDtypeStruct((REACH, SPAN, HALF, BS), F32)
     full = jax.ShapeDtypeStruct((2, groups, WIDE, 3 * WIDE), BF)
     mine = jax.ShapeDtypeStruct((2, groups, GROUP * HALF, 3 * WIDE), BF)
     keep = jax.ShapeDtypeStruct((2, 3 * groups, WIDE, WIDE), BF)
-    square, sign, low_seed, full, mine, keep = pl.pallas_call(
+    lines = jax.ShapeDtypeStruct(((groups + 2) * GROUP, 3 * WIDE), F32)
+    rows = jax.ShapeDtypeStruct((GROUP,) + matrix.shape[1:], F32)
+    square, sign, low_seed, full, mine, keep, lines, square_left, sign_left = pl.pallas_call(
         functools.partial(first_kernel, axes=axes, half_axis=half_axis),
-        out_shape=[band, band, seed, full, mine, keep],
-        in_specs=[vmem, vmem, smem],
-        out_specs=[hbm] * 2 + [vmem] * 4,
+        out_shape=[band, band, seed, full, mine, keep, lines, rows, rows],
+        in_specs=[vmem, vmem, hbm],
+        out_specs=[hbm] * 2 + [vmem] * 7,
         scratch_shapes=[
-            pltpu.VMEM(matrix.shape, F32),
-            pltpu.VMEM(matrix.shape, F32),
+            pltpu.SMEM(flags.shape, jnp.int32),
+            pltpu.VMEM((groups - 1,) + rows.shape, F32),
+            pltpu.VMEM((groups - 2,) + rows.shape, F32),
             pltpu.SemaphoreType.DMA((2, count)),
+            pltpu.SemaphoreType.DMA,
         ],
         compiler_params=params,
         cost_estimate=pl.CostEstimate(
@@ -459,27 +439,27 @@
         jax.ShapeDtypeStruct((2, REACH * BS, WIDE), BF),
         jax.ShapeDtypeStruct((2, 2, REACH * HALF, WIDE), BF),
     ]
-    sign, high_seed, *ends = pl.pallas_call(
-        functools.partial(last_kernel, axes=axes),
-        out_shape=[band, seed] + ends_out * 2,
-        in_specs=[vmem, smem] + [vmem] * 3 + [hbm],
-        out_specs=[hbm] + [vmem] * 9,
+    square, sign, high_seed, *ends = pl.pallas_call(
+        last_kernel,
+        out_shape=[band, band, seed] + ends_out * 2,
+        in_specs=[vmem] * 7 + [hbm] * 2,
+        out_specs=[hbm] * 2 + [vmem] * 9,
         scratch_shapes=[
-            pltpu.VMEM((GROUP, SPAN, HALF, BS), F32),
+            pltpu.VMEM(rows.shape, F32),
             pltpu.SemaphoreType.DMA((2, count)),
         ],
-        input_output_aliases={5: 0},
+        input_output_aliases={7: 0, 8: 1},
         compiler_params=params,
         cost_estimate=pl.CostEstimate(
             flops=3 * 2 * 4 * WIDE**3, bytes_accessed=4 * 2**20, transcendentals=0
         ),
-    )(matrix, flags, full, mine, keep, sign)
+    )(matrix, lines, full, mine, keep, square_left, sign_left, square, sign)
 
     return tuple(
         pl.pallas_call(
-            functools.partial(border_kernel, axes=axes, half_axis=half_axis),
+            functools.partial(border_kernel, half_axis=half_axis),
             out_shape=(band, band),
-            in_specs=[vmem] * 4 + [smem] + [vmem] * 10 + [hbm] * 2,
+            in_specs=[vmem] * 15 + [hbm] * 2,
             out_specs=[hbm] * 2,
             scratch_shapes=[
                 pltpu.VMEM((2, 2, WIDE, 2 * WIDE), BF),
@@ -492,7 +472,7 @@
                 flops=3 * 2 * 4 * WIDE**3, bytes_accessed=2 * 2**20, transcendentals=0
             ),
         )(
-            low_own, low_other, high_own, high_other, flags, low_seed, *ends[:4], high_seed,
+            low_own, low_other, high_own, high_other, lines, low_seed, *ends[:4], high_seed,
             *ends[4:], square, sign,
         )
     )

time: 18.9 us -> 17 us (0.90)
  Pallas kernels: 11.2 us -> 8.33 us
  local copies, waits for them, and re-layouts: 0.01 us -> 1.07 us
    pallas_call x3, Pallas kernels: 6.7 us -> 4.18 us  [the longest x1 2.36 us: shards(): pl.pallas_call(functools.partial(border_kernel, half_axis=half_axis), out...]
    slice x0 -> x1, local copies, waits for them, and re-layouts: none -> 1.06 us  [shards(): top, bottom = (matrix[:REACH, REACH:], matrix[count - REACH:, :REACH + 1])]
    pallas_call x1, Pallas kernels: 4.53 us -> 4.14 us  [shards(): pl.pallas_call(functools.partial(first_kernel, axes=axes, half_axis=half_...]
  transfers between devices with their start and end apart: 5 -> 5, of which waited for: 0 -> 0; matrix products, arithmetic and copies ran while one was open for 0% -> 0% of each run, Pallas kernels for 44% -> 35%
where the time goes in v4:
time: 17 us; the launch traced here: 16.9 us
  Pallas kernels  8.33 us (49%)
  starting transfers between devices  6.75 us (40%)
  local copies, waits for them, and re-layouts  1.07 us (6%)
  between operations  0.71 us (4%)
    pallas_call x1, Pallas kernels, shards(): pl.pallas_call(functools.partial(first_kernel, axes=axes, half_axis=half_...  4.14 us
    ppermute x1, starting transfers between devices, shards(): high_own = lax.ppermute(to_left, axes, backward)  3.1 us
    ppermute x1, starting transfers between devices, shards(): low_own = lax.ppermute(to_right, axes, forward)  2.55 us
    pallas_call x1, Pallas kernels, shards(): pl.pallas_call(functools.partial(border_kernel, half_axis=half_axis), out...  2.36 us
    pallas_call x1, Pallas kernels, shards(): pl.pallas_call(last_kernel, out_shape=[band, band, seed] + ends_out * 2,...  1.71 us
    slice x1, local copies, waits for them, and re-layouts, shards(): top, bottom = (matrix[:REACH, REACH:], matrix[count - REACH:, :REACH + 1])  1.06 us
    ppermute x1, starting transfers between devices, shards(): other = lax.ppermute(matrix, half_axis, swap)  0.52 us
  transfers between devices with their start and end apart: 5, of which 0 were waited for; matrix products, arithmetic and copies ran while one was open for 0% of the time, Pallas kernels for 35%

profile of v4, /device:TPU:0, one launch (start us, length us, event | category | flops | bytes accessed | tf_op | source)
XLA Modules:
  0.0 16.9 jit_solution(15235333890899174247)
XLA Ops:
  0.6 1.1 %fusion = (f32[3,4,32,64]{3,2,1,0:T(8,128)S(1)}, f32[3,4,32,64]{3,2,1,0:T(8,128)S(1)}) fusion(f32[12,7,32,64]{3,2,1,0:T(8,128)} %own.1), kind=kLoop, calls=%fused_computation | loop fusion | bytes 393216 | tf_op jit(solution)/shard_map/slice | solution.py:384
  1.7 0.0 copy-start
  1.7 0.0 copy-start.1
  1.7 0.5 %collective-permute-start.2 = (f32[12,7,32,64]{3,2,1,0:T(8,128)}, f32[12,7,32,64]{3,2,1,0:T(8,128)S(1)}, u32[]{:S(2)}, u32[]{:S(2)}) collective-permute-start(f32[12,7,32,64]{3,2,1,0:T(8,128)} %own.1), channel_id=1, source_target_pairs={{0,1},{1,0},{2,3},{3,2},{4,5},{5,4},{6,7},{7,6},{8,9},{9,8},{10,11... | collective-permute-start | bytes 2064392 | tf_op jit(solution)/shard_map/ppermute | solution.py:401
  2.2 0.1 shard_map.41
  2.4 2.6 %collective-permute-start = (f32[96,256]{1,0:T(8,128)S(1)}, f32[96,256]{1,0:T(8,128)S(1)}, u32[]{:S(2)}, u32[]{:S(2)}) collective-permute-start(f32[96,256]{1,0:T(8,128)S(1)} %get-tuple-element.32), channel_id=1, source_target_pairs={{0,2},{2,4},{4,6},{6,8},{8,10},{10,12},{12,14},{14,0},{1,3},{3,5},... | collective-permute-start | bytes 294920 | tf_op jit(solution)/shard_map/ppermute | solution.py:405
  4.9 3.1 %collective-permute-start.1 = (f32[96,256]{1,0:T(8,128)S(1)}, f32[96,256]{1,0:T(8,128)S(1)}, u32[]{:S(2)}, u32[]{:S(2)}) collective-permute-start(f32[96,256]{1,0:T(8,128)S(1)} %get-tuple-element.33), channel_id=1, source_target_pairs={{2,0},{4,2},{6,4},{8,6},{10,8},{12,10},{14,12},{0,14},{3,1},{5,3},... | collective-permute-start | bytes 294920 | tf_op jit(solution)/shard_map/ppermute | solution.py:404
  8.0 0.0 collective-permute-done.2.other
  8.0 0.0 copy-done
  8.0 0.0 copy-done.1
  8.0 4.1 %shard_map.42 = (f32[12,7,32,64]{3,2,1,0:T(8,128)}, f32[12,7,32,64]{3,2,1,0:T(8,128)}, f32[3,7,32,64]{3,2,1,0:T(8,128)S(1)}, bf16[2,3,256,768]{3,2,1,0:T(8,128)(...) custom-call(f32[12,7,32,64]{3,2,1,0:T(8,128)S(1)} %copy-done, ...), custom_call_target="tpu_custom_call" | custom-call | flops 1610612736 | bytes 16777216 | tf_op jit(solution)/shard_map/pallas_call | solution.py:414
  12.2 0.0 collective-permute-done.low_own
  12.2 0.0 collective-permute-done.1.high_own
  12.2 0.3 %collective-permute-start.3 = (f32[96,256]{1,0:T(8,128)S(1)}, f32[96,256]{1,0:T(8,128)S(1)}, u32[]{:S(2)}, u32[]{:S(2)}) collective-permute-start(f32[96,256]{1,0:T(8,128)S(1)} %collective-permute-done.low_own), channel_id=1, source_target_pairs={{0,1},{1,0},{2,3},{3,2},{4,5},{5,4},{6,7},{7,6},{8,9},{9,8},{10,11... | collective-permute-start | bytes 294920 | tf_op jit(solution)/shard_map/ppermute | solution.py:433
  12.5 0.3 %collective-permute-start.4 = (f32[96,256]{1,0:T(8,128)S(1)}, f32[96,256]{1,0:T(8,128)S(1)}, u32[]{:S(2)}, u32[]{:S(2)}) collective-permute-start(f32[96,256]{1,0:T(8,128)S(1)} %collective-permute-done.1.high_own), channel_id=1, source_target_pairs={{0,1},{1,0},{2,3},{3,2},{4,5},{5,4},{6,7},{7,6},{8,9},{9,8},{10,11... | collective-permute-start | bytes 294920 | tf_op jit(solution)/shard_map/ppermute | solution.py:434
  12.8 1.7 %shard_map.43 = (f32[12,7,32,64]{3,2,1,0:T(8,128)}, f32[12,7,32,64]{3,2,1,0:T(8,128)}, f32[3,7,32,64]{3,2,1,0:T(8,128)S(1)}, f32[192,256]{1,0:T(8,128)S(1)}, f32...) custom-call(f32[12,7,32,64]{3,2,1,0:T(8,128)S(1)} %copy-done, ...), custom_call_target="tpu_custom_call", output_to_operand_aliasing={{0}: (7, {}), {1}: (8, {})} | custom-call | flops 402653184 | bytes 4194304 | tf_op jit(solution)/shard_map/pallas_call | solution.py:442
  14.5 0.0 collective-permute-done.3.low_other
  14.5 0.0 collective-permute-done.4.high_other
  14.5 2.4 %shard_map.44 = (f32[12,7,32,64]{3,2,1,0:T(8,128)}, f32[12,7,32,64]{3,2,1,0:T(8,128)}) custom-call(f32[96,256]{1,0:T(8,128)S(1)} %collective-permute-done.low_own, f32[96,256]{1,0:T(8,128)S(1)} %collective-permute-done.3.low_other, f32[96,256]{1,0:T(8,128)S(1)} %collective-permute-done.1.high_own, ...), custom_call_target="tpu_custom_call", output_to_operand_aliasing={{0}: (15, {}), {1}: (16, {})} | custom-call | flops 402653184 | bytes 2097152 | tf_op jit(solution)/shard_map/pallas_call | solution.py:459
Async XLA Ops:
  1.7 6.3 %copy-start = (f32[12,7,32,64]{3,2,1,0:T(8,128)S(1)}, f32[12,7,32,64]{3,2,1,0:T(8,128)}, u32[]{:S(2)}) copy-start(f32[12,7,32,64]{3,2,1,0:T(8,128)} %own.1) | copy-start | bytes 2064388
  1.7 6.3 %copy-start.1 = (s32[96,7]{0,1:T(8,128)S(1)}, s32[96,7]{0,1:T(8,128)}, u32[]{:S(2)}) copy-start(s32[96,7]{0,1:T(8,128)} %param.3) | copy-start | bytes 8068
  1.7 6.3 %collective-permute-start.2 = (f32[12,7,32,64]{3,2,1,0:T(8,128)}, f32[12,7,32,64]{3,2,1,0:T(8,128)S(1)}, u32[]{:S(2)}, u32[]{:S(2)}) collective-permute-start(f32[12,7,32,64]{3,2,1,0:T(8,128)} %own.1), channel_id=1, source_target_pairs={{0,1},{1,0},{2,3},{3,2},{4,5},{5,4},{6,7},{7,6},{8,9},{9,8},{10,11... | collective-permute-start | bytes 2064392 | tf_op jit(solution)/shard_map/ppermute | solution.py:401
  2.4 9.8 %collective-permute-start = (f32[96,256]{1,0:T(8,128)S(1)}, f32[96,256]{1,0:T(8,128)S(1)}, u32[]{:S(2)}, u32[]{:S(2)}) collective-permute-start(f32[96,256]{1,0:T(8,128)S(1)} %get-tuple-element.32), channel_id=1, source_target_pairs={{0,2},{2,4},{4,6},{6,8},{8,10},{10,12},{12,14},{14,0},{1,3},{3,5},... | collective-permute-start | bytes 294920 | tf_op jit(solution)/shard_map/ppermute | solution.py:405
  4.9 7.3 %collective-permute-start.1 = (f32[96,256]{1,0:T(8,128)S(1)}, f32[96,256]{1,0:T(8,128)S(1)}, u32[]{:S(2)}, u32[]{:S(2)}) collective-permute-start(f32[96,256]{1,0:T(8,128)S(1)} %get-tuple-element.33), channel_id=1, source_target_pairs={{2,0},{4,2},{6,4},{8,6},{10,8},{12,10},{14,12},{0,14},{3,1},{5,3},... | collective-permute-start | bytes 294920 | tf_op jit(solution)/shard_map/ppermute | solution.py:404
  12.2 2.3 %collective-permute-start.3 = (f32[96,256]{1,0:T(8,128)S(1)}, f32[96,256]{1,0:T(8,128)S(1)}, u32[]{:S(2)}, u32[]{:S(2)}) collective-permute-start(f32[96,256]{1,0:T(8,128)S(1)} %collective-permute-done.low_own), channel_id=1, source_target_pairs={{0,1},{1,0},{2,3},{3,2},{4,5},{5,4},{6,7},{7,6},{8,9},{9,8},{10,11... | collective-permute-start | bytes 294920 | tf_op jit(solution)/shard_map/ppermute | solution.py:433
  12.5 2.0 %collective-permute-start.4 = (f32[96,256]{1,0:T(8,128)S(1)}, f32[96,256]{1,0:T(8,128)S(1)}, u32[]{:S(2)}, u32[]{:S(2)}) collective-permute-start(f32[96,256]{1,0:T(8,128)S(1)} %collective-permute-done.1.high_own), channel_id=1, source_target_pairs={{0,1},{1,0},{2,3},{3,2},{4,5},{5,4},{6,7},{7,6},{8,9},{9,8},{10,11... | collective-permute-start | bytes 294920 | tf_op jit(solution)/shard_map/ppermute | solution.py:434

commit v5 on v4

--- a/solution.py
+++ b/solution.py
@@ -101,14 +101,27 @@
     def kept(self, g, h):
         return [self.keep[p, self.tile(g, h)] for p in range(2)]
 
-    def second(self, g, sign, seed):
-        near = [e for e in (g - 1, g, g + 1) if 0 <= e < self.groups]
-        for h in near:
-            value = product([(self.my_part(g, e), self.kept(e, h)) for e in near if abs(e - h) <= 1])
-            for s in range(GROUP):
+    def near(self, g):
+        return [e for e in (g - 1, g, g + 1) if 0 <= e < self.groups]
+
+    def second(self, g, h, sign, seed, result):
+        span = range(1 if h > g else 0, GROUP - 1 if h < g else GROUP)
+        rows = slice(span[0] * HALF, (span[-1] + 1) * HALF)
+
+        def dot():
+            result[rows] = product(
+                [
+                    ([x[rows] for x in self.my_part(g, e)], self.kept(e, h))
+                    for e in self.near(g)
+                    if abs(e - h) <= 1
+                ]
+            )
+
+        def post():
+            for s in span:
                 a = g * GROUP + s
                 k0, k1 = span_of(a, self.count, False)
-                part = value[s * HALF : (s + 1) * HALF] * (line_of(self.lines, g, s, h) * 0.5)
+                part = result[s * HALF : (s + 1) * HALF] * (line_of(self.lines, g, s, h) * 0.5)
                 for t in range(GROUP):
                     k = t + GROUP * (h - g) - s + REACH
                     if 0 <= k < SPAN:
@@ -117,6 +130,8 @@
                             sign[s, k] = block
                         else:
                             seed[a if a < REACH else a - (self.count - REACH), k] = block
+
+        return dot, post
 
     def far_seed(self, g, seed):
         for s in range(REACH):
@@ -139,9 +154,28 @@
             store.wait()
 
 
+def count_dots(steps):
+    return sum(isinstance(step, tuple) for step in steps)
+
+
+def staggered(steps):
+    pending = []
+    for step in steps:
+        if not isinstance(step, tuple):
+            pending.append(step)
+            continue
+        dot, post = step
+        dot()
+        for work in pending:
+            work()
+        pending = [post]
+    for work in pending:
+        work()
+
+
 def first_kernel(
     own, other, pattern, square_out, sign_out, seed, full, mine, keep, lines, square_left, sign_left,
-    pat, square, sign, sems, pat_sem, *, axes, half_axis
+    pat, square, sign, results, sems, pat_sem, *, axes, half_axis
 ):
     load = pltpu.make_async_copy(pattern, pat, pat_sem)
     load.start()
@@ -175,83 +209,115 @@
                         [jnp.where(upper_half, y, x), jnp.where(upper_half, x, y)], axis=0
                     )
 
-    def emit(g, h, value):
-        for s in range(GROUP):
-            rows = value[s * BS : (s + 1) * BS]
-            part = jnp.where(upper_half, rows[HALF:], rows[:HALF])
-            for t in range(GROUP):
-                k = t + GROUP * (h - g) - s + REACH
-                if 0 <= k < SPAN:
-                    staged[g][s, k] = part[:, t * BS : (t + 1) * BS]
-        for p, x in enumerate(split(value)):
-            keep[p, it.tile(g, h)] = x
-
-    def squares(g, h):
+    def squares(g, h, result):
         pairs = []
         for e in (g - 1, g, g + 1):
             if abs(e - h) <= 1:
                 inside = 0 <= e < groups
-                pairs.append((it.part(g, e), it.part(e, h) if inside else turn(it.part(h, e))))
-        value = product(pairs)
-        value = jnp.concatenate(
-            [value[s * BS : (s + 1) * BS] * line_of(lines, g, s, h) for s in range(GROUP)], axis=0
-        )
-        emit(g, h, value)
-        if h > g:
-            emit(h, g, value.T)
+                pairs.append((e, (lambda e=e: it.part(e, h)) if inside else (lambda e=e: turn(it.part(h, e)))))
+        span = range(1 if h > g else 0, GROUP)
+        rows = slice(span[0] * BS, WIDE)
+
+        def dot():
+            result[rows] = product([([x[rows] for x in it.part(g, e)], f()) for e, f in pairs])
+
+        def post():
+            masked = [jnp.zeros((BS, WIDE), F32)] * GROUP
+            for s in span:
+                masked[s] = result[s * BS : (s + 1) * BS] * line_of(lines, g, s, h)
+            for s in range(GROUP):
+                for p, x in enumerate(split(masked[s])):
+                    keep[p, it.tile(g, h), s * BS : (s + 1) * BS] = x
+            for s in span:
+                part = jnp.where(upper_half, masked[s][HALF:], masked[s][:HALF])
+                for t in range(GROUP):
+                    k = t + GROUP * (h - g) - s + REACH
+                    if 0 <= k < SPAN:
+                        staged[g][s, k] = part[:, t * BS : (t + 1) * BS]
+            if h == g:
+                return
+            for c in range(0, GROUP, 2):
+                turned = jnp.concatenate(masked[c : c + 2], axis=0).T
+                lanes = slice(c * BS, (c + 2) * BS)
+                for p, x in enumerate(split(turned)):
+                    keep[p, it.tile(h, g), :, lanes] = x
+                for t in range(GROUP):
+                    rows = turned[t * BS : (t + 1) * BS]
+                    part = jnp.where(upper_half, rows[HALF:], rows[:HALF])
+                    for s in range(c, c + 2):
+                        k = s + GROUP * (g - h) - t + REACH
+                        if 0 <= k < SPAN:
+                            staged[h][t, k] = part[:, (s - c) * BS : (s - c + 1) * BS]
+
+        return dot, post
 
     staged = [square.at[g] for g in range(groups - 1)] + [square_left]
+    signs = [sign.at[g] for g in range(groups - 2)] + [sign_left]
+
+    def begin():
+        load.wait()
+        write_lines(pat, lines, lax.axis_index(axes) * it.count, groups)
+        it.far_seed(0, seed)
+
     build(0)
+    build(1)
+    steps = [begin]
     for g in range(groups):
         if g + 1 < groups:
-            build(g + 1)
-        if g == 0:
-            load.wait()
-            write_lines(pat, lines, lax.axis_index(axes) * it.count, groups)
-        squares(g, g)
+            steps.append(squares(g, g + 1, results.at[count_dots(steps)]))
+            if g + 2 < groups:
+                steps.append(functools.partial(build, g + 2))
+        steps.append(squares(g, g, results.at[count_dots(steps)]))
         if g + 1 < groups:
-            squares(g, g + 1)
-            it.send(g, 0, staged[g], square_out, sems)
-        if 0 < g < groups - 1:
-            it.second(g - 1, sign.at[g - 1], seed)
-            it.send(g - 1, 1, sign.at[g - 1], sign_out, sems)
-    it.far_seed(0, seed)
-    it.second(groups - 2, sign_left, seed)
+            steps.append(functools.partial(it.send, g, 0, staged[g], square_out, sems))
+        if g > 0:
+            for h in it.near(g - 1):
+                steps.append(it.second(g - 1, h, signs[g - 1], seed, results.at[count_dots(steps)]))
+            if g < groups - 1:
+                steps.append(functools.partial(it.send, g - 1, 1, signs[g - 1], sign_out, sems))
+    staggered(steps)
     it.finish()
 
 
 def last_kernel(
     own, lines, full, mine, keep, square_left, sign_left, square_in, sign_in, square_out, sign_out,
-    seed, low_a, low_b, low_m, low_p, high_a, high_b, high_m, high_p, sign, sems
+    seed, low_a, low_b, low_m, low_p, high_a, high_b, high_m, high_p, sign, results, sems
 ):
     it = Interior(own, lines, full, mine, keep)
     last = it.groups - 1
     it.send(last, 0, square_left, square_out, sems)
     it.send(last - 1, 1, sign_left, sign_out, sems)
-    it.second(last, sign, seed)
-    it.send(last, 1, sign, sign_out, sems)
-    it.far_seed(last, seed)
-    for a_ref, b_ref, m_ref, p_ref, g, e, r0 in (
-        (low_a, low_b, low_m, low_p, 0, -1, 0),
-        (high_a, high_b, high_m, high_p, last, last + 1, BS),
-    ):
+    steps = [it.second(last, h, sign, seed, results.at[i]) for i, h in enumerate(it.near(last))]
+    steps.append(functools.partial(it.send, last, 1, sign, sign_out, sems))
+    steps.append(functools.partial(it.far_seed, last, seed))
+
+    def reaching(a_ref, b_ref, m_ref, p_ref, g, e, r0):
         rows = slice(r0, r0 + REACH * BS)
         mine_rows = slice(r0 // 2, r0 // 2 + REACH * HALF)
-        out = it.part(g, e)
-        turned = turn(out)
         outer = slice(BS - r0, BS - r0 + REACH * BS)
-        a_ref[...] = product([([x[outer] for x in turned], out)])
-        b_ref[...] = product([(it.part(g, g, rows), out)])
-        for p in range(2):
-            m_ref[p] = out[p][rows]
-            p_ref[p, 0] = it.my_part(g, e)[p][mine_rows]
-            p_ref[p, 1] = it.my_part(g, g)[p][mine_rows]
+
+        def dot():
+            out = it.part(g, e)
+            a_ref[...] = product([([x[outer] for x in turn(out)], out)])
+            b_ref[...] = product([(it.part(g, g, rows), out)])
+
+        def post():
+            for p in range(2):
+                m_ref[p] = it.part(g, e)[p][rows]
+                p_ref[p, 0] = it.my_part(g, e)[p][mine_rows]
+                p_ref[p, 1] = it.my_part(g, g)[p][mine_rows]
+
+        return dot, post
+
+    steps.append(reaching(low_a, low_b, low_m, low_p, 0, -1, 0))
+    steps.append(reaching(high_a, high_b, high_m, high_p, last, last + 1, BS))
+    staggered(steps)
     it.finish()
 
 
 def border_kernel(
     low_own, low_other, high_own, high_other, lines, low_seed, low_a, low_b, low_m, low_p, high_seed,
-    high_a, high_b, high_m, high_p, square_in, sign_in, square_out, sign_out, halo, blocks, sems,
+    high_a, high_b, high_m, high_p, square_in, sign_in, square_out, sign_out, halo, first, last, blocks, sems,
     *, half_axis
 ):
     count = square_in.shape[0]
@@ -265,7 +331,7 @@
     shift = (1, 0)
     zero = jnp.zeros((BS, WIDE), F32)
 
-    for side in range(2):
+    def build(side):
         mine, theirs = given[side][:2]
         below = REACH if side == 0 else 0
         whole_rows = []
@@ -301,74 +367,93 @@
         for q in range(2):
             halo[side, q, rows, :] = jnp.zeros((BS, 2 * WIDE), BF)
 
-    corners = []
-    across = []
-    for side in range(2):
+    edge_groups, outer_groups = (0, groups - 1), (-1, groups)
+    offsets = (0, 2 * REACH)
+    corners = [None, None]
+    across = [None, None]
+    stores = []
+
+    def dots(side):
         _, _, _, a_ref, b_ref, m_ref, _ = given[side]
+        whole = [halo[side, q] for q in range(2)]
+        outer_rows = slice(shift[side] * BS, (shift[side] + REACH) * BS)
+        inner = slice(WIDE, 2 * WIDE) if side == 0 else slice(0, WIDE)
+        first[side, 0] = product([([x[outer_rows] for x in whole], whole)], True) + a_ref[...]
+        first[side, 1] = (
+            product([([m_ref[q] for q in range(2)], [x[:, inner] for x in whole])], True) + b_ref[...]
+        )
+
+    def masks(side):
         at = shift[side]
-        whole = [halo[side, q] for q in range(2)]
-        outer_rows = slice(at * BS, (at + REACH) * BS)
-        inner = slice(WIDE, 2 * WIDE) if side == 0 else slice(0, WIDE)
-        edge_group, outer_group = ((0, -1), (groups - 1, groups))[side]
-        low_row = 1 - at
-
-        value = product([([x[outer_rows] for x in whole], whole)], True) + a_ref[...]
-        rows = []
-        for p in range(REACH):
-            line = line_of(lines, outer_group, p + at, outer_group)
-            rows.append(value[p * BS : (p + 1) * BS] * line)
-        rows = [zero] + rows if side == 0 else rows + [zero]
-        corners.append(split(jnp.concatenate(rows, axis=0)))
-
-        value = product([([m_ref[q] for q in range(2)], [x[:, inner] for x in whole])], True)
-        value = value + b_ref[...]
-        rows = []
-        offset = 0 if side == 0 else 2 * REACH
+        edge_group, outer_group = edge_groups[side], outer_groups[side]
+        pad = (lambda rows: [zero] + rows, lambda rows: rows + [zero])
+        rows = [
+            first[side, 0, p * BS : (p + 1) * BS] * line_of(lines, outer_group, p + at, outer_group)
+            for p in range(REACH)
+        ]
+        corners[side] = split(jnp.concatenate(pad[side](rows), axis=0))
+        rows = [
+            first[side, 1, s * BS : (s + 1) * BS]
+            * line_of(lines, edge_group, s + 1 - at, outer_group)
+            for s in range(REACH)
+        ]
+        across[side] = split(jnp.concatenate(pad[1 - side](rows), axis=0))
         for s in range(REACH):
-            line = line_of(lines, edge_group, s + low_row, outer_group)
-            rows.append(value[s * BS : (s + 1) * BS] * line)
             part = jnp.where(upper_half, rows[s][HALF:], rows[s][:HALF])
             for t in range(REACH):
-                k = t - s + offset
+                k = t - s + offsets[side]
                 if 0 <= k < SPAN:
                     blocks[0, side, s, k] = part[:, (t + at) * BS : (t + at + 1) * BS]
-        rows = rows + [zero] if side == 0 else [zero] + rows
-        across.append(split(jnp.concatenate(rows, axis=0)))
-
-    stores = []
-    for side in range(2):
-        seed, p_ref = given[side][2], given[side][6]
-        at = shift[side]
+        send(side, 0, square_out)
+
+    def send(side, i, ref):
+        for s in range(REACH):
+            a = ends[side] + s
+            k0, k1 = span_of(a, count, i == 0)
+            k0, k1 = (0, k0) if side == 0 else (k1, SPAN)
+            store = pltpu.make_async_copy(
+                blocks.at[i, side, s, pl.ds(k0, k1 - k0)],
+                ref.at[a, pl.ds(k0, k1 - k0)],
+                sems.at[i, side, s],
+            )
+            store.start()
+            stores.append(store)
+
+    def second_dots(side):
+        p_ref = given[side][6]
         reach_out = [p_ref[q, 0] for q in range(2)]
         inside = [p_ref[q, 1] for q in range(2)]
-        out = product([(reach_out, corners[side]), (inside, across[side])])
-        back = product([(reach_out, across[side])], True)
-        offset = 0 if side == 0 else 2 * REACH
-        edge_group, outer_group = ((0, -1), (groups - 1, groups))[side]
+        last[side, 0] = product([(reach_out, corners[side]), (inside, across[side])])
+        last[side, 1] = product([(reach_out, across[side])], True)
+
+    def emit(side):
+        seed = given[side][2]
+        at = shift[side]
+        edge_group, outer_group = edge_groups[side], outer_groups[side]
         for s in range(REACH):
-            a = ends[side] + s
-            far_line = line_of(lines, edge_group, s + 1 - at, outer_group)
-            line = line_of(lines, edge_group, s + 1 - at, edge_group)
-            far = out[s * HALF : (s + 1) * HALF] * (far_line * 0.5)
-            close = back[s * HALF : (s + 1) * HALF] * (line * 0.5)
+            rows = slice(s * HALF, (s + 1) * HALF)
+            far = last[side, 0, rows] * (line_of(lines, edge_group, s + 1 - at, outer_group) * 0.5)
+            close = last[side, 1, rows] * (line_of(lines, edge_group, s + 1 - at, edge_group) * 0.5)
             for t in range(REACH):
-                k = t - s + offset
+                k = t - s + offsets[side]
                 if 0 <= k < SPAN:
                     lanes = slice((t + at) * BS, (t + at + 1) * BS)
                     blocks[1, side, s, k] = seed[s, k] - far[:, lanes]
                 k = t - s + REACH
                 lanes = slice((t + 1 - at) * BS, (t + 2 - at) * BS)
                 blocks[1, side, s, k] = seed[s, k] - close[:, lanes]
-            for i, ref in enumerate((square_out, sign_out)):
-                k0, k1 = span_of(a, count, i == 0)
-                k0, k1 = (0, k0) if side == 0 else (k1, SPAN)
-                store = pltpu.make_async_copy(
-                    blocks.at[i, side, s, pl.ds(k0, k1 - k0)],
-                    ref.at[a, pl.ds(k0, k1 - k0)],
-                    sems.at[i, side, s],
-                )
-                store.start()
-                stores.append(store)
+        send(side, 1, sign_out)
+
+    build(0)
+    dots(0)
+    build(1)
+    dots(1)
+    masks(0)
+    second_dots(0)
+    masks(1)
+    second_dots(1)
+    emit(0)
+    emit(1)
     for store in stores:
         store.wait()
 
@@ -420,6 +505,7 @@
             pltpu.SMEM(flags.shape, jnp.int32),
             pltpu.VMEM((groups - 1,) + rows.shape, F32),
             pltpu.VMEM((groups - 2,) + rows.shape, F32),
+            pltpu.VMEM((2 * groups - 1 + 3 * groups - 4, WIDE, WIDE), F32),
             pltpu.SemaphoreType.DMA((2, count)),
             pltpu.SemaphoreType.DMA,
         ],
@@ -446,6 +532,7 @@
         out_specs=[hbm] * 2 + [vmem] * 9,
         scratch_shapes=[
             pltpu.VMEM(rows.shape, F32),
+            pltpu.VMEM((2, GROUP * HALF, WIDE), F32),
             pltpu.SemaphoreType.DMA((2, count)),
         ],
         input_output_aliases={7: 0, 8: 1},
@@ -463,6 +550,8 @@
             out_specs=[hbm] * 2,
             scratch_shapes=[
                 pltpu.VMEM((2, 2, WIDE, 2 * WIDE), BF),
+                pltpu.VMEM((2, 2, REACH * BS, WIDE), F32),
+                pltpu.VMEM((2, 2, REACH * HALF, WIDE), F32),
                 pltpu.VMEM((2, 2, REACH, SPAN, HALF, BS), F32),
                 pltpu.SemaphoreType.DMA((2, 2, REACH)),
             ],

time: 17 us -> 17 us (level)
  no operation moved by 1% of the time
where the time goes in v5:
time: 17 us; the launch traced here: 16.8 us
  Pallas kernels  8.26 us (49%)
  starting transfers between devices  6.75 us (40%)
  local copies, waits for them, and re-layouts  1.07 us (6%)
  between operations  0.71 us (4%)
    pallas_call x1, Pallas kernels, shards(): pl.pallas_call(functools.partial(first_kernel, axes=axes, half_axis=half_...  4.08 us
    ppermute x1, starting transfers between devices, shards(): high_own = lax.ppermute(to_left, axes, backward)  3.1 us
    ppermute x1, starting transfers between devices, shards(): low_own = lax.ppermute(to_right, axes, forward)  2.55 us
    pallas_call x1, Pallas kernels, shards(): pl.pallas_call(functools.partial(border_kernel, half_axis=half_axis), out...  2.36 us
    pallas_call x1, Pallas kernels, shards(): pl.pallas_call(last_kernel, out_shape=[band, band, seed] + ends_out * 2,...  1.72 us
    slice x1, local copies, waits for them, and re-layouts, shards(): top, bottom = (matrix[:REACH, REACH:], matrix[count - REACH:, :REACH + 1])  1.06 us
    ppermute x1, starting transfers between devices, shards(): other = lax.ppermute(matrix, half_axis, swap)  0.52 us
  transfers between devices with their start and end apart: 5, of which 0 were waited for; matrix products, arithmetic and copies ran while one was open for 0% of the time, Pallas kernels for 35%

profile of v5, /device:TPU:0, one launch (start us, length us, event | category | flops | bytes accessed | tf_op | source)
XLA Modules:
  0.0 16.8 jit_solution(14151268024350897057)
XLA Ops:
  0.6 1.1 %fusion = (f32[3,4,32,64]{3,2,1,0:T(8,128)S(1)}, f32[3,4,32,64]{3,2,1,0:T(8,128)S(1)}) fusion(f32[12,7,32,64]{3,2,1,0:T(8,128)} %own.1), kind=kLoop, calls=%fused_computation | loop fusion | bytes 393216 | tf_op jit(solution)/shard_map/slice | solution.py:469
  1.7 0.0 copy-start
  1.7 0.0 copy-start.1
  1.7 0.5 %collective-permute-start.2 = (f32[12,7,32,64]{3,2,1,0:T(8,128)}, f32[12,7,32,64]{3,2,1,0:T(8,128)S(1)}, u32[]{:S(2)}, u32[]{:S(2)}) collective-permute-start(f32[12,7,32,64]{3,2,1,0:T(8,128)} %own.1), channel_id=1, source_target_pairs={{0,1},{1,0},{2,3},{3,2},{4,5},{5,4},{6,7},{7,6},{8,9},{9,8},{10,11... | collective-permute-start | bytes 2064392 | tf_op jit(solution)/shard_map/ppermute | solution.py:486
  2.2 0.1 shard_map.41
  2.4 2.6 %collective-permute-start = (f32[96,256]{1,0:T(8,128)S(1)}, f32[96,256]{1,0:T(8,128)S(1)}, u32[]{:S(2)}, u32[]{:S(2)}) collective-permute-start(f32[96,256]{1,0:T(8,128)S(1)} %get-tuple-element.32), channel_id=1, source_target_pairs={{0,2},{2,4},{4,6},{6,8},{8,10},{10,12},{12,14},{14,0},{1,3},{3,5},... | collective-permute-start | bytes 294920 | tf_op jit(solution)/shard_map/ppermute | solution.py:490
  4.9 3.1 %collective-permute-start.1 = (f32[96,256]{1,0:T(8,128)S(1)}, f32[96,256]{1,0:T(8,128)S(1)}, u32[]{:S(2)}, u32[]{:S(2)}) collective-permute-start(f32[96,256]{1,0:T(8,128)S(1)} %get-tuple-element.33), channel_id=1, source_target_pairs={{2,0},{4,2},{6,4},{8,6},{10,8},{12,10},{14,12},{0,14},{3,1},{5,3},... | collective-permute-start | bytes 294920 | tf_op jit(solution)/shard_map/ppermute | solution.py:489
  8.0 0.0 collective-permute-done.2.other
  8.0 0.0 copy-done
  8.0 0.0 copy-done.1
  8.0 4.1 %shard_map.42 = (f32[12,7,32,64]{3,2,1,0:T(8,128)}, f32[12,7,32,64]{3,2,1,0:T(8,128)}, f32[3,7,32,64]{3,2,1,0:T(8,128)S(1)}, bf16[2,3,256,768]{3,2,1,0:T(8,128)(...) custom-call(f32[12,7,32,64]{3,2,1,0:T(8,128)S(1)} %copy-done, ...), custom_call_target="tpu_custom_call" | custom-call | flops 1610612736 | bytes 16777216 | tf_op jit(solution)/shard_map/pallas_call | solution.py:499
  12.1 0.0 collective-permute-done.low_own
  12.1 0.0 collective-permute-done.1.high_own
  12.1 0.3 %collective-permute-start.3 = (f32[96,256]{1,0:T(8,128)S(1)}, f32[96,256]{1,0:T(8,128)S(1)}, u32[]{:S(2)}, u32[]{:S(2)}) collective-permute-start(f32[96,256]{1,0:T(8,128)S(1)} %collective-permute-done.low_own), channel_id=1, source_target_pairs={{0,1},{1,0},{2,3},{3,2},{4,5},{5,4},{6,7},{7,6},{8,9},{9,8},{10,11... | collective-permute-start | bytes 294920 | tf_op jit(solution)/shard_map/ppermute | solution.py:519
  12.4 0.3 %collective-permute-start.4 = (f32[96,256]{1,0:T(8,128)S(1)}, f32[96,256]{1,0:T(8,128)S(1)}, u32[]{:S(2)}, u32[]{:S(2)}) collective-permute-start(f32[96,256]{1,0:T(8,128)S(1)} %collective-permute-done.1.high_own), channel_id=1, source_target_pairs={{0,1},{1,0},{2,3},{3,2},{4,5},{5,4},{6,7},{7,6},{8,9},{9,8},{10,11... | collective-permute-start | bytes 294920 | tf_op jit(solution)/shard_map/ppermute | solution.py:520
  12.7 1.7 %shard_map.43 = (f32[12,7,32,64]{3,2,1,0:T(8,128)}, f32[12,7,32,64]{3,2,1,0:T(8,128)}, f32[3,7,32,64]{3,2,1,0:T(8,128)S(1)}, f32[192,256]{1,0:T(8,128)S(1)}, f32...) custom-call(f32[12,7,32,64]{3,2,1,0:T(8,128)S(1)} %copy-done, ...), custom_call_target="tpu_custom_call", output_to_operand_aliasing={{0}: (7, {}), {1}: (8, {})} | custom-call | flops 402653184 | bytes 4194304 | tf_op jit(solution)/shard_map/pallas_call | solution.py:528
  14.4 0.0 collective-permute-done.3.low_other
  14.4 0.0 collective-permute-done.4.high_other
  14.5 2.4 %shard_map.44 = (f32[12,7,32,64]{3,2,1,0:T(8,128)}, f32[12,7,32,64]{3,2,1,0:T(8,128)}) custom-call(f32[96,256]{1,0:T(8,128)S(1)} %collective-permute-done.low_own, f32[96,256]{1,0:T(8,128)S(1)} %collective-permute-done.3.low_other, f32[96,256]{1,0:T(8,128)S(1)} %collective-permute-done.1.high_own, ...), custom_call_target="tpu_custom_call", output_to_operand_aliasing={{0}: (15, {}), {1}: (16, {})} | custom-call | flops 402653184 | bytes 2097152 | tf_op jit(solution)/shard_map/pallas_call | solution.py:546
Async XLA Ops:
  1.7 6.3 %copy-start = (f32[12,7,32,64]{3,2,1,0:T(8,128)S(1)}, f32[12,7,32,64]{3,2,1,0:T(8,128)}, u32[]{:S(2)}) copy-start(f32[12,7,32,64]{3,2,1,0:T(8,128)} %own.1) | copy-start | bytes 2064388
  1.7 6.3 %copy-start.1 = (s32[96,7]{0,1:T(8,128)S(1)}, s32[96,7]{0,1:T(8,128)}, u32[]{:S(2)}) copy-start(s32[96,7]{0,1:T(8,128)} %param.3) | copy-start | bytes 8068
  1.7 6.3 %collective-permute-start.2 = (f32[12,7,32,64]{3,2,1,0:T(8,128)}, f32[12,7,32,64]{3,2,1,0:T(8,128)S(1)}, u32[]{:S(2)}, u32[]{:S(2)}) collective-permute-start(f32[12,7,32,64]{3,2,1,0:T(8,128)} %own.1), channel_id=1, source_target_pairs={{0,1},{1,0},{2,3},{3,2},{4,5},{5,4},{6,7},{7,6},{8,9},{9,8},{10,11... | collective-permute-start | bytes 2064392 | tf_op jit(solution)/shard_map/ppermute | solution.py:486
  2.4 9.8 %collective-permute-start = (f32[96,256]{1,0:T(8,128)S(1)}, f32[96,256]{1,0:T(8,128)S(1)}, u32[]{:S(2)}, u32[]{:S(2)}) collective-permute-start(f32[96,256]{1,0:T(8,128)S(1)} %get-tuple-element.32), channel_id=1, source_target_pairs={{0,2},{2,4},{4,6},{6,8},{8,10},{10,12},{12,14},{14,0},{1,3},{3,5},... | collective-permute-start | bytes 294920 | tf_op jit(solution)/shard_map/ppermute | solution.py:490
  4.9 7.2 %collective-permute-start.1 = (f32[96,256]{1,0:T(8,128)S(1)}, f32[96,256]{1,0:T(8,128)S(1)}, u32[]{:S(2)}, u32[]{:S(2)}) collective-permute-start(f32[96,256]{1,0:T(8,128)S(1)} %get-tuple-element.33), channel_id=1, source_target_pairs={{2,0},{4,2},{6,4},{8,6},{10,8},{12,10},{14,12},{0,14},{3,1},{5,3},... | collective-permute-start | bytes 294920 | tf_op jit(solution)/shard_map/ppermute | solution.py:489
  12.1 2.3 %collective-permute-start.3 = (f32[96,256]{1,0:T(8,128)S(1)}, f32[96,256]{1,0:T(8,128)S(1)}, u32[]{:S(2)}, u32[]{:S(2)}) collective-permute-start(f32[96,256]{1,0:T(8,128)S(1)} %collective-permute-done.low_own), channel_id=1, source_target_pairs={{0,1},{1,0},{2,3},{3,2},{4,5},{5,4},{6,7},{7,6},{8,9},{9,8},{10,11... | collective-permute-start | bytes 294920 | tf_op jit(solution)/shard_map/ppermute | solution.py:519
  12.4 2.0 %collective-permute-start.4 = (f32[96,256]{1,0:T(8,128)S(1)}, f32[96,256]{1,0:T(8,128)S(1)}, u32[]{:S(2)}, u32[]{:S(2)}) collective-permute-start(f32[96,256]{1,0:T(8,128)S(1)} %collective-permute-done.1.high_own), channel_id=1, source_target_pairs={{0,1},{1,0},{2,3},{3,2},{4,5},{5,4},{6,7},{7,6},{8,9},{9,8},{10,11... | collective-permute-start | bytes 294920 | tf_op jit(solution)/shard_map/ppermute | solution.py:520

commit v6 on v5

--- a/solution.py
+++ b/solution.py
@@ -109,13 +109,16 @@
         rows = slice(span[0] * HALF, (span[-1] + 1) * HALF)
 
         def dot():
-            result[rows] = product(
+            return product(
                 [
                     ([x[rows] for x in self.my_part(g, e)], self.kept(e, h))
                     for e in self.near(g)
                     if abs(e - h) <= 1
                 ]
             )
+
+        def store(value):
+            result[rows] = value
 
         def post():
             for s in span:
@@ -131,7 +134,7 @@
                         else:
                             seed[a if a < REACH else a - (self.count - REACH), k] = block
 
-        return dot, post
+        return dot, store, post
 
     def far_seed(self, g, seed):
         for s in range(REACH):
@@ -164,10 +167,11 @@
         if not isinstance(step, tuple):
             pending.append(step)
             continue
-        dot, post = step
-        dot()
+        dot, store, post = step
+        value = dot()
         for work in pending:
             work()
+        store(value)
         pending = [post]
     for work in pending:
         work()
@@ -219,7 +223,10 @@
         rows = slice(span[0] * BS, WIDE)
 
         def dot():
-            result[rows] = product([([x[rows] for x in it.part(g, e)], f()) for e, f in pairs])
+            return product([([x[rows] for x in it.part(g, e)], f()) for e, f in pairs])
+
+        def store(value):
+            result[rows] = value
 
         def post():
             masked = [jnp.zeros((BS, WIDE), F32)] * GROUP
@@ -249,7 +256,7 @@
                         if 0 <= k < SPAN:
                             staged[h][t, k] = part[:, (s - c) * BS : (s - c + 1) * BS]
 
-        return dot, post
+        return dot, store, post
 
     staged = [square.at[g] for g in range(groups - 1)] + [square_left]
     signs = [sign.at[g] for g in range(groups - 2)] + [sign_left]
@@ -298,8 +305,13 @@
 
         def dot():
             out = it.part(g, e)
-            a_ref[...] = product([([x[outer] for x in turn(out)], out)])
-            b_ref[...] = product([(it.part(g, g, rows), out)])
+            return (
+                product([([x[outer] for x in turn(out)], out)]),
+                product([(it.part(g, g, rows), out)]),
+            )
+
+        def store(value):
+            a_ref[...], b_ref[...] = value
 
         def post():
             for p in range(2):
@@ -307,7 +319,7 @@
                 p_ref[p, 0] = it.my_part(g, e)[p][mine_rows]
                 p_ref[p, 1] = it.my_part(g, g)[p][mine_rows]
 
-        return dot, post
+        return dot, store, post
 
     steps.append(reaching(low_a, low_b, low_m, low_p, 0, -1, 0))
     steps.append(reaching(high_a, high_b, high_m, high_p, last, last + 1, BS))
@@ -374,14 +386,19 @@
     stores = []
 
     def dots(side):
-        _, _, _, a_ref, b_ref, m_ref, _ = given[side]
+        m_ref = given[side][5]
         whole = [halo[side, q] for q in range(2)]
         outer_rows = slice(shift[side] * BS, (shift[side] + REACH) * BS)
         inner = slice(WIDE, 2 * WIDE) if side == 0 else slice(0, WIDE)
-        first[side, 0] = product([([x[outer_rows] for x in whole], whole)], True) + a_ref[...]
-        first[side, 1] = (
-            product([([m_ref[q] for q in range(2)], [x[:, inner] for x in whole])], True) + b_ref[...]
+        return (
+            product([([x[outer_rows] for x in whole], whole)], True),
+            product([([m_ref[q] for q in range(2)], [x[:, inner] for x in whole])], True),
         )
+
+    def keep_first(side, value):
+        _, _, _, a_ref, b_ref, _, _ = given[side]
+        first[side, 0] = value[0] + a_ref[...]
+        first[side, 1] = value[1] + b_ref[...]
 
     def masks(side):
         at = shift[side]
@@ -423,8 +440,13 @@
         p_ref = given[side][6]
         reach_out = [p_ref[q, 0] for q in range(2)]
         inside = [p_ref[q, 1] for q in range(2)]
-        last[side, 0] = product([(reach_out, corners[side]), (inside, across[side])])
-        last[side, 1] = product([(reach_out, across[side])], True)
+        return (
+            product([(reach_out, corners[side]), (inside, across[side])]),
+            product([(reach_out, across[side])], True),
+        )
+
+    def keep_last(side, value):
+        last[side, 0], last[side, 1] = value
 
     def emit(side):
         seed = given[side][2]
@@ -445,14 +467,18 @@
         send(side, 1, sign_out)
 
     build(0)
-    dots(0)
+    value = dots(0)
     build(1)
-    dots(1)
+    keep_first(0, value)
+    value = dots(1)
     masks(0)
-    second_dots(0)
+    keep_first(1, value)
+    value = second_dots(0)
     masks(1)
-    second_dots(1)
+    keep_last(0, value)
+    value = second_dots(1)
     emit(0)
+    keep_last(1, value)
     emit(1)
     for store in stores:
         store.wait()

time: 17 us -> 17 us (level)
  no operation moved by 1% of the time
where the time goes in v6:
time: 17 us; the launch traced here: 16.8 us
  Pallas kernels  8.26 us (49%)
  starting transfers between devices  6.75 us (40%)
  local copies, waits for them, and re-layouts  1.07 us (6%)
  between operations  0.71 us (4%)
    pallas_call x1, Pallas kernels, shards(): pl.pallas_call(functools.partial(first_kernel, axes=axes, half_axis=half_...  4.08 us
    ppermute x1, starting transfers between devices, shards(): high_own = lax.ppermute(to_left, axes, backward)  3.1 us
    ppermute x1, starting transfers between devices, shards(): low_own = lax.ppermute(to_right, axes, forward)  2.55 us
    pallas_call x1, Pallas kernels, shards(): pl.pallas_call(functools.partial(border_kernel, half_axis=half_axis), out...  2.36 us
    pallas_call x1, Pallas kernels, shards(): pl.pallas_call(last_kernel, out_shape=[band, band, seed] + ends_out * 2,...  1.72 us
    slice x1, local copies, waits for them, and re-layouts, shards(): top, bottom = (matrix[:REACH, REACH:], matrix[count - REACH:, :REACH + 1])  1.06 us
    ppermute x1, starting transfers between devices, shards(): other = lax.ppermute(matrix, half_axis, swap)  0.52 us
  transfers between devices with their start and end apart: 5, of which 0 were waited for; matrix products, arithmetic and copies ran while one was open for 0% of the time, Pallas kernels for 35%

profile of v6, /device:TPU:0, one launch (start us, length us, event | category | flops | bytes accessed | tf_op | source)
XLA Modules:
  0.0 16.8 jit_solution(14151268024350897057)
XLA Ops:
  0.6 1.1 %fusion = (f32[3,4,32,64]{3,2,1,0:T(8,128)S(1)}, f32[3,4,32,64]{3,2,1,0:T(8,128)S(1)}) fusion(f32[12,7,32,64]{3,2,1,0:T(8,128)} %own.1), kind=kLoop, calls=%fused_computation | loop fusion | bytes 393216 | tf_op jit(solution)/shard_map/slice | solution.py:495
  1.7 0.0 copy-start
  1.7 0.0 copy-start.1
  1.7 0.5 %collective-permute-start.2 = (f32[12,7,32,64]{3,2,1,0:T(8,128)}, f32[12,7,32,64]{3,2,1,0:T(8,128)S(1)}, u32[]{:S(2)}, u32[]{:S(2)}) collective-permute-start(f32[12,7,32,64]{3,2,1,0:T(8,128)} %own.1), channel_id=1, source_target_pairs={{0,1},{1,0},{2,3},{3,2},{4,5},{5,4},{6,7},{7,6},{8,9},{9,8},{10,11... | collective-permute-start | bytes 2064392 | tf_op jit(solution)/shard_map/ppermute | solution.py:512
  2.2 0.1 shard_map.41
  2.4 2.6 %collective-permute-start = (f32[96,256]{1,0:T(8,128)S(1)}, f32[96,256]{1,0:T(8,128)S(1)}, u32[]{:S(2)}, u32[]{:S(2)}) collective-permute-start(f32[96,256]{1,0:T(8,128)S(1)} %get-tuple-element.32), channel_id=1, source_target_pairs={{0,2},{2,4},{4,6},{6,8},{8,10},{10,12},{12,14},{14,0},{1,3},{3,5},... | collective-permute-start | bytes 294920 | tf_op jit(solution)/shard_map/ppermute | solution.py:516
  4.9 3.1 %collective-permute-start.1 = (f32[96,256]{1,0:T(8,128)S(1)}, f32[96,256]{1,0:T(8,128)S(1)}, u32[]{:S(2)}, u32[]{:S(2)}) collective-permute-start(f32[96,256]{1,0:T(8,128)S(1)} %get-tuple-element.33), channel_id=1, source_target_pairs={{2,0},{4,2},{6,4},{8,6},{10,8},{12,10},{14,12},{0,14},{3,1},{5,3},... | collective-permute-start | bytes 294920 | tf_op jit(solution)/shard_map/ppermute | solution.py:515
  8.0 0.0 collective-permute-done.2.other
  8.0 0.0 copy-done
  8.0 0.0 copy-done.1
  8.0 4.1 %shard_map.42 = (f32[12,7,32,64]{3,2,1,0:T(8,128)}, f32[12,7,32,64]{3,2,1,0:T(8,128)}, f32[3,7,32,64]{3,2,1,0:T(8,128)S(1)}, bf16[2,3,256,768]{3,2,1,0:T(8,128)(...) custom-call(f32[12,7,32,64]{3,2,1,0:T(8,128)S(1)} %copy-done, ...), custom_call_target="tpu_custom_call" | custom-call | flops 1610612736 | bytes 16777216 | tf_op jit(solution)/shard_map/pallas_call | solution.py:525
  12.1 0.0 collective-permute-done.low_own
  12.1 0.0 collective-permute-done.1.high_own
  12.1 0.3 %collective-permute-start.3 = (f32[96,256]{1,0:T(8,128)S(1)}, f32[96,256]{1,0:T(8,128)S(1)}, u32[]{:S(2)}, u32[]{:S(2)}) collective-permute-start(f32[96,256]{1,0:T(8,128)S(1)} %collective-permute-done.low_own), channel_id=1, source_target_pairs={{0,1},{1,0},{2,3},{3,2},{4,5},{5,4},{6,7},{7,6},{8,9},{9,8},{10,11... | collective-permute-start | bytes 294920 | tf_op jit(solution)/shard_map/ppermute | solution.py:545
  12.4 0.3 %collective-permute-start.4 = (f32[96,256]{1,0:T(8,128)S(1)}, f32[96,256]{1,0:T(8,128)S(1)}, u32[]{:S(2)}, u32[]{:S(2)}) collective-permute-start(f32[96,256]{1,0:T(8,128)S(1)} %collective-permute-done.1.high_own), channel_id=1, source_target_pairs={{0,1},{1,0},{2,3},{3,2},{4,5},{5,4},{6,7},{7,6},{8,9},{9,8},{10,11... | collective-permute-start | bytes 294920 | tf_op jit(solution)/shard_map/ppermute | solution.py:546
  12.7 1.7 %shard_map.43 = (f32[12,7,32,64]{3,2,1,0:T(8,128)}, f32[12,7,32,64]{3,2,1,0:T(8,128)}, f32[3,7,32,64]{3,2,1,0:T(8,128)S(1)}, f32[192,256]{1,0:T(8,128)S(1)}, f32...) custom-call(f32[12,7,32,64]{3,2,1,0:T(8,128)S(1)} %copy-done, ...), custom_call_target="tpu_custom_call", output_to_operand_aliasing={{0}: (7, {}), {1}: (8, {})} | custom-call | flops 402653184 | bytes 4194304 | tf_op jit(solution)/shard_map/pallas_call | solution.py:554
  14.4 0.0 collective-permute-done.3.low_other
  14.4 0.0 collective-permute-done.4.high_other
  14.5 2.4 %shard_map.44 = (f32[12,7,32,64]{3,2,1,0:T(8,128)}, f32[12,7,32,64]{3,2,1,0:T(8,128)}) custom-call(f32[96,256]{1,0:T(8,128)S(1)} %collective-permute-done.low_own, f32[96,256]{1,0:T(8,128)S(1)} %collective-permute-done.3.low_other, f32[96,256]{1,0:T(8,128)S(1)} %collective-permute-done.1.high_own, ...), custom_call_target="tpu_custom_call", output_to_operand_aliasing={{0}: (15, {}), {1}: (16, {})} | custom-call | flops 402653184 | bytes 2097152 | tf_op jit(solution)/shard_map/pallas_call | solution.py:572
Async XLA Ops:
  1.7 6.3 %copy-start = (f32[12,7,32,64]{3,2,1,0:T(8,128)S(1)}, f32[12,7,32,64]{3,2,1,0:T(8,128)}, u32[]{:S(2)}) copy-start(f32[12,7,32,64]{3,2,1,0:T(8,128)} %own.1) | copy-start | bytes 2064388
  1.7 6.3 %copy-start.1 = (s32[96,7]{0,1:T(8,128)S(1)}, s32[96,7]{0,1:T(8,128)}, u32[]{:S(2)}) copy-start(s32[96,7]{0,1:T(8,128)} %param.3) | copy-start | bytes 8068
  1.7 6.3 %collective-permute-start.2 = (f32[12,7,32,64]{3,2,1,0:T(8,128)}, f32[12,7,32,64]{3,2,1,0:T(8,128)S(1)}, u32[]{:S(2)}, u32[]{:S(2)}) collective-permute-start(f32[12,7,32,64]{3,2,1,0:T(8,128)} %own.1), channel_id=1, source_target_pairs={{0,1},{1,0},{2,3},{3,2},{4,5},{5,4},{6,7},{7,6},{8,9},{9,8},{10,11... | collective-permute-start | bytes 2064392 | tf_op jit(solution)/shard_map/ppermute | solution.py:512
  2.4 9.8 %collective-permute-start = (f32[96,256]{1,0:T(8,128)S(1)}, f32[96,256]{1,0:T(8,128)S(1)}, u32[]{:S(2)}, u32[]{:S(2)}) collective-permute-start(f32[96,256]{1,0:T(8,128)S(1)} %get-tuple-element.32), channel_id=1, source_target_pairs={{0,2},{2,4},{4,6},{6,8},{8,10},{10,12},{12,14},{14,0},{1,3},{3,5},... | collective-permute-start | bytes 294920 | tf_op jit(solution)/shard_map/ppermute | solution.py:516
  4.9 7.2 %collective-permute-start.1 = (f32[96,256]{1,0:T(8,128)S(1)}, f32[96,256]{1,0:T(8,128)S(1)}, u32[]{:S(2)}, u32[]{:S(2)}) collective-permute-start(f32[96,256]{1,0:T(8,128)S(1)} %get-tuple-element.33), channel_id=1, source_target_pairs={{2,0},{4,2},{6,4},{8,6},{10,8},{12,10},{14,12},{0,14},{3,1},{5,3},... | collective-permute-start | bytes 294920 | tf_op jit(solution)/shard_map/ppermute | solution.py:515
  12.1 2.3 %collective-permute-start.3 = (f32[96,256]{1,0:T(8,128)S(1)}, f32[96,256]{1,0:T(8,128)S(1)}, u32[]{:S(2)}, u32[]{:S(2)}) collective-permute-start(f32[96,256]{1,0:T(8,128)S(1)} %collective-permute-done.low_own), channel_id=1, source_target_pairs={{0,1},{1,0},{2,3},{3,2},{4,5},{5,4},{6,7},{7,6},{8,9},{9,8},{10,11... | collective-permute-start | bytes 294920 | tf_op jit(solution)/shard_map/ppermute | solution.py:545
  12.4 2.0 %collective-permute-start.4 = (f32[96,256]{1,0:T(8,128)S(1)}, f32[96,256]{1,0:T(8,128)S(1)}, u32[]{:S(2)}, u32[]{:S(2)}) collective-permute-start(f32[96,256]{1,0:T(8,128)S(1)} %collective-permute-done.1.high_own), channel_id=1, source_target_pairs={{0,1},{1,0},{2,3},{3,2},{4,5},{5,4},{6,7},{7,6},{8,9},{9,8},{10,11... | collective-permute-start | bytes 294920 | tf_op jit(solution)/shard_map/ppermute | solution.py:546

commit v7 on v6

--- a/solution.py
+++ b/solution.py
@@ -178,7 +178,7 @@
 
 
 def first_kernel(
-    own, other, pattern, square_out, sign_out, seed, full, mine, keep, lines, square_left, sign_left,
+    own, other, pattern, square_out, sign_out, seed, full, mine, keep, lines, sign_left,
     pat, square, sign, results, sems, pat_sem, *, axes, half_axis
 ):
     load = pltpu.make_async_copy(pattern, pat, pat_sem)
@@ -258,7 +258,7 @@
 
         return dot, store, post
 
-    staged = [square.at[g] for g in range(groups - 1)] + [square_left]
+    staged = [square.at[g] for g in range(groups)]
     signs = [sign.at[g] for g in range(groups - 2)] + [sign_left]
 
     def begin():
@@ -275,8 +275,7 @@
             if g + 2 < groups:
                 steps.append(functools.partial(build, g + 2))
         steps.append(squares(g, g, results.at[count_dots(steps)]))
-        if g + 1 < groups:
-            steps.append(functools.partial(it.send, g, 0, staged[g], square_out, sems))
+        steps.append(functools.partial(it.send, g, 0, staged[g], square_out, sems))
         if g > 0:
             for h in it.near(g - 1):
                 steps.append(it.second(g - 1, h, signs[g - 1], seed, results.at[count_dots(steps)]))
@@ -287,15 +286,12 @@
 
 
 def last_kernel(
-    own, lines, full, mine, keep, square_left, sign_left, square_in, sign_in, square_out, sign_out,
-    seed, low_a, low_b, low_m, low_p, high_a, high_b, high_m, high_p, sign, results, sems
+    own, lines, full, mine, keep, sign_left, sign_in, sign_out, sign, seed, low_a, low_b, low_m, low_p, high_a, high_b, high_m, high_p, results, sems
 ):
     it = Interior(own, lines, full, mine, keep)
     last = it.groups - 1
-    it.send(last, 0, square_left, square_out, sems)
     it.send(last - 1, 1, sign_left, sign_out, sems)
     steps = [it.second(last, h, sign, seed, results.at[i]) for i, h in enumerate(it.near(last))]
-    steps.append(functools.partial(it.send, last, 1, sign, sign_out, sems))
     steps.append(functools.partial(it.far_seed, last, seed))
 
     def reaching(a_ref, b_ref, m_ref, p_ref, g, e, r0):
@@ -328,8 +324,8 @@
 
 
 def border_kernel(
-    low_own, low_other, high_own, high_other, lines, low_seed, low_a, low_b, low_m, low_p, high_seed,
-    high_a, high_b, high_m, high_p, square_in, sign_in, square_out, sign_out, halo, first, last, blocks, sems,
+    low_own, low_other, high_own, high_other, lines, sign_last, low_seed, low_a, low_b, low_m, low_p, high_seed,
+    high_a, high_b, high_m, high_p, square_in, sign_in, square_out, sign_out, halo, first, last, blocks, sems, last_sems,
     *, half_axis
 ):
     count = square_in.shape[0]
@@ -466,6 +462,14 @@
                 blocks[1, side, s, k] = seed[s, k] - close[:, lanes]
         send(side, 1, sign_out)
 
+    for s in range(GROUP):
+        a = count - GROUP + s
+        k0, k1 = span_of(a, count, False)
+        store = pltpu.make_async_copy(
+            sign_last.at[s, pl.ds(k0, k1 - k0)], sign_out.at[a, pl.ds(k0, k1 - k0)], last_sems.at[s]
+        )
+        store.start()
+        stores.append(store)
     build(0)
     value = dots(0)
     build(1)
@@ -522,14 +526,14 @@
     keep = jax.ShapeDtypeStruct((2, 3 * groups, WIDE, WIDE), BF)
     lines = jax.ShapeDtypeStruct(((groups + 2) * GROUP, 3 * WIDE), F32)
     rows = jax.ShapeDtypeStruct((GROUP,) + matrix.shape[1:], F32)
-    square, sign, low_seed, full, mine, keep, lines, square_left, sign_left = pl.pallas_call(
+    square, sign, low_seed, full, mine, keep, lines, sign_left = pl.pallas_call(
         functools.partial(first_kernel, axes=axes, half_axis=half_axis),
-        out_shape=[band, band, seed, full, mine, keep, lines, rows, rows],
+        out_shape=[band, band, seed, full, mine, keep, lines, rows],
         in_specs=[vmem, vmem, hbm],
-        out_specs=[hbm] * 2 + [vmem] * 7,
+        out_specs=[hbm] * 2 + [vmem] * 6,
         scratch_shapes=[
             pltpu.SMEM(flags.shape, jnp.int32),
-            pltpu.VMEM((groups - 1,) + rows.shape, F32),
+            pltpu.VMEM((groups,) + rows.shape, F32),
             pltpu.VMEM((groups - 2,) + rows.shape, F32),
             pltpu.VMEM((2 * groups - 1 + 3 * groups - 4, WIDE, WIDE), F32),
             pltpu.SemaphoreType.DMA((2, count)),
@@ -551,28 +555,27 @@
         jax.ShapeDtypeStruct((2, REACH * BS, WIDE), BF),
         jax.ShapeDtypeStruct((2, 2, REACH * HALF, WIDE), BF),
     ]
-    square, sign, high_seed, *ends = pl.pallas_call(
+    sign, sign_last, high_seed, *ends = pl.pallas_call(
         last_kernel,
-        out_shape=[band, band, seed] + ends_out * 2,
-        in_specs=[vmem] * 7 + [hbm] * 2,
-        out_specs=[hbm] * 2 + [vmem] * 9,
+        out_shape=[band, rows, seed] + ends_out * 2,
+        in_specs=[vmem] * 6 + [hbm],
+        out_specs=[hbm] + [vmem] * 10,
         scratch_shapes=[
-            pltpu.VMEM(rows.shape, F32),
             pltpu.VMEM((2, GROUP * HALF, WIDE), F32),
             pltpu.SemaphoreType.DMA((2, count)),
         ],
-        input_output_aliases={7: 0, 8: 1},
+        input_output_aliases={6: 0},
         compiler_params=params,
         cost_estimate=pl.CostEstimate(
             flops=3 * 2 * 4 * WIDE**3, bytes_accessed=4 * 2**20, transcendentals=0
         ),
-    )(matrix, lines, full, mine, keep, square_left, sign_left, square, sign)
+    )(matrix, lines, full, mine, keep, sign_left, sign)
 
     return tuple(
         pl.pallas_call(
             functools.partial(border_kernel, half_axis=half_axis),
             out_shape=(band, band),
-            in_specs=[vmem] * 15 + [hbm] * 2,
+            in_specs=[vmem] * 16 + [hbm] * 2,
             out_specs=[hbm] * 2,
             scratch_shapes=[
                 pltpu.VMEM((2, 2, WIDE, 2 * WIDE), BF),
@@ -580,14 +583,15 @@
                 pltpu.VMEM((2, 2, REACH * HALF, WIDE), F32),
                 pltpu.VMEM((2, 2, REACH, SPAN, HALF, BS), F32),
                 pltpu.SemaphoreType.DMA((2, 2, REACH)),
+                pltpu.SemaphoreType.DMA((GROUP,)),
             ],
-            input_output_aliases={15: 0, 16: 1},
+            input_output_aliases={16: 0, 17: 1},
             compiler_params=params,
             cost_estimate=pl.CostEstimate(
                 flops=3 * 2 * 4 * WIDE**3, bytes_accessed=2 * 2**20, transcendentals=0
             ),
         )(
-            low_own, low_other, high_own, high_other, lines, low_seed, *ends[:4], high_seed,
+            low_own, low_other, high_own, high_other, lines, sign_last, low_seed, *ends[:4], high_seed,
             *ends[4:], square, sign,
         )
     )

time: 17 us -> 16.7 us (0.982)
  Pallas kernels: 8.26 us -> 7.96 us
    pallas_call x1, Pallas kernels: 1.72 us -> 1.51 us  [shards(): pl.pallas_call(last_kernel, out_shape=[band, rows, seed] + ends_out * 2,...]
  transfers between devices with their start and end apart: 5 -> 5, of which waited for: 0 -> 0; matrix products, arithmetic and copies ran while one was open for 0% -> 0% of each run, Pallas kernels for 35% -> 34%
where the time goes in v7:
time: 16.7 us; the launch traced here: 16.5 us
  Pallas kernels  7.96 us (48%)
  starting transfers between devices  6.75 us (40%)
  local copies, waits for them, and re-layouts  1.07 us (6%)
  between operations  0.71 us (4%)
    pallas_call x1, Pallas kernels, shards(): pl.pallas_call(functools.partial(first_kernel, axes=axes, half_axis=half_...  3.95 us
    ppermute x1, starting transfers between devices, shards(): high_own = lax.ppermute(to_left, axes, backward)  3.1 us
    ppermute x1, starting transfers between devices, shards(): low_own = lax.ppermute(to_right, axes, forward)  2.55 us
    pallas_call x1, Pallas kernels, shards(): pl.pallas_call(functools.partial(border_kernel, half_axis=half_axis), out...  2.39 us
    pallas_call x1, Pallas kernels, shards(): pl.pallas_call(last_kernel, out_shape=[band, rows, seed] + ends_out * 2,...  1.51 us
    slice x1, local copies, waits for them, and re-layouts, shards(): top, bottom = (matrix[:REACH, REACH:], matrix[count - REACH:, :REACH + 1])  1.06 us
    ppermute x1, starting transfers between devices, shards(): other = lax.ppermute(matrix, half_axis, swap)  0.52 us
  transfers between devices with their start and end apart: 5, of which 0 were waited for; matrix products, arithmetic and copies ran while one was open for 0% of the time, Pallas kernels for 34%

profile of v7, /device:TPU:0, one launch (start us, length us, event | category | flops | bytes accessed | tf_op | source)
XLA Modules:
  0.0 16.5 jit_solution(13926041356915756554)
XLA Ops:
  0.6 1.1 %fusion = (f32[3,4,32,64]{3,2,1,0:T(8,128)S(1)}, f32[3,4,32,64]{3,2,1,0:T(8,128)S(1)}) fusion(f32[12,7,32,64]{3,2,1,0:T(8,128)} %own.1), kind=kLoop, calls=%fused_computation | loop fusion | bytes 393216 | tf_op jit(solution)/shard_map/slice | solution.py:499
  1.7 0.0 copy-start
  1.7 0.0 copy-start.1
  1.7 0.5 %collective-permute-start.2 = (f32[12,7,32,64]{3,2,1,0:T(8,128)}, f32[12,7,32,64]{3,2,1,0:T(8,128)S(1)}, u32[]{:S(2)}, u32[]{:S(2)}) collective-permute-start(f32[12,7,32,64]{3,2,1,0:T(8,128)} %own.1), channel_id=1, source_target_pairs={{0,1},{1,0},{2,3},{3,2},{4,5},{5,4},{6,7},{7,6},{8,9},{9,8},{10,11... | collective-permute-start | bytes 2064392 | tf_op jit(solution)/shard_map/ppermute | solution.py:516
  2.2 0.1 shard_map.41
  2.4 2.6 %collective-permute-start = (f32[96,256]{1,0:T(8,128)S(1)}, f32[96,256]{1,0:T(8,128)S(1)}, u32[]{:S(2)}, u32[]{:S(2)}) collective-permute-start(f32[96,256]{1,0:T(8,128)S(1)} %get-tuple-element.31), channel_id=1, source_target_pairs={{0,2},{2,4},{4,6},{6,8},{8,10},{10,12},{12,14},{14,0},{1,3},{3,5},... | collective-permute-start | bytes 294920 | tf_op jit(solution)/shard_map/ppermute | solution.py:520
  4.9 3.1 %collective-permute-start.1 = (f32[96,256]{1,0:T(8,128)S(1)}, f32[96,256]{1,0:T(8,128)S(1)}, u32[]{:S(2)}, u32[]{:S(2)}) collective-permute-start(f32[96,256]{1,0:T(8,128)S(1)} %get-tuple-element.32), channel_id=1, source_target_pairs={{2,0},{4,2},{6,4},{8,6},{10,8},{12,10},{14,12},{0,14},{3,1},{5,3},... | collective-permute-start | bytes 294920 | tf_op jit(solution)/shard_map/ppermute | solution.py:519
  8.0 0.0 collective-permute-done.2.other
  8.0 0.0 copy-done
  8.0 0.0 copy-done.1
  8.0 3.9 %shard_map.42 = (f32[12,7,32,64]{3,2,1,0:T(8,128)}, f32[12,7,32,64]{3,2,1,0:T(8,128)}, f32[3,7,32,64]{3,2,1,0:T(8,128)S(1)}, bf16[2,3,256,768]{3,2,1,0:T(8,128)(...) custom-call(f32[12,7,32,64]{3,2,1,0:T(8,128)S(1)} %copy-done, ...), custom_call_target="tpu_custom_call" | custom-call | flops 1610612736 | bytes 16777216 | tf_op jit(solution)/shard_map/pallas_call | solution.py:529
  12.0 0.0 collective-permute-done.low_own
  12.0 0.0 collective-permute-done.1.high_own
  12.0 0.3 %collective-permute-start.3 = (f32[96,256]{1,0:T(8,128)S(1)}, f32[96,256]{1,0:T(8,128)S(1)}, u32[]{:S(2)}, u32[]{:S(2)}) collective-permute-start(f32[96,256]{1,0:T(8,128)S(1)} %collective-permute-done.low_own), channel_id=1, source_target_pairs={{0,1},{1,0},{2,3},{3,2},{4,5},{5,4},{6,7},{7,6},{8,9},{9,8},{10,11... | collective-permute-start | bytes 294920 | tf_op jit(solution)/shard_map/ppermute | solution.py:549
  12.3 0.3 %collective-permute-start.4 = (f32[96,256]{1,0:T(8,128)S(1)}, f32[96,256]{1,0:T(8,128)S(1)}, u32[]{:S(2)}, u32[]{:S(2)}) collective-permute-start(f32[96,256]{1,0:T(8,128)S(1)} %collective-permute-done.1.high_own), channel_id=1, source_target_pairs={{0,1},{1,0},{2,3},{3,2},{4,5},{5,4},{6,7},{7,6},{8,9},{9,8},{10,11... | collective-permute-start | bytes 294920 | tf_op jit(solution)/shard_map/ppermute | solution.py:550
  12.6 1.5 %shard_map.43 = (f32[12,7,32,64]{3,2,1,0:T(8,128)}, f32[4,7,32,64]{3,2,1,0:T(8,128)S(1)}, f32[3,7,32,64]{3,2,1,0:T(8,128)S(1)}, f32[192,256]{1,0:T(8,128)S(1)}, ...) custom-call(f32[12,7,32,64]{3,2,1,0:T(8,128)S(1)} %copy-done, ...), custom_call_target="tpu_custom_call", output_to_operand_aliasing={{0}: (6, {})} | custom-call | flops 402653184 | bytes 4194304 | tf_op jit(solution)/shard_map/pallas_call | solution.py:558
  14.1 0.0 collective-permute-done.3.low_other
  14.1 0.0 collective-permute-done.4.high_other
  14.1 2.4 %shard_map.44 = (f32[12,7,32,64]{3,2,1,0:T(8,128)}, f32[12,7,32,64]{3,2,1,0:T(8,128)}) custom-call(f32[96,256]{1,0:T(8,128)S(1)} %collective-permute-done.low_own, f32[96,256]{1,0:T(8,128)S(1)} %collective-permute-done.3.low_other, f32[96,256]{1,0:T(8,128)S(1)} %collective-permute-done.1.high_own, ...), custom_call_target="tpu_custom_call", output_to_operand_aliasing={{0}: (16, {}), {1}: (17, {})} | custom-call | flops 402653184 | bytes 2097152 | tf_op jit(solution)/shard_map/pallas_call | solution.py:575
Async XLA Ops:
  1.7 6.3 %copy-start = (f32[12,7,32,64]{3,2,1,0:T(8,128)S(1)}, f32[12,7,32,64]{3,2,1,0:T(8,128)}, u32[]{:S(2)}) copy-start(f32[12,7,32,64]{3,2,1,0:T(8,128)} %own.1) | copy-start | bytes 2064388
  1.7 6.3 %copy-start.1 = (s32[96,7]{0,1:T(8,128)S(1)}, s32[96,7]{0,1:T(8,128)}, u32[]{:S(2)}) copy-start(s32[96,7]{0,1:T(8,128)} %param.3) | copy-start | bytes 8068
  1.7 6.3 %collective-permute-start.2 = (f32[12,7,32,64]{3,2,1,0:T(8,128)}, f32[12,7,32,64]{3,2,1,0:T(8,128)S(1)}, u32[]{:S(2)}, u32[]{:S(2)}) collective-permute-start(f32[12,7,32,64]{3,2,1,0:T(8,128)} %own.1), channel_id=1, source_target_pairs={{0,1},{1,0},{2,3},{3,2},{4,5},{5,4},{6,7},{7,6},{8,9},{9,8},{10,11... | collective-permute-start | bytes 2064392 | tf_op jit(solution)/shard_map/ppermute | solution.py:516
  2.4 9.6 %collective-permute-start = (f32[96,256]{1,0:T(8,128)S(1)}, f32[96,256]{1,0:T(8,128)S(1)}, u32[]{:S(2)}, u32[]{:S(2)}) collective-permute-start(f32[96,256]{1,0:T(8,128)S(1)} %get-tuple-element.31), channel_id=1, source_target_pairs={{0,2},{2,4},{4,6},{6,8},{8,10},{10,12},{12,14},{14,0},{1,3},{3,5},... | collective-permute-start | bytes 294920 | tf_op jit(solution)/shard_map/ppermute | solution.py:520
  4.9 7.1 %collective-permute-start.1 = (f32[96,256]{1,0:T(8,128)S(1)}, f32[96,256]{1,0:T(8,128)S(1)}, u32[]{:S(2)}, u32[]{:S(2)}) collective-permute-start(f32[96,256]{1,0:T(8,128)S(1)} %get-tuple-element.32), channel_id=1, source_target_pairs={{2,0},{4,2},{6,4},{8,6},{10,8},{12,10},{14,12},{0,14},{3,1},{5,3},... | collective-permute-start | bytes 294920 | tf_op jit(solution)/shard_map/ppermute | solution.py:519
  12.0 2.1 %collective-permute-start.3 = (f32[96,256]{1,0:T(8,128)S(1)}, f32[96,256]{1,0:T(8,128)S(1)}, u32[]{:S(2)}, u32[]{:S(2)}) collective-permute-start(f32[96,256]{1,0:T(8,128)S(1)} %collective-permute-done.low_own), channel_id=1, source_target_pairs={{0,1},{1,0},{2,3},{3,2},{4,5},{5,4},{6,7},{7,6},{8,9},{9,8},{10,11... | collective-permute-start | bytes 294920 | tf_op jit(solution)/shard_map/ppermute | solution.py:549
  12.3 1.8 %collective-permute-start.4 = (f32[96,256]{1,0:T(8,128)S(1)}, f32[96,256]{1,0:T(8,128)S(1)}, u32[]{:S(2)}, u32[]{:S(2)}) collective-permute-start(f32[96,256]{1,0:T(8,128)S(1)} %collective-permute-done.1.high_own), channel_id=1, source_target_pairs={{0,1},{1,0},{2,3},{3,2},{4,5},{5,4},{6,7},{7,6},{8,9},{9,8},{10,11... | collective-permute-start | bytes 294920 | tf_op jit(solution)/shard_map/ppermute | solution.py:550

commit v8 on v7

--- a/solution.py
+++ b/solution.py
@@ -25,14 +25,16 @@
 
 def product(pairs, transposed=False):
     side = 1 if transposed else 0
-    left = [x for a, _ in pairs for x in (a[0], a[0], a[1])]
-    right = [x for _, b in pairs for x in (b[0], b[1], b[0])]
-    return lax.dot_general(
-        jnp.concatenate(left, axis=1),
-        jnp.concatenate(right, axis=side),
-        (((1,), (side,)), ((), ())),
+    high, low = [jnp.concatenate([a[p] for a, _ in pairs], axis=1) for p in range(2)]
+    right = [jnp.concatenate([b[p] for _, b in pairs], axis=side) for p in range(2)]
+    dot = functools.partial(
+        lax.dot_general,
+        dimension_numbers=(((1,), (side,)), ((), ())),
         preferred_element_type=F32,
     )
+    both = dot(jnp.concatenate([high, low], axis=0), right[0])
+    count = high.shape[0]
+    return both[:count] + (both[count:] + dot(high, right[1]))
 
 
 def turn(x):

time: 16.7 us -> 16.6 us (level)
    pallas_call x1, Pallas kernels: 2.39 us -> 2.19 us  [shards(): pl.pallas_call(functools.partial(border_kernel, half_axis=half_axis), out...]
    pallas_call x1, Pallas kernels: 3.95 us -> 4.13 us  [shards(): pl.pallas_call(functools.partial(first_kernel, axes=axes, half_axis=half_...]
  transfers between devices with their start and end apart: 5 -> 5, of which waited for: 0 -> 0; matrix products, arithmetic and copies ran while one was open for 0% -> 0% of each run, Pallas kernels for 34% -> 35%
where the time goes in v8:
time: 16.6 us; the launch traced here: 16.4 us
  Pallas kernels  7.86 us (47%)
  starting transfers between devices  6.75 us (41%)
  local copies, waits for them, and re-layouts  1.07 us (6%)
  between operations  0.71 us (4%)
    pallas_call x1, Pallas kernels, shards(): pl.pallas_call(functools.partial(first_kernel, axes=axes, half_axis=half_...  4.13 us
    ppermute x1, starting transfers between devices, shards(): high_own = lax.ppermute(to_left, axes, backward)  3.1 us
    ppermute x1, starting transfers between devices, shards(): low_own = lax.ppermute(to_right, axes, forward)  2.55 us
    pallas_call x1, Pallas kernels, shards(): pl.pallas_call(functools.partial(border_kernel, half_axis=half_axis), out...  2.19 us
    pallas_call x1, Pallas kernels, shards(): pl.pallas_call(last_kernel, out_shape=[band, rows, seed] + ends_out * 2,...  1.43 us
    slice x1, local copies, waits for them, and re-layouts, shards(): top, bottom = (matrix[:REACH, REACH:], matrix[count - REACH:, :REACH + 1])  1.06 us
    ppermute x1, starting transfers between devices, shards(): other = lax.ppermute(matrix, half_axis, swap)  0.52 us
  transfers between devices with their start and end apart: 5, of which 0 were waited for; matrix products, arithmetic and copies ran while one was open for 0% of the time, Pallas kernels for 35%

profile of v8, /device:TPU:0, one launch (start us, length us, event | category | flops | bytes accessed | tf_op | source)
XLA Modules:
  0.0 16.4 jit_solution(1656233756626302267)
XLA Ops:
  0.6 1.1 %fusion = (f32[3,4,32,64]{3,2,1,0:T(8,128)S(1)}, f32[3,4,32,64]{3,2,1,0:T(8,128)S(1)}) fusion(f32[12,7,32,64]{3,2,1,0:T(8,128)} %own.1), kind=kLoop, calls=%fused_computation | loop fusion | bytes 393216 | tf_op jit(solution)/shard_map/slice | solution.py:501
  1.7 0.0 copy-start
  1.7 0.0 copy-start.1
  1.7 0.5 %collective-permute-start.2 = (f32[12,7,32,64]{3,2,1,0:T(8,128)}, f32[12,7,32,64]{3,2,1,0:T(8,128)S(1)}, u32[]{:S(2)}, u32[]{:S(2)}) collective-permute-start(f32[12,7,32,64]{3,2,1,0:T(8,128)} %own.1), channel_id=1, source_target_pairs={{0,1},{1,0},{2,3},{3,2},{4,5},{5,4},{6,7},{7,6},{8,9},{9,8},{10,11... | collective-permute-start | bytes 2064392 | tf_op jit(solution)/shard_map/ppermute | solution.py:518
  2.2 0.1 shard_map.41
  2.4 2.6 %collective-permute-start = (f32[96,256]{1,0:T(8,128)S(1)}, f32[96,256]{1,0:T(8,128)S(1)}, u32[]{:S(2)}, u32[]{:S(2)}) collective-permute-start(f32[96,256]{1,0:T(8,128)S(1)} %get-tuple-element.31), channel_id=1, source_target_pairs={{0,2},{2,4},{4,6},{6,8},{8,10},{10,12},{12,14},{14,0},{1,3},{3,5},... | collective-permute-start | bytes 294920 | tf_op jit(solution)/shard_map/ppermute | solution.py:522
  4.9 3.1 %collective-permute-start.1 = (f32[96,256]{1,0:T(8,128)S(1)}, f32[96,256]{1,0:T(8,128)S(1)}, u32[]{:S(2)}, u32[]{:S(2)}) collective-permute-start(f32[96,256]{1,0:T(8,128)S(1)} %get-tuple-element.32), channel_id=1, source_target_pairs={{2,0},{4,2},{6,4},{8,6},{10,8},{12,10},{14,12},{0,14},{3,1},{5,3},... | collective-permute-start | bytes 294920 | tf_op jit(solution)/shard_map/ppermute | solution.py:521
  8.0 0.0 collective-permute-done.2.other
  8.0 0.0 copy-done
  8.0 0.0 copy-done.1
  8.0 4.1 %shard_map.42 = (f32[12,7,32,64]{3,2,1,0:T(8,128)}, f32[12,7,32,64]{3,2,1,0:T(8,128)}, f32[3,7,32,64]{3,2,1,0:T(8,128)S(1)}, bf16[2,3,256,768]{3,2,1,0:T(8,128)(...) custom-call(f32[12,7,32,64]{3,2,1,0:T(8,128)S(1)} %copy-done, ...), custom_call_target="tpu_custom_call" | custom-call | flops 1610612736 | bytes 16777216 | tf_op jit(solution)/shard_map/pallas_call | solution.py:531
  12.2 0.0 collective-permute-done.low_own
  12.2 0.0 collective-permute-done.1.high_own
  12.2 0.3 %collective-permute-start.3 = (f32[96,256]{1,0:T(8,128)S(1)}, f32[96,256]{1,0:T(8,128)S(1)}, u32[]{:S(2)}, u32[]{:S(2)}) collective-permute-start(f32[96,256]{1,0:T(8,128)S(1)} %collective-permute-done.low_own), channel_id=1, source_target_pairs={{0,1},{1,0},{2,3},{3,2},{4,5},{5,4},{6,7},{7,6},{8,9},{9,8},{10,11... | collective-permute-start | bytes 294920 | tf_op jit(solution)/shard_map/ppermute | solution.py:551
  12.5 0.3 %collective-permute-start.4 = (f32[96,256]{1,0:T(8,128)S(1)}, f32[96,256]{1,0:T(8,128)S(1)}, u32[]{:S(2)}, u32[]{:S(2)}) collective-permute-start(f32[96,256]{1,0:T(8,128)S(1)} %collective-permute-done.1.high_own), channel_id=1, source_target_pairs={{0,1},{1,0},{2,3},{3,2},{4,5},{5,4},{6,7},{7,6},{8,9},{9,8},{10,11... | collective-permute-start | bytes 294920 | tf_op jit(solution)/shard_map/ppermute | solution.py:552
  12.8 1.4 %shard_map.43 = (f32[12,7,32,64]{3,2,1,0:T(8,128)}, f32[4,7,32,64]{3,2,1,0:T(8,128)S(1)}, f32[3,7,32,64]{3,2,1,0:T(8,128)S(1)}, f32[192,256]{1,0:T(8,128)S(1)}, ...) custom-call(f32[12,7,32,64]{3,2,1,0:T(8,128)S(1)} %copy-done, ...), custom_call_target="tpu_custom_call", output_to_operand_aliasing={{0}: (6, {})} | custom-call | flops 402653184 | bytes 4194304 | tf_op jit(solution)/shard_map/pallas_call | solution.py:560
  14.2 0.0 collective-permute-done.3.low_other
  14.2 0.0 collective-permute-done.4.high_other
  14.2 2.2 %shard_map.44 = (f32[12,7,32,64]{3,2,1,0:T(8,128)}, f32[12,7,32,64]{3,2,1,0:T(8,128)}) custom-call(f32[96,256]{1,0:T(8,128)S(1)} %collective-permute-done.low_own, f32[96,256]{1,0:T(8,128)S(1)} %collective-permute-done.3.low_other, f32[96,256]{1,0:T(8,128)S(1)} %collective-permute-done.1.high_own, ...), custom_call_target="tpu_custom_call", output_to_operand_aliasing={{0}: (16, {}), {1}: (17, {})} | custom-call | flops 402653184 | bytes 2097152 | tf_op jit(solution)/shard_map/pallas_call | solution.py:577
Async XLA Ops:
  1.7 6.3 %copy-start = (f32[12,7,32,64]{3,2,1,0:T(8,128)S(1)}, f32[12,7,32,64]{3,2,1,0:T(8,128)}, u32[]{:S(2)}) copy-start(f32[12,7,32,64]{3,2,1,0:T(8,128)} %own.1) | copy-start | bytes 2064388
  1.7 6.3 %copy-start.1 = (s32[96,7]{0,1:T(8,128)S(1)}, s32[96,7]{0,1:T(8,128)}, u32[]{:S(2)}) copy-start(s32[96,7]{0,1:T(8,128)} %param.3) | copy-start | bytes 8068
  1.7 6.3 %collective-permute-start.2 = (f32[12,7,32,64]{3,2,1,0:T(8,128)}, f32[12,7,32,64]{3,2,1,0:T(8,128)S(1)}, u32[]{:S(2)}, u32[]{:S(2)}) collective-permute-start(f32[12,7,32,64]{3,2,1,0:T(8,128)} %own.1), channel_id=1, source_target_pairs={{0,1},{1,0},{2,3},{3,2},{4,5},{5,4},{6,7},{7,6},{8,9},{9,8},{10,11... | collective-permute-start | bytes 2064392 | tf_op jit(solution)/shard_map/ppermute | solution.py:518
  2.4 9.8 %collective-permute-start = (f32[96,256]{1,0:T(8,128)S(1)}, f32[96,256]{1,0:T(8,128)S(1)}, u32[]{:S(2)}, u32[]{:S(2)}) collective-permute-start(f32[96,256]{1,0:T(8,128)S(1)} %get-tuple-element.31), channel_id=1, source_target_pairs={{0,2},{2,4},{4,6},{6,8},{8,10},{10,12},{12,14},{14,0},{1,3},{3,5},... | collective-permute-start | bytes 294920 | tf_op jit(solution)/shard_map/ppermute | solution.py:522
  4.9 7.3 %collective-permute-start.1 = (f32[96,256]{1,0:T(8,128)S(1)}, f32[96,256]{1,0:T(8,128)S(1)}, u32[]{:S(2)}, u32[]{:S(2)}) collective-permute-start(f32[96,256]{1,0:T(8,128)S(1)} %get-tuple-element.32), channel_id=1, source_target_pairs={{2,0},{4,2},{6,4},{8,6},{10,8},{12,10},{14,12},{0,14},{3,1},{5,3},... | collective-permute-start | bytes 294920 | tf_op jit(solution)/shard_map/ppermute | solution.py:521
  12.2 2.0 %collective-permute-start.3 = (f32[96,256]{1,0:T(8,128)S(1)}, f32[96,256]{1,0:T(8,128)S(1)}, u32[]{:S(2)}, u32[]{:S(2)}) collective-permute-start(f32[96,256]{1,0:T(8,128)S(1)} %collective-permute-done.low_own), channel_id=1, source_target_pairs={{0,1},{1,0},{2,3},{3,2},{4,5},{5,4},{6,7},{7,6},{8,9},{9,8},{10,11... | collective-permute-start | bytes 294920 | tf_op jit(solution)/shard_map/ppermute | solution.py:551
  12.5 1.7 %collective-permute-start.4 = (f32[96,256]{1,0:T(8,128)S(1)}, f32[96,256]{1,0:T(8,128)S(1)}, u32[]{:S(2)}, u32[]{:S(2)}) collective-permute-start(f32[96,256]{1,0:T(8,128)S(1)} %collective-permute-done.1.high_own), channel_id=1, source_target_pairs={{0,1},{1,0},{2,3},{3,2},{4,5},{5,4},{6,7},{7,6},{8,9},{9,8},{10,11... | collective-permute-start | bytes 294920 | tf_op jit(solution)/shard_map/ppermute | solution.py:552

commit v9 on v8

--- a/solution.py
+++ b/solution.py
@@ -268,14 +268,11 @@
         write_lines(pat, lines, lax.axis_index(axes) * it.count, groups)
         it.far_seed(0, seed)
 
-    build(0)
-    build(1)
+    lax.fori_loop(0, groups, lambda g, _: build(g), None)
     steps = [begin]
     for g in range(groups):
         if g + 1 < groups:
             steps.append(squares(g, g + 1, results.at[count_dots(steps)]))
-            if g + 2 < groups:
-                steps.append(functools.partial(build, g + 2))
         steps.append(squares(g, g, results.at[count_dots(steps)]))
         steps.append(functools.partial(it.send, g, 0, staged[g], square_out, sems))
         if g > 0:

time: 16.6 us -> 16.9 us (1.018)
  Pallas kernels: 7.86 us -> 8.24 us
    pallas_call x1, Pallas kernels: 4.13 us -> 4.52 us  [shards(): pl.pallas_call(functools.partial(first_kernel, axes=axes, half_axis=half_...]
  transfers between devices with their start and end apart: 5 -> 5, of which waited for: 0 -> 0; matrix products, arithmetic and copies ran while one was open for 0% -> 0% of each run, Pallas kernels for 35% -> 36%
where the time goes in v9:
time: 16.9 us; the launch traced here: 16.8 us
  Pallas kernels  8.24 us (49%)
  starting transfers between devices  6.75 us (40%)
  local copies, waits for them, and re-layouts  1.07 us (6%)
  between operations  0.71 us (4%)
    pallas_call x1, Pallas kernels, shards(): pl.pallas_call(functools.partial(first_kernel, axes=axes, half_axis=half_...  4.52 us
    ppermute x1, starting transfers between devices, shards(): high_own = lax.ppermute(to_left, axes, backward)  3.1 us
    ppermute x1, starting transfers between devices, shards(): low_own = lax.ppermute(to_right, axes, forward)  2.55 us
    pallas_call x1, Pallas kernels, shards(): pl.pallas_call(functools.partial(border_kernel, half_axis=half_axis), out...  2.18 us
    pallas_call x1, Pallas kernels, shards(): pl.pallas_call(last_kernel, out_shape=[band, rows, seed] + ends_out * 2,...  1.43 us
    slice x1, local copies, waits for them, and re-layouts, shards(): top, bottom = (matrix[:REACH, REACH:], matrix[count - REACH:, :REACH + 1])  1.06 us
    ppermute x1, starting transfers between devices, shards(): other = lax.ppermute(matrix, half_axis, swap)  0.52 us
  transfers between devices with their start and end apart: 5, of which 0 were waited for; matrix products, arithmetic and copies ran while one was open for 0% of the time, Pallas kernels for 36%

profile of v9, /device:TPU:0, one launch (start us, length us, event | category | flops | bytes accessed | tf_op | source)
XLA Modules:
  0.0 16.8 jit_solution(17588648040170477156)
XLA Ops:
  0.6 1.1 %fusion = (f32[3,4,32,64]{3,2,1,0:T(8,128)S(1)}, f32[3,4,32,64]{3,2,1,0:T(8,128)S(1)}) fusion(f32[12,7,32,64]{3,2,1,0:T(8,128)} %own.1), kind=kLoop, calls=%fused_computation | loop fusion | bytes 393216 | tf_op jit(solution)/shard_map/slice | solution.py:498
  1.7 0.0 copy-start
  1.7 0.0 copy-start.1
  1.7 0.5 %collective-permute-start.2 = (f32[12,7,32,64]{3,2,1,0:T(8,128)}, f32[12,7,32,64]{3,2,1,0:T(8,128)S(1)}, u32[]{:S(2)}, u32[]{:S(2)}) collective-permute-start(f32[12,7,32,64]{3,2,1,0:T(8,128)} %own.1), channel_id=1, source_target_pairs={{0,1},{1,0},{2,3},{3,2},{4,5},{5,4},{6,7},{7,6},{8,9},{9,8},{10,11... | collective-permute-start | bytes 2064392 | tf_op jit(solution)/shard_map/ppermute | solution.py:515
  2.2 0.1 shard_map.41
  2.4 2.6 %collective-permute-start = (f32[96,256]{1,0:T(8,128)S(1)}, f32[96,256]{1,0:T(8,128)S(1)}, u32[]{:S(2)}, u32[]{:S(2)}) collective-permute-start(f32[96,256]{1,0:T(8,128)S(1)} %get-tuple-element.31), channel_id=1, source_target_pairs={{0,2},{2,4},{4,6},{6,8},{8,10},{10,12},{12,14},{14,0},{1,3},{3,5},... | collective-permute-start | bytes 294920 | tf_op jit(solution)/shard_map/ppermute | solution.py:519
  4.9 3.1 %collective-permute-start.1 = (f32[96,256]{1,0:T(8,128)S(1)}, f32[96,256]{1,0:T(8,128)S(1)}, u32[]{:S(2)}, u32[]{:S(2)}) collective-permute-start(f32[96,256]{1,0:T(8,128)S(1)} %get-tuple-element.32), channel_id=1, source_target_pairs={{2,0},{4,2},{6,4},{8,6},{10,8},{12,10},{14,12},{0,14},{3,1},{5,3},... | collective-permute-start | bytes 294920 | tf_op jit(solution)/shard_map/ppermute | solution.py:518
  8.0 0.0 collective-permute-done.2.other
  8.0 0.0 copy-done
  8.0 0.0 copy-done.1
  8.0 4.5 %shard_map.42 = (f32[12,7,32,64]{3,2,1,0:T(8,128)}, f32[12,7,32,64]{3,2,1,0:T(8,128)}, f32[3,7,32,64]{3,2,1,0:T(8,128)S(1)}, bf16[2,3,256,768]{3,2,1,0:T(8,128)(...) custom-call(f32[12,7,32,64]{3,2,1,0:T(8,128)S(1)} %copy-done, ...), custom_call_target="tpu_custom_call" | custom-call | flops 1610612736 | bytes 16777216 | tf_op jit(solution)/shard_map/pallas_call | solution.py:528
  12.6 0.0 collective-permute-done.low_own
  12.6 0.0 collective-permute-done.1.high_own
  12.6 0.3 %collective-permute-start.3 = (f32[96,256]{1,0:T(8,128)S(1)}, f32[96,256]{1,0:T(8,128)S(1)}, u32[]{:S(2)}, u32[]{:S(2)}) collective-permute-start(f32[96,256]{1,0:T(8,128)S(1)} %collective-permute-done.low_own), channel_id=1, source_target_pairs={{0,1},{1,0},{2,3},{3,2},{4,5},{5,4},{6,7},{7,6},{8,9},{9,8},{10,11... | collective-permute-start | bytes 294920 | tf_op jit(solution)/shard_map/ppermute | solution.py:548
  12.9 0.3 %collective-permute-start.4 = (f32[96,256]{1,0:T(8,128)S(1)}, f32[96,256]{1,0:T(8,128)S(1)}, u32[]{:S(2)}, u32[]{:S(2)}) collective-permute-start(f32[96,256]{1,0:T(8,128)S(1)} %collective-permute-done.1.high_own), channel_id=1, source_target_pairs={{0,1},{1,0},{2,3},{3,2},{4,5},{5,4},{6,7},{7,6},{8,9},{9,8},{10,11... | collective-permute-start | bytes 294920 | tf_op jit(solution)/shard_map/ppermute | solution.py:549
  13.1 1.4 %shard_map.43 = (f32[12,7,32,64]{3,2,1,0:T(8,128)}, f32[4,7,32,64]{3,2,1,0:T(8,128)S(1)}, f32[3,7,32,64]{3,2,1,0:T(8,128)S(1)}, f32[192,256]{1,0:T(8,128)S(1)}, ...) custom-call(f32[12,7,32,64]{3,2,1,0:T(8,128)S(1)} %copy-done, ...), custom_call_target="tpu_custom_call", output_to_operand_aliasing={{0}: (6, {})} | custom-call | flops 402653184 | bytes 4194304 | tf_op jit(solution)/shard_map/pallas_call | solution.py:557
  14.6 0.0 collective-permute-done.3.low_other
  14.6 0.0 collective-permute-done.4.high_other
  14.6 2.2 %shard_map.44 = (f32[12,7,32,64]{3,2,1,0:T(8,128)}, f32[12,7,32,64]{3,2,1,0:T(8,128)}) custom-call(f32[96,256]{1,0:T(8,128)S(1)} %collective-permute-done.low_own, f32[96,256]{1,0:T(8,128)S(1)} %collective-permute-done.3.low_other, f32[96,256]{1,0:T(8,128)S(1)} %collective-permute-done.1.high_own, ...), custom_call_target="tpu_custom_call", output_to_operand_aliasing={{0}: (16, {}), {1}: (17, {})} | custom-call | flops 402653184 | bytes 2097152 | tf_op jit(solution)/shard_map/pallas_call | solution.py:574
Async XLA Ops:
  1.7 6.3 %copy-start = (f32[12,7,32,64]{3,2,1,0:T(8,128)S(1)}, f32[12,7,32,64]{3,2,1,0:T(8,128)}, u32[]{:S(2)}) copy-start(f32[12,7,32,64]{3,2,1,0:T(8,128)} %own.1) | copy-start | bytes 2064388
  1.7 6.3 %copy-start.1 = (s32[96,7]{0,1:T(8,128)S(1)}, s32[96,7]{0,1:T(8,128)}, u32[]{:S(2)}) copy-start(s32[96,7]{0,1:T(8,128)} %param.3) | copy-start | bytes 8068
  1.7 6.3 %collective-permute-start.2 = (f32[12,7,32,64]{3,2,1,0:T(8,128)}, f32[12,7,32,64]{3,2,1,0:T(8,128)S(1)}, u32[]{:S(2)}, u32[]{:S(2)}) collective-permute-start(f32[12,7,32,64]{3,2,1,0:T(8,128)} %own.1), channel_id=1, source_target_pairs={{0,1},{1,0},{2,3},{3,2},{4,5},{5,4},{6,7},{7,6},{8,9},{9,8},{10,11... | collective-permute-start | bytes 2064392 | tf_op jit(solution)/shard_map/ppermute | solution.py:515
  2.4 10.2 %collective-permute-start = (f32[96,256]{1,0:T(8,128)S(1)}, f32[96,256]{1,0:T(8,128)S(1)}, u32[]{:S(2)}, u32[]{:S(2)}) collective-permute-start(f32[96,256]{1,0:T(8,128)S(1)} %get-tuple-element.31), channel_id=1, source_target_pairs={{0,2},{2,4},{4,6},{6,8},{8,10},{10,12},{12,14},{14,0},{1,3},{3,5},... | collective-permute-start | bytes 294920 | tf_op jit(solution)/shard_map/ppermute | solution.py:519
  4.9 7.7 %collective-permute-start.1 = (f32[96,256]{1,0:T(8,128)S(1)}, f32[96,256]{1,0:T(8,128)S(1)}, u32[]{:S(2)}, u32[]{:S(2)}) collective-permute-start(f32[96,256]{1,0:T(8,128)S(1)} %get-tuple-element.32), channel_id=1, source_target_pairs={{2,0},{4,2},{6,4},{8,6},{10,8},{12,10},{14,12},{0,14},{3,1},{5,3},... | collective-permute-start | bytes 294920 | tf_op jit(solution)/shard_map/ppermute | solution.py:518
  12.6 2.0 %collective-permute-start.3 = (f32[96,256]{1,0:T(8,128)S(1)}, f32[96,256]{1,0:T(8,128)S(1)}, u32[]{:S(2)}, u32[]{:S(2)}) collective-permute-start(f32[96,256]{1,0:T(8,128)S(1)} %collective-permute-done.low_own), channel_id=1, source_target_pairs={{0,1},{1,0},{2,3},{3,2},{4,5},{5,4},{6,7},{7,6},{8,9},{9,8},{10,11... | collective-permute-start | bytes 294920 | tf_op jit(solution)/shard_map/ppermute | solution.py:548
  12.9 1.7 %collective-permute-start.4 = (f32[96,256]{1,0:T(8,128)S(1)}, f32[96,256]{1,0:T(8,128)S(1)}, u32[]{:S(2)}, u32[]{:S(2)}) collective-permute-start(f32[96,256]{1,0:T(8,128)S(1)} %collective-permute-done.1.high_own), channel_id=1, source_target_pairs={{0,1},{1,0},{2,3},{3,2},{4,5},{5,4},{6,7},{7,6},{8,9},{9,8},{10,11... | collective-permute-start | bytes 294920 | tf_op jit(solution)/shard_map/ppermute | solution.py:549

commit v10 on v8

--- a/solution.py
+++ b/solution.py
@@ -43,15 +43,19 @@
 
 def write_lines(pat, lines, first, groups):
     total = pat.shape[1]
-    lane = lax.broadcasted_iota(jnp.int32, (1, 2 * BS), 1)
-    for g in range(-1, groups + 1):
-        for s in range(GROUP):
-            row = lax.rem(first + g * GROUP + s + total, total)
-            for t in range(3 * GROUP // 2):
-                ks = [2 * t + e - s - 1 for e in range(2)]
-                f = [pat[k, row].astype(F32) if 0 <= k < SPAN else F32(0) for k in ks]
-                at = (g + 1) * GROUP + s
-                lines[at : at + 1, t * 2 * BS : (t + 1) * 2 * BS] = jnp.where(lane < BS, f[0], f[1])
+    rows = lines.shape[0]
+    iota = functools.partial(lax.broadcasted_iota, jnp.int32)
+    dot = functools.partial(lax.dot_general, preferred_element_type=F32)
+    wanted = lax.rem(first - GROUP + total + iota((rows, total), 0), total)
+    chosen = (iota((rows, total), 1) == wanted).astype(BF)
+    flags = dot(chosen, pat[...].astype(BF), (((1,), (1,)), ((), ())))
+    place = iota((rows, 1), 0) % GROUP
+    spread = jnp.concatenate(
+        [jnp.where(place == s, flags, 0.0) for s in range(GROUP)], axis=1
+    ).astype(BF)
+    block = iota((SPAN, 3 * WIDE), 1) // BS - iota((SPAN, 3 * WIDE), 0) - 1
+    spots = jnp.concatenate([(block == s).astype(BF) for s in range(GROUP)], axis=0)
+    lines[...] = dot(spread, spots, (((1,), (0,)), ((), ())))
 
 
 def line_of(lines, g, s, h):
@@ -180,11 +184,9 @@
 
 
 def first_kernel(
-    own, other, pattern, square_out, sign_out, seed, full, mine, keep, lines, sign_left,
-    pat, square, sign, results, sems, pat_sem, *, axes, half_axis
+    own, other, pat, square_out, seed, full, mine, keep, lines, sign,
+    square, results, sems, *, axes, half_axis
 ):
-    load = pltpu.make_async_copy(pattern, pat, pat_sem)
-    load.start()
     it = Interior(own, lines, full, mine, keep)
     groups = it.groups
     upper_half = lax.axis_index(half_axis) == 1
@@ -261,10 +263,8 @@
         return dot, store, post
 
     staged = [square.at[g] for g in range(groups)]
-    signs = [sign.at[g] for g in range(groups - 2)] + [sign_left]
 
     def begin():
-        load.wait()
         write_lines(pat, lines, lax.axis_index(axes) * it.count, groups)
         it.far_seed(0, seed)
 
@@ -278,21 +278,20 @@
                 steps.append(functools.partial(build, g + 2))
         steps.append(squares(g, g, results.at[count_dots(steps)]))
         steps.append(functools.partial(it.send, g, 0, staged[g], square_out, sems))
-        if g > 0:
-            for h in it.near(g - 1):
-                steps.append(it.second(g - 1, h, signs[g - 1], seed, results.at[count_dots(steps)]))
-            if g < groups - 1:
-                steps.append(functools.partial(it.send, g - 1, 1, signs[g - 1], sign_out, sems))
+    for g in range(groups - 1):
+        for h in it.near(g):
+            steps.append(it.second(g, h, sign.at[g], seed, results.at[count_dots(steps)]))
     staggered(steps)
     it.finish()
 
 
 def last_kernel(
-    own, lines, full, mine, keep, sign_left, sign_in, sign_out, sign, seed, low_a, low_b, low_m, low_p, high_a, high_b, high_m, high_p, results, sems
+    own, lines, full, mine, keep, sign_first, sign_out, sign, seed, low_a, low_b, low_m, low_p, high_a, high_b, high_m, high_p, results, sems
 ):
     it = Interior(own, lines, full, mine, keep)
     last = it.groups - 1
-    it.send(last - 1, 1, sign_left, sign_out, sems)
+    for g in range(last):
+        it.send(g, 1, sign_first.at[g], sign_out, sems)
     steps = [it.second(last, h, sign, seed, results.at[i]) for i, h in enumerate(it.near(last))]
     steps.append(functools.partial(it.far_seed, last, seed))
 
@@ -528,18 +527,16 @@
     keep = jax.ShapeDtypeStruct((2, 3 * groups, WIDE, WIDE), BF)
     lines = jax.ShapeDtypeStruct(((groups + 2) * GROUP, 3 * WIDE), F32)
     rows = jax.ShapeDtypeStruct((GROUP,) + matrix.shape[1:], F32)
-    square, sign, low_seed, full, mine, keep, lines, sign_left = pl.pallas_call(
+    first_rows = jax.ShapeDtypeStruct((groups - 1,) + rows.shape, F32)
+    square, low_seed, full, mine, keep, lines, sign_first = pl.pallas_call(
         functools.partial(first_kernel, axes=axes, half_axis=half_axis),
-        out_shape=[band, band, seed, full, mine, keep, lines, rows],
-        in_specs=[vmem, vmem, hbm],
-        out_specs=[hbm] * 2 + [vmem] * 6,
+        out_shape=[band, seed, full, mine, keep, lines, first_rows],
+        in_specs=[vmem] * 3,
+        out_specs=[hbm] + [vmem] * 6,
         scratch_shapes=[
-            pltpu.SMEM(flags.shape, jnp.int32),
             pltpu.VMEM((groups,) + rows.shape, F32),
-            pltpu.VMEM((groups - 2,) + rows.shape, F32),
             pltpu.VMEM((2 * groups - 1 + 3 * groups - 4, WIDE, WIDE), F32),
             pltpu.SemaphoreType.DMA((2, count)),
-            pltpu.SemaphoreType.DMA,
         ],
         compiler_params=params,
         cost_estimate=pl.CostEstimate(
@@ -560,18 +557,17 @@
     sign, sign_last, high_seed, *ends = pl.pallas_call(
         last_kernel,
         out_shape=[band, rows, seed] + ends_out * 2,
-        in_specs=[vmem] * 6 + [hbm],
+        in_specs=[vmem] * 6,
         out_specs=[hbm] + [vmem] * 10,
         scratch_shapes=[
             pltpu.VMEM((2, GROUP * HALF, WIDE), F32),
             pltpu.SemaphoreType.DMA((2, count)),
         ],
-        input_output_aliases={6: 0},
         compiler_params=params,
         cost_estimate=pl.CostEstimate(
             flops=3 * 2 * 4 * WIDE**3, bytes_accessed=4 * 2**20, transcendentals=0
         ),
-    )(matrix, lines, full, mine, keep, sign_left, sign)
+    )(matrix, lines, full, mine, keep, sign_first)
 
     return tuple(
         pl.pallas_call(

time: 16.6 us -> 16.4 us (0.988)
  Pallas kernels: 7.86 us -> 7.17 us
  waiting for transfers between devices: 0.01 us -> 0.6 us
    pallas_call x1, Pallas kernels: 4.13 us -> 3.3 us  [shards(): pl.pallas_call(functools.partial(first_kernel, axes=axes, half_axis=half_...]
    ppermute x1, waiting for transfers between devices: 0.01 us -> 0.42 us  [shards(): high_own = lax.ppermute(to_left, axes, backward)]
    ppermute x1, starting transfers between devices: 0.29 us -> 0.01 us  [shards(): low_other = lax.ppermute(low_own, half_axis, swap)]
    ppermute x1, starting transfers between devices: 0.29 us -> 0.51 us  [shards(): high_other = lax.ppermute(high_own, half_axis, swap)]
    ppermute x1, waiting for transfers between devices: 0.01 us -> 0.17 us  [shards(): low_own = lax.ppermute(to_right, axes, forward)]
  transfers between devices with their start and end apart: 5 -> 5, of which waited for: 0 -> 2; matrix products, arithmetic and copies ran while one was open for 0% -> 0% of each run, Pallas kernels for 35% -> 31%
where the time goes in v10:
time: 16.4 us; the launch traced here: 16.2 us
  Pallas kernels  7.17 us (44%)
  starting transfers between devices  6.68 us (41%)
  local copies, waits for them, and re-layouts  1.07 us (7%)
  between operations  0.7 us (4%)
  waiting for transfers between devices  0.6 us (4%)
    pallas_call x1, Pallas kernels, shards(): pl.pallas_call(functools.partial(first_kernel, axes=axes, half_axis=half_...  3.3 us
    ppermute x1, starting transfers between devices, shards(): high_own = lax.ppermute(to_left, axes, backward)  3.1 us
    ppermute x1, starting transfers between devices, shards(): low_own = lax.ppermute(to_right, axes, forward)  2.55 us
    pallas_call x1, Pallas kernels, shards(): pl.pallas_call(functools.partial(border_kernel, half_axis=half_axis), out...  2.19 us
    pallas_call x1, Pallas kernels, shards(): pl.pallas_call(last_kernel, out_shape=[band, rows, seed] + ends_out * 2,...  1.57 us
    slice x1, local copies, waits for them, and re-layouts, shards(): top, bottom = (matrix[:REACH, REACH:], matrix[count - REACH:, :REACH + 1])  1.06 us
    ppermute x1, starting transfers between devices, shards(): other = lax.ppermute(matrix, half_axis, swap)  0.52 us
    ppermute x1, starting transfers between devices, shards(): high_other = lax.ppermute(high_own, half_axis, swap)  0.51 us
  transfers between devices with their start and end apart: 5, of which 2 were waited for; matrix products, arithmetic and copies ran while one was open for 0% of the time, Pallas kernels for 31%

profile of v10, /device:TPU:0, one launch (start us, length us, event | category | flops | bytes accessed | tf_op | source)
XLA Modules:
  0.0 16.2 jit_solution(4601247500430883089)
XLA Ops:
  0.6 1.1 %fusion = (f32[3,4,32,64]{3,2,1,0:T(8,128)S(1)}, f32[3,4,32,64]{3,2,1,0:T(8,128)S(1)}) fusion(f32[12,7,32,64]{3,2,1,0:T(8,128)} %own.1), kind=kLoop, calls=%fused_computation | loop fusion | bytes 393216 | tf_op jit(solution)/shard_map/slice | solution.py:500
  1.7 0.0 copy-start
  1.7 0.0 copy-start.1
  1.7 0.5 %collective-permute-start.2 = (f32[12,7,32,64]{3,2,1,0:T(8,128)}, f32[12,7,32,64]{3,2,1,0:T(8,128)S(1)}, u32[]{:S(2)}, u32[]{:S(2)}) collective-permute-start(f32[12,7,32,64]{3,2,1,0:T(8,128)} %own.1), channel_id=1, source_target_pairs={{0,1},{1,0},{2,3},{3,2},{4,5},{5,4},{6,7},{7,6},{8,9},{9,8},{10,11... | collective-permute-start | bytes 2064392 | tf_op jit(solution)/shard_map/ppermute | solution.py:517
  2.2 0.1 shard_map.41
  2.4 2.6 %collective-permute-start = (f32[96,256]{1,0:T(8,128)S(1)}, f32[96,256]{1,0:T(8,128)S(1)}, u32[]{:S(2)}, u32[]{:S(2)}) collective-permute-start(f32[96,256]{1,0:T(8,128)S(1)} %get-tuple-element.30), channel_id=1, source_target_pairs={{0,2},{2,4},{4,6},{6,8},{8,10},{10,12},{12,14},{14,0},{1,3},{3,5},... | collective-permute-start | bytes 294920 | tf_op jit(solution)/shard_map/ppermute | solution.py:521
  4.9 3.1 %collective-permute-start.1 = (f32[96,256]{1,0:T(8,128)S(1)}, f32[96,256]{1,0:T(8,128)S(1)}, u32[]{:S(2)}, u32[]{:S(2)}) collective-permute-start(f32[96,256]{1,0:T(8,128)S(1)} %get-tuple-element.31), channel_id=1, source_target_pairs={{2,0},{4,2},{6,4},{8,6},{10,8},{12,10},{14,12},{0,14},{3,1},{5,3},... | collective-permute-start | bytes 294920 | tf_op jit(solution)/shard_map/ppermute | solution.py:520
  8.0 0.0 collective-permute-done.2.other
  8.0 0.0 copy-done
  8.0 0.0 copy-done.1
  8.0 3.3 %shard_map.42 = (f32[12,7,32,64]{3,2,1,0:T(8,128)}, f32[3,7,32,64]{3,2,1,0:T(8,128)S(1)}, bf16[2,3,256,768]{3,2,1,0:T(8,128)(2,1)S(1)}, bf16[2,3,128,768]{3,2,1,...) custom-call(f32[12,7,32,64]{3,2,1,0:T(8,128)S(1)} %copy-done, ...), custom_call_target="tpu_custom_call" | custom-call | flops 1610612736 | bytes 16777216 | tf_op jit(solution)/shard_map/pallas_call | solution.py:531
  11.3 0.2 %collective-permute-done.low_own = f32[96,256]{1,0:T(8,128)S(1)} collective-permute-done((f32[96,256]{1,0:T(8,128)S(1)}, f32[96,256]{1,0:T(8,128)S(1)}, u32[]{:S(2)}, u32[]{:S(2)}) %collective-permute-start) | collective-permute-done | bytes 98336 | tf_op jit(solution)/shard_map/ppermute | solution.py:521
  11.5 0.4 %collective-permute-done.1.high_own = f32[96,256]{1,0:T(8,128)S(1)} collective-permute-done((f32[96,256]{1,0:T(8,128)S(1)}, f32[96,256]{1,0:T(8,128)S(1)}, u32[]{:S(2)}, u32[]{:S(2)}) %collective-permute-start.1) | collective-permute-done | bytes 98336 | tf_op jit(solution)/shard_map/ppermute | solution.py:520
  11.9 0.0 collective-permute-start.3
  11.9 0.5 %collective-permute-start.4 = (f32[96,256]{1,0:T(8,128)S(1)}, f32[96,256]{1,0:T(8,128)S(1)}, u32[]{:S(2)}, u32[]{:S(2)}) collective-permute-start(f32[96,256]{1,0:T(8,128)S(1)} %collective-permute-done.1.high_own), channel_id=1, source_target_pairs={{0,1},{1,0},{2,3},{3,2},{4,5},{5,4},{6,7},{7,6},{8,9},{9,8},{10,11... | collective-permute-start | bytes 294920 | tf_op jit(solution)/shard_map/ppermute | solution.py:549
  12.4 1.6 %shard_map.43 = (f32[12,7,32,64]{3,2,1,0:T(8,128)}, f32[4,7,32,64]{3,2,1,0:T(8,128)S(1)}, f32[3,7,32,64]{3,2,1,0:T(8,128)S(1)}, f32[192,256]{1,0:T(8,128)S(1)}, ...) custom-call(f32[12,7,32,64]{3,2,1,0:T(8,128)S(1)} %copy-done, ...), custom_call_target="tpu_custom_call" | custom-call | flops 402653184 | bytes 4194304 | tf_op jit(solution)/shard_map/pallas_call | solution.py:557
  14.0 0.0 collective-permute-done.3.low_other
  14.0 0.0 collective-permute-done.4.high_other
  14.0 2.2 %shard_map.44 = (f32[12,7,32,64]{3,2,1,0:T(8,128)}, f32[12,7,32,64]{3,2,1,0:T(8,128)}) custom-call(f32[96,256]{1,0:T(8,128)S(1)} %collective-permute-done.low_own, f32[96,256]{1,0:T(8,128)S(1)} %collective-permute-done.3.low_other, f32[96,256]{1,0:T(8,128)S(1)} %collective-permute-done.1.high_own, ...), custom_call_target="tpu_custom_call", output_to_operand_aliasing={{0}: (16, {}), {1}: (17, {})} | custom-call | flops 402653184 | bytes 2097152 | tf_op jit(solution)/shard_map/pallas_call | solution.py:573
Async XLA Ops:
  1.7 6.3 %copy-start = (f32[12,7,32,64]{3,2,1,0:T(8,128)S(1)}, f32[12,7,32,64]{3,2,1,0:T(8,128)}, u32[]{:S(2)}) copy-start(f32[12,7,32,64]{3,2,1,0:T(8,128)} %own.1) | copy-start | bytes 2064388
  1.7 6.3 %copy-start.1 = (s32[96,7]{0,1:T(8,128)S(1)}, s32[96,7]{0,1:T(8,128)}, u32[]{:S(2)}) copy-start(s32[96,7]{0,1:T(8,128)} %param.3) | copy-start | bytes 8068
  1.7 6.3 %collective-permute-start.2 = (f32[12,7,32,64]{3,2,1,0:T(8,128)}, f32[12,7,32,64]{3,2,1,0:T(8,128)S(1)}, u32[]{:S(2)}, u32[]{:S(2)}) collective-permute-start(f32[12,7,32,64]{3,2,1,0:T(8,128)} %own.1), channel_id=1, source_target_pairs={{0,1},{1,0},{2,3},{3,2},{4,5},{5,4},{6,7},{7,6},{8,9},{9,8},{10,11... | collective-permute-start | bytes 2064392 | tf_op jit(solution)/shard_map/ppermute | solution.py:517
  2.4 9.2 %collective-permute-start = (f32[96,256]{1,0:T(8,128)S(1)}, f32[96,256]{1,0:T(8,128)S(1)}, u32[]{:S(2)}, u32[]{:S(2)}) collective-permute-start(f32[96,256]{1,0:T(8,128)S(1)} %get-tuple-element.30), channel_id=1, source_target_pairs={{0,2},{2,4},{4,6},{6,8},{8,10},{10,12},{12,14},{14,0},{1,3},{3,5},... | collective-permute-start | bytes 294920 | tf_op jit(solution)/shard_map/ppermute | solution.py:521
  4.9 7.0 %collective-permute-start.1 = (f32[96,256]{1,0:T(8,128)S(1)}, f32[96,256]{1,0:T(8,128)S(1)}, u32[]{:S(2)}, u32[]{:S(2)}) collective-permute-start(f32[96,256]{1,0:T(8,128)S(1)} %get-tuple-element.31), channel_id=1, source_target_pairs={{2,0},{4,2},{6,4},{8,6},{10,8},{12,10},{14,12},{0,14},{3,1},{5,3},... | collective-permute-start | bytes 294920 | tf_op jit(solution)/shard_map/ppermute | solution.py:520
  11.9 2.1 %collective-permute-start.3 = (f32[96,256]{1,0:T(8,128)S(1)}, f32[96,256]{1,0:T(8,128)S(1)}, u32[]{:S(2)}, u32[]{:S(2)}) collective-permute-start(f32[96,256]{1,0:T(8,128)S(1)} %collective-permute-done.low_own), channel_id=1, source_target_pairs={{0,1},{1,0},{2,3},{3,2},{4,5},{5,4},{6,7},{7,6},{8,9},{9,8},{10,11... | collective-permute-start | bytes 294920 | tf_op jit(solution)/shard_map/ppermute | solution.py:548
  11.9 2.1 %collective-permute-start.4 = (f32[96,256]{1,0:T(8,128)S(1)}, f32[96,256]{1,0:T(8,128)S(1)}, u32[]{:S(2)}, u32[]{:S(2)}) collective-permute-start(f32[96,256]{1,0:T(8,128)S(1)} %collective-permute-done.1.high_own), channel_id=1, source_target_pairs={{0,1},{1,0},{2,3},{3,2},{4,5},{5,4},{6,7},{7,6},{8,9},{9,8},{10,11... | collective-permute-start | bytes 294920 | tf_op jit(solution)/shard_map/ppermute | solution.py:549

commit v11 on v10

--- a/solution.py
+++ b/solution.py
@@ -148,6 +148,29 @@
             for k in range(0, REACH - s) if g == 0 else range(2 * REACH - s, SPAN):
                 seed[s, k] = 1.5 * self.own[a, k]
 
+    def reaching(self, a_ref, b_ref, m_ref, p_ref, g, e, r0):
+        rows = slice(r0, r0 + REACH * BS)
+        mine_rows = slice(r0 // 2, r0 // 2 + REACH * HALF)
+        outer = slice(BS - r0, BS - r0 + REACH * BS)
+
+        def dot():
+            out = self.part(g, e)
+            return (
+                product([([x[outer] for x in turn(out)], out)]),
+                product([(self.part(g, g, rows), out)]),
+            )
+
+        def store(value):
+            a_ref[...], b_ref[...] = value
+
+        def post():
+            for p in range(2):
+                m_ref[p] = self.part(g, e)[p][rows]
+                p_ref[p, 0] = self.my_part(g, e)[p][mine_rows]
+                p_ref[p, 1] = self.my_part(g, g)[p][mine_rows]
+
+        return dot, store, post
+
     def send(self, g, i, source, target, sems):
         for s in range(GROUP):
             a = g * GROUP + s
@@ -184,8 +207,8 @@
 
 
 def first_kernel(
-    own, other, pat, square_out, seed, full, mine, keep, lines, sign,
-    square, results, sems, *, axes, half_axis
+    own, other, pat, square_out, sign_out, seed, full, mine, keep, lines, low_a, low_b, low_m, low_p,
+    high_a, high_b, high_m, high_p, square, sign, results, sems, *, axes, half_axis
 ):
     it = Interior(own, lines, full, mine, keep)
     groups = it.groups
@@ -281,47 +304,20 @@
     for g in range(groups - 1):
         for h in it.near(g):
             steps.append(it.second(g, h, sign.at[g], seed, results.at[count_dots(steps)]))
+        steps.append(functools.partial(it.send, g, 1, sign.at[g], sign_out, sems))
+    steps.append(it.reaching(low_a, low_b, low_m, low_p, 0, -1, 0))
+    steps.append(it.reaching(high_a, high_b, high_m, high_p, groups - 1, groups, BS))
     staggered(steps)
     it.finish()
 
 
-def last_kernel(
-    own, lines, full, mine, keep, sign_first, sign_out, sign, seed, low_a, low_b, low_m, low_p, high_a, high_b, high_m, high_p, results, sems
-):
+def last_kernel(own, lines, full, mine, keep, sign, seed, results):
     it = Interior(own, lines, full, mine, keep)
     last = it.groups - 1
-    for g in range(last):
-        it.send(g, 1, sign_first.at[g], sign_out, sems)
     steps = [it.second(last, h, sign, seed, results.at[i]) for i, h in enumerate(it.near(last))]
     steps.append(functools.partial(it.far_seed, last, seed))
 
-    def reaching(a_ref, b_ref, m_ref, p_ref, g, e, r0):
-        rows = slice(r0, r0 + REACH * BS)
-        mine_rows = slice(r0 // 2, r0 // 2 + REACH * HALF)
-        outer = slice(BS - r0, BS - r0 + REACH * BS)
-
-        def dot():
-            out = it.part(g, e)
-            return (
-                product([([x[outer] for x in turn(out)], out)]),
-                product([(it.part(g, g, rows), out)]),
-            )
-
-        def store(value):
-            a_ref[...], b_ref[...] = value
-
-        def post():
-            for p in range(2):
-                m_ref[p] = it.part(g, e)[p][rows]
-                p_ref[p, 0] = it.my_part(g, e)[p][mine_rows]
-                p_ref[p, 1] = it.my_part(g, g)[p][mine_rows]
-
-        return dot, store, post
-
-    steps.append(reaching(low_a, low_b, low_m, low_p, 0, -1, 0))
-    steps.append(reaching(high_a, high_b, high_m, high_p, last, last + 1, BS))
     staggered(steps)
-    it.finish()
 
 
 def border_kernel(
@@ -526,15 +522,21 @@
     mine = jax.ShapeDtypeStruct((2, groups, GROUP * HALF, 3 * WIDE), BF)
     keep = jax.ShapeDtypeStruct((2, 3 * groups, WIDE, WIDE), BF)
     lines = jax.ShapeDtypeStruct(((groups + 2) * GROUP, 3 * WIDE), F32)
+    ends_out = [
+        jax.ShapeDtypeStruct((REACH * BS, WIDE), F32),
+        jax.ShapeDtypeStruct((REACH * BS, WIDE), F32),
+        jax.ShapeDtypeStruct((2, REACH * BS, WIDE), BF),
+        jax.ShapeDtypeStruct((2, 2, REACH * HALF, WIDE), BF),
+    ]
     rows = jax.ShapeDtypeStruct((GROUP,) + matrix.shape[1:], F32)
-    first_rows = jax.ShapeDtypeStruct((groups - 1,) + rows.shape, F32)
-    square, low_seed, full, mine, keep, lines, sign_first = pl.pallas_call(
+    square, sign, low_seed, full, mine, keep, lines, *ends = pl.pallas_call(
         functools.partial(first_kernel, axes=axes, half_axis=half_axis),
-        out_shape=[band, seed, full, mine, keep, lines, first_rows],
+        out_shape=[band, band, seed, full, mine, keep, lines] + ends_out * 2,
         in_specs=[vmem] * 3,
-        out_specs=[hbm] + [vmem] * 6,
+        out_specs=[hbm] * 2 + [vmem] * 13,
         scratch_shapes=[
             pltpu.VMEM((groups,) + rows.shape, F32),
+            pltpu.VMEM((groups - 1,) + rows.shape, F32),
             pltpu.VMEM((2 * groups - 1 + 3 * groups - 4, WIDE, WIDE), F32),
             pltpu.SemaphoreType.DMA((2, count)),
         ],
@@ -548,26 +550,17 @@
     low_other = lax.ppermute(low_own, half_axis, swap)
     high_other = lax.ppermute(high_own, half_axis, swap)
 
-    ends_out = [
-        jax.ShapeDtypeStruct((REACH * BS, WIDE), F32),
-        jax.ShapeDtypeStruct((REACH * BS, WIDE), F32),
-        jax.ShapeDtypeStruct((2, REACH * BS, WIDE), BF),
-        jax.ShapeDtypeStruct((2, 2, REACH * HALF, WIDE), BF),
-    ]
-    sign, sign_last, high_seed, *ends = pl.pallas_call(
+    sign_last, high_seed = pl.pallas_call(
         last_kernel,
-        out_shape=[band, rows, seed] + ends_out * 2,
-        in_specs=[vmem] * 6,
-        out_specs=[hbm] + [vmem] * 10,
-        scratch_shapes=[
-            pltpu.VMEM((2, GROUP * HALF, WIDE), F32),
-            pltpu.SemaphoreType.DMA((2, count)),
-        ],
+        out_shape=[rows, seed],
+        in_specs=[vmem] * 5,
+        out_specs=[vmem] * 2,
+        scratch_shapes=[pltpu.VMEM((2, GROUP * HALF, WIDE), F32)],
         compiler_params=params,
         cost_estimate=pl.CostEstimate(
             flops=3 * 2 * 4 * WIDE**3, bytes_accessed=4 * 2**20, transcendentals=0
         ),
-    )(matrix, lines, full, mine, keep, sign_first)
+    )(matrix, lines, full, mine, keep)
 
     return tuple(
         pl.pallas_call(

time: 16.4 us -> 15.7 us (0.957)
  Pallas kernels: 7.17 us -> 6.51 us
    pallas_call x1, Pallas kernels: 1.57 us -> 0.45 us  [shards(): pl.pallas_call(last_kernel, out_shape=[rows, seed], in_specs=[vmem] * 5,...]
    pallas_call x1, Pallas kernels: 3.3 us -> 3.78 us  [shards(): pl.pallas_call(functools.partial(first_kernel, axes=axes, half_axis=half_...]
    ppermute x1, waiting for transfers between devices: 0.01 us -> 0.34 us  [shards(): low_other = lax.ppermute(low_own, half_axis, swap)]
    ppermute x1, waiting for transfers between devices: 0.42 us -> 0.11 us  [shards(): high_own = lax.ppermute(to_left, axes, backward)]
    ppermute x1, starting transfers between devices: 0.01 us -> 0.18 us  [shards(): low_other = lax.ppermute(low_own, half_axis, swap)]
    ppermute x1, starting transfers between devices: 0.51 us -> 0.33 us  [shards(): high_other = lax.ppermute(high_own, half_axis, swap)]
    ppermute x1, waiting for transfers between devices: 0.01 us -> 0.18 us  [shards(): high_other = lax.ppermute(high_own, half_axis, swap)]
    ppermute x1, waiting for transfers between devices: 0.17 us -> 0.01 us  [shards(): low_own = lax.ppermute(to_right, axes, forward)]
  transfers between devices with their start and end apart: 5 -> 5, of which waited for: 2 -> 3; matrix products, arithmetic and copies ran while one was open for 0% -> 0% of each run, Pallas kernels for 31% -> 28%
where the time goes in v11:
time: 15.7 us; the launch traced here: 15.6 us
  starting transfers between devices  6.68 us (43%)
  Pallas kernels  6.51 us (41%)
  local copies, waits for them, and re-layouts  1.07 us (7%)
  between operations  0.69 us (4%)
  waiting for transfers between devices  0.63 us (4%)
    pallas_call x1, Pallas kernels, shards(): pl.pallas_call(functools.partial(first_kernel, axes=axes, half_axis=half_...  3.78 us
    ppermute x1, starting transfers between devices, shards(): high_own = lax.ppermute(to_left, axes, backward)  3.1 us
    ppermute x1, starting transfers between devices, shards(): low_own = lax.ppermute(to_right, axes, forward)  2.55 us
    pallas_call x1, Pallas kernels, shards(): pl.pallas_call(functools.partial(border_kernel, half_axis=half_axis), out...  2.17 us
    slice x1, local copies, waits for them, and re-layouts, shards(): top, bottom = (matrix[:REACH, REACH:], matrix[count - REACH:, :REACH + 1])  1.06 us
    ppermute x1, starting transfers between devices, shards(): other = lax.ppermute(matrix, half_axis, swap)  0.52 us
    pallas_call x1, Pallas kernels, shards(): pl.pallas_call(last_kernel, out_shape=[rows, seed], in_specs=[vmem] * 5,...  0.45 us
    ppermute x1, waiting for transfers between devices, shards(): low_other = lax.ppermute(low_own, half_axis, swap)  0.34 us
  transfers between devices with their start and end apart: 5, of which 3 were waited for; matrix products, arithmetic and copies ran while one was open for 0% of the time, Pallas kernels for 28%

profile of v11, /device:TPU:0, one launch (start us, length us, event | category | flops | bytes accessed | tf_op | source)
XLA Modules:
  0.0 15.6 jit_solution(11177142595668266442)
XLA Ops:
  0.6 1.1 %fusion = (f32[3,4,32,64]{3,2,1,0:T(8,128)S(1)}, f32[3,4,32,64]{3,2,1,0:T(8,128)S(1)}) fusion(f32[12,7,32,64]{3,2,1,0:T(8,128)} %own.1), kind=kLoop, calls=%fused_computation | loop fusion | bytes 393216 | tf_op jit(solution)/shard_map/slice | solution.py:496
  1.7 0.0 copy-start
  1.7 0.0 copy-start.1
  1.7 0.5 %collective-permute-start.2 = (f32[12,7,32,64]{3,2,1,0:T(8,128)}, f32[12,7,32,64]{3,2,1,0:T(8,128)S(1)}, u32[]{:S(2)}, u32[]{:S(2)}) collective-permute-start(f32[12,7,32,64]{3,2,1,0:T(8,128)} %own.1), channel_id=1, source_target_pairs={{0,1},{1,0},{2,3},{3,2},{4,5},{5,4},{6,7},{7,6},{8,9},{9,8},{10,11... | collective-permute-start | bytes 2064392 | tf_op jit(solution)/shard_map/ppermute | solution.py:513
  2.2 0.1 shard_map.41
  2.4 2.6 %collective-permute-start = (f32[96,256]{1,0:T(8,128)S(1)}, f32[96,256]{1,0:T(8,128)S(1)}, u32[]{:S(2)}, u32[]{:S(2)}) collective-permute-start(f32[96,256]{1,0:T(8,128)S(1)} %get-tuple-element.29), channel_id=1, source_target_pairs={{0,2},{2,4},{4,6},{6,8},{8,10},{10,12},{12,14},{14,0},{1,3},{3,5},... | collective-permute-start | bytes 294920 | tf_op jit(solution)/shard_map/ppermute | solution.py:517
  4.9 3.1 %collective-permute-start.1 = (f32[96,256]{1,0:T(8,128)S(1)}, f32[96,256]{1,0:T(8,128)S(1)}, u32[]{:S(2)}, u32[]{:S(2)}) collective-permute-start(f32[96,256]{1,0:T(8,128)S(1)} %get-tuple-element.30), channel_id=1, source_target_pairs={{2,0},{4,2},{6,4},{8,6},{10,8},{12,10},{14,12},{0,14},{3,1},{5,3},... | collective-permute-start | bytes 294920 | tf_op jit(solution)/shard_map/ppermute | solution.py:516
  8.0 0.0 collective-permute-done.2.other
  8.0 0.0 copy-done
  8.0 0.0 copy-done.1
  8.0 3.8 %shard_map.42 = (f32[12,7,32,64]{3,2,1,0:T(8,128)}, f32[12,7,32,64]{3,2,1,0:T(8,128)}, f32[3,7,32,64]{3,2,1,0:T(8,128)S(1)}, bf16[2,3,256,768]{3,2,1,0:T(8,128)(...) custom-call(f32[12,7,32,64]{3,2,1,0:T(8,128)S(1)} %copy-done, ...), custom_call_target="tpu_custom_call" | custom-call | flops 1610612736 | bytes 16777216 | tf_op jit(solution)/shard_map/pallas_call | solution.py:532
  11.8 0.0 collective-permute-done.low_own
  11.8 0.1 collective-permute-done.1.high_own
  11.9 0.2 %collective-permute-start.3 = (f32[96,256]{1,0:T(8,128)S(1)}, f32[96,256]{1,0:T(8,128)S(1)}, u32[]{:S(2)}, u32[]{:S(2)}) collective-permute-start(f32[96,256]{1,0:T(8,128)S(1)} %collective-permute-done.low_own), channel_id=1, source_target_pairs={{0,1},{1,0},{2,3},{3,2},{4,5},{5,4},{6,7},{7,6},{8,9},{9,8},{10,11... | collective-permute-start | bytes 294920 | tf_op jit(solution)/shard_map/ppermute | solution.py:550
  12.1 0.3 %collective-permute-start.4 = (f32[96,256]{1,0:T(8,128)S(1)}, f32[96,256]{1,0:T(8,128)S(1)}, u32[]{:S(2)}, u32[]{:S(2)}) collective-permute-start(f32[96,256]{1,0:T(8,128)S(1)} %collective-permute-done.1.high_own), channel_id=1, source_target_pairs={{0,1},{1,0},{2,3},{3,2},{4,5},{5,4},{6,7},{7,6},{8,9},{9,8},{10,11... | collective-permute-start | bytes 294920 | tf_op jit(solution)/shard_map/ppermute | solution.py:551
  12.4 0.4 %shard_map.43 = (f32[4,7,32,64]{3,2,1,0:T(8,128)S(1)}, f32[3,7,32,64]{3,2,1,0:T(8,128)S(1)}) custom-call(f32[12,7,32,64]{3,2,1,0:T(8,128)S(1)} %copy-done, f32[20,768]{1,0:T(8,128)S(1)} %get-tuple-element.35.lines, bf16[2,3,256,768]{3,2,1,0:T(8,128)(2,1)S(1)} %get-tuple-element.36.full, bf16[2,3,128,768]{3,2,1,0:T(8,128)(2,1)S(1)} %get-tuple-element.37.mine, ...), custom_call_target="tpu_custom_call" | custom-call | flops 402653184 | bytes 4194304 | tf_op jit(solution)/shard_map/pallas_call | solution.py:553
  12.9 0.3 %collective-permute-done.3.low_other = f32[96,256]{1,0:T(8,128)S(1)} collective-permute-done((f32[96,256]{1,0:T(8,128)S(1)}, f32[96,256]{1,0:T(8,128)S(1)}, u32[]{:S(2)}, u32[]{:S(2)}) %collective-permute-start.3) | collective-permute-done | bytes 98336 | tf_op jit(solution)/shard_map/ppermute | solution.py:550
  13.2 0.2 %collective-permute-done.4.high_other = f32[96,256]{1,0:T(8,128)S(1)} collective-permute-done((f32[96,256]{1,0:T(8,128)S(1)}, f32[96,256]{1,0:T(8,128)S(1)}, u32[]{:S(2)}, u32[]{:S(2)}) %collective-permute-start.4) | collective-permute-done | bytes 98336 | tf_op jit(solution)/shard_map/ppermute | solution.py:551
  13.4 2.2 %shard_map.44 = (f32[12,7,32,64]{3,2,1,0:T(8,128)}, f32[12,7,32,64]{3,2,1,0:T(8,128)}) custom-call(f32[96,256]{1,0:T(8,128)S(1)} %collective-permute-done.low_own, f32[96,256]{1,0:T(8,128)S(1)} %collective-permute-done.3.low_other, f32[96,256]{1,0:T(8,128)S(1)} %collective-permute-done.1.high_own, ...), custom_call_target="tpu_custom_call", output_to_operand_aliasing={{0}: (16, {}), {1}: (17, {})} | custom-call | flops 402653184 | bytes 2097152 | tf_op jit(solution)/shard_map/pallas_call | solution.py:566
Async XLA Ops:
  1.7 6.3 %copy-start = (f32[12,7,32,64]{3,2,1,0:T(8,128)S(1)}, f32[12,7,32,64]{3,2,1,0:T(8,128)}, u32[]{:S(2)}) copy-start(f32[12,7,32,64]{3,2,1,0:T(8,128)} %own.1) | copy-start | bytes 2064388
  1.7 6.3 %copy-start.1 = (s32[96,7]{0,1:T(8,128)S(1)}, s32[96,7]{0,1:T(8,128)}, u32[]{:S(2)}) copy-start(s32[96,7]{0,1:T(8,128)} %param.3) | copy-start | bytes 8068
  1.7 6.3 %collective-permute-start.2 = (f32[12,7,32,64]{3,2,1,0:T(8,128)}, f32[12,7,32,64]{3,2,1,0:T(8,128)S(1)}, u32[]{:S(2)}, u32[]{:S(2)}) collective-permute-start(f32[12,7,32,64]{3,2,1,0:T(8,128)} %own.1), channel_id=1, source_target_pairs={{0,1},{1,0},{2,3},{3,2},{4,5},{5,4},{6,7},{7,6},{8,9},{9,8},{10,11... | collective-permute-start | bytes 2064392 | tf_op jit(solution)/shard_map/ppermute | solution.py:513
  2.4 9.5 %collective-permute-start = (f32[96,256]{1,0:T(8,128)S(1)}, f32[96,256]{1,0:T(8,128)S(1)}, u32[]{:S(2)}, u32[]{:S(2)}) collective-permute-start(f32[96,256]{1,0:T(8,128)S(1)} %get-tuple-element.29), channel_id=1, source_target_pairs={{0,2},{2,4},{4,6},{6,8},{8,10},{10,12},{12,14},{14,0},{1,3},{3,5},... | collective-permute-start | bytes 294920 | tf_op jit(solution)/shard_map/ppermute | solution.py:517
  4.9 7.0 %collective-permute-start.1 = (f32[96,256]{1,0:T(8,128)S(1)}, f32[96,256]{1,0:T(8,128)S(1)}, u32[]{:S(2)}, u32[]{:S(2)}) collective-permute-start(f32[96,256]{1,0:T(8,128)S(1)} %get-tuple-element.30), channel_id=1, source_target_pairs={{2,0},{4,2},{6,4},{8,6},{10,8},{12,10},{14,12},{0,14},{3,1},{5,3},... | collective-permute-start | bytes 294920 | tf_op jit(solution)/shard_map/ppermute | solution.py:516
  11.9 1.3 %collective-permute-start.3 = (f32[96,256]{1,0:T(8,128)S(1)}, f32[96,256]{1,0:T(8,128)S(1)}, u32[]{:S(2)}, u32[]{:S(2)}) collective-permute-start(f32[96,256]{1,0:T(8,128)S(1)} %collective-permute-done.low_own), channel_id=1, source_target_pairs={{0,1},{1,0},{2,3},{3,2},{4,5},{5,4},{6,7},{7,6},{8,9},{9,8},{10,11... | collective-permute-start | bytes 294920 | tf_op jit(solution)/shard_map/ppermute | solution.py:550
  12.1 1.3 %collective-permute-start.4 = (f32[96,256]{1,0:T(8,128)S(1)}, f32[96,256]{1,0:T(8,128)S(1)}, u32[]{:S(2)}, u32[]{:S(2)}) collective-permute-start(f32[96,256]{1,0:T(8,128)S(1)} %collective-permute-done.1.high_own), channel_id=1, source_target_pairs={{0,1},{1,0},{2,3},{3,2},{4,5},{5,4},{6,7},{7,6},{8,9},{9,8},{10,11... | collective-permute-start | bytes 294920 | tf_op jit(solution)/shard_map/ppermute | solution.py:551

commit v12 on v11

--- a/solution.py
+++ b/solution.py
@@ -16,6 +16,7 @@
 BF = jnp.bfloat16
 F32 = jnp.float32
 LIMIT = 32 * 1024 * 1024
+EDGE_LIMIT = int(53 * 1024 * 1024)
 
 
 def split(x):
@@ -41,7 +42,8 @@
     return split((x[0].astype(F32) + x[1].astype(F32)).T)
 
 
-def write_lines(pat, lines, first, groups):
+def line_kernel(pat, lines, *, axes, count):
+    first = lax.axis_index(axes) * count
     total = pat.shape[1]
     rows = lines.shape[0]
     iota = functools.partial(lax.broadcasted_iota, jnp.int32)
@@ -73,12 +75,25 @@
     return 0, SPAN
 
 
-def edge_kernel(top, bottom, to_left, to_right):
-    for source, target in ((top, to_left), (bottom, to_right)):
+def edge_kernel(matrix, to_left, to_right, blocks, sems):
+    count = matrix.shape[0]
+    loads = [
+        pltpu.make_async_copy(source, blocks.at[i], sems.at[i])
+        for i, source in enumerate(
+            (
+                matrix.at[pl.ds(0, REACH), pl.ds(REACH, REACH + 1)],
+                matrix.at[pl.ds(count - REACH, REACH), pl.ds(0, REACH + 1)],
+            )
+        )
+    ]
+    for load in loads:
+        load.start()
+    for i, target in enumerate((to_left, to_right)):
+        loads[i].wait()
         for s in range(REACH):
             for t in range(2):
                 target[s * HALF : (s + 1) * HALF, t * 2 * BS : (t + 1) * 2 * BS] = jnp.concatenate(
-                    [source[s, 2 * t], source[s, 2 * t + 1]], axis=1
+                    [blocks[i, s, 2 * t], blocks[i, s, 2 * t + 1]], axis=1
                 )
 
 
@@ -207,8 +222,8 @@
 
 
 def first_kernel(
-    own, other, pat, square_out, sign_out, seed, full, mine, keep, lines, low_a, low_b, low_m, low_p,
-    high_a, high_b, high_m, high_p, square, sign, results, sems, *, axes, half_axis
+    own, other, lines, square_out, sign_out, seed, full, mine, keep, low_a, low_b, low_m, low_p,
+    high_a, high_b, high_m, high_p, square, sign, results, sems, *, half_axis
 ):
     it = Interior(own, lines, full, mine, keep)
     groups = it.groups
@@ -288,7 +303,6 @@
     staged = [square.at[g] for g in range(groups)]
 
     def begin():
-        write_lines(pat, lines, lax.axis_index(axes) * it.count, groups)
         it.far_seed(0, seed)
 
     build(0)
@@ -493,19 +507,29 @@
     hbm = pl.BlockSpec(memory_space=pl.ANY)
     params = pltpu.CompilerParams(vmem_limit_bytes=LIMIT)
 
-    top, bottom = matrix[:REACH, REACH:], matrix[count - REACH :, : REACH + 1]
-    matrix, top, bottom = lax.optimization_barrier((matrix, top, bottom))
     edge = jax.ShapeDtypeStruct((REACH * HALF, (REACH + 1) * BS), F32)
     to_left, to_right = pl.pallas_call(
         edge_kernel,
         out_shape=(edge, edge),
-        in_specs=[vmem] * 2,
+        in_specs=[hbm],
         out_specs=[vmem] * 2,
+        scratch_shapes=[
+            pltpu.VMEM((2, REACH, REACH + 1, HALF, BS), F32),
+            pltpu.SemaphoreType.DMA((2,)),
+        ],
+        compiler_params=pltpu.CompilerParams(vmem_limit_bytes=EDGE_LIMIT),
+        cost_estimate=pl.CostEstimate(flops=1, bytes_accessed=2**18, transcendentals=0),
+    )(matrix)
+    lines = pl.pallas_call(
+        functools.partial(line_kernel, axes=axes, count=count),
+        out_shape=jax.ShapeDtypeStruct(((groups + 2) * GROUP, 3 * WIDE), F32),
+        in_specs=[vmem],
+        out_specs=vmem,
         compiler_params=params,
-        cost_estimate=pl.CostEstimate(
-            flops=1 * 10**9, bytes_accessed=2**20, transcendentals=0
-        ),
-    )(top, bottom)
+        cost_estimate=pl.CostEstimate(flops=2*10**9, bytes_accessed=2**16, transcendentals=0),
+    )(flags)
+
+    to_left, to_right, lines = lax.optimization_barrier((to_left, to_right, lines))
     size = 1
     for axis in axes:
         size *= lax.axis_size(axis)
@@ -521,7 +545,6 @@
     full = jax.ShapeDtypeStruct((2, groups, WIDE, 3 * WIDE), BF)
     mine = jax.ShapeDtypeStruct((2, groups, GROUP * HALF, 3 * WIDE), BF)
     keep = jax.ShapeDtypeStruct((2, 3 * groups, WIDE, WIDE), BF)
-    lines = jax.ShapeDtypeStruct(((groups + 2) * GROUP, 3 * WIDE), F32)
     ends_out = [
         jax.ShapeDtypeStruct((REACH * BS, WIDE), F32),
         jax.ShapeDtypeStruct((REACH * BS, WIDE), F32),
@@ -529,11 +552,11 @@
         jax.ShapeDtypeStruct((2, 2, REACH * HALF, WIDE), BF),
     ]
     rows = jax.ShapeDtypeStruct((GROUP,) + matrix.shape[1:], F32)
-    square, sign, low_seed, full, mine, keep, lines, *ends = pl.pallas_call(
-        functools.partial(first_kernel, axes=axes, half_axis=half_axis),
-        out_shape=[band, band, seed, full, mine, keep, lines] + ends_out * 2,
+    square, sign, low_seed, full, mine, keep, *ends = pl.pallas_call(
+        functools.partial(first_kernel, half_axis=half_axis),
+        out_shape=[band, band, seed, full, mine, keep] + ends_out * 2,
         in_specs=[vmem] * 3,
-        out_specs=[hbm] * 2 + [vmem] * 13,
+        out_specs=[hbm] * 2 + [vmem] * 12,
         scratch_shapes=[
             pltpu.VMEM((groups,) + rows.shape, F32),
             pltpu.VMEM((groups - 1,) + rows.shape, F32),
@@ -544,7 +567,7 @@
         cost_estimate=pl.CostEstimate(
             flops=3 * 2 * 16 * WIDE**3, bytes_accessed=16 * 2**20, transcendentals=0
         ),
-    )(matrix, other, flags)
+    )(matrix, other, lines)
 
     low_own, high_own, low_seed = lax.optimization_barrier((low_own, high_own, low_seed))
     low_other = lax.ppermute(low_own, half_axis, swap)

time: 15.7 us -> 16 us (1.019)
  Pallas kernels: 6.51 us -> 7.85 us
  local copies, waits for them, and re-layouts: 1.07 us -> 0.01 us
    pallas_call x2 -> x3, Pallas kernels: 3.89 us -> 5.24 us  [the longest x1 3.78 us: shards(): pl.pallas_call(functools.partial(first_kernel, half_axis=half_axis), out_...]
    slice x1 -> x0, local copies, waits for them, and re-layouts: 1.06 us -> none  [shards(): top, bottom = (matrix[:REACH, REACH:], matrix[count - REACH:, :REACH + 1])]
  transfers between devices with their start and end apart: 5 -> 5, of which waited for: 3 -> 3; matrix products, arithmetic and copies ran while one was open for 0% -> 0% of each run, Pallas kernels for 28% -> 36%
where the time goes in v12:
time: 16 us; the launch traced here: 15.9 us
  Pallas kernels  7.85 us (49%)
  starting transfers between devices  6.69 us (42%)
  between operations  0.7 us (4%)
  waiting for transfers between devices  0.63 us (4%)
    pallas_call x1, Pallas kernels, shards(): pl.pallas_call(functools.partial(first_kernel, half_axis=half_axis), out_...  3.78 us
    ppermute x1, starting transfers between devices, shards(): high_own = lax.ppermute(to_left, axes, backward)  3.1 us
    ppermute x1, starting transfers between devices, shards(): low_own = lax.ppermute(to_right, axes, forward)  2.56 us
    pallas_call x1, Pallas kernels, shards(): pl.pallas_call(functools.partial(border_kernel, half_axis=half_axis), out...  2.17 us
    pallas_call x1, Pallas kernels, shards(): pl.pallas_call(edge_kernel, out_shape=(edge, edge), in_specs=[hbm], out_s...  1.13 us
    ppermute x1, starting transfers between devices, shards(): other = lax.ppermute(matrix, half_axis, swap)  0.52 us
    pallas_call x1, Pallas kernels, shards(): pl.pallas_call(last_kernel, out_shape=[rows, seed], in_specs=[vmem] * 5,...  0.45 us
    ppermute x1, waiting for transfers between devices, shards(): low_other = lax.ppermute(low_own, half_axis, swap)  0.34 us
  transfers between devices with their start and end apart: 5, of which 3 were waited for; matrix products, arithmetic and copies ran while one was open for 0% of the time, Pallas kernels for 36%

profile of v12, /device:TPU:0, one launch (start us, length us, event | category | flops | bytes accessed | tf_op | source)
XLA Modules:
  0.0 15.9 jit_solution(3493231310477557298)
XLA Ops:
  0.6 0.0 copy-start.1
  0.6 0.5 %collective-permute-start.2 = (f32[12,7,32,64]{3,2,1,0:T(8,128)}, f32[12,7,32,64]{3,2,1,0:T(8,128)S(1)}, u32[]{:S(2)}, u32[]{:S(2)}) collective-permute-start(f32[12,7,32,64]{3,2,1,0:T(8,128)} %own.3), channel_id=1, source_target_pairs={{0,1},{1,0},{2,3},{3,2},{4,5},{5,4},{6,7},{7,6},{8,9},{9,8},{10,11... | collective-permute-start | bytes 2064392 | tf_op jit(solution)/shard_map/ppermute | solution.py:537
  1.2 1.1 %shard_map.41 = (f32[96,256]{1,0:T(8,128)S(1)}, f32[96,256]{1,0:T(8,128)S(1)}) custom-call(f32[12,7,32,64]{3,2,1,0:T(8,128)} %own.3), custom_call_target="tpu_custom_call" | custom-call | flops 1 | bytes 262144 | tf_op jit(solution)/shard_map/pallas_call | solution.py:511
  2.3 0.0 copy-done.1
  2.3 0.0 copy-start
  2.3 0.3 %shard_map.42.lines = f32[20,768]{1,0:T(8,128)S(1)} custom-call(s32[7,96]{1,0:T(8,128)S(1)} %bitcast.1), custom_call_target="tpu_custom_call" | custom-call | flops 2000000000 | bytes 65536 | tf_op jit(solution)/shard_map/pallas_call | solution.py:523
  2.6 2.6 %collective-permute-start = (f32[96,256]{1,0:T(8,128)S(1)}, f32[96,256]{1,0:T(8,128)S(1)}, u32[]{:S(2)}, u32[]{:S(2)}) collective-permute-start(f32[96,256]{1,0:T(8,128)S(1)} %get-tuple-element.28), channel_id=1, source_target_pairs={{0,2},{2,4},{4,6},{6,8},{8,10},{10,12},{12,14},{14,0},{1,3},{3,5},... | collective-permute-start | bytes 294920 | tf_op jit(solution)/shard_map/ppermute | solution.py:541
  5.2 3.1 %collective-permute-start.1 = (f32[96,256]{1,0:T(8,128)S(1)}, f32[96,256]{1,0:T(8,128)S(1)}, u32[]{:S(2)}, u32[]{:S(2)}) collective-permute-start(f32[96,256]{1,0:T(8,128)S(1)} %get-tuple-element.29), channel_id=1, source_target_pairs={{2,0},{4,2},{6,4},{8,6},{10,8},{12,10},{14,12},{0,14},{3,1},{5,3},... | collective-permute-start | bytes 294920 | tf_op jit(solution)/shard_map/ppermute | solution.py:540
  8.3 0.0 collective-permute-done.2.other
  8.3 0.0 copy-done
  8.3 3.8 %shard_map.43 = (f32[12,7,32,64]{3,2,1,0:T(8,128)}, f32[12,7,32,64]{3,2,1,0:T(8,128)}, f32[3,7,32,64]{3,2,1,0:T(8,128)S(1)}, bf16[2,3,256,768]{3,2,1,0:T(8,128)(...) custom-call(f32[12,7,32,64]{3,2,1,0:T(8,128)S(1)} %copy-done, ...), custom_call_target="tpu_custom_call" | custom-call | flops 1610612736 | bytes 16777216 | tf_op jit(solution)/shard_map/pallas_call | solution.py:555
  12.1 0.0 collective-permute-done.low_own
  12.1 0.1 collective-permute-done.1.high_own
  12.2 0.2 %collective-permute-start.3 = (f32[96,256]{1,0:T(8,128)S(1)}, f32[96,256]{1,0:T(8,128)S(1)}, u32[]{:S(2)}, u32[]{:S(2)}) collective-permute-start(f32[96,256]{1,0:T(8,128)S(1)} %collective-permute-done.low_own), channel_id=1, source_target_pairs={{0,1},{1,0},{2,3},{3,2},{4,5},{5,4},{6,7},{7,6},{8,9},{9,8},{10,11... | collective-permute-start | bytes 294920 | tf_op jit(solution)/shard_map/ppermute | solution.py:573
  12.4 0.3 %collective-permute-start.4 = (f32[96,256]{1,0:T(8,128)S(1)}, f32[96,256]{1,0:T(8,128)S(1)}, u32[]{:S(2)}, u32[]{:S(2)}) collective-permute-start(f32[96,256]{1,0:T(8,128)S(1)} %collective-permute-done.1.high_own), channel_id=1, source_target_pairs={{0,1},{1,0},{2,3},{3,2},{4,5},{5,4},{6,7},{7,6},{8,9},{9,8},{10,11... | collective-permute-start | bytes 294920 | tf_op jit(solution)/shard_map/ppermute | solution.py:574
  12.7 0.4 %shard_map.44 = (f32[4,7,32,64]{3,2,1,0:T(8,128)S(1)}, f32[3,7,32,64]{3,2,1,0:T(8,128)S(1)}) custom-call(f32[12,7,32,64]{3,2,1,0:T(8,128)S(1)} %copy-done, f32[20,768]{1,0:T(8,128)S(1)} %shard_map.42.lines, bf16[2,3,256,768]{3,2,1,0:T(8,128)(2,1)S(1)} %get-tuple-element.34.full, bf16[2,3,128,768]{3,2,1,0:T(8,128)(2,1)S(1)} %get-tuple-element.35.mine, ...), custom_call_target="tpu_custom_call" | custom-call | flops 402653184 | bytes 4194304 | tf_op jit(solution)/shard_map/pallas_call | solution.py:576
  13.2 0.3 %collective-permute-done.3.low_other = f32[96,256]{1,0:T(8,128)S(1)} collective-permute-done((f32[96,256]{1,0:T(8,128)S(1)}, f32[96,256]{1,0:T(8,128)S(1)}, u32[]{:S(2)}, u32[]{:S(2)}) %collective-permute-start.3) | collective-permute-done | bytes 98336 | tf_op jit(solution)/shard_map/ppermute | solution.py:573
  13.5 0.2 %collective-permute-done.4.high_other = f32[96,256]{1,0:T(8,128)S(1)} collective-permute-done((f32[96,256]{1,0:T(8,128)S(1)}, f32[96,256]{1,0:T(8,128)S(1)}, u32[]{:S(2)}, u32[]{:S(2)}) %collective-permute-start.4) | collective-permute-done | bytes 98336 | tf_op jit(solution)/shard_map/ppermute | solution.py:574
  13.7 2.2 %shard_map.45 = (f32[12,7,32,64]{3,2,1,0:T(8,128)}, f32[12,7,32,64]{3,2,1,0:T(8,128)}) custom-call(f32[96,256]{1,0:T(8,128)S(1)} %collective-permute-done.low_own, f32[96,256]{1,0:T(8,128)S(1)} %collective-permute-done.3.low_other, f32[96,256]{1,0:T(8,128)S(1)} %collective-permute-done.1.high_own, ...), custom_call_target="tpu_custom_call", output_to_operand_aliasing={{0}: (16, {}), {1}: (17, {})} | custom-call | flops 402653184 | bytes 2097152 | tf_op jit(solution)/shard_map/pallas_call | solution.py:589
Async XLA Ops:
  0.6 1.7 %copy-start.1 = (s32[96,7]{0,1:T(8,128)S(1)}, s32[96,7]{0,1:T(8,128)}, u32[]{:S(2)}) copy-start(s32[96,7]{0,1:T(8,128)} %param.3) | copy-start | bytes 8068
  0.6 7.7 %collective-permute-start.2 = (f32[12,7,32,64]{3,2,1,0:T(8,128)}, f32[12,7,32,64]{3,2,1,0:T(8,128)S(1)}, u32[]{:S(2)}, u32[]{:S(2)}) collective-permute-start(f32[12,7,32,64]{3,2,1,0:T(8,128)} %own.3), channel_id=1, source_target_pairs={{0,1},{1,0},{2,3},{3,2},{4,5},{5,4},{6,7},{7,6},{8,9},{9,8},{10,11... | collective-permute-start | bytes 2064392 | tf_op jit(solution)/shard_map/ppermute | solution.py:537
  2.3 6.0 %copy-start = (f32[12,7,32,64]{3,2,1,0:T(8,128)S(1)}, f32[12,7,32,64]{3,2,1,0:T(8,128)}, u32[]{:S(2)}) copy-start(f32[12,7,32,64]{3,2,1,0:T(8,128)} %own.3) | copy-start | bytes 2064388
  2.6 9.5 %collective-permute-start = (f32[96,256]{1,0:T(8,128)S(1)}, f32[96,256]{1,0:T(8,128)S(1)}, u32[]{:S(2)}, u32[]{:S(2)}) collective-permute-start(f32[96,256]{1,0:T(8,128)S(1)} %get-tuple-element.28), channel_id=1, source_target_pairs={{0,2},{2,4},{4,6},{6,8},{8,10},{10,12},{12,14},{14,0},{1,3},{3,5},... | collective-permute-start | bytes 294920 | tf_op jit(solution)/shard_map/ppermute | solution.py:541
  5.2 7.0 %collective-permute-start.1 = (f32[96,256]{1,0:T(8,128)S(1)}, f32[96,256]{1,0:T(8,128)S(1)}, u32[]{:S(2)}, u32[]{:S(2)}) collective-permute-start(f32[96,256]{1,0:T(8,128)S(1)} %get-tuple-element.29), channel_id=1, source_target_pairs={{2,0},{4,2},{6,4},{8,6},{10,8},{12,10},{14,12},{0,14},{3,1},{5,3},... | collective-permute-start | bytes 294920 | tf_op jit(solution)/shard_map/ppermute | solution.py:540
  12.2 1.3 %collective-permute-start.3 = (f32[96,256]{1,0:T(8,128)S(1)}, f32[96,256]{1,0:T(8,128)S(1)}, u32[]{:S(2)}, u32[]{:S(2)}) collective-permute-start(f32[96,256]{1,0:T(8,128)S(1)} %collective-permute-done.low_own), channel_id=1, source_target_pairs={{0,1},{1,0},{2,3},{3,2},{4,5},{5,4},{6,7},{7,6},{8,9},{9,8},{10,11... | collective-permute-start | bytes 294920 | tf_op jit(solution)/shard_map/ppermute | solution.py:573
  12.4 1.3 %collective-permute-start.4 = (f32[96,256]{1,0:T(8,128)S(1)}, f32[96,256]{1,0:T(8,128)S(1)}, u32[]{:S(2)}, u32[]{:S(2)}) collective-permute-start(f32[96,256]{1,0:T(8,128)S(1)} %collective-permute-done.1.high_own), channel_id=1, source_target_pairs={{0,1},{1,0},{2,3},{3,2},{4,5},{5,4},{6,7},{7,6},{8,9},{9,8},{10,11... | collective-permute-start | bytes 294920 | tf_op jit(solution)/shard_map/ppermute | solution.py:574

commit v13 on v11

--- a/solution.py
+++ b/solution.py
@@ -320,167 +320,138 @@
     staggered(steps)
 
 
-def border_kernel(
-    low_own, low_other, high_own, high_other, lines, sign_last, low_seed, low_a, low_b, low_m, low_p, high_seed,
-    high_a, high_b, high_m, high_p, square_in, sign_in, square_out, sign_out, halo, first, last, blocks, sems, last_sems,
-    *, half_axis
+def border(
+    side, groups, half_axis, mine, theirs, lines, seed, a_ref, b_ref, m_ref, p_ref, halo, first, last,
+    square, sign, sent
+):
+    upper_half = lax.axis_index(half_axis) == 1
+    at = 1 - side
+    edge_group, outer_group = (0, -1) if side == 0 else (groups - 1, groups)
+    offset = 0 if side == 0 else 2 * REACH
+    below = REACH if side == 0 else 0
+    zero = jnp.zeros((BS, WIDE), F32)
+
+    def padded(rows, front):
+        return split(jnp.concatenate([zero] + rows if front else rows + [zero], axis=0))
+
+    whole_rows = []
+    for p in range(REACH):
+        rows = slice(p * HALF, (p + 1) * HALF)
+        whole_rows.append(
+            jnp.concatenate(
+                [
+                    jnp.where(upper_half, theirs[rows, :], mine[rows, :]),
+                    jnp.where(upper_half, mine[rows, :], theirs[rows, :]),
+                ],
+                axis=0,
+            )
+        )
+
+    def block(p, c):
+        k = c - p + below
+        if 0 <= k <= REACH:
+            return whole_rows[p][:, k * BS : (k + 1) * BS]
+        k = p - c + below
+        if 0 <= c < REACH and 0 <= k <= REACH:
+            return whole_rows[c][:, k * BS : (k + 1) * BS].T
+        return jnp.zeros((BS, BS), F32)
+
+    base = -5 if side == 0 else 0
+    for p in range(REACH):
+        rows = slice((p + at) * BS, (p + at + 1) * BS)
+        for t in range(4):
+            value = jnp.concatenate([block(p, base + 2 * t), block(p, base + 2 * t + 1)], axis=1)
+            for q, x in enumerate(split(value)):
+                halo[q, rows, t * 2 * BS : (t + 1) * 2 * BS] = x
+    rows = slice(0, BS) if side == 0 else slice(REACH * BS, WIDE)
+    for q in range(2):
+        halo[q, rows, :] = jnp.zeros((BS, 2 * WIDE), BF)
+
+    whole = [halo[q] for q in range(2)]
+    outer_rows = slice(at * BS, (at + REACH) * BS)
+    inner = slice(WIDE, 2 * WIDE) if side == 0 else slice(0, WIDE)
+    to_edge = product([([m_ref[q] for q in range(2)], [x[:, inner] for x in whole])], True)
+    among = product([([x[outer_rows] for x in whole], whole)], True)
+    first[0] = to_edge + b_ref[...]
+    rows = [
+        first[0, s * BS : (s + 1) * BS] * line_of(lines, edge_group, s + 1 - at, outer_group)
+        for s in range(REACH)
+    ]
+    across = padded(rows, side == 1)
+    reach_out = [p_ref[q, 0] for q in range(2)]
+    back = product([(reach_out, across)], True)
+    for s in range(REACH):
+        part = jnp.where(upper_half, rows[s][HALF:], rows[s][:HALF])
+        for t in range(REACH):
+            k = t - s + offset
+            if 0 <= k < SPAN:
+                square[s, k] = part[:, (t + at) * BS : (t + at + 1) * BS]
+        sent(0, s)
+    first[1] = among + a_ref[...]
+    rows = [
+        first[1, p * BS : (p + 1) * BS] * line_of(lines, outer_group, p + at, outer_group)
+        for p in range(REACH)
+    ]
+    inside = [p_ref[q, 1] for q in range(2)]
+    last[0] = product([(reach_out, padded(rows, side == 0)), (inside, across)])
+    last[1] = back
+    for s in range(REACH):
+        rows = slice(s * HALF, (s + 1) * HALF)
+        far = last[0, rows] * (line_of(lines, edge_group, s + 1 - at, outer_group) * 0.5)
+        close = last[1, rows] * (line_of(lines, edge_group, s + 1 - at, edge_group) * 0.5)
+        for t in range(REACH):
+            k = t - s + offset
+            if 0 <= k < SPAN:
+                lanes = slice((t + at) * BS, (t + at + 1) * BS)
+                sign[s, k] = seed[s, k] - far[:, lanes]
+            k = t - s + REACH
+            lanes = slice((t + 1 - at) * BS, (t + 2 - at) * BS)
+            sign[s, k] = seed[s, k] - close[:, lanes]
+        sent(1, s)
+
+
+def low_kernel(
+    mine, theirs, lines, seed, a_ref, b_ref, m_ref, p_ref, square, sign, halo, first, last, *,
+    groups, half_axis
+):
+    border(
+        0, groups, half_axis, mine, theirs, lines, seed, a_ref, b_ref, m_ref, p_ref, halo, first,
+        last, square, sign, lambda i, s: None,
+    )
+
+
+def high_kernel(
+    mine, theirs, lines, seed, a_ref, b_ref, m_ref, p_ref, low_square, low_sign, sign_last, square_in,
+    sign_in, square_out, sign_out, halo, first, last, square, sign, sems, last_sems, *, groups,
+    half_axis
 ):
     count = square_in.shape[0]
-    groups = count // GROUP
-    upper_half = lax.axis_index(half_axis) == 1
-    ends = (0, count - REACH)
-    given = (
-        (low_own, low_other, low_seed, low_a, low_b, low_m, low_p),
-        (high_own, high_other, high_seed, high_a, high_b, high_m, high_p),
-    )
-    shift = (1, 0)
-    zero = jnp.zeros((BS, WIDE), F32)
-
-    def build(side):
-        mine, theirs = given[side][:2]
-        below = REACH if side == 0 else 0
-        whole_rows = []
-        for p in range(REACH):
-            rows = slice(p * HALF, (p + 1) * HALF)
-            whole_rows.append(
-                jnp.concatenate(
-                    [
-                        jnp.where(upper_half, theirs[rows, :], mine[rows, :]),
-                        jnp.where(upper_half, mine[rows, :], theirs[rows, :]),
-                    ],
-                    axis=0,
-                )
-            )
-
-        def block(p, c):
-            k = c - p + below
-            if 0 <= k <= REACH:
-                return whole_rows[p][:, k * BS : (k + 1) * BS]
-            k = p - c + below
-            if 0 <= c < REACH and 0 <= k <= REACH:
-                return whole_rows[c][:, k * BS : (k + 1) * BS].T
-            return jnp.zeros((BS, BS), F32)
-
-        base = -5 if side == 0 else 0
-        for p in range(REACH):
-            rows = slice((p + shift[side]) * BS, (p + shift[side] + 1) * BS)
-            for t in range(4):
-                value = jnp.concatenate([block(p, base + 2 * t), block(p, base + 2 * t + 1)], axis=1)
-                for q, x in enumerate(split(value)):
-                    halo[side, q, rows, t * 2 * BS : (t + 1) * 2 * BS] = x
-        rows = slice(0, BS) if side == 0 else slice(REACH * BS, WIDE)
-        for q in range(2):
-            halo[side, q, rows, :] = jnp.zeros((BS, 2 * WIDE), BF)
-
-    edge_groups, outer_groups = (0, groups - 1), (-1, groups)
-    offsets = (0, 2 * REACH)
-    corners = [None, None]
-    across = [None, None]
     stores = []
 
-    def dots(side):
-        m_ref = given[side][5]
-        whole = [halo[side, q] for q in range(2)]
-        outer_rows = slice(shift[side] * BS, (shift[side] + REACH) * BS)
-        inner = slice(WIDE, 2 * WIDE) if side == 0 else slice(0, WIDE)
-        return (
-            product([([x[outer_rows] for x in whole], whole)], True),
-            product([([m_ref[q] for q in range(2)], [x[:, inner] for x in whole])], True),
-        )
-
-    def keep_first(side, value):
-        _, _, _, a_ref, b_ref, _, _ = given[side]
-        first[side, 0] = value[0] + a_ref[...]
-        first[side, 1] = value[1] + b_ref[...]
-
-    def masks(side):
-        at = shift[side]
-        edge_group, outer_group = edge_groups[side], outer_groups[side]
-        pad = (lambda rows: [zero] + rows, lambda rows: rows + [zero])
-        rows = [
-            first[side, 0, p * BS : (p + 1) * BS] * line_of(lines, outer_group, p + at, outer_group)
-            for p in range(REACH)
-        ]
-        corners[side] = split(jnp.concatenate(pad[side](rows), axis=0))
-        rows = [
-            first[side, 1, s * BS : (s + 1) * BS]
-            * line_of(lines, edge_group, s + 1 - at, outer_group)
-            for s in range(REACH)
-        ]
-        across[side] = split(jnp.concatenate(pad[1 - side](rows), axis=0))
-        for s in range(REACH):
-            part = jnp.where(upper_half, rows[s][HALF:], rows[s][:HALF])
-            for t in range(REACH):
-                k = t - s + offsets[side]
-                if 0 <= k < SPAN:
-                    blocks[0, side, s, k] = part[:, (t + at) * BS : (t + at + 1) * BS]
-        send(side, 0, square_out)
-
-    def send(side, i, ref):
-        for s in range(REACH):
-            a = ends[side] + s
-            k0, k1 = span_of(a, count, i == 0)
-            k0, k1 = (0, k0) if side == 0 else (k1, SPAN)
-            store = pltpu.make_async_copy(
-                blocks.at[i, side, s, pl.ds(k0, k1 - k0)],
-                ref.at[a, pl.ds(k0, k1 - k0)],
-                sems.at[i, side, s],
-            )
-            store.start()
-            stores.append(store)
-
-    def second_dots(side):
-        p_ref = given[side][6]
-        reach_out = [p_ref[q, 0] for q in range(2)]
-        inside = [p_ref[q, 1] for q in range(2)]
-        return (
-            product([(reach_out, corners[side]), (inside, across[side])]),
-            product([(reach_out, across[side])], True),
-        )
-
-    def keep_last(side, value):
-        last[side, 0], last[side, 1] = value
-
-    def emit(side):
-        seed = given[side][2]
-        at = shift[side]
-        edge_group, outer_group = edge_groups[side], outer_groups[side]
-        for s in range(REACH):
-            rows = slice(s * HALF, (s + 1) * HALF)
-            far = last[side, 0, rows] * (line_of(lines, edge_group, s + 1 - at, outer_group) * 0.5)
-            close = last[side, 1, rows] * (line_of(lines, edge_group, s + 1 - at, edge_group) * 0.5)
-            for t in range(REACH):
-                k = t - s + offsets[side]
-                if 0 <= k < SPAN:
-                    lanes = slice((t + at) * BS, (t + at + 1) * BS)
-                    blocks[1, side, s, k] = seed[s, k] - far[:, lanes]
-                k = t - s + REACH
-                lanes = slice((t + 1 - at) * BS, (t + 2 - at) * BS)
-                blocks[1, side, s, k] = seed[s, k] - close[:, lanes]
-        send(side, 1, sign_out)
-
-    for s in range(GROUP):
-        a = count - GROUP + s
-        k0, k1 = span_of(a, count, False)
+    def send(source, s, a, i, k0, k1, sem):
+        target = (square_out, sign_out)[i]
         store = pltpu.make_async_copy(
-            sign_last.at[s, pl.ds(k0, k1 - k0)], sign_out.at[a, pl.ds(k0, k1 - k0)], last_sems.at[s]
+            source.at[s, pl.ds(k0, k1 - k0)], target.at[a, pl.ds(k0, k1 - k0)], sem
         )
         store.start()
         stores.append(store)
-    build(0)
-    value = dots(0)
-    build(1)
-    keep_first(0, value)
-    value = dots(1)
-    masks(0)
-    keep_first(1, value)
-    value = second_dots(0)
-    masks(1)
-    keep_last(0, value)
-    value = second_dots(1)
-    emit(0)
-    keep_last(1, value)
-    emit(1)
+
+    for i, source in enumerate((low_square, low_sign)):
+        for s in range(REACH):
+            send(source, s, s, i, 0, span_of(s, count, i == 0)[0], sems.at[0, i, s])
+    for s in range(GROUP):
+        a = count - GROUP + s
+        send(sign_last, s, a, 1, *span_of(a, count, False), last_sems.at[s])
+
+    def sent(i, s):
+        a = count - REACH + s
+        source = (square, sign)[i]
+        send(source, s, a, i, span_of(a, count, i == 0)[1], SPAN, sems.at[1, i, s])
+
+    border(
+        1, groups, half_axis, mine, theirs, lines, seed, a_ref, b_ref, m_ref, p_ref, halo, first,
+        last, square, sign, sent,
+    )
     for store in stores:
         store.wait()
 
@@ -562,28 +533,43 @@
         ),
     )(matrix, lines, full, mine, keep)
 
+    names = dict(groups=groups, half_axis=half_axis)
+    scratch = [
+        pltpu.VMEM((2, WIDE, 2 * WIDE), BF),
+        pltpu.VMEM((2, REACH * BS, WIDE), F32),
+        pltpu.VMEM((2, REACH * HALF, WIDE), F32),
+    ]
+    cost = pl.CostEstimate(
+        flops=3 * 2 * 2 * WIDE**3, bytes_accessed=2 * 2**20, transcendentals=0
+    )
+    low_square, low_sign = pl.pallas_call(
+        functools.partial(low_kernel, **names),
+        out_shape=(seed, seed),
+        in_specs=[vmem] * 8,
+        out_specs=[vmem] * 2,
+        scratch_shapes=scratch,
+        compiler_params=params,
+        cost_estimate=cost,
+    )(low_own, low_other, lines, low_seed, *ends[:4])
     return tuple(
         pl.pallas_call(
-            functools.partial(border_kernel, half_axis=half_axis),
+            functools.partial(high_kernel, **names),
             out_shape=(band, band),
-            in_specs=[vmem] * 16 + [hbm] * 2,
+            in_specs=[vmem] * 11 + [hbm] * 2,
             out_specs=[hbm] * 2,
-            scratch_shapes=[
-                pltpu.VMEM((2, 2, WIDE, 2 * WIDE), BF),
-                pltpu.VMEM((2, 2, REACH * BS, WIDE), F32),
-                pltpu.VMEM((2, 2, REACH * HALF, WIDE), F32),
-                pltpu.VMEM((2, 2, REACH, SPAN, HALF, BS), F32),
+            scratch_shapes=scratch
+            + [
+                pltpu.VMEM(seed.shape, F32),
+                pltpu.VMEM(seed.shape, F32),
                 pltpu.SemaphoreType.DMA((2, 2, REACH)),
                 pltpu.SemaphoreType.DMA((GROUP,)),
             ],
-            input_output_aliases={16: 0, 17: 1},
+            input_output_aliases={11: 0, 12: 1},
             compiler_params=params,
-            cost_estimate=pl.CostEstimate(
-                flops=3 * 2 * 4 * WIDE**3, bytes_accessed=2 * 2**20, transcendentals=0
-            ),
+            cost_estimate=cost,
         )(
-            low_own, low_other, high_own, high_other, lines, sign_last, low_seed, *ends[:4], high_seed,
-            *ends[4:], square, sign,
+            high_own, high_other, lines, high_seed, *ends[4:], low_square, low_sign, sign_last,
+            square, sign,
         )
     )
 

time: 15.7 us -> 16.3 us (1.038)
  Pallas kernels: 6.51 us -> 7.26 us
  waiting for transfers between devices: 0.63 us -> 0.45 us
    pallas_call x1 -> x2, Pallas kernels: 2.17 us -> 2.92 us  [the longest x1 1.88 us: shards(): pl.pallas_call(functools.partial(high_kernel, **names), out_shape=(band,...]
    ppermute x1, waiting for transfers between devices: 0.18 us -> 0.01 us  [shards(): high_other = lax.ppermute(high_own, half_axis, swap)]
  transfers between devices with their start and end apart: 5 -> 5, of which waited for: 3 -> 2; matrix products, arithmetic and copies ran while one was open for 0% -> 0% of each run, Pallas kernels for 28% -> 33%
where the time goes in v13:
time: 16.3 us; the launch traced here: 16.2 us
  Pallas kernels  7.26 us (45%)
  starting transfers between devices  6.68 us (41%)
  local copies, waits for them, and re-layouts  1.07 us (7%)
  between operations  0.7 us (4%)
  waiting for transfers between devices  0.45 us (3%)
    pallas_call x1, Pallas kernels, shards(): pl.pallas_call(functools.partial(first_kernel, axes=axes, half_axis=half_...  3.79 us
    ppermute x1, starting transfers between devices, shards(): high_own = lax.ppermute(to_left, axes, backward)  3.1 us
    ppermute x1, starting transfers between devices, shards(): low_own = lax.ppermute(to_right, axes, forward)  2.55 us
    pallas_call x1, Pallas kernels, shards(): pl.pallas_call(functools.partial(high_kernel, **names), out_shape=(band,...  1.88 us
    slice x1, local copies, waits for them, and re-layouts, shards(): top, bottom = (matrix[:REACH, REACH:], matrix[count - REACH:, :REACH + 1])  1.06 us
    pallas_call x1, Pallas kernels, shards(): pl.pallas_call(functools.partial(low_kernel, **names), out_shape=(seed, s...  1.04 us
    ppermute x1, starting transfers between devices, shards(): other = lax.ppermute(matrix, half_axis, swap)  0.52 us
    pallas_call x1, Pallas kernels, shards(): pl.pallas_call(last_kernel, out_shape=[rows, seed], in_specs=[vmem] * 5,...  0.45 us
  transfers between devices with their start and end apart: 5, of which 2 were waited for; matrix products, arithmetic and copies ran while one was open for 0% of the time, Pallas kernels for 33%

profile of v13, /device:TPU:0, one launch (start us, length us, event | category | flops | bytes accessed | tf_op | source)
XLA Modules:
  0.0 16.2 jit_solution(15492239037890134477)
XLA Ops:
  0.6 1.1 %fusion = (f32[3,4,32,64]{3,2,1,0:T(8,128)S(1)}, f32[3,4,32,64]{3,2,1,0:T(8,128)S(1)}) fusion(f32[12,7,32,64]{3,2,1,0:T(8,128)} %own.1), kind=kLoop, calls=%fused_computation | loop fusion | bytes 393216 | tf_op jit(solution)/shard_map/slice | solution.py:467
  1.7 0.0 copy-start
  1.7 0.0 copy-start.1
  1.7 0.5 %collective-permute-start.2 = (f32[12,7,32,64]{3,2,1,0:T(8,128)}, f32[12,7,32,64]{3,2,1,0:T(8,128)S(1)}, u32[]{:S(2)}, u32[]{:S(2)}) collective-permute-start(f32[12,7,32,64]{3,2,1,0:T(8,128)} %own.1), channel_id=1, source_target_pairs={{0,1},{1,0},{2,3},{3,2},{4,5},{5,4},{6,7},{7,6},{8,9},{9,8},{10,11... | collective-permute-start | bytes 2064392 | tf_op jit(solution)/shard_map/ppermute | solution.py:484
  2.2 0.1 shard_map.41
  2.4 2.6 %collective-permute-start = (f32[96,256]{1,0:T(8,128)S(1)}, f32[96,256]{1,0:T(8,128)S(1)}, u32[]{:S(2)}, u32[]{:S(2)}) collective-permute-start(f32[96,256]{1,0:T(8,128)S(1)} %get-tuple-element.31), channel_id=1, source_target_pairs={{0,2},{2,4},{4,6},{6,8},{8,10},{10,12},{12,14},{14,0},{1,3},{3,5},... | collective-permute-start | bytes 294920 | tf_op jit(solution)/shard_map/ppermute | solution.py:488
  4.9 3.1 %collective-permute-start.1 = (f32[96,256]{1,0:T(8,128)S(1)}, f32[96,256]{1,0:T(8,128)S(1)}, u32[]{:S(2)}, u32[]{:S(2)}) collective-permute-start(f32[96,256]{1,0:T(8,128)S(1)} %get-tuple-element.32), channel_id=1, source_target_pairs={{2,0},{4,2},{6,4},{8,6},{10,8},{12,10},{14,12},{0,14},{3,1},{5,3},... | collective-permute-start | bytes 294920 | tf_op jit(solution)/shard_map/ppermute | solution.py:487
  8.0 0.0 collective-permute-done.2.other
  8.0 0.0 copy-done
  8.0 0.0 copy-done.1
  8.0 3.8 %shard_map.42 = (f32[12,7,32,64]{3,2,1,0:T(8,128)}, f32[12,7,32,64]{3,2,1,0:T(8,128)}, f32[3,7,32,64]{3,2,1,0:T(8,128)S(1)}, bf16[2,3,256,768]{3,2,1,0:T(8,128)(...) custom-call(f32[12,7,32,64]{3,2,1,0:T(8,128)S(1)} %copy-done, ...), custom_call_target="tpu_custom_call" | custom-call | flops 1610612736 | bytes 16777216 | tf_op jit(solution)/shard_map/pallas_call | solution.py:503
  11.8 0.0 collective-permute-done.mine
  11.8 0.1 collective-permute-done.1.mine
  11.9 0.2 %collective-permute-start.4 = (f32[96,256]{1,0:T(8,128)S(1)}, f32[96,256]{1,0:T(8,128)S(1)}, u32[]{:S(2)}, u32[]{:S(2)}) collective-permute-start(f32[96,256]{1,0:T(8,128)S(1)} %collective-permute-done.mine), channel_id=1, source_target_pairs={{0,1},{1,0},{2,3},{3,2},{4,5},{5,4},{6,7},{7,6},{8,9},{9,8},{10,11... | collective-permute-start | bytes 294920 | tf_op jit(solution)/shard_map/ppermute | solution.py:521
  12.1 0.3 %collective-permute-start.3 = (f32[96,256]{1,0:T(8,128)S(1)}, f32[96,256]{1,0:T(8,128)S(1)}, u32[]{:S(2)}, u32[]{:S(2)}) collective-permute-start(f32[96,256]{1,0:T(8,128)S(1)} %collective-permute-done.1.mine), channel_id=1, source_target_pairs={{0,1},{1,0},{2,3},{3,2},{4,5},{5,4},{6,7},{7,6},{8,9},{9,8},{10,11... | collective-permute-start | bytes 294920 | tf_op jit(solution)/shard_map/ppermute | solution.py:522
  12.4 0.4 %shard_map.43 = (f32[4,7,32,64]{3,2,1,0:T(8,128)S(1)}, f32[3,7,32,64]{3,2,1,0:T(8,128)S(1)}) custom-call(f32[12,7,32,64]{3,2,1,0:T(8,128)S(1)} %copy-done, f32[20,768]{1,0:T(8,128)S(1)} %get-tuple-element.36.lines, bf16[2,3,256,768]{3,2,1,0:T(8,128)(2,1)S(1)} %get-tuple-element.37.full, bf16[2,3,128,768]{3,2,1,0:T(8,128)(2,1)S(1)} %get-tuple-element.38.mine, ...), custom_call_target="tpu_custom_call" | custom-call | flops 402653184 | bytes 4194304 | tf_op jit(solution)/shard_map/pallas_call | solution.py:524
  12.9 0.3 %collective-permute-done.4.theirs = f32[96,256]{1,0:T(8,128)S(1)} collective-permute-done((f32[96,256]{1,0:T(8,128)S(1)}, f32[96,256]{1,0:T(8,128)S(1)}, u32[]{:S(2)}, u32[]{:S(2)}) %collective-permute-start.4) | collective-permute-done | bytes 98336 | tf_op jit(solution)/shard_map/ppermute | solution.py:521
  13.2 1.0 %shard_map.44 = (f32[3,7,32,64]{3,2,1,0:T(8,128)S(1)}, f32[3,7,32,64]{3,2,1,0:T(8,128)S(1)}) custom-call(f32[96,256]{1,0:T(8,128)S(1)} %collective-permute-done.mine, f32[96,256]{1,0:T(8,128)S(1)} %collective-permute-done.4.theirs, f32[20,768]{1,0:T(8,128)S(1)} %get-tuple-element.36.lines, f32[3,7,32,64]{3,2,1,0:T(8,128)S(1)} %get-tuple-element.46.seed, ...), custom_call_target="tpu_custom_call" | custom-call | flops 201326592 | bytes 2097152 | tf_op jit(solution)/shard_map/pallas_call | solution.py:545
  14.3 0.0 collective-permute-done.3.theirs
  14.3 1.9 %shard_map.45 = (f32[12,7,32,64]{3,2,1,0:T(8,128)}, f32[12,7,32,64]{3,2,1,0:T(8,128)}) custom-call(f32[96,256]{1,0:T(8,128)S(1)} %collective-permute-done.1.mine, f32[96,256]{1,0:T(8,128)S(1)} %collective-permute-done.3.theirs, f32[20,768]{1,0:T(8,128)S(1)} %get-tuple-element.36.lines, ...), custom_call_target="tpu_custom_call", output_to_operand_aliasing={{0}: (11, {}), {1}: (12, {})} | custom-call | flops 201326592 | bytes 2097152 | tf_op jit(solution)/shard_map/pallas_call | solution.py:555
Async XLA Ops:
  1.7 6.3 %copy-start = (f32[12,7,32,64]{3,2,1,0:T(8,128)S(1)}, f32[12,7,32,64]{3,2,1,0:T(8,128)}, u32[]{:S(2)}) copy-start(f32[12,7,32,64]{3,2,1,0:T(8,128)} %own.1) | copy-start | bytes 2064388
  1.7 6.3 %copy-start.1 = (s32[96,7]{0,1:T(8,128)S(1)}, s32[96,7]{0,1:T(8,128)}, u32[]{:S(2)}) copy-start(s32[96,7]{0,1:T(8,128)} %param.3) | copy-start | bytes 8068
  1.7 6.3 %collective-permute-start.2 = (f32[12,7,32,64]{3,2,1,0:T(8,128)}, f32[12,7,32,64]{3,2,1,0:T(8,128)S(1)}, u32[]{:S(2)}, u32[]{:S(2)}) collective-permute-start(f32[12,7,32,64]{3,2,1,0:T(8,128)} %own.1), channel_id=1, source_target_pairs={{0,1},{1,0},{2,3},{3,2},{4,5},{5,4},{6,7},{7,6},{8,9},{9,8},{10,11... | collective-permute-start | bytes 2064392 | tf_op jit(solution)/shard_map/ppermute | solution.py:484
  2.4 9.5 %collective-permute-start = (f32[96,256]{1,0:T(8,128)S(1)}, f32[96,256]{1,0:T(8,128)S(1)}, u32[]{:S(2)}, u32[]{:S(2)}) collective-permute-start(f32[96,256]{1,0:T(8,128)S(1)} %get-tuple-element.31), channel_id=1, source_target_pairs={{0,2},{2,4},{4,6},{6,8},{8,10},{10,12},{12,14},{14,0},{1,3},{3,5},... | collective-permute-start | bytes 294920 | tf_op jit(solution)/shard_map/ppermute | solution.py:488
  4.9 7.0 %collective-permute-start.1 = (f32[96,256]{1,0:T(8,128)S(1)}, f32[96,256]{1,0:T(8,128)S(1)}, u32[]{:S(2)}, u32[]{:S(2)}) collective-permute-start(f32[96,256]{1,0:T(8,128)S(1)} %get-tuple-element.32), channel_id=1, source_target_pairs={{2,0},{4,2},{6,4},{8,6},{10,8},{12,10},{14,12},{0,14},{3,1},{5,3},... | collective-permute-start | bytes 294920 | tf_op jit(solution)/shard_map/ppermute | solution.py:487
  11.9 1.3 %collective-permute-start.4 = (f32[96,256]{1,0:T(8,128)S(1)}, f32[96,256]{1,0:T(8,128)S(1)}, u32[]{:S(2)}, u32[]{:S(2)}) collective-permute-start(f32[96,256]{1,0:T(8,128)S(1)} %collective-permute-done.mine), channel_id=1, source_target_pairs={{0,1},{1,0},{2,3},{3,2},{4,5},{5,4},{6,7},{7,6},{8,9},{9,8},{10,11... | collective-permute-start | bytes 294920 | tf_op jit(solution)/shard_map/ppermute | solution.py:521
  12.1 2.2 %collective-permute-start.3 = (f32[96,256]{1,0:T(8,128)S(1)}, f32[96,256]{1,0:T(8,128)S(1)}, u32[]{:S(2)}, u32[]{:S(2)}) collective-permute-start(f32[96,256]{1,0:T(8,128)S(1)} %collective-permute-done.1.mine), channel_id=1, source_target_pairs={{0,1},{1,0},{2,3},{3,2},{4,5},{5,4},{6,7},{7,6},{8,9},{9,8},{10,11... | collective-permute-start | bytes 294920 | tf_op jit(solution)/shard_map/ppermute | solution.py:522

commit v14 on v13

--- a/solution.py
+++ b/solution.py
@@ -64,13 +64,14 @@
     return lines[at : at + 1, lo : lo + WIDE]
 
 
-def span_of(a, count, is_square):
-    if a < REACH:
-        return (REACH - a if is_square else 2 * REACH - a), SPAN
-    s = a - (count - REACH)
-    if s >= 0:
-        return 0, (2 * REACH - s if is_square else REACH - s)
-    return 0, SPAN
+def inner_rows(g, groups):
+    return range(REACH if g == 0 else 0, GROUP - REACH if g == groups - 1 else GROUP)
+
+
+def row_of(g, s, groups, rows, low, high):
+    if s in inner_rows(g, groups):
+        return rows.at[s]
+    return low.at[s] if g == 0 else high.at[s - (GROUP - REACH)]
 
 
 def edge_kernel(top, bottom, to_left, to_right):
@@ -110,7 +111,7 @@
     def near(self, g):
         return [e for e in (g - 1, g, g + 1) if 0 <= e < self.groups]
 
-    def second(self, g, h, sign, seed, result):
+    def second(self, g, h, sign, low, high, result):
         span = range(1 if h > g else 0, GROUP - 1 if h < g else GROUP)
         rows = slice(span[0] * HALF, (span[-1] + 1) * HALF)
 
@@ -129,16 +130,12 @@
         def post():
             for s in span:
                 a = g * GROUP + s
-                k0, k1 = span_of(a, self.count, False)
+                target = row_of(g, s, self.groups, sign, low, high)
                 part = result[s * HALF : (s + 1) * HALF] * (line_of(self.lines, g, s, h) * 0.5)
                 for t in range(GROUP):
                     k = t + GROUP * (h - g) - s + REACH
                     if 0 <= k < SPAN:
-                        block = 1.5 * self.own[a, k] - part[:, t * BS : (t + 1) * BS]
-                        if k0 <= k < k1:
-                            sign[s, k] = block
-                        else:
-                            seed[a if a < REACH else a - (self.count - REACH), k] = block
+                        target[k] = 1.5 * self.own[a, k] - part[:, t * BS : (t + 1) * BS]
 
         return dot, store, post
 
@@ -172,14 +169,14 @@
         return dot, store, post
 
     def send(self, g, i, source, target, sems):
-        for s in range(GROUP):
-            a = g * GROUP + s
-            k0, k1 = span_of(a, self.count, i == 0)
-            store = pltpu.make_async_copy(
-                source.at[s, pl.ds(k0, k1 - k0)], target.at[a, pl.ds(k0, k1 - k0)], sems.at[i, a]
-            )
-            store.start()
-            self.stores.append(store)
+        rows = inner_rows(g, self.groups)
+        store = pltpu.make_async_copy(
+            source.at[pl.ds(rows[0], len(rows))],
+            target.at[pl.ds(g * GROUP + rows[0], len(rows))],
+            sems.at[i, g],
+        )
+        store.start()
+        self.stores.append(store)
 
     def finish(self):
         for store in self.stores:
@@ -207,7 +204,7 @@
 
 
 def first_kernel(
-    own, other, pat, square_out, sign_out, seed, full, mine, keep, lines, low_a, low_b, low_m, low_p,
+    own, other, pat, square_out, sign_out, low_square, high_square, low_sign, full, mine, keep, lines, low_a, low_b, low_m, low_p,
     high_a, high_b, high_m, high_p, square, sign, results, sems, *, axes, half_axis
 ):
     it = Interior(own, lines, full, mine, keep)
@@ -267,7 +264,9 @@
                 for t in range(GROUP):
                     k = t + GROUP * (h - g) - s + REACH
                     if 0 <= k < SPAN:
-                        staged[g][s, k] = part[:, t * BS : (t + 1) * BS]
+                        row_of(g, s, groups, square.at[g], low_square, high_square)[k] = part[
+                            :, t * BS : (t + 1) * BS
+                        ]
             if h == g:
                 return
             for c in range(0, GROUP, 2):
@@ -281,15 +280,16 @@
                     for s in range(c, c + 2):
                         k = s + GROUP * (g - h) - t + REACH
                         if 0 <= k < SPAN:
-                            staged[h][t, k] = part[:, (s - c) * BS : (s - c + 1) * BS]
+                            row_of(h, t, groups, square.at[h], low_square, high_square)[k] = part[
+                                :, (s - c) * BS : (s - c + 1) * BS
+                            ]
 
         return dot, store, post
 
-    staged = [square.at[g] for g in range(groups)]
 
     def begin():
         write_lines(pat, lines, lax.axis_index(axes) * it.count, groups)
-        it.far_seed(0, seed)
+        it.far_seed(0, low_sign)
 
     build(0)
     build(1)
@@ -300,10 +300,10 @@
             if g + 2 < groups:
                 steps.append(functools.partial(build, g + 2))
         steps.append(squares(g, g, results.at[count_dots(steps)]))
-        steps.append(functools.partial(it.send, g, 0, staged[g], square_out, sems))
+        steps.append(functools.partial(it.send, g, 0, square.at[g], square_out, sems))
     for g in range(groups - 1):
         for h in it.near(g):
-            steps.append(it.second(g, h, sign.at[g], seed, results.at[count_dots(steps)]))
+            steps.append(it.second(g, h, sign.at[g], low_sign, None, results.at[count_dots(steps)]))
         steps.append(functools.partial(it.send, g, 1, sign.at[g], sign_out, sems))
     steps.append(it.reaching(low_a, low_b, low_m, low_p, 0, -1, 0))
     steps.append(it.reaching(high_a, high_b, high_m, high_p, groups - 1, groups, BS))
@@ -311,20 +311,19 @@
     it.finish()
 
 
-def last_kernel(own, lines, full, mine, keep, sign, seed, results):
+def last_kernel(own, lines, full, mine, keep, sign, high_sign, results):
     it = Interior(own, lines, full, mine, keep)
     last = it.groups - 1
-    steps = [it.second(last, h, sign, seed, results.at[i]) for i, h in enumerate(it.near(last))]
-    steps.append(functools.partial(it.far_seed, last, seed))
+    steps = [it.second(last, h, sign, None, high_sign, results.at[i]) for i, h in enumerate(it.near(last))]
+    steps.append(functools.partial(it.far_seed, last, high_sign))
 
     staggered(steps)
 
 
 def border(
-    side, groups, half_axis, mine, theirs, lines, seed, a_ref, b_ref, m_ref, p_ref, halo, first, last,
-    square, sign, sent
+    side, groups, upper_half, lines, mine, theirs, a_ref, b_ref, m_ref, p_ref, square, sign, halo,
+    first, last, sent
 ):
-    upper_half = lax.axis_index(half_axis) == 1
     at = 1 - side
     edge_group, outer_group = (0, -1) if side == 0 else (groups - 1, groups)
     offset = 0 if side == 0 else 2 * REACH
@@ -372,6 +371,7 @@
     inner = slice(WIDE, 2 * WIDE) if side == 0 else slice(0, WIDE)
     to_edge = product([([m_ref[q] for q in range(2)], [x[:, inner] for x in whole])], True)
     among = product([([x[outer_rows] for x in whole], whole)], True)
+    yield
     first[0] = to_edge + b_ref[...]
     rows = [
         first[0, s * BS : (s + 1) * BS] * line_of(lines, edge_group, s + 1 - at, outer_group)
@@ -386,72 +386,71 @@
             k = t - s + offset
             if 0 <= k < SPAN:
                 square[s, k] = part[:, (t + at) * BS : (t + at + 1) * BS]
-        sent(0, s)
+    sent(0)
+    yield
     first[1] = among + a_ref[...]
     rows = [
         first[1, p * BS : (p + 1) * BS] * line_of(lines, outer_group, p + at, outer_group)
         for p in range(REACH)
     ]
     inside = [p_ref[q, 1] for q in range(2)]
-    last[0] = product([(reach_out, padded(rows, side == 0)), (inside, across)])
+    out = product([(reach_out, padded(rows, side == 0)), (inside, across)])
     last[1] = back
     for s in range(REACH):
-        rows = slice(s * HALF, (s + 1) * HALF)
-        far = last[0, rows] * (line_of(lines, edge_group, s + 1 - at, outer_group) * 0.5)
-        close = last[1, rows] * (line_of(lines, edge_group, s + 1 - at, edge_group) * 0.5)
+        close = last[1, s * HALF : (s + 1) * HALF] * (
+            line_of(lines, edge_group, s + 1 - at, edge_group) * 0.5
+        )
+        for t in range(REACH):
+            k = t - s + REACH
+            sign[s, k] = sign[s, k] - close[:, (t + 1 - at) * BS : (t + 2 - at) * BS]
+    yield
+    last[0] = out
+    for s in range(REACH):
+        far = last[0, s * HALF : (s + 1) * HALF] * (
+            line_of(lines, edge_group, s + 1 - at, outer_group) * 0.5
+        )
         for t in range(REACH):
             k = t - s + offset
             if 0 <= k < SPAN:
-                lanes = slice((t + at) * BS, (t + at + 1) * BS)
-                sign[s, k] = seed[s, k] - far[:, lanes]
-            k = t - s + REACH
-            lanes = slice((t + 1 - at) * BS, (t + 2 - at) * BS)
-            sign[s, k] = seed[s, k] - close[:, lanes]
-        sent(1, s)
-
-
-def low_kernel(
-    mine, theirs, lines, seed, a_ref, b_ref, m_ref, p_ref, square, sign, halo, first, last, *,
-    groups, half_axis
-):
-    border(
-        0, groups, half_axis, mine, theirs, lines, seed, a_ref, b_ref, m_ref, p_ref, halo, first,
-        last, square, sign, lambda i, s: None,
-    )
-
-
-def high_kernel(
-    mine, theirs, lines, seed, a_ref, b_ref, m_ref, p_ref, low_square, low_sign, sign_last, square_in,
-    sign_in, square_out, sign_out, halo, first, last, square, sign, sems, last_sems, *, groups,
-    half_axis
+                sign[s, k] = sign[s, k] - far[:, (t + at) * BS : (t + at + 1) * BS]
+    sent(1)
+
+
+def border_kernel(
+    low_own, low_other, high_own, high_other, lines, sign_last, low_a, low_b, low_m, low_p, high_a,
+    high_b, high_m, high_p, low_square_in, high_square_in, low_sign_in, high_sign_in, square_in,
+    sign_in, low_square, high_square, low_sign, high_sign, square_out, sign_out, halo, first, last,
+    sems, last_sem, *, groups, half_axis
 ):
     count = square_in.shape[0]
+    upper_half = lax.axis_index(half_axis) == 1
     stores = []
 
-    def send(source, s, a, i, k0, k1, sem):
-        target = (square_out, sign_out)[i]
-        store = pltpu.make_async_copy(
-            source.at[s, pl.ds(k0, k1 - k0)], target.at[a, pl.ds(k0, k1 - k0)], sem
-        )
+    def send(source, target, a, sem):
+        store = pltpu.make_async_copy(source, target.at[pl.ds(a, source.shape[0])], sem)
         store.start()
         stores.append(store)
 
-    for i, source in enumerate((low_square, low_sign)):
-        for s in range(REACH):
-            send(source, s, s, i, 0, span_of(s, count, i == 0)[0], sems.at[0, i, s])
-    for s in range(GROUP):
-        a = count - GROUP + s
-        send(sign_last, s, a, 1, *span_of(a, count, False), last_sems.at[s])
-
-    def sent(i, s):
-        a = count - REACH + s
-        source = (square, sign)[i]
-        send(source, s, a, i, span_of(a, count, i == 0)[1], SPAN, sems.at[1, i, s])
-
-    border(
-        1, groups, half_axis, mine, theirs, lines, seed, a_ref, b_ref, m_ref, p_ref, halo, first,
-        last, square, sign, sent,
-    )
+    send(sign_last.at[pl.ds(0, GROUP - REACH)], sign_out, count - GROUP, last_sem)
+    squares, signs = (low_square, high_square), (low_sign, high_sign)
+
+    def side(n, *refs):
+        def sent(i):
+            source, target = ((squares[n], square_out), (signs[n], sign_out))[i]
+            send(source, target, (0, count - REACH)[n], sems.at[n, i])
+
+        return border(
+            n, groups, upper_half, lines, *refs, squares[n], signs[n], halo.at[n], first.at[n],
+            last.at[n], sent,
+        )
+
+    works = [
+        side(0, low_own, low_other, low_a, low_b, low_m, low_p),
+        side(1, high_own, high_other, high_a, high_b, high_m, high_p),
+    ]
+    for _ in range(4):
+        for work in works:
+            next(work, None)
     for store in stores:
         store.wait()
 
@@ -488,7 +487,7 @@
     low_own = lax.ppermute(to_right, axes, forward)
 
     band = jax.ShapeDtypeStruct(matrix.shape, F32)
-    seed = jax.ShapeDtypeStruct((REACH, SPAN, HALF, BS), F32)
+    edges = jax.ShapeDtypeStruct((REACH, SPAN, HALF, BS), F32)
     full = jax.ShapeDtypeStruct((2, groups, WIDE, 3 * WIDE), BF)
     mine = jax.ShapeDtypeStruct((2, groups, GROUP * HALF, 3 * WIDE), BF)
     keep = jax.ShapeDtypeStruct((2, 3 * groups, WIDE, WIDE), BF)
@@ -500,16 +499,16 @@
         jax.ShapeDtypeStruct((2, 2, REACH * HALF, WIDE), BF),
     ]
     rows = jax.ShapeDtypeStruct((GROUP,) + matrix.shape[1:], F32)
-    square, sign, low_seed, full, mine, keep, lines, *ends = pl.pallas_call(
+    square, sign, low_square, high_square, low_sign, full, mine, keep, lines, *ends = pl.pallas_call(
         functools.partial(first_kernel, axes=axes, half_axis=half_axis),
-        out_shape=[band, band, seed, full, mine, keep, lines] + ends_out * 2,
+        out_shape=[band, band, edges, edges, edges, full, mine, keep, lines] + ends_out * 2,
         in_specs=[vmem] * 3,
-        out_specs=[hbm] * 2 + [vmem] * 13,
+        out_specs=[hbm] * 2 + [vmem] * 15,
         scratch_shapes=[
             pltpu.VMEM((groups,) + rows.shape, F32),
             pltpu.VMEM((groups - 1,) + rows.shape, F32),
             pltpu.VMEM((2 * groups - 1 + 3 * groups - 4, WIDE, WIDE), F32),
-            pltpu.SemaphoreType.DMA((2, count)),
+            pltpu.SemaphoreType.DMA((2, groups)),
         ],
         compiler_params=params,
         cost_estimate=pl.CostEstimate(
@@ -517,13 +516,13 @@
         ),
     )(matrix, other, flags)
 
-    low_own, high_own, low_seed = lax.optimization_barrier((low_own, high_own, low_seed))
+    low_own, high_own, low_sign = lax.optimization_barrier((low_own, high_own, low_sign))
     low_other = lax.ppermute(low_own, half_axis, swap)
     high_other = lax.ppermute(high_own, half_axis, swap)
 
-    sign_last, high_seed = pl.pallas_call(
+    sign_last, high_sign = pl.pallas_call(
         last_kernel,
-        out_shape=[rows, seed],
+        out_shape=[rows, edges],
         in_specs=[vmem] * 5,
         out_specs=[vmem] * 2,
         scratch_shapes=[pltpu.VMEM((2, GROUP * HALF, WIDE), F32)],
@@ -533,45 +532,28 @@
         ),
     )(matrix, lines, full, mine, keep)
 
-    names = dict(groups=groups, half_axis=half_axis)
-    scratch = [
-        pltpu.VMEM((2, WIDE, 2 * WIDE), BF),
-        pltpu.VMEM((2, REACH * BS, WIDE), F32),
-        pltpu.VMEM((2, REACH * HALF, WIDE), F32),
-    ]
-    cost = pl.CostEstimate(
-        flops=3 * 2 * 2 * WIDE**3, bytes_accessed=2 * 2**20, transcendentals=0
+    outs = pl.pallas_call(
+        functools.partial(border_kernel, groups=groups, half_axis=half_axis),
+        out_shape=[edges] * 4 + [band] * 2,
+        in_specs=[vmem] * 18 + [hbm] * 2,
+        out_specs=[vmem] * 4 + [hbm] * 2,
+        scratch_shapes=[
+            pltpu.VMEM((2, 2, WIDE, 2 * WIDE), BF),
+            pltpu.VMEM((2, 2, REACH * BS, WIDE), F32),
+            pltpu.VMEM((2, 2, REACH * HALF, WIDE), F32),
+            pltpu.SemaphoreType.DMA((2, 2)),
+            pltpu.SemaphoreType.DMA,
+        ],
+        input_output_aliases={14 + i: i for i in range(6)},
+        compiler_params=params,
+        cost_estimate=pl.CostEstimate(
+            flops=3 * 2 * 4 * WIDE**3, bytes_accessed=2 * 2**20, transcendentals=0
+        ),
+    )(
+        low_own, low_other, high_own, high_other, lines, sign_last, *ends, low_square, high_square,
+        low_sign, high_sign, square, sign,
     )
-    low_square, low_sign = pl.pallas_call(
-        functools.partial(low_kernel, **names),
-        out_shape=(seed, seed),
-        in_specs=[vmem] * 8,
-        out_specs=[vmem] * 2,
-        scratch_shapes=scratch,
-        compiler_params=params,
-        cost_estimate=cost,
-    )(low_own, low_other, lines, low_seed, *ends[:4])
-    return tuple(
-        pl.pallas_call(
-            functools.partial(high_kernel, **names),
-            out_shape=(band, band),
-            in_specs=[vmem] * 11 + [hbm] * 2,
-            out_specs=[hbm] * 2,
-            scratch_shapes=scratch
-            + [
-                pltpu.VMEM(seed.shape, F32),
-                pltpu.VMEM(seed.shape, F32),
-                pltpu.SemaphoreType.DMA((2, 2, REACH)),
-                pltpu.SemaphoreType.DMA((GROUP,)),
-            ],
-            input_output_aliases={11: 0, 12: 1},
-            compiler_params=params,
-            cost_estimate=cost,
-        )(
-            high_own, high_other, lines, high_seed, *ends[4:], low_square, low_sign, sign_last,
-            square, sign,
-        )
-    )
+    return tuple(outs[4:])
 
 
 def solution(mesh):

time: 16.3 us -> 15.8 us (0.969)
  Pallas kernels: 7.26 us -> 6.37 us
  waiting for transfers between devices: 0.45 us -> 0.79 us
    pallas_call x3 -> x2, Pallas kernels: 3.36 us -> 2.67 us  [the longest x1 2.22 us: shards(): pl.pallas_call(functools.partial(border_kernel, groups=groups, half_axis=...]
    pallas_call x1, Pallas kernels: 3.79 us -> 3.59 us  [shards(): pl.pallas_call(functools.partial(first_kernel, axes=axes, half_axis=half_...]
    ppermute x1, waiting for transfers between devices: 0.1 us -> 0.3 us  [shards(): high_own = lax.ppermute(to_left, axes, backward)]
    ppermute x1, starting transfers between devices: 0.32 us -> 0.51 us  [shards(): high_other = lax.ppermute(high_own, half_axis, swap)]
    ppermute x1, starting transfers between devices: 0.19 us -> 0.01 us  [shards(): low_other = lax.ppermute(low_own, half_axis, swap)]
  transfers between devices with their start and end apart: 5 -> 5, of which waited for: 2 -> 3; matrix products, arithmetic and copies ran while one was open for 0% -> 0% of each run, Pallas kernels for 33% -> 27%
where the time goes in v14:
time: 15.8 us; the launch traced here: 15.6 us
  starting transfers between devices  6.68 us (42%)
  Pallas kernels  6.37 us (40%)
  local copies, waits for them, and re-layouts  1.07 us (7%)
  waiting for transfers between devices  0.79 us (5%)
  between operations  0.69 us (4%)
    pallas_call x1, Pallas kernels, shards(): pl.pallas_call(functools.partial(first_kernel, axes=axes, half_axis=half_...  3.59 us
    ppermute x1, starting transfers between devices, shards(): high_own = lax.ppermute(to_left, axes, backward)  3.1 us
    ppermute x1, starting transfers between devices, shards(): low_own = lax.ppermute(to_right, axes, forward)  2.55 us
    pallas_call x1, Pallas kernels, shards(): pl.pallas_call(functools.partial(border_kernel, groups=groups, half_axis=...  2.22 us
    slice x1, local copies, waits for them, and re-layouts, shards(): top, bottom = (matrix[:REACH, REACH:], matrix[count - REACH:, :REACH + 1])  1.06 us
    ppermute x1, starting transfers between devices, shards(): other = lax.ppermute(matrix, half_axis, swap)  0.52 us
    ppermute x1, starting transfers between devices, shards(): high_other = lax.ppermute(high_own, half_axis, swap)  0.51 us
    pallas_call x1, Pallas kernels, shards(): pl.pallas_call(last_kernel, out_shape=[rows, edges], in_specs=[vmem] * 5,...  0.45 us
  transfers between devices with their start and end apart: 5, of which 3 were waited for; matrix products, arithmetic and copies ran while one was open for 0% of the time, Pallas kernels for 27%

profile of v14, /device:TPU:0, one launch (start us, length us, event | category | flops | bytes accessed | tf_op | source)
XLA Modules:
  0.0 15.6 jit_solution(6144849625257016138)
XLA Ops:
  0.6 1.1 %fusion = (f32[3,4,32,64]{3,2,1,0:T(8,128)S(1)}, f32[3,4,32,64]{3,2,1,0:T(8,128)S(1)}) fusion(f32[12,7,32,64]{3,2,1,0:T(8,128)} %own.1), kind=kLoop, calls=%fused_computation | loop fusion | bytes 393216 | tf_op jit(solution)/shard_map/slice | solution.py:466
  1.7 0.0 copy-start
  1.7 0.0 copy-start.1
  1.7 0.5 %collective-permute-start.2 = (f32[12,7,32,64]{3,2,1,0:T(8,128)}, f32[12,7,32,64]{3,2,1,0:T(8,128)S(1)}, u32[]{:S(2)}, u32[]{:S(2)}) collective-permute-start(f32[12,7,32,64]{3,2,1,0:T(8,128)} %own.1), channel_id=1, source_target_pairs={{0,1},{1,0},{2,3},{3,2},{4,5},{5,4},{6,7},{7,6},{8,9},{9,8},{10,11... | collective-permute-start | bytes 2064392 | tf_op jit(solution)/shard_map/ppermute | solution.py:483
  2.2 0.1 shard_map.41
  2.4 2.6 %collective-permute-start = (f32[96,256]{1,0:T(8,128)S(1)}, f32[96,256]{1,0:T(8,128)S(1)}, u32[]{:S(2)}, u32[]{:S(2)}) collective-permute-start(f32[96,256]{1,0:T(8,128)S(1)} %get-tuple-element.33), channel_id=1, source_target_pairs={{0,2},{2,4},{4,6},{6,8},{8,10},{10,12},{12,14},{14,0},{1,3},{3,5},... | collective-permute-start | bytes 294920 | tf_op jit(solution)/shard_map/ppermute | solution.py:487
  4.9 3.1 %collective-permute-start.1 = (f32[96,256]{1,0:T(8,128)S(1)}, f32[96,256]{1,0:T(8,128)S(1)}, u32[]{:S(2)}, u32[]{:S(2)}) collective-permute-start(f32[96,256]{1,0:T(8,128)S(1)} %get-tuple-element.34), channel_id=1, source_target_pairs={{2,0},{4,2},{6,4},{8,6},{10,8},{12,10},{14,12},{0,14},{3,1},{5,3},... | collective-permute-start | bytes 294920 | tf_op jit(solution)/shard_map/ppermute | solution.py:486
  8.0 0.0 collective-permute-done.2.other
  8.0 0.0 copy-done
  8.0 0.0 copy-done.1
  8.0 3.6 %shard_map.42 = (f32[12,7,32,64]{3,2,1,0:T(8,128)}, f32[12,7,32,64]{3,2,1,0:T(8,128)}, f32[3,7,32,64]{3,2,1,0:T(8,128)S(1)}, f32[3,7,32,64]{3,2,1,0:T(8,128)S(1)...) custom-call(f32[12,7,32,64]{3,2,1,0:T(8,128)S(1)} %copy-done, ...), custom_call_target="tpu_custom_call" | custom-call | flops 1610612736 | bytes 16777216 | tf_op jit(solution)/shard_map/pallas_call | solution.py:502
  11.6 0.0 collective-permute-done.low_own
  11.6 0.3 %collective-permute-done.1.high_own = f32[96,256]{1,0:T(8,128)S(1)} collective-permute-done((f32[96,256]{1,0:T(8,128)S(1)}, f32[96,256]{1,0:T(8,128)S(1)}, u32[]{:S(2)}, u32[]{:S(2)}) %collective-permute-start.1) | collective-permute-done | bytes 98336 | tf_op jit(solution)/shard_map/ppermute | solution.py:486
  11.9 0.0 collective-permute-start.3
  11.9 0.5 %collective-permute-start.4 = (f32[96,256]{1,0:T(8,128)S(1)}, f32[96,256]{1,0:T(8,128)S(1)}, u32[]{:S(2)}, u32[]{:S(2)}) collective-permute-start(f32[96,256]{1,0:T(8,128)S(1)} %collective-permute-done.1.high_own), channel_id=1, source_target_pairs={{0,1},{1,0},{2,3},{3,2},{4,5},{5,4},{6,7},{7,6},{8,9},{9,8},{10,11... | collective-permute-start | bytes 294920 | tf_op jit(solution)/shard_map/ppermute | solution.py:521
  12.4 0.4 %shard_map.43 = (f32[4,7,32,64]{3,2,1,0:T(8,128)S(1)}, f32[3,7,32,64]{3,2,1,0:T(8,128)S(1)}) custom-call(f32[12,7,32,64]{3,2,1,0:T(8,128)S(1)} %copy-done, f32[20,768]{1,0:T(8,128)S(1)} %get-tuple-element.39.lines, bf16[2,3,256,768]{3,2,1,0:T(8,128)(2,1)S(1)} %get-tuple-element.40.full, bf16[2,3,128,768]{3,2,1,0:T(8,128)(2,1)S(1)} %get-tuple-element.41.mine, ...), custom_call_target="tpu_custom_call" | custom-call | flops 402653184 | bytes 4194304 | tf_op jit(solution)/shard_map/pallas_call | solution.py:523
  12.9 0.3 %collective-permute-done.3.low_other = f32[96,256]{1,0:T(8,128)S(1)} collective-permute-done((f32[96,256]{1,0:T(8,128)S(1)}, f32[96,256]{1,0:T(8,128)S(1)}, u32[]{:S(2)}, u32[]{:S(2)}) %collective-permute-start.3) | collective-permute-done | bytes 98336 | tf_op jit(solution)/shard_map/ppermute | solution.py:520
  13.2 0.2 collective-permute-done.4.high_other
  13.4 2.2 %shard_map.44 = (f32[3,7,32,64]{3,2,1,0:T(8,128)S(1)}, f32[3,7,32,64]{3,2,1,0:T(8,128)S(1)}, f32[3,7,32,64]{3,2,1,0:T(8,128)S(1)}, f32[3,7,32,64]{3,2,1,0:T(8,12...) custom-call(f32[96,256]{1,0:T(8,128)S(1)} %collective-permute-done.l, ...), custom_call_target="tpu_custom_call", output_to_operand_aliasing={{0}: (14, {}), {1}: (15, {}), {2}: (16, {}), {3}: (17, {}),... | custom-call | flops 402653184 | bytes 2097152 | tf_op jit(solution)/shard_map/pallas_call | solution.py:535
Async XLA Ops:
  1.7 6.3 %copy-start = (f32[12,7,32,64]{3,2,1,0:T(8,128)S(1)}, f32[12,7,32,64]{3,2,1,0:T(8,128)}, u32[]{:S(2)}) copy-start(f32[12,7,32,64]{3,2,1,0:T(8,128)} %own.1) | copy-start | bytes 2064388
  1.7 6.3 %copy-start.1 = (s32[96,7]{0,1:T(8,128)S(1)}, s32[96,7]{0,1:T(8,128)}, u32[]{:S(2)}) copy-start(s32[96,7]{0,1:T(8,128)} %param.3) | copy-start | bytes 8068
  1.7 6.3 %collective-permute-start.2 = (f32[12,7,32,64]{3,2,1,0:T(8,128)}, f32[12,7,32,64]{3,2,1,0:T(8,128)S(1)}, u32[]{:S(2)}, u32[]{:S(2)}) collective-permute-start(f32[12,7,32,64]{3,2,1,0:T(8,128)} %own.1), channel_id=1, source_target_pairs={{0,1},{1,0},{2,3},{3,2},{4,5},{5,4},{6,7},{7,6},{8,9},{9,8},{10,11... | collective-permute-start | bytes 2064392 | tf_op jit(solution)/shard_map/ppermute | solution.py:483
  2.4 9.3 %collective-permute-start = (f32[96,256]{1,0:T(8,128)S(1)}, f32[96,256]{1,0:T(8,128)S(1)}, u32[]{:S(2)}, u32[]{:S(2)}) collective-permute-start(f32[96,256]{1,0:T(8,128)S(1)} %get-tuple-element.33), channel_id=1, source_target_pairs={{0,2},{2,4},{4,6},{6,8},{8,10},{10,12},{12,14},{14,0},{1,3},{3,5},... | collective-permute-start | bytes 294920 | tf_op jit(solution)/shard_map/ppermute | solution.py:487
  4.9 7.0 %collective-permute-start.1 = (f32[96,256]{1,0:T(8,128)S(1)}, f32[96,256]{1,0:T(8,128)S(1)}, u32[]{:S(2)}, u32[]{:S(2)}) collective-permute-start(f32[96,256]{1,0:T(8,128)S(1)} %get-tuple-element.34), channel_id=1, source_target_pairs={{2,0},{4,2},{6,4},{8,6},{10,8},{12,10},{14,12},{0,14},{3,1},{5,3},... | collective-permute-start | bytes 294920 | tf_op jit(solution)/shard_map/ppermute | solution.py:486
  11.9 1.3 %collective-permute-start.3 = (f32[96,256]{1,0:T(8,128)S(1)}, f32[96,256]{1,0:T(8,128)S(1)}, u32[]{:S(2)}, u32[]{:S(2)}) collective-permute-start(f32[96,256]{1,0:T(8,128)S(1)} %collective-permute-done.low_own), channel_id=1, source_target_pairs={{0,1},{1,0},{2,3},{3,2},{4,5},{5,4},{6,7},{7,6},{8,9},{9,8},{10,11... | collective-permute-start | bytes 294920 | tf_op jit(solution)/shard_map/ppermute | solution.py:520
  11.9 1.5 %collective-permute-start.4 = (f32[96,256]{1,0:T(8,128)S(1)}, f32[96,256]{1,0:T(8,128)S(1)}, u32[]{:S(2)}, u32[]{:S(2)}) collective-permute-start(f32[96,256]{1,0:T(8,128)S(1)} %collective-permute-done.1.high_own), channel_id=1, source_target_pairs={{0,1},{1,0},{2,3},{3,2},{4,5},{5,4},{6,7},{7,6},{8,9},{9,8},{10,11... | collective-permute-start | bytes 294920 | tf_op jit(solution)/shard_map/ppermute | solution.py:521

commit v15 on v14

--- a/solution.py
+++ b/solution.py
@@ -68,6 +68,20 @@
     return range(REACH if g == 0 else 0, GROUP - REACH if g == groups - 1 else GROUP)
 
 
+def inner_blocks(side, is_square):
+    first = REACH if is_square else 2 * REACH
+    return (first, SPAN) if side == 0 else (0, SPAN - first)
+
+
+def outer_blocks(side, is_square):
+    k0, k1 = inner_blocks(side, is_square)
+    return (0, k0) if side == 0 else (k1, SPAN)
+
+
+def blocks_of(ref, rows, blocks):
+    return ref.at[pl.ds(rows[0], rows[1] - rows[0]), pl.ds(blocks[0], blocks[1] - blocks[0])]
+
+
 def row_of(g, s, groups, rows, low, high):
     if s in inner_rows(g, groups):
         return rows.at[s]
@@ -174,6 +188,17 @@
             source.at[pl.ds(rows[0], len(rows))],
             target.at[pl.ds(g * GROUP + rows[0], len(rows))],
             sems.at[i, g],
+        )
+        store.start()
+        self.stores.append(store)
+
+    def send_edge(self, side, i, source, target, sem):
+        first = 0 if side == 0 else self.count - REACH
+        blocks = inner_blocks(side, i == 0)
+        store = pltpu.make_async_copy(
+            blocks_of(source, (0, REACH), blocks),
+            blocks_of(target, (first, first + REACH), blocks),
+            sem,
         )
         store.start()
         self.stores.append(store)
@@ -205,7 +230,7 @@
 
 def first_kernel(
     own, other, pat, square_out, sign_out, low_square, high_square, low_sign, full, mine, keep, lines, low_a, low_b, low_m, low_p,
-    high_a, high_b, high_m, high_p, square, sign, results, sems, *, axes, half_axis
+    high_a, high_b, high_m, high_p, square, sign, results, sems, edge_sems, *, axes, half_axis
 ):
     it = Interior(own, lines, full, mine, keep)
     groups = it.groups
@@ -301,10 +326,17 @@
                 steps.append(functools.partial(build, g + 2))
         steps.append(squares(g, g, results.at[count_dots(steps)]))
         steps.append(functools.partial(it.send, g, 0, square.at[g], square_out, sems))
+        if g in (0, groups - 1):
+            side, source = (0, low_square) if g == 0 else (1, high_square)
+            steps.append(
+                functools.partial(it.send_edge, side, 0, source, square_out, edge_sems.at[side])
+            )
     for g in range(groups - 1):
         for h in it.near(g):
             steps.append(it.second(g, h, sign.at[g], low_sign, None, results.at[count_dots(steps)]))
         steps.append(functools.partial(it.send, g, 1, sign.at[g], sign_out, sems))
+        if g == 0:
+            steps.append(functools.partial(it.send_edge, 0, 1, low_sign, sign_out, edge_sems.at[2]))
     steps.append(it.reaching(low_a, low_b, low_m, low_p, 0, -1, 0))
     steps.append(it.reaching(high_a, high_b, high_m, high_p, groups - 1, groups, BS))
     staggered(steps)
@@ -420,24 +452,29 @@
     low_own, low_other, high_own, high_other, lines, sign_last, low_a, low_b, low_m, low_p, high_a,
     high_b, high_m, high_p, low_square_in, high_square_in, low_sign_in, high_sign_in, square_in,
     sign_in, low_square, high_square, low_sign, high_sign, square_out, sign_out, halo, first, last,
-    sems, last_sem, *, groups, half_axis
+    sems, last_sems, *, groups, half_axis
 ):
     count = square_in.shape[0]
     upper_half = lax.axis_index(half_axis) == 1
     stores = []
 
-    def send(source, target, a, sem):
-        store = pltpu.make_async_copy(source, target.at[pl.ds(a, source.shape[0])], sem)
+    def send(source, target, rows, blocks, sem):
+        from_rows = (0, rows[1] - rows[0])
+        store = pltpu.make_async_copy(
+            blocks_of(source, from_rows, blocks), blocks_of(target, rows, blocks), sem
+        )
         store.start()
         stores.append(store)
 
-    send(sign_last.at[pl.ds(0, GROUP - REACH)], sign_out, count - GROUP, last_sem)
+    send(sign_last, sign_out, (count - GROUP, count - REACH), (0, SPAN), last_sems.at[0])
+    send(high_sign, sign_out, (count - REACH, count), inner_blocks(1, False), last_sems.at[1])
     squares, signs = (low_square, high_square), (low_sign, high_sign)
 
     def side(n, *refs):
         def sent(i):
             source, target = ((squares[n], square_out), (signs[n], sign_out))[i]
-            send(source, target, (0, count - REACH)[n], sems.at[n, i])
+            rows = (0, REACH) if n == 0 else (count - REACH, count)
+            send(source, target, rows, outer_blocks(n, i == 0), sems.at[n, i])
 
         return border(
             n, groups, upper_half, lines, *refs, squares[n], signs[n], halo.at[n], first.at[n],
@@ -509,6 +546,7 @@
             pltpu.VMEM((groups - 1,) + rows.shape, F32),
             pltpu.VMEM((2 * groups - 1 + 3 * groups - 4, WIDE, WIDE), F32),
             pltpu.SemaphoreType.DMA((2, groups)),
+            pltpu.SemaphoreType.DMA((3,)),
         ],
         compiler_params=params,
         cost_estimate=pl.CostEstimate(
@@ -516,7 +554,8 @@
         ),
     )(matrix, other, flags)
 
-    low_own, high_own, low_sign = lax.optimization_barrier((low_own, high_own, low_sign))
+    low_own, low_sign = lax.optimization_barrier((low_own, low_sign))
+    high_own, low_sign = lax.optimization_barrier((high_own, low_sign))
     low_other = lax.ppermute(low_own, half_axis, swap)
     high_other = lax.ppermute(high_own, half_axis, swap)
 
@@ -542,7 +581,7 @@
             pltpu.VMEM((2, 2, REACH * BS, WIDE), F32),
             pltpu.VMEM((2, 2, REACH * HALF, WIDE), F32),
             pltpu.SemaphoreType.DMA((2, 2)),
-            pltpu.SemaphoreType.DMA,
+            pltpu.SemaphoreType.DMA((2,)),
         ],
         input_output_aliases={14 + i: i for i in range(6)},
         compiler_params=params,

time: 15.8 us -> 15.7 us (level)
  waiting for transfers between devices: 0.79 us -> 0.63 us
    ppermute x1, starting transfers between devices: 0.51 us -> 0.17 us  [shards(): high_other = lax.ppermute(high_own, half_axis, swap)]
    ppermute x1, starting transfers between devices: 0.01 us -> 0.34 us  [shards(): low_other = lax.ppermute(low_own, half_axis, swap)]
    ppermute x1, waiting for transfers between devices: 0.15 us -> 0.34 us  [shards(): high_other = lax.ppermute(high_own, half_axis, swap)]
    ppermute x1, waiting for transfers between devices: 0.3 us -> 0.12 us  [shards(): high_own = lax.ppermute(to_left, axes, backward)]
    pallas_call x1, Pallas kernels: 3.59 us -> 3.77 us  [shards(): pl.pallas_call(functools.partial(first_kernel, axes=axes, half_axis=half_...]
    ppermute x1, waiting for transfers between devices: 0.34 us -> 0.17 us  [shards(): low_other = lax.ppermute(low_own, half_axis, swap)]
  transfers between devices with their start and end apart: 5 -> 5, of which waited for: 3 -> 3; matrix products, arithmetic and copies ran while one was open for 0% -> 0% of each run, Pallas kernels for 27% -> 28%
where the time goes in v15:
time: 15.7 us; the launch traced here: 15.6 us
  starting transfers between devices  6.68 us (43%)
  Pallas kernels  6.5 us (41%)
  local copies, waits for them, and re-layouts  1.07 us (7%)
  between operations  0.69 us (4%)
  waiting for transfers between devices  0.63 us (4%)
    pallas_call x1, Pallas kernels, shards(): pl.pallas_call(functools.partial(first_kernel, axes=axes, half_axis=half_...  3.77 us
    ppermute x1, starting transfers between devices, shards(): high_own = lax.ppermute(to_left, axes, backward)  3.1 us
    ppermute x1, starting transfers between devices, shards(): low_own = lax.ppermute(to_right, axes, forward)  2.55 us
    pallas_call x1, Pallas kernels, shards(): pl.pallas_call(functools.partial(border_kernel, groups=groups, half_axis=...  2.18 us
    slice x1, local copies, waits for them, and re-layouts, shards(): top, bottom = (matrix[:REACH, REACH:], matrix[count - REACH:, :REACH + 1])  1.06 us
    ppermute x1, starting transfers between devices, shards(): other = lax.ppermute(matrix, half_axis, swap)  0.52 us
    pallas_call x1, Pallas kernels, shards(): pl.pallas_call(last_kernel, out_shape=[rows, edges], in_specs=[vmem] * 5,...  0.45 us
    ppermute x1, starting transfers between devices, shards(): low_other = lax.ppermute(low_own, half_axis, swap)  0.34 us
  transfers between devices with their start and end apart: 5, of which 3 were waited for; matrix products, arithmetic and copies ran while one was open for 0% of the time, Pallas kernels for 28%

profile of v15, /device:TPU:0, one launch (start us, length us, event | category | flops | bytes accessed | tf_op | source)
XLA Modules:
  0.0 15.6 jit_solution(2133646087225543145)
XLA Ops:
  0.6 1.1 %fusion = (f32[3,4,32,64]{3,2,1,0:T(8,128)S(1)}, f32[3,4,32,64]{3,2,1,0:T(8,128)S(1)}) fusion(f32[12,7,32,64]{3,2,1,0:T(8,128)} %own.1), kind=kLoop, calls=%fused_computation | loop fusion | bytes 393216 | tf_op jit(solution)/shard_map/slice | solution.py:503
  1.7 0.0 copy-start
  1.7 0.0 copy-start.1
  1.7 0.5 %collective-permute-start.1 = (f32[12,7,32,64]{3,2,1,0:T(8,128)}, f32[12,7,32,64]{3,2,1,0:T(8,128)S(1)}, u32[]{:S(2)}, u32[]{:S(2)}) collective-permute-start(f32[12,7,32,64]{3,2,1,0:T(8,128)} %own.1), channel_id=1, source_target_pairs={{0,1},{1,0},{2,3},{3,2},{4,5},{5,4},{6,7},{7,6},{8,9},{9,8},{10,11... | collective-permute-start | bytes 2064392 | tf_op jit(solution)/shard_map/ppermute | solution.py:520
  2.2 0.1 shard_map.41
  2.4 2.6 %collective-permute-start = (f32[96,256]{1,0:T(8,128)S(1)}, f32[96,256]{1,0:T(8,128)S(1)}, u32[]{:S(2)}, u32[]{:S(2)}) collective-permute-start(f32[96,256]{1,0:T(8,128)S(1)} %get-tuple-element.34), channel_id=1, source_target_pairs={{0,2},{2,4},{4,6},{6,8},{8,10},{10,12},{12,14},{14,0},{1,3},{3,5},... | collective-permute-start | bytes 294920 | tf_op jit(solution)/shard_map/ppermute | solution.py:524
  4.9 3.1 %collective-permute-start.3 = (f32[96,256]{1,0:T(8,128)S(1)}, f32[96,256]{1,0:T(8,128)S(1)}, u32[]{:S(2)}, u32[]{:S(2)}) collective-permute-start(f32[96,256]{1,0:T(8,128)S(1)} %get-tuple-element.38), channel_id=1, source_target_pairs={{2,0},{4,2},{6,4},{8,6},{10,8},{12,10},{14,12},{0,14},{3,1},{5,3},... | collective-permute-start | bytes 294920 | tf_op jit(solution)/shard_map/ppermute | solution.py:523
  8.0 0.0 collective-permute-done.1.other
  8.0 0.0 copy-done
  8.0 0.0 copy-done.1
  8.0 3.8 %shard_map.42 = (f32[12,7,32,64]{3,2,1,0:T(8,128)}, f32[12,7,32,64]{3,2,1,0:T(8,128)}, f32[3,7,32,64]{3,2,1,0:T(8,128)S(1)}, f32[3,7,32,64]{3,2,1,0:T(8,128)S(1)...) custom-call(f32[12,7,32,64]{3,2,1,0:T(8,128)S(1)} %copy-done, ...), custom_call_target="tpu_custom_call" | custom-call | flops 1610612736 | bytes 16777216 | tf_op jit(solution)/shard_map/pallas_call | solution.py:539
  11.8 0.0 collective-permute-done.low_own
  11.8 0.1 collective-permute-done.3.high_own
  11.9 0.2 %collective-permute-start.4 = (f32[96,256]{1,0:T(8,128)S(1)}, f32[96,256]{1,0:T(8,128)S(1)}, u32[]{:S(2)}, u32[]{:S(2)}) collective-permute-start(f32[96,256]{1,0:T(8,128)S(1)} %collective-permute-done.3.high_own), channel_id=1, source_target_pairs={{0,1},{1,0},{2,3},{3,2},{4,5},{5,4},{6,7},{7,6},{8,9},{9,8},{10,11... | collective-permute-start | bytes 294920 | tf_op jit(solution)/shard_map/ppermute | solution.py:560
  12.1 0.3 %collective-permute-start.2 = (f32[96,256]{1,0:T(8,128)S(1)}, f32[96,256]{1,0:T(8,128)S(1)}, u32[]{:S(2)}, u32[]{:S(2)}) collective-permute-start(f32[96,256]{1,0:T(8,128)S(1)} %collective-permute-done.low_own), channel_id=1, source_target_pairs={{0,1},{1,0},{2,3},{3,2},{4,5},{5,4},{6,7},{7,6},{8,9},{9,8},{10,11... | collective-permute-start | bytes 294920 | tf_op jit(solution)/shard_map/ppermute | solution.py:559
  12.4 0.4 %shard_map.43 = (f32[4,7,32,64]{3,2,1,0:T(8,128)S(1)}, f32[3,7,32,64]{3,2,1,0:T(8,128)S(1)}) custom-call(f32[12,7,32,64]{3,2,1,0:T(8,128)S(1)} %copy-done, f32[20,768]{1,0:T(8,128)S(1)} %get-tuple-element.41.lines, bf16[2,3,256,768]{3,2,1,0:T(8,128)(2,1)S(1)} %get-tuple-element.42.full, bf16[2,3,128,768]{3,2,1,0:T(8,128)(2,1)S(1)} %get-tuple-element.43.mine, ...), custom_call_target="tpu_custom_call" | custom-call | flops 402653184 | bytes 4194304 | tf_op jit(solution)/shard_map/pallas_call | solution.py:562
  12.9 0.3 %collective-permute-done.4.high_other = f32[96,256]{1,0:T(8,128)S(1)} collective-permute-done((f32[96,256]{1,0:T(8,128)S(1)}, f32[96,256]{1,0:T(8,128)S(1)}, u32[]{:S(2)}, u32[]{:S(2)}) %collective-permute-start.4) | collective-permute-done | bytes 98336 | tf_op jit(solution)/shard_map/ppermute | solution.py:560
  13.2 0.2 %collective-permute-done.2.low_other = f32[96,256]{1,0:T(8,128)S(1)} collective-permute-done((f32[96,256]{1,0:T(8,128)S(1)}, f32[96,256]{1,0:T(8,128)S(1)}, u32[]{:S(2)}, u32[]{:S(2)}) %collective-permute-start.2) | collective-permute-done | bytes 98336 | tf_op jit(solution)/shard_map/ppermute | solution.py:559
  13.4 2.2 %shard_map.44 = (f32[3,7,32,64]{3,2,1,0:T(8,128)S(1)}, f32[3,7,32,64]{3,2,1,0:T(8,128)S(1)}, f32[3,7,32,64]{3,2,1,0:T(8,128)S(1)}, f32[3,7,32,64]{3,2,1,0:T(8,12...) custom-call(f32[96,256]{1,0:T(8,128)S(1)} %collective-permute-done.l, ...), custom_call_target="tpu_custom_call", output_to_operand_aliasing={{0}: (14, {}), {1}: (15, {}), {2}: (16, {}), {3}: (17, {}),... | custom-call | flops 402653184 | bytes 2097152 | tf_op jit(solution)/shard_map/pallas_call | solution.py:574
Async XLA Ops:
  1.7 6.3 %copy-start = (f32[12,7,32,64]{3,2,1,0:T(8,128)S(1)}, f32[12,7,32,64]{3,2,1,0:T(8,128)}, u32[]{:S(2)}) copy-start(f32[12,7,32,64]{3,2,1,0:T(8,128)} %own.1) | copy-start | bytes 2064388
  1.7 6.3 %copy-start.1 = (s32[96,7]{0,1:T(8,128)S(1)}, s32[96,7]{0,1:T(8,128)}, u32[]{:S(2)}) copy-start(s32[96,7]{0,1:T(8,128)} %param.3) | copy-start | bytes 8068
  1.7 6.3 %collective-permute-start.1 = (f32[12,7,32,64]{3,2,1,0:T(8,128)}, f32[12,7,32,64]{3,2,1,0:T(8,128)S(1)}, u32[]{:S(2)}, u32[]{:S(2)}) collective-permute-start(f32[12,7,32,64]{3,2,1,0:T(8,128)} %own.1), channel_id=1, source_target_pairs={{0,1},{1,0},{2,3},{3,2},{4,5},{5,4},{6,7},{7,6},{8,9},{9,8},{10,11... | collective-permute-start | bytes 2064392 | tf_op jit(solution)/shard_map/ppermute | solution.py:520
  2.4 9.4 %collective-permute-start = (f32[96,256]{1,0:T(8,128)S(1)}, f32[96,256]{1,0:T(8,128)S(1)}, u32[]{:S(2)}, u32[]{:S(2)}) collective-permute-start(f32[96,256]{1,0:T(8,128)S(1)} %get-tuple-element.34), channel_id=1, source_target_pairs={{0,2},{2,4},{4,6},{6,8},{8,10},{10,12},{12,14},{14,0},{1,3},{3,5},... | collective-permute-start | bytes 294920 | tf_op jit(solution)/shard_map/ppermute | solution.py:524
  4.9 7.0 %collective-permute-start.3 = (f32[96,256]{1,0:T(8,128)S(1)}, f32[96,256]{1,0:T(8,128)S(1)}, u32[]{:S(2)}, u32[]{:S(2)}) collective-permute-start(f32[96,256]{1,0:T(8,128)S(1)} %get-tuple-element.38), channel_id=1, source_target_pairs={{2,0},{4,2},{6,4},{8,6},{10,8},{12,10},{14,12},{0,14},{3,1},{5,3},... | collective-permute-start | bytes 294920 | tf_op jit(solution)/shard_map/ppermute | solution.py:523
  11.9 1.3 %collective-permute-start.4 = (f32[96,256]{1,0:T(8,128)S(1)}, f32[96,256]{1,0:T(8,128)S(1)}, u32[]{:S(2)}, u32[]{:S(2)}) collective-permute-start(f32[96,256]{1,0:T(8,128)S(1)} %collective-permute-done.3.high_own), channel_id=1, source_target_pairs={{0,1},{1,0},{2,3},{3,2},{4,5},{5,4},{6,7},{7,6},{8,9},{9,8},{10,11... | collective-permute-start | bytes 294920 | tf_op jit(solution)/shard_map/ppermute | solution.py:560
  12.1 1.3 %collective-permute-start.2 = (f32[96,256]{1,0:T(8,128)S(1)}, f32[96,256]{1,0:T(8,128)S(1)}, u32[]{:S(2)}, u32[]{:S(2)}) collective-permute-start(f32[96,256]{1,0:T(8,128)S(1)} %collective-permute-done.low_own), channel_id=1, source_target_pairs={{0,1},{1,0},{2,3},{3,2},{4,5},{5,4},{6,7},{7,6},{8,9},{9,8},{10,11... | collective-permute-start | bytes 294920 | tf_op jit(solution)/shard_map/ppermute | solution.py:559

commit v16 on v15

--- a/solution.py
+++ b/solution.py
@@ -88,13 +88,22 @@
     return low.at[s] if g == 0 else high.at[s - (GROUP - REACH)]
 
 
-def edge_kernel(top, bottom, to_left, to_right):
-    for source, target in ((top, to_left), (bottom, to_right)):
-        for s in range(REACH):
-            for t in range(2):
-                target[s * HALF : (s + 1) * HALF, t * 2 * BS : (t + 1) * 2 * BS] = jnp.concatenate(
-                    [source[s, 2 * t], source[s, 2 * t + 1]], axis=1
-                )
+def is_odd(axes):
+    return lax.rem(lax.axis_index(axes), 2) == 1
+
+
+def edge_kernel(top, bottom, across, along, *, axes):
+    odd = is_odd(axes)
+    for s in range(REACH):
+        rows = slice(s * HALF, (s + 1) * HALF)
+        for t in range(2):
+            lanes = slice(t * 2 * BS, (t + 1) * 2 * BS)
+            low, high = [
+                jnp.concatenate([source[s, 2 * t], source[s, 2 * t + 1]], axis=1)
+                for source in (top, bottom)
+            ]
+            across[rows, lanes] = jnp.where(odd, high, low)
+            along[rows, lanes] = jnp.where(odd, low, high)
 
 
 class Interior:
@@ -230,7 +239,7 @@
 
 def first_kernel(
     own, other, pat, square_out, sign_out, low_square, high_square, low_sign, full, mine, keep, lines, low_a, low_b, low_m, low_p,
-    high_a, high_b, high_m, high_p, square, sign, results, sems, edge_sems, *, axes, half_axis
+    square, sign, results, sems, edge_sems, *, axes, half_axis
 ):
     it = Interior(own, lines, full, mine, keep)
     groups = it.groups
@@ -338,16 +347,18 @@
         if g == 0:
             steps.append(functools.partial(it.send_edge, 0, 1, low_sign, sign_out, edge_sems.at[2]))
     steps.append(it.reaching(low_a, low_b, low_m, low_p, 0, -1, 0))
-    steps.append(it.reaching(high_a, high_b, high_m, high_p, groups - 1, groups, BS))
     staggered(steps)
     it.finish()
 
 
-def last_kernel(own, lines, full, mine, keep, sign, high_sign, results):
+def last_kernel(
+    own, lines, full, mine, keep, sign, high_sign, high_a, high_b, high_m, high_p, results
+):
     it = Interior(own, lines, full, mine, keep)
     last = it.groups - 1
     steps = [it.second(last, h, sign, None, high_sign, results.at[i]) for i, h in enumerate(it.near(last))]
     steps.append(functools.partial(it.far_seed, last, high_sign))
+    steps.append(it.reaching(high_a, high_b, high_m, high_p, last, it.groups, BS))
 
     staggered(steps)
 
@@ -401,7 +412,7 @@
     whole = [halo[q] for q in range(2)]
     outer_rows = slice(at * BS, (at + REACH) * BS)
     inner = slice(WIDE, 2 * WIDE) if side == 0 else slice(0, WIDE)
-    to_edge = product([([m_ref[q] for q in range(2)], [x[:, inner] for x in whole])], True)
+    to_edge = product([([m_ref[q] for q in range(2)], [x[:, inner] for x in whole])])
     among = product([([x[outer_rows] for x in whole], whole)], True)
     yield
     first[0] = to_edge + b_ref[...]
@@ -449,13 +460,14 @@
 
 
 def border_kernel(
-    low_own, low_other, high_own, high_other, lines, sign_last, low_a, low_b, low_m, low_p, high_a,
+    across_own, across_other, along_own, along_other, lines, sign_last, low_a, low_b, low_m, low_p, high_a,
     high_b, high_m, high_p, low_square_in, high_square_in, low_sign_in, high_sign_in, square_in,
     sign_in, low_square, high_square, low_sign, high_sign, square_out, sign_out, halo, first, last,
-    sems, last_sems, *, groups, half_axis
+    sems, last_sems, *, groups, axes, half_axis
 ):
     count = square_in.shape[0]
     upper_half = lax.axis_index(half_axis) == 1
+    odd = is_odd(axes)
     stores = []
 
     def send(source, target, rows, blocks, sem):
@@ -481,6 +493,10 @@
             last.at[n], sent,
         )
 
+    low_own = jnp.where(odd, along_own[...], across_own[...])
+    low_other = jnp.where(odd, along_other[...], across_other[...])
+    high_own = jnp.where(odd, across_own[...], along_own[...])
+    high_other = jnp.where(odd, across_other[...], along_other[...])
     works = [
         side(0, low_own, low_other, low_a, low_b, low_m, low_p),
         side(1, high_own, high_other, high_a, high_b, high_m, high_p),
@@ -503,8 +519,8 @@
     top, bottom = matrix[:REACH, REACH:], matrix[count - REACH :, : REACH + 1]
     matrix, top, bottom = lax.optimization_barrier((matrix, top, bottom))
     edge = jax.ShapeDtypeStruct((REACH * HALF, (REACH + 1) * BS), F32)
-    to_left, to_right = pl.pallas_call(
-        edge_kernel,
+    across, along = pl.pallas_call(
+        functools.partial(edge_kernel, axes=axes),
         out_shape=(edge, edge),
         in_specs=[vmem] * 2,
         out_specs=[vmem] * 2,
@@ -518,10 +534,10 @@
         size *= lax.axis_size(axis)
     swap = [(0, 1), (1, 0)]
     other = lax.ppermute(matrix, half_axis, swap)
-    forward = [(i, (i + 1) % size) for i in range(size)]
-    backward = [(target, source) for source, target in forward]
-    high_own = lax.ppermute(to_left, axes, backward)
-    low_own = lax.ppermute(to_right, axes, forward)
+    pairs = [(i, (i + 1) % size) for i in range(1, size, 2)]
+    across = lax.ppermute(across, axes, pairs + [(b, a) for a, b in pairs])
+    pairs = [(i, i + 1) for i in range(0, size, 2)]
+    along = lax.ppermute(along, axes, pairs + [(b, a) for a, b in pairs])
 
     band = jax.ShapeDtypeStruct(matrix.shape, F32)
     edges = jax.ShapeDtypeStruct((REACH, SPAN, HALF, BS), F32)
@@ -536,11 +552,11 @@
         jax.ShapeDtypeStruct((2, 2, REACH * HALF, WIDE), BF),
     ]
     rows = jax.ShapeDtypeStruct((GROUP,) + matrix.shape[1:], F32)
-    square, sign, low_square, high_square, low_sign, full, mine, keep, lines, *ends = pl.pallas_call(
+    square, sign, low_square, high_square, low_sign, full, mine, keep, lines, *low_ends = pl.pallas_call(
         functools.partial(first_kernel, axes=axes, half_axis=half_axis),
-        out_shape=[band, band, edges, edges, edges, full, mine, keep, lines] + ends_out * 2,
+        out_shape=[band, band, edges, edges, edges, full, mine, keep, lines] + ends_out,
         in_specs=[vmem] * 3,
-        out_specs=[hbm] * 2 + [vmem] * 15,
+        out_specs=[hbm] * 2 + [vmem] * 11,
         scratch_shapes=[
             pltpu.VMEM((groups,) + rows.shape, F32),
             pltpu.VMEM((groups - 1,) + rows.shape, F32),
@@ -554,16 +570,16 @@
         ),
     )(matrix, other, flags)
 
-    low_own, low_sign = lax.optimization_barrier((low_own, low_sign))
-    high_own, low_sign = lax.optimization_barrier((high_own, low_sign))
-    low_other = lax.ppermute(low_own, half_axis, swap)
-    high_other = lax.ppermute(high_own, half_axis, swap)
-
-    sign_last, high_sign = pl.pallas_call(
+    across, low_sign = lax.optimization_barrier((across, low_sign))
+    along, low_sign = lax.optimization_barrier((along, low_sign))
+    across_other = lax.ppermute(across, half_axis, swap)
+    along_other = lax.ppermute(along, half_axis, swap)
+
+    sign_last, high_sign, *high_ends = pl.pallas_call(
         last_kernel,
-        out_shape=[rows, edges],
+        out_shape=[rows, edges] + ends_out,
         in_specs=[vmem] * 5,
-        out_specs=[vmem] * 2,
+        out_specs=[vmem] * 6,
         scratch_shapes=[pltpu.VMEM((2, GROUP * HALF, WIDE), F32)],
         compiler_params=params,
         cost_estimate=pl.CostEstimate(
@@ -572,7 +588,7 @@
     )(matrix, lines, full, mine, keep)
 
     outs = pl.pallas_call(
-        functools.partial(border_kernel, groups=groups, half_axis=half_axis),
+        functools.partial(border_kernel, groups=groups, axes=axes, half_axis=half_axis),
         out_shape=[edges] * 4 + [band] * 2,
         in_specs=[vmem] * 18 + [hbm] * 2,
         out_specs=[vmem] * 4 + [hbm] * 2,
@@ -589,7 +605,7 @@
             flops=3 * 2 * 4 * WIDE**3, bytes_accessed=2 * 2**20, transcendentals=0
         ),
     )(
-        low_own, low_other, high_own, high_other, lines, sign_last, *ends, low_square, high_square,
+        across, across_other, along, along_other, lines, sign_last, *low_ends, *high_ends, low_square, high_square,
         low_sign, high_sign, square, sign,
     )
     return tuple(outs[4:])

time: 15.7 us -> 17.4 us (1.11)
  waiting for transfers between devices: 0.63 us -> 2.38 us
    ppermute x4, waiting for transfers between devices: 0.63 us -> 2.38 us  [the longest x1 1.96 us: shards(): along = lax.ppermute(along, axes, pairs + [(b, a) for a, b in pairs])]
    pallas_call x1, Pallas kernels: 3.77 us -> 3.56 us  [shards(): pl.pallas_call(functools.partial(first_kernel, axes=axes, half_axis=half_...]
  transfers between devices with their start and end apart: 5 -> 5, of which waited for: 3 -> 3; matrix products, arithmetic and copies ran while one was open for 0% -> 0% of each run, Pallas kernels for 28% -> 24%
where the time goes in v16:
time: 17.4 us; the launch traced here: 17.2 us
  starting transfers between devices  6.63 us (38%)
  Pallas kernels  6.43 us (37%)
  waiting for transfers between devices  2.38 us (14%)
  local copies, waits for them, and re-layouts  1.07 us (6%)
  between operations  0.7 us (4%)
    ppermute x1, starting transfers between devices, shards(): across = lax.ppermute(across, axes, pairs + [(b, a) for a, b in pairs])  5.6 us
    pallas_call x1, Pallas kernels, shards(): pl.pallas_call(functools.partial(first_kernel, axes=axes, half_axis=half_...  3.56 us
    pallas_call x1, Pallas kernels, shards(): pl.pallas_call(functools.partial(border_kernel, groups=groups, axes=axes,...  2.24 us
    ppermute x1, waiting for transfers between devices, shards(): along = lax.ppermute(along, axes, pairs + [(b, a) for a, b in pairs])  1.96 us
    slice x1, local copies, waits for them, and re-layouts, shards(): top, bottom = (matrix[:REACH, REACH:], matrix[count - REACH:, :REACH + 1])  1.06 us
    pallas_call x1, Pallas kernels, shards(): pl.pallas_call(last_kernel, out_shape=[rows, edges] + ends_out, in_specs=...  0.52 us
    ppermute x1, starting transfers between devices, shards(): other = lax.ppermute(matrix, half_axis, swap)  0.52 us
    ppermute x1, starting transfers between devices, shards(): across_other = lax.ppermute(across, half_axis, swap)  0.5 us
  transfers between devices with their start and end apart: 5, of which 3 were waited for; matrix products, arithmetic and copies ran while one was open for 0% of the time, Pallas kernels for 24%

profile of v16, /device:TPU:0, one launch (start us, length us, event | category | flops | bytes accessed | tf_op | source)
XLA Modules:
  0.0 17.2 jit_solution(12733304236572778931)
XLA Ops:
  0.6 1.1 %fusion = (f32[3,4,32,64]{3,2,1,0:T(8,128)S(1)}, f32[3,4,32,64]{3,2,1,0:T(8,128)S(1)}) fusion(f32[12,7,32,64]{3,2,1,0:T(8,128)} %own.1), kind=kLoop, calls=%fused_computation | loop fusion | bytes 393216 | tf_op jit(solution)/shard_map/slice | solution.py:519
  1.7 0.0 copy-start
  1.7 0.0 copy-start.1
  1.7 0.5 %collective-permute-start.1 = (f32[12,7,32,64]{3,2,1,0:T(8,128)}, f32[12,7,32,64]{3,2,1,0:T(8,128)S(1)}, u32[]{:S(2)}, u32[]{:S(2)}) collective-permute-start(f32[12,7,32,64]{3,2,1,0:T(8,128)} %own.1), channel_id=1, source_target_pairs={{0,1},{1,0},{2,3},{3,2},{4,5},{5,4},{6,7},{7,6},{8,9},{9,8},{10,11... | collective-permute-start | bytes 2064392 | tf_op jit(solution)/shard_map/ppermute | solution.py:536
  2.2 0.1 shard_map.41
  2.4 5.6 %collective-permute-start = (f32[96,256]{1,0:T(8,128)S(1)}, f32[96,256]{1,0:T(8,128)S(1)}, u32[]{:S(2)}, u32[]{:S(2)}) collective-permute-start(f32[96,256]{1,0:T(8,128)S(1)} %get-tuple-element.34), channel_id=1, source_target_pairs={{2,4},{6,8},{10,12},{14,0},{4,2},{8,6},{12,10},{0,14},{3,5},{7,9},... | collective-permute-start | bytes 294920 | tf_op jit(solution)/shard_map/ppermute | solution.py:538
  8.0 0.0 collective-permute-start.3
  8.0 0.0 collective-permute-done.1.other
  8.0 0.0 copy-done
  8.0 0.0 copy-done.1
  8.0 3.6 %shard_map.42 = (f32[12,7,32,64]{3,2,1,0:T(8,128)}, f32[12,7,32,64]{3,2,1,0:T(8,128)}, f32[3,7,32,64]{3,2,1,0:T(8,128)S(1)}, f32[3,7,32,64]{3,2,1,0:T(8,128)S(1)...) custom-call(f32[12,7,32,64]{3,2,1,0:T(8,128)S(1)} %copy-done, ...), custom_call_target="tpu_custom_call" | custom-call | flops 1610612736 | bytes 16777216 | tf_op jit(solution)/shard_map/pallas_call | solution.py:555
  11.6 0.0 collective-permute-done.across_own
  11.6 2.0 %collective-permute-done.3.along_own = f32[96,256]{1,0:T(8,128)S(1)} collective-permute-done((f32[96,256]{1,0:T(8,128)S(1)}, f32[96,256]{1,0:T(8,128)S(1)}, u32[]{:S(2)}, u32[]{:S(2)}) %collective-permute-start.3) | collective-permute-done | bytes 98336 | tf_op jit(solution)/shard_map/ppermute | solution.py:540
  13.5 0.0 collective-permute-start.4
  13.5 0.5 %collective-permute-start.2 = (f32[96,256]{1,0:T(8,128)S(1)}, f32[96,256]{1,0:T(8,128)S(1)}, u32[]{:S(2)}, u32[]{:S(2)}) collective-permute-start(f32[96,256]{1,0:T(8,128)S(1)} %collective-permute-done.across_own), channel_id=1, source_target_pairs={{0,1},{1,0},{2,3},{3,2},{4,5},{5,4},{6,7},{7,6},{8,9},{9,8},{10,11... | collective-permute-start | bytes 294920 | tf_op jit(solution)/shard_map/ppermute | solution.py:575
  14.0 0.5 %shard_map.43 = (f32[4,7,32,64]{3,2,1,0:T(8,128)S(1)}, f32[3,7,32,64]{3,2,1,0:T(8,128)S(1)}, f32[192,256]{1,0:T(8,128)S(1)}, f32[192,256]{1,0:T(8,128)S(1)}, bf1...) custom-call(f32[12,7,32,64]{3,2,1,0:T(8,128)S(1)} %copy-done, f32[20,768]{1,0:T(8,128)S(1)} %get-tuple-element.41.lines, ...), custom_call_target="tpu_custom_call" | custom-call | flops 402653184 | bytes 4194304 | tf_op jit(solution)/shard_map/pallas_call | solution.py:578
  14.6 0.3 %collective-permute-done.4.along_other = f32[96,256]{1,0:T(8,128)S(1)} collective-permute-done((f32[96,256]{1,0:T(8,128)S(1)}, f32[96,256]{1,0:T(8,128)S(1)}, u32[]{:S(2)}, u32[]{:S(2)}) %collective-permute-start.4) | collective-permute-done | bytes 98336 | tf_op jit(solution)/shard_map/ppermute | solution.py:576
  14.8 0.2 collective-permute-done.2.across_other
  15.0 2.2 %shard_map.44 = (f32[3,7,32,64]{3,2,1,0:T(8,128)S(1)}, f32[3,7,32,64]{3,2,1,0:T(8,128)S(1)}, f32[3,7,32,64]{3,2,1,0:T(8,128)S(1)}, f32[3,7,32,64]{3,2,1,0:T(8,12...) custom-call(f32[96,256]{1,0:T(8,128)S(1)} %collective-permute-done.a, ...), custom_call_target="tpu_custom_call", output_to_operand_aliasing={{0}: (14, {}), {1}: (15, {}), {2}: (16, {}), {3}: (17, {}),... | custom-call | flops 402653184 | bytes 2097152 | tf_op jit(solution)/shard_map/pallas_call | solution.py:590
Async XLA Ops:
  1.7 6.3 %copy-start = (f32[12,7,32,64]{3,2,1,0:T(8,128)S(1)}, f32[12,7,32,64]{3,2,1,0:T(8,128)}, u32[]{:S(2)}) copy-start(f32[12,7,32,64]{3,2,1,0:T(8,128)} %own.1) | copy-start | bytes 2064388
  1.7 6.3 %copy-start.1 = (s32[96,7]{0,1:T(8,128)S(1)}, s32[96,7]{0,1:T(8,128)}, u32[]{:S(2)}) copy-start(s32[96,7]{0,1:T(8,128)} %param.3) | copy-start | bytes 8068
  1.7 6.2 %collective-permute-start.1 = (f32[12,7,32,64]{3,2,1,0:T(8,128)}, f32[12,7,32,64]{3,2,1,0:T(8,128)S(1)}, u32[]{:S(2)}, u32[]{:S(2)}) collective-permute-start(f32[12,7,32,64]{3,2,1,0:T(8,128)} %own.1), channel_id=1, source_target_pairs={{0,1},{1,0},{2,3},{3,2},{4,5},{5,4},{6,7},{7,6},{8,9},{9,8},{10,11... | collective-permute-start | bytes 2064392 | tf_op jit(solution)/shard_map/ppermute | solution.py:536
  2.4 9.2 %collective-permute-start = (f32[96,256]{1,0:T(8,128)S(1)}, f32[96,256]{1,0:T(8,128)S(1)}, u32[]{:S(2)}, u32[]{:S(2)}) collective-permute-start(f32[96,256]{1,0:T(8,128)S(1)} %get-tuple-element.34), channel_id=1, source_target_pairs={{2,4},{6,8},{10,12},{14,0},{4,2},{8,6},{12,10},{0,14},{3,5},{7,9},... | collective-permute-start | bytes 294920 | tf_op jit(solution)/shard_map/ppermute | solution.py:538
  8.0 5.6 %collective-permute-start.3 = (f32[96,256]{1,0:T(8,128)S(1)}, f32[96,256]{1,0:T(8,128)S(1)}, u32[]{:S(2)}, u32[]{:S(2)}) collective-permute-start(f32[96,256]{1,0:T(8,128)S(1)} %get-tuple-element.38), channel_id=1, source_target_pairs={{0,2},{4,6},{8,10},{12,14},{2,0},{6,4},{10,8},{14,12},{1,3},{5,7},... | collective-permute-start | bytes 294920 | tf_op jit(solution)/shard_map/ppermute | solution.py:540
  13.5 1.3 %collective-permute-start.4 = (f32[96,256]{1,0:T(8,128)S(1)}, f32[96,256]{1,0:T(8,128)S(1)}, u32[]{:S(2)}, u32[]{:S(2)}) collective-permute-start(f32[96,256]{1,0:T(8,128)S(1)} %collective-permute-done.3.along_own), channel_id=1, source_target_pairs={{0,1},{1,0},{2,3},{3,2},{4,5},{5,4},{6,7},{7,6},{8,9},{9,8},{10,11... | collective-permute-start | bytes 294920 | tf_op jit(solution)/shard_map/ppermute | solution.py:576
  13.5 1.4 %collective-permute-start.2 = (f32[96,256]{1,0:T(8,128)S(1)}, f32[96,256]{1,0:T(8,128)S(1)}, u32[]{:S(2)}, u32[]{:S(2)}) collective-permute-start(f32[96,256]{1,0:T(8,128)S(1)} %collective-permute-done.across_own), channel_id=1, source_target_pairs={{0,1},{1,0},{2,3},{3,2},{4,5},{5,4},{6,7},{7,6},{8,9},{9,8},{10,11... | collective-permute-start | bytes 294920 | tf_op jit(solution)/shard_map/ppermute | solution.py:575

commit v17 on v15

--- a/solution.py
+++ b/solution.py
@@ -166,13 +166,13 @@
 
         def dot():
             out = self.part(g, e)
-            return (
-                product([([x[outer] for x in turn(out)], out)]),
-                product([(self.part(g, g, rows), out)]),
-            )
+            turned = turn(out)
+            middle = self.part(g, g, rows)
+            left = [jnp.concatenate([turned[p][outer], middle[p]], axis=0) for p in range(2)]
+            return product([(left, out)])
 
         def store(value):
-            a_ref[...], b_ref[...] = value
+            a_ref[...], b_ref[...] = value[: REACH * BS], value[REACH * BS :]
 
         def post():
             for p in range(2):
@@ -401,7 +401,7 @@
     whole = [halo[q] for q in range(2)]
     outer_rows = slice(at * BS, (at + REACH) * BS)
     inner = slice(WIDE, 2 * WIDE) if side == 0 else slice(0, WIDE)
-    to_edge = product([([m_ref[q] for q in range(2)], [x[:, inner] for x in whole])], True)
+    to_edge = product([([m_ref[q] for q in range(2)], [x[:, inner] for x in whole])])
     among = product([([x[outer_rows] for x in whole], whole)], True)
     yield
     first[0] = to_edge + b_ref[...]

time: 15.7 us -> 15.8 us (level)
  no operation moved by 1% of the time
where the time goes in v17:
time: 15.8 us; the launch traced here: 15.7 us
  starting transfers between devices  6.68 us (42%)
  Pallas kernels  6.59 us (42%)
  local copies, waits for them, and re-layouts  1.07 us (7%)
  between operations  0.69 us (4%)
  waiting for transfers between devices  0.63 us (4%)
    pallas_call x1, Pallas kernels, shards(): pl.pallas_call(functools.partial(first_kernel, axes=axes, half_axis=half_...  3.8 us
    ppermute x1, starting transfers between devices, shards(): high_own = lax.ppermute(to_left, axes, backward)  3.1 us
    ppermute x1, starting transfers between devices, shards(): low_own = lax.ppermute(to_right, axes, forward)  2.55 us
    pallas_call x1, Pallas kernels, shards(): pl.pallas_call(functools.partial(border_kernel, groups=groups, half_axis=...  2.24 us
    slice x1, local copies, waits for them, and re-layouts, shards(): top, bottom = (matrix[:REACH, REACH:], matrix[count - REACH:, :REACH + 1])  1.06 us
    ppermute x1, starting transfers between devices, shards(): other = lax.ppermute(matrix, half_axis, swap)  0.52 us
    pallas_call x1, Pallas kernels, shards(): pl.pallas_call(last_kernel, out_shape=[rows, edges], in_specs=[vmem] * 5,...  0.45 us
    ppermute x1, waiting for transfers between devices, shards(): high_other = lax.ppermute(high_own, half_axis, swap)  0.34 us
  transfers between devices with their start and end apart: 5, of which 3 were waited for; matrix products, arithmetic and copies ran while one was open for 0% of the time, Pallas kernels for 28%

profile of v17, /device:TPU:0, one launch (start us, length us, event | category | flops | bytes accessed | tf_op | source)
XLA Modules:
  0.0 15.7 jit_solution(9894220089304243258)
XLA Ops:
  0.6 1.1 %fusion = (f32[3,4,32,64]{3,2,1,0:T(8,128)S(1)}, f32[3,4,32,64]{3,2,1,0:T(8,128)S(1)}) fusion(f32[12,7,32,64]{3,2,1,0:T(8,128)} %own.1), kind=kLoop, calls=%fused_computation | loop fusion | bytes 393216 | tf_op jit(solution)/shard_map/slice | solution.py:503
  1.7 0.0 copy-start
  1.7 0.0 copy-start.1
  1.7 0.5 %collective-permute-start.1 = (f32[12,7,32,64]{3,2,1,0:T(8,128)}, f32[12,7,32,64]{3,2,1,0:T(8,128)S(1)}, u32[]{:S(2)}, u32[]{:S(2)}) collective-permute-start(f32[12,7,32,64]{3,2,1,0:T(8,128)} %own.1), channel_id=1, source_target_pairs={{0,1},{1,0},{2,3},{3,2},{4,5},{5,4},{6,7},{7,6},{8,9},{9,8},{10,11... | collective-permute-start | bytes 2064392 | tf_op jit(solution)/shard_map/ppermute | solution.py:520
  2.2 0.1 shard_map.41
  2.4 2.6 %collective-permute-start = (f32[96,256]{1,0:T(8,128)S(1)}, f32[96,256]{1,0:T(8,128)S(1)}, u32[]{:S(2)}, u32[]{:S(2)}) collective-permute-start(f32[96,256]{1,0:T(8,128)S(1)} %get-tuple-element.34), channel_id=1, source_target_pairs={{0,2},{2,4},{4,6},{6,8},{8,10},{10,12},{12,14},{14,0},{1,3},{3,5},... | collective-permute-start | bytes 294920 | tf_op jit(solution)/shard_map/ppermute | solution.py:524
  4.9 3.1 %collective-permute-start.3 = (f32[96,256]{1,0:T(8,128)S(1)}, f32[96,256]{1,0:T(8,128)S(1)}, u32[]{:S(2)}, u32[]{:S(2)}) collective-permute-start(f32[96,256]{1,0:T(8,128)S(1)} %get-tuple-element.38), channel_id=1, source_target_pairs={{2,0},{4,2},{6,4},{8,6},{10,8},{12,10},{14,12},{0,14},{3,1},{5,3},... | collective-permute-start | bytes 294920 | tf_op jit(solution)/shard_map/ppermute | solution.py:523
  8.0 0.0 collective-permute-done.1.other
  8.0 0.0 copy-done
  8.0 0.0 copy-done.1
  8.0 3.8 %shard_map.42 = (f32[12,7,32,64]{3,2,1,0:T(8,128)}, f32[12,7,32,64]{3,2,1,0:T(8,128)}, f32[3,7,32,64]{3,2,1,0:T(8,128)S(1)}, f32[3,7,32,64]{3,2,1,0:T(8,128)S(1)...) custom-call(f32[12,7,32,64]{3,2,1,0:T(8,128)S(1)} %copy-done, ...), custom_call_target="tpu_custom_call" | custom-call | flops 1610612736 | bytes 16777216 | tf_op jit(solution)/shard_map/pallas_call | solution.py:539
  11.8 0.0 collective-permute-done.low_own
  11.8 0.1 collective-permute-done.3.high_own
  11.9 0.2 %collective-permute-start.4 = (f32[96,256]{1,0:T(8,128)S(1)}, f32[96,256]{1,0:T(8,128)S(1)}, u32[]{:S(2)}, u32[]{:S(2)}) collective-permute-start(f32[96,256]{1,0:T(8,128)S(1)} %collective-permute-done.3.high_own), channel_id=1, source_target_pairs={{0,1},{1,0},{2,3},{3,2},{4,5},{5,4},{6,7},{7,6},{8,9},{9,8},{10,11... | collective-permute-start | bytes 294920 | tf_op jit(solution)/shard_map/ppermute | solution.py:560
  12.1 0.3 %collective-permute-start.2 = (f32[96,256]{1,0:T(8,128)S(1)}, f32[96,256]{1,0:T(8,128)S(1)}, u32[]{:S(2)}, u32[]{:S(2)}) collective-permute-start(f32[96,256]{1,0:T(8,128)S(1)} %collective-permute-done.low_own), channel_id=1, source_target_pairs={{0,1},{1,0},{2,3},{3,2},{4,5},{5,4},{6,7},{7,6},{8,9},{9,8},{10,11... | collective-permute-start | bytes 294920 | tf_op jit(solution)/shard_map/ppermute | solution.py:559
  12.4 0.4 %shard_map.43 = (f32[4,7,32,64]{3,2,1,0:T(8,128)S(1)}, f32[3,7,32,64]{3,2,1,0:T(8,128)S(1)}) custom-call(f32[12,7,32,64]{3,2,1,0:T(8,128)S(1)} %copy-done, f32[20,768]{1,0:T(8,128)S(1)} %get-tuple-element.41.lines, bf16[2,3,256,768]{3,2,1,0:T(8,128)(2,1)S(1)} %get-tuple-element.42.full, bf16[2,3,128,768]{3,2,1,0:T(8,128)(2,1)S(1)} %get-tuple-element.43.mine, ...), custom_call_target="tpu_custom_call" | custom-call | flops 402653184 | bytes 4194304 | tf_op jit(solution)/shard_map/pallas_call | solution.py:562
  12.9 0.3 %collective-permute-done.4.high_other = f32[96,256]{1,0:T(8,128)S(1)} collective-permute-done((f32[96,256]{1,0:T(8,128)S(1)}, f32[96,256]{1,0:T(8,128)S(1)}, u32[]{:S(2)}, u32[]{:S(2)}) %collective-permute-start.4) | collective-permute-done | bytes 98336 | tf_op jit(solution)/shard_map/ppermute | solution.py:560
  13.2 0.2 %collective-permute-done.2.low_other = f32[96,256]{1,0:T(8,128)S(1)} collective-permute-done((f32[96,256]{1,0:T(8,128)S(1)}, f32[96,256]{1,0:T(8,128)S(1)}, u32[]{:S(2)}, u32[]{:S(2)}) %collective-permute-start.2) | collective-permute-done | bytes 98336 | tf_op jit(solution)/shard_map/ppermute | solution.py:559
  13.4 2.2 %shard_map.44 = (f32[3,7,32,64]{3,2,1,0:T(8,128)S(1)}, f32[3,7,32,64]{3,2,1,0:T(8,128)S(1)}, f32[3,7,32,64]{3,2,1,0:T(8,128)S(1)}, f32[3,7,32,64]{3,2,1,0:T(8,12...) custom-call(f32[96,256]{1,0:T(8,128)S(1)} %collective-permute-done.l, ...), custom_call_target="tpu_custom_call", output_to_operand_aliasing={{0}: (14, {}), {1}: (15, {}), {2}: (16, {}), {3}: (17, {}),... | custom-call | flops 402653184 | bytes 2097152 | tf_op jit(solution)/shard_map/pallas_call | solution.py:574
Async XLA Ops:
  1.7 6.3 %copy-start = (f32[12,7,32,64]{3,2,1,0:T(8,128)S(1)}, f32[12,7,32,64]{3,2,1,0:T(8,128)}, u32[]{:S(2)}) copy-start(f32[12,7,32,64]{3,2,1,0:T(8,128)} %own.1) | copy-start | bytes 2064388
  1.7 6.3 %copy-start.1 = (s32[96,7]{0,1:T(8,128)S(1)}, s32[96,7]{0,1:T(8,128)}, u32[]{:S(2)}) copy-start(s32[96,7]{0,1:T(8,128)} %param.3) | copy-start | bytes 8068
  1.7 6.3 %collective-permute-start.1 = (f32[12,7,32,64]{3,2,1,0:T(8,128)}, f32[12,7,32,64]{3,2,1,0:T(8,128)S(1)}, u32[]{:S(2)}, u32[]{:S(2)}) collective-permute-start(f32[12,7,32,64]{3,2,1,0:T(8,128)} %own.1), channel_id=1, source_target_pairs={{0,1},{1,0},{2,3},{3,2},{4,5},{5,4},{6,7},{7,6},{8,9},{9,8},{10,11... | collective-permute-start | bytes 2064392 | tf_op jit(solution)/shard_map/ppermute | solution.py:520
  2.4 9.5 %collective-permute-start = (f32[96,256]{1,0:T(8,128)S(1)}, f32[96,256]{1,0:T(8,128)S(1)}, u32[]{:S(2)}, u32[]{:S(2)}) collective-permute-start(f32[96,256]{1,0:T(8,128)S(1)} %get-tuple-element.34), channel_id=1, source_target_pairs={{0,2},{2,4},{4,6},{6,8},{8,10},{10,12},{12,14},{14,0},{1,3},{3,5},... | collective-permute-start | bytes 294920 | tf_op jit(solution)/shard_map/ppermute | solution.py:524
  4.9 7.0 %collective-permute-start.3 = (f32[96,256]{1,0:T(8,128)S(1)}, f32[96,256]{1,0:T(8,128)S(1)}, u32[]{:S(2)}, u32[]{:S(2)}) collective-permute-start(f32[96,256]{1,0:T(8,128)S(1)} %get-tuple-element.38), channel_id=1, source_target_pairs={{2,0},{4,2},{6,4},{8,6},{10,8},{12,10},{14,12},{0,14},{3,1},{5,3},... | collective-permute-start | bytes 294920 | tf_op jit(solution)/shard_map/ppermute | solution.py:523
  11.9 1.3 %collective-permute-start.4 = (f32[96,256]{1,0:T(8,128)S(1)}, f32[96,256]{1,0:T(8,128)S(1)}, u32[]{:S(2)}, u32[]{:S(2)}) collective-permute-start(f32[96,256]{1,0:T(8,128)S(1)} %collective-permute-done.3.high_own), channel_id=1, source_target_pairs={{0,1},{1,0},{2,3},{3,2},{4,5},{5,4},{6,7},{7,6},{8,9},{9,8},{10,11... | collective-permute-start | bytes 294920 | tf_op jit(solution)/shard_map/ppermute | solution.py:560
  12.1 1.3 %collective-permute-start.2 = (f32[96,256]{1,0:T(8,128)S(1)}, f32[96,256]{1,0:T(8,128)S(1)}, u32[]{:S(2)}, u32[]{:S(2)}) collective-permute-start(f32[96,256]{1,0:T(8,128)S(1)} %collective-permute-done.low_own), channel_id=1, source_target_pairs={{0,1},{1,0},{2,3},{3,2},{4,5},{5,4},{6,7},{7,6},{8,9},{9,8},{10,11... | collective-permute-start | bytes 294920 | tf_op jit(solution)/shard_map/ppermute | solution.py:559

commit v18 on v15

--- a/solution.py
+++ b/solution.py
@@ -501,14 +501,15 @@
     params = pltpu.CompilerParams(vmem_limit_bytes=LIMIT)
 
     top, bottom = matrix[:REACH, REACH:], matrix[count - REACH :, : REACH + 1]
-    matrix, top, bottom = lax.optimization_barrier((matrix, top, bottom))
     edge = jax.ShapeDtypeStruct((REACH * HALF, (REACH + 1) * BS), F32)
     to_left, to_right = pl.pallas_call(
         edge_kernel,
         out_shape=(edge, edge),
         in_specs=[vmem] * 2,
         out_specs=[vmem] * 2,
-        compiler_params=params,
+        compiler_params=pltpu.CompilerParams(
+            vmem_limit_bytes=LIMIT, allow_input_fusion=[True, True]
+        ),
         cost_estimate=pl.CostEstimate(
             flops=1 * 10**9, bytes_accessed=2**20, transcendentals=0
         ),

time: 15.7 us -> 15.7 us (level)
  transfers between devices with their start and end apart: 5 -> 5, of which waited for: 3 -> 3; matrix products, arithmetic and copies ran while one was open for 0% -> 7% of each run, Pallas kernels for 28% -> 28%
where the time goes in v18:
time: 15.7 us; the launch traced here: 15.6 us
  starting transfers between devices  6.69 us (43%)
  Pallas kernels  6.5 us (41%)
  local copies, waits for them, and re-layouts  1.06 us (7%)
  between operations  0.69 us (4%)
  waiting for transfers between devices  0.63 us (4%)
    pallas_call x1, Pallas kernels, shards(): pl.pallas_call(functools.partial(first_kernel, axes=axes, half_axis=half_...  3.77 us
    ppermute x1, starting transfers between devices, shards(): high_own = lax.ppermute(to_left, axes, backward)  3.1 us
    ppermute x1, starting transfers between devices, shards(): low_own = lax.ppermute(to_right, axes, forward)  2.56 us
    pallas_call x1, Pallas kernels, shards(): pl.pallas_call(functools.partial(border_kernel, groups=groups, half_axis=...  2.18 us
    slice x1, local copies, waits for them, and re-layouts, shards(): top, bottom = (matrix[:REACH, REACH:], matrix[count - REACH:, :REACH + 1])  1.05 us
    ppermute x1, starting transfers between devices, shards(): other = lax.ppermute(matrix, half_axis, swap)  0.52 us
    pallas_call x1, Pallas kernels, shards(): pl.pallas_call(last_kernel, out_shape=[rows, edges], in_specs=[vmem] * 5,...  0.44 us
    ppermute x1, starting transfers between devices, shards(): low_other = lax.ppermute(low_own, half_axis, swap)  0.34 us
  transfers between devices with their start and end apart: 5, of which 3 were waited for; matrix products, arithmetic and copies ran while one was open for 7% of the time, Pallas kernels for 28%

profile of v18, /device:TPU:0, one launch (start us, length us, event | category | flops | bytes accessed | tf_op | source)
XLA Modules:
  0.0 15.6 jit_solution(5659573707451369258)
XLA Ops:
  0.6 0.5 %collective-permute-start.1 = (f32[12,7,32,64]{3,2,1,0:T(8,128)}, f32[12,7,32,64]{3,2,1,0:T(8,128)S(1)}, u32[]{:S(2)}, u32[]{:S(2)}) collective-permute-start(f32[12,7,32,64]{3,2,1,0:T(8,128)} %own.3), channel_id=1, source_target_pairs={{0,1},{1,0},{2,3},{3,2},{4,5},{5,4},{6,7},{7,6},{8,9},{9,8},{10,11... | collective-permute-start | bytes 2064392 | tf_op jit(solution)/shard_map/ppermute | solution.py:521
  1.1 1.0 %fusion = (f32[3,4,32,64]{3,2,1,0:T(8,128)S(1)}, f32[3,4,32,64]{3,2,1,0:T(8,128)S(1)}) fusion(f32[12,7,32,64]{3,2,1,0:T(8,128)} %own.3), kind=kLoop, calls=%fused_computation | loop fusion | bytes 393216 | tf_op jit(solution)/shard_map/slice | solution.py:503
  2.2 0.0 copy-start
  2.2 0.0 copy-start.1
  2.2 0.1 shard_map.41
  2.3 2.6 %collective-permute-start = (f32[96,256]{1,0:T(8,128)S(1)}, f32[96,256]{1,0:T(8,128)S(1)}, u32[]{:S(2)}, u32[]{:S(2)}) collective-permute-start(f32[96,256]{1,0:T(8,128)S(1)} %get-tuple-element.29), channel_id=1, source_target_pairs={{0,2},{2,4},{4,6},{6,8},{8,10},{10,12},{12,14},{14,0},{1,3},{3,5},... | collective-permute-start | bytes 294920 | tf_op jit(solution)/shard_map/ppermute | solution.py:525
  4.9 3.1 %collective-permute-start.3 = (f32[96,256]{1,0:T(8,128)S(1)}, f32[96,256]{1,0:T(8,128)S(1)}, u32[]{:S(2)}, u32[]{:S(2)}) collective-permute-start(f32[96,256]{1,0:T(8,128)S(1)} %get-tuple-element.32), channel_id=1, source_target_pairs={{2,0},{4,2},{6,4},{8,6},{10,8},{12,10},{14,12},{0,14},{3,1},{5,3},... | collective-permute-start | bytes 294920 | tf_op jit(solution)/shard_map/ppermute | solution.py:524
  8.0 0.0 collective-permute-done.1.other
  8.0 0.0 copy-done
  8.0 0.0 copy-done.1
  8.0 3.8 %shard_map.42 = (f32[12,7,32,64]{3,2,1,0:T(8,128)}, f32[12,7,32,64]{3,2,1,0:T(8,128)}, f32[3,7,32,64]{3,2,1,0:T(8,128)S(1)}, f32[3,7,32,64]{3,2,1,0:T(8,128)S(1)...) custom-call(f32[12,7,32,64]{3,2,1,0:T(8,128)S(1)} %copy-done, ...), custom_call_target="tpu_custom_call" | custom-call | flops 1610612736 | bytes 16777216 | tf_op jit(solution)/shard_map/pallas_call | solution.py:540
  11.8 0.0 collective-permute-done.low_own
  11.8 0.1 collective-permute-done.3.high_own
  11.9 0.2 %collective-permute-start.4 = (f32[96,256]{1,0:T(8,128)S(1)}, f32[96,256]{1,0:T(8,128)S(1)}, u32[]{:S(2)}, u32[]{:S(2)}) collective-permute-start(f32[96,256]{1,0:T(8,128)S(1)} %collective-permute-done.3.high_own), channel_id=1, source_target_pairs={{0,1},{1,0},{2,3},{3,2},{4,5},{5,4},{6,7},{7,6},{8,9},{9,8},{10,11... | collective-permute-start | bytes 294920 | tf_op jit(solution)/shard_map/ppermute | solution.py:561
  12.1 0.3 %collective-permute-start.2 = (f32[96,256]{1,0:T(8,128)S(1)}, f32[96,256]{1,0:T(8,128)S(1)}, u32[]{:S(2)}, u32[]{:S(2)}) collective-permute-start(f32[96,256]{1,0:T(8,128)S(1)} %collective-permute-done.low_own), channel_id=1, source_target_pairs={{0,1},{1,0},{2,3},{3,2},{4,5},{5,4},{6,7},{7,6},{8,9},{9,8},{10,11... | collective-permute-start | bytes 294920 | tf_op jit(solution)/shard_map/ppermute | solution.py:560
  12.4 0.4 %shard_map.43 = (f32[4,7,32,64]{3,2,1,0:T(8,128)S(1)}, f32[3,7,32,64]{3,2,1,0:T(8,128)S(1)}) custom-call(f32[12,7,32,64]{3,2,1,0:T(8,128)S(1)} %copy-done, f32[20,768]{1,0:T(8,128)S(1)} %get-tuple-element.35.lines, bf16[2,3,256,768]{3,2,1,0:T(8,128)(2,1)S(1)} %get-tuple-element.36.full, bf16[2,3,128,768]{3,2,1,0:T(8,128)(2,1)S(1)} %get-tuple-element.37.mine, ...), custom_call_target="tpu_custom_call" | custom-call | flops 402653184 | bytes 4194304 | tf_op jit(solution)/shard_map/pallas_call | solution.py:563
  12.9 0.3 %collective-permute-done.4.high_other = f32[96,256]{1,0:T(8,128)S(1)} collective-permute-done((f32[96,256]{1,0:T(8,128)S(1)}, f32[96,256]{1,0:T(8,128)S(1)}, u32[]{:S(2)}, u32[]{:S(2)}) %collective-permute-start.4) | collective-permute-done | bytes 98336 | tf_op jit(solution)/shard_map/ppermute | solution.py:561
  13.2 0.2 %collective-permute-done.2.low_other = f32[96,256]{1,0:T(8,128)S(1)} collective-permute-done((f32[96,256]{1,0:T(8,128)S(1)}, f32[96,256]{1,0:T(8,128)S(1)}, u32[]{:S(2)}, u32[]{:S(2)}) %collective-permute-start.2) | collective-permute-done | bytes 98336 | tf_op jit(solution)/shard_map/ppermute | solution.py:560
  13.4 2.2 %shard_map.44 = (f32[3,7,32,64]{3,2,1,0:T(8,128)S(1)}, f32[3,7,32,64]{3,2,1,0:T(8,128)S(1)}, f32[3,7,32,64]{3,2,1,0:T(8,128)S(1)}, f32[3,7,32,64]{3,2,1,0:T(8,12...) custom-call(f32[96,256]{1,0:T(8,128)S(1)} %collective-permute-done.l, ...), custom_call_target="tpu_custom_call", output_to_operand_aliasing={{0}: (14, {}), {1}: (15, {}), {2}: (16, {}), {3}: (17, {}),... | custom-call | flops 402653184 | bytes 2097152 | tf_op jit(solution)/shard_map/pallas_call | solution.py:575
Async XLA Ops:
  0.6 7.4 %collective-permute-start.1 = (f32[12,7,32,64]{3,2,1,0:T(8,128)}, f32[12,7,32,64]{3,2,1,0:T(8,128)S(1)}, u32[]{:S(2)}, u32[]{:S(2)}) collective-permute-start(f32[12,7,32,64]{3,2,1,0:T(8,128)} %own.3), channel_id=1, source_target_pairs={{0,1},{1,0},{2,3},{3,2},{4,5},{5,4},{6,7},{7,6},{8,9},{9,8},{10,11... | collective-permute-start | bytes 2064392 | tf_op jit(solution)/shard_map/ppermute | solution.py:521
  2.2 5.8 %copy-start = (f32[12,7,32,64]{3,2,1,0:T(8,128)S(1)}, f32[12,7,32,64]{3,2,1,0:T(8,128)}, u32[]{:S(2)}) copy-start(f32[12,7,32,64]{3,2,1,0:T(8,128)} %own.3) | copy-start | bytes 2064388
  2.2 5.8 %copy-start.1 = (s32[96,7]{0,1:T(8,128)S(1)}, s32[96,7]{0,1:T(8,128)}, u32[]{:S(2)}) copy-start(s32[96,7]{0,1:T(8,128)} %param.3) | copy-start | bytes 8068
  2.3 9.5 %collective-permute-start = (f32[96,256]{1,0:T(8,128)S(1)}, f32[96,256]{1,0:T(8,128)S(1)}, u32[]{:S(2)}, u32[]{:S(2)}) collective-permute-start(f32[96,256]{1,0:T(8,128)S(1)} %get-tuple-element.29), channel_id=1, source_target_pairs={{0,2},{2,4},{4,6},{6,8},{8,10},{10,12},{12,14},{14,0},{1,3},{3,5},... | collective-permute-start | bytes 294920 | tf_op jit(solution)/shard_map/ppermute | solution.py:525
  4.9 7.0 %collective-permute-start.3 = (f32[96,256]{1,0:T(8,128)S(1)}, f32[96,256]{1,0:T(8,128)S(1)}, u32[]{:S(2)}, u32[]{:S(2)}) collective-permute-start(f32[96,256]{1,0:T(8,128)S(1)} %get-tuple-element.32), channel_id=1, source_target_pairs={{2,0},{4,2},{6,4},{8,6},{10,8},{12,10},{14,12},{0,14},{3,1},{5,3},... | collective-permute-start | bytes 294920 | tf_op jit(solution)/shard_map/ppermute | solution.py:524
  11.9 1.3 %collective-permute-start.4 = (f32[96,256]{1,0:T(8,128)S(1)}, f32[96,256]{1,0:T(8,128)S(1)}, u32[]{:S(2)}, u32[]{:S(2)}) collective-permute-start(f32[96,256]{1,0:T(8,128)S(1)} %collective-permute-done.3.high_own), channel_id=1, source_target_pairs={{0,1},{1,0},{2,3},{3,2},{4,5},{5,4},{6,7},{7,6},{8,9},{9,8},{10,11... | collective-permute-start | bytes 294920 | tf_op jit(solution)/shard_map/ppermute | solution.py:561
  12.1 1.3 %collective-permute-start.2 = (f32[96,256]{1,0:T(8,128)S(1)}, f32[96,256]{1,0:T(8,128)S(1)}, u32[]{:S(2)}, u32[]{:S(2)}) collective-permute-start(f32[96,256]{1,0:T(8,128)S(1)} %collective-permute-done.low_own), channel_id=1, source_target_pairs={{0,1},{1,0},{2,3},{3,2},{4,5},{5,4},{6,7},{7,6},{8,9},{9,8},{10,11... | collective-permute-start | bytes 294920 | tf_op jit(solution)/shard_map/ppermute | solution.py:560

commit v19 on v18

--- a/solution.py
+++ b/solution.py
@@ -418,7 +418,7 @@
             k = t - s + offset
             if 0 <= k < SPAN:
                 square[s, k] = part[:, (t + at) * BS : (t + at + 1) * BS]
-    sent(0)
+    sent(0, None, outer_blocks(side, True))
     yield
     first[1] = among + a_ref[...]
     rows = [
@@ -435,6 +435,8 @@
         for t in range(REACH):
             k = t - s + REACH
             sign[s, k] = sign[s, k] - close[:, (t + 1 - at) * BS : (t + 2 - at) * BS]
+        k0, k1 = outer_blocks(side, False)
+        sent(1, s, (REACH - s, k1) if side == 0 else (k0, 2 * REACH - s))
     yield
     last[0] = out
     for s in range(REACH):
@@ -445,7 +447,7 @@
             k = t - s + offset
             if 0 <= k < SPAN:
                 sign[s, k] = sign[s, k] - far[:, (t + at) * BS : (t + at + 1) * BS]
-    sent(1)
+        sent(2, s, (0, REACH - s) if side == 0 else (2 * REACH - s, SPAN))
 
 
 def border_kernel(
@@ -471,10 +473,17 @@
     squares, signs = (low_square, high_square), (low_sign, high_sign)
 
     def side(n, *refs):
-        def sent(i):
-            source, target = ((squares[n], square_out), (signs[n], sign_out))[i]
-            rows = (0, REACH) if n == 0 else (count - REACH, count)
-            send(source, target, rows, outer_blocks(n, i == 0), sems.at[n, i])
+        def sent(i, s, blocks):
+            source, target = (squares[n], square_out) if i == 0 else (signs[n], sign_out)
+            first_row = 0 if n == 0 else count - REACH
+            rows = (0, REACH) if s is None else (s, s + 1)
+            store = pltpu.make_async_copy(
+                blocks_of(source, rows, blocks),
+                blocks_of(target, (first_row + rows[0], first_row + rows[1]), blocks),
+                sems.at[n, i, 0 if s is None else s],
+            )
+            store.start()
+            stores.append(store)
 
         return border(
             n, groups, upper_half, lines, *refs, squares[n], signs[n], halo.at[n], first.at[n],
@@ -581,7 +590,7 @@
             pltpu.VMEM((2, 2, WIDE, 2 * WIDE), BF),
             pltpu.VMEM((2, 2, REACH * BS, WIDE), F32),
             pltpu.VMEM((2, 2, REACH * HALF, WIDE), F32),
-            pltpu.SemaphoreType.DMA((2, 2)),
+            pltpu.SemaphoreType.DMA((2, 3, REACH)),
             pltpu.SemaphoreType.DMA((2,)),
         ],
         input_output_aliases={14 + i: i for i in range(6)},

time: 15.7 us -> 15.8 us (level)
  no operation moved by 1% of the time
where the time goes in v19:
time: 15.8 us; the launch traced here: 15.6 us
  starting transfers between devices  6.69 us (42%)
  Pallas kernels  6.54 us (41%)
  local copies, waits for them, and re-layouts  1.06 us (7%)
  between operations  0.69 us (4%)
  waiting for transfers between devices  0.63 us (4%)
    pallas_call x1, Pallas kernels, shards(): pl.pallas_call(functools.partial(first_kernel, axes=axes, half_axis=half_...  3.77 us
    ppermute x1, starting transfers between devices, shards(): high_own = lax.ppermute(to_left, axes, backward)  3.1 us
    ppermute x1, starting transfers between devices, shards(): low_own = lax.ppermute(to_right, axes, forward)  2.56 us
    pallas_call x1, Pallas kernels, shards(): pl.pallas_call(functools.partial(border_kernel, groups=groups, half_axis=...  2.21 us
    slice x1, local copies, waits for them, and re-layouts, shards(): top, bottom = (matrix[:REACH, REACH:], matrix[count - REACH:, :REACH + 1])  1.05 us
    ppermute x1, starting transfers between devices, shards(): other = lax.ppermute(matrix, half_axis, swap)  0.52 us
    pallas_call x1, Pallas kernels, shards(): pl.pallas_call(last_kernel, out_shape=[rows, edges], in_specs=[vmem] * 5,...  0.44 us
    ppermute x1, starting transfers between devices, shards(): low_other = lax.ppermute(low_own, half_axis, swap)  0.34 us
  transfers between devices with their start and end apart: 5, of which 3 were waited for; matrix products, arithmetic and copies ran while one was open for 7% of the time, Pallas kernels for 28%

profile of v19, /device:TPU:0, one launch (start us, length us, event | category | flops | bytes accessed | tf_op | source)
XLA Modules:
  0.0 15.6 jit_solution(6018059604333861026)
XLA Ops:
  0.6 0.5 %collective-permute-start.1 = (f32[12,7,32,64]{3,2,1,0:T(8,128)}, f32[12,7,32,64]{3,2,1,0:T(8,128)S(1)}, u32[]{:S(2)}, u32[]{:S(2)}) collective-permute-start(f32[12,7,32,64]{3,2,1,0:T(8,128)} %own.3), channel_id=1, source_target_pairs={{0,1},{1,0},{2,3},{3,2},{4,5},{5,4},{6,7},{7,6},{8,9},{9,8},{10,11... | collective-permute-start | bytes 2064392 | tf_op jit(solution)/shard_map/ppermute | solution.py:530
  1.1 1.0 %fusion = (f32[3,4,32,64]{3,2,1,0:T(8,128)S(1)}, f32[3,4,32,64]{3,2,1,0:T(8,128)S(1)}) fusion(f32[12,7,32,64]{3,2,1,0:T(8,128)} %own.3), kind=kLoop, calls=%fused_computation | loop fusion | bytes 393216 | tf_op jit(solution)/shard_map/slice | solution.py:512
  2.2 0.0 copy-start
  2.2 0.0 copy-start.1
  2.2 0.1 shard_map.41
  2.3 2.6 %collective-permute-start = (f32[96,256]{1,0:T(8,128)S(1)}, f32[96,256]{1,0:T(8,128)S(1)}, u32[]{:S(2)}, u32[]{:S(2)}) collective-permute-start(f32[96,256]{1,0:T(8,128)S(1)} %get-tuple-element.29), channel_id=1, source_target_pairs={{0,2},{2,4},{4,6},{6,8},{8,10},{10,12},{12,14},{14,0},{1,3},{3,5},... | collective-permute-start | bytes 294920 | tf_op jit(solution)/shard_map/ppermute | solution.py:534
  4.9 3.1 %collective-permute-start.3 = (f32[96,256]{1,0:T(8,128)S(1)}, f32[96,256]{1,0:T(8,128)S(1)}, u32[]{:S(2)}, u32[]{:S(2)}) collective-permute-start(f32[96,256]{1,0:T(8,128)S(1)} %get-tuple-element.32), channel_id=1, source_target_pairs={{2,0},{4,2},{6,4},{8,6},{10,8},{12,10},{14,12},{0,14},{3,1},{5,3},... | collective-permute-start | bytes 294920 | tf_op jit(solution)/shard_map/ppermute | solution.py:533
  8.0 0.0 collective-permute-done.1.other
  8.0 0.0 copy-done
  8.0 0.0 copy-done.1
  8.0 3.8 %shard_map.42 = (f32[12,7,32,64]{3,2,1,0:T(8,128)}, f32[12,7,32,64]{3,2,1,0:T(8,128)}, f32[3,7,32,64]{3,2,1,0:T(8,128)S(1)}, f32[3,7,32,64]{3,2,1,0:T(8,128)S(1)...) custom-call(f32[12,7,32,64]{3,2,1,0:T(8,128)S(1)} %copy-done, ...), custom_call_target="tpu_custom_call" | custom-call | flops 1610612736 | bytes 16777216 | tf_op jit(solution)/shard_map/pallas_call | solution.py:549
  11.8 0.0 collective-permute-done.low_own
  11.8 0.1 collective-permute-done.3.high_own
  11.9 0.2 %collective-permute-start.4 = (f32[96,256]{1,0:T(8,128)S(1)}, f32[96,256]{1,0:T(8,128)S(1)}, u32[]{:S(2)}, u32[]{:S(2)}) collective-permute-start(f32[96,256]{1,0:T(8,128)S(1)} %collective-permute-done.3.high_own), channel_id=1, source_target_pairs={{0,1},{1,0},{2,3},{3,2},{4,5},{5,4},{6,7},{7,6},{8,9},{9,8},{10,11... | collective-permute-start | bytes 294920 | tf_op jit(solution)/shard_map/ppermute | solution.py:570
  12.1 0.3 %collective-permute-start.2 = (f32[96,256]{1,0:T(8,128)S(1)}, f32[96,256]{1,0:T(8,128)S(1)}, u32[]{:S(2)}, u32[]{:S(2)}) collective-permute-start(f32[96,256]{1,0:T(8,128)S(1)} %collective-permute-done.low_own), channel_id=1, source_target_pairs={{0,1},{1,0},{2,3},{3,2},{4,5},{5,4},{6,7},{7,6},{8,9},{9,8},{10,11... | collective-permute-start | bytes 294920 | tf_op jit(solution)/shard_map/ppermute | solution.py:569
  12.4 0.4 %shard_map.43 = (f32[4,7,32,64]{3,2,1,0:T(8,128)S(1)}, f32[3,7,32,64]{3,2,1,0:T(8,128)S(1)}) custom-call(f32[12,7,32,64]{3,2,1,0:T(8,128)S(1)} %copy-done, f32[20,768]{1,0:T(8,128)S(1)} %get-tuple-element.35.lines, bf16[2,3,256,768]{3,2,1,0:T(8,128)(2,1)S(1)} %get-tuple-element.36.full, bf16[2,3,128,768]{3,2,1,0:T(8,128)(2,1)S(1)} %get-tuple-element.37.mine, ...), custom_call_target="tpu_custom_call" | custom-call | flops 402653184 | bytes 4194304 | tf_op jit(solution)/shard_map/pallas_call | solution.py:572
  12.9 0.3 %collective-permute-done.4.high_other = f32[96,256]{1,0:T(8,128)S(1)} collective-permute-done((f32[96,256]{1,0:T(8,128)S(1)}, f32[96,256]{1,0:T(8,128)S(1)}, u32[]{:S(2)}, u32[]{:S(2)}) %collective-permute-start.4) | collective-permute-done | bytes 98336 | tf_op jit(solution)/shard_map/ppermute | solution.py:570
  13.2 0.2 %collective-permute-done.2.low_other = f32[96,256]{1,0:T(8,128)S(1)} collective-permute-done((f32[96,256]{1,0:T(8,128)S(1)}, f32[96,256]{1,0:T(8,128)S(1)}, u32[]{:S(2)}, u32[]{:S(2)}) %collective-permute-start.2) | collective-permute-done | bytes 98336 | tf_op jit(solution)/shard_map/ppermute | solution.py:569
  13.4 2.2 %shard_map.44 = (f32[3,7,32,64]{3,2,1,0:T(8,128)S(1)}, f32[3,7,32,64]{3,2,1,0:T(8,128)S(1)}, f32[3,7,32,64]{3,2,1,0:T(8,128)S(1)}, f32[3,7,32,64]{3,2,1,0:T(8,12...) custom-call(f32[96,256]{1,0:T(8,128)S(1)} %collective-permute-done.l, ...), custom_call_target="tpu_custom_call", output_to_operand_aliasing={{0}: (14, {}), {1}: (15, {}), {2}: (16, {}), {3}: (17, {}),... | custom-call | flops 402653184 | bytes 2097152 | tf_op jit(solution)/shard_map/pallas_call | solution.py:584
Async XLA Ops:
  0.6 7.4 %collective-permute-start.1 = (f32[12,7,32,64]{3,2,1,0:T(8,128)}, f32[12,7,32,64]{3,2,1,0:T(8,128)S(1)}, u32[]{:S(2)}, u32[]{:S(2)}) collective-permute-start(f32[12,7,32,64]{3,2,1,0:T(8,128)} %own.3), channel_id=1, source_target_pairs={{0,1},{1,0},{2,3},{3,2},{4,5},{5,4},{6,7},{7,6},{8,9},{9,8},{10,11... | collective-permute-start | bytes 2064392 | tf_op jit(solution)/shard_map/ppermute | solution.py:530
  2.2 5.8 %copy-start = (f32[12,7,32,64]{3,2,1,0:T(8,128)S(1)}, f32[12,7,32,64]{3,2,1,0:T(8,128)}, u32[]{:S(2)}) copy-start(f32[12,7,32,64]{3,2,1,0:T(8,128)} %own.3) | copy-start | bytes 2064388
  2.2 5.8 %copy-start.1 = (s32[96,7]{0,1:T(8,128)S(1)}, s32[96,7]{0,1:T(8,128)}, u32[]{:S(2)}) copy-start(s32[96,7]{0,1:T(8,128)} %param.3) | copy-start | bytes 8068
  2.3 9.5 %collective-permute-start = (f32[96,256]{1,0:T(8,128)S(1)}, f32[96,256]{1,0:T(8,128)S(1)}, u32[]{:S(2)}, u32[]{:S(2)}) collective-permute-start(f32[96,256]{1,0:T(8,128)S(1)} %get-tuple-element.29), channel_id=1, source_target_pairs={{0,2},{2,4},{4,6},{6,8},{8,10},{10,12},{12,14},{14,0},{1,3},{3,5},... | collective-permute-start | bytes 294920 | tf_op jit(solution)/shard_map/ppermute | solution.py:534
  4.9 7.0 %collective-permute-start.3 = (f32[96,256]{1,0:T(8,128)S(1)}, f32[96,256]{1,0:T(8,128)S(1)}, u32[]{:S(2)}, u32[]{:S(2)}) collective-permute-start(f32[96,256]{1,0:T(8,128)S(1)} %get-tuple-element.32), channel_id=1, source_target_pairs={{2,0},{4,2},{6,4},{8,6},{10,8},{12,10},{14,12},{0,14},{3,1},{5,3},... | collective-permute-start | bytes 294920 | tf_op jit(solution)/shard_map/ppermute | solution.py:533
  11.9 1.3 %collective-permute-start.4 = (f32[96,256]{1,0:T(8,128)S(1)}, f32[96,256]{1,0:T(8,128)S(1)}, u32[]{:S(2)}, u32[]{:S(2)}) collective-permute-start(f32[96,256]{1,0:T(8,128)S(1)} %collective-permute-done.3.high_own), channel_id=1, source_target_pairs={{0,1},{1,0},{2,3},{3,2},{4,5},{5,4},{6,7},{7,6},{8,9},{9,8},{10,11... | collective-permute-start | bytes 294920 | tf_op jit(solution)/shard_map/ppermute | solution.py:570
  12.1 1.3 %collective-permute-start.2 = (f32[96,256]{1,0:T(8,128)S(1)}, f32[96,256]{1,0:T(8,128)S(1)}, u32[]{:S(2)}, u32[]{:S(2)}) collective-permute-start(f32[96,256]{1,0:T(8,128)S(1)} %collective-permute-done.low_own), channel_id=1, source_target_pairs={{0,1},{1,0},{2,3},{3,2},{4,5},{5,4},{6,7},{7,6},{8,9},{9,8},{10,11... | collective-permute-start | bytes 294920 | tf_op jit(solution)/shard_map/ppermute | solution.py:569

commit v20 on v15

--- a/solution.py
+++ b/solution.py
@@ -388,21 +388,28 @@
         return jnp.zeros((BS, BS), F32)
 
     base = -5 if side == 0 else 0
-    for p in range(REACH):
-        rows = slice((p + at) * BS, (p + at + 1) * BS)
-        for t in range(4):
-            value = jnp.concatenate([block(p, base + 2 * t), block(p, base + 2 * t + 1)], axis=1)
-            for q, x in enumerate(split(value)):
-                halo[q, rows, t * 2 * BS : (t + 1) * 2 * BS] = x
-    rows = slice(0, BS) if side == 0 else slice(REACH * BS, WIDE)
-    for q in range(2):
-        halo[q, rows, :] = jnp.zeros((BS, 2 * WIDE), BF)
-
-    whole = [halo[q] for q in range(2)]
+    empty = slice(0, BS) if side == 0 else slice(REACH * BS, WIDE)
+
+    def build(part):
+        for p in range(REACH):
+            rows = slice((p + at) * BS, (p + at + 1) * BS)
+            for t in (2 * part, 2 * part + 1):
+                value = jnp.concatenate(
+                    [block(p, base + 2 * t), block(p, base + 2 * t + 1)], axis=1
+                )
+                for q, x in enumerate(split(value)):
+                    halo[q, rows, t * 2 * BS : (t + 1) * 2 * BS] = x
+        for q in range(2):
+            halo[q, empty, part * WIDE : (part + 1) * WIDE] = jnp.zeros((BS, WIDE), BF)
+        return [halo[q, :, part * WIDE : (part + 1) * WIDE] for q in range(2)]
+
     outer_rows = slice(at * BS, (at + REACH) * BS)
-    inner = slice(WIDE, 2 * WIDE) if side == 0 else slice(0, WIDE)
-    to_edge = product([([m_ref[q] for q in range(2)], [x[:, inner] for x in whole])], True)
-    among = product([([x[outer_rows] for x in whole], whole)], True)
+    beyond = build(0 if side == 0 else 1)
+    further = product([([x[outer_rows] for x in beyond], beyond)], True)
+    yield
+    tile = build(1 if side == 0 else 0)
+    to_edge = product([([m_ref[q] for q in range(2)], tile)])
+    among = product([([x[outer_rows] for x in tile], tile)], True)
     yield
     first[0] = to_edge + b_ref[...]
     rows = [
@@ -420,7 +427,7 @@
                 square[s, k] = part[:, (t + at) * BS : (t + at + 1) * BS]
     sent(0)
     yield
-    first[1] = among + a_ref[...]
+    first[1] = among + (further + a_ref[...])
     rows = [
         first[1, p * BS : (p + 1) * BS] * line_of(lines, outer_group, p + at, outer_group)
         for p in range(REACH)
@@ -485,7 +492,7 @@
         side(0, low_own, low_other, low_a, low_b, low_m, low_p),
         side(1, high_own, high_other, high_a, high_b, high_m, high_p),
     ]
-    for _ in range(4):
+    for _ in range(5):
         for work in works:
             next(work, None)
     for store in stores:

time: 15.7 us -> 15.7 us (level)
  no operation moved by 1% of the time
where the time goes in v20:
time: 15.7 us; the launch traced here: 15.6 us
  starting transfers between devices  6.68 us (43%)
  Pallas kernels  6.5 us (41%)
  local copies, waits for them, and re-layouts  1.07 us (7%)
  between operations  0.69 us (4%)
  waiting for transfers between devices  0.63 us (4%)
    pallas_call x1, Pallas kernels, shards(): pl.pallas_call(functools.partial(first_kernel, axes=axes, half_axis=half_...  3.77 us
    ppermute x1, starting transfers between devices, shards(): high_own = lax.ppermute(to_left, axes, backward)  3.1 us
    ppermute x1, starting transfers between devices, shards(): low_own = lax.ppermute(to_right, axes, forward)  2.55 us
    pallas_call x1, Pallas kernels, shards(): pl.pallas_call(functools.partial(border_kernel, groups=groups, half_axis=...  2.17 us
    slice x1, local copies, waits for them, and re-layouts, shards(): top, bottom = (matrix[:REACH, REACH:], matrix[count - REACH:, :REACH + 1])  1.06 us
    ppermute x1, starting transfers between devices, shards(): other = lax.ppermute(matrix, half_axis, swap)  0.52 us
    pallas_call x1, Pallas kernels, shards(): pl.pallas_call(last_kernel, out_shape=[rows, edges], in_specs=[vmem] * 5,...  0.45 us
    ppermute x1, starting transfers between devices, shards(): low_other = lax.ppermute(low_own, half_axis, swap)  0.34 us
  transfers between devices with their start and end apart: 5, of which 3 were waited for; matrix products, arithmetic and copies ran while one was open for 0% of the time, Pallas kernels for 28%

profile of v20, /device:TPU:0, one launch (start us, length us, event | category | flops | bytes accessed | tf_op | source)
XLA Modules:
  0.0 15.6 jit_solution(2221643550044667609)
XLA Ops:
  0.6 1.1 %fusion = (f32[3,4,32,64]{3,2,1,0:T(8,128)S(1)}, f32[3,4,32,64]{3,2,1,0:T(8,128)S(1)}) fusion(f32[12,7,32,64]{3,2,1,0:T(8,128)} %own.1), kind=kLoop, calls=%fused_computation | loop fusion | bytes 393216 | tf_op jit(solution)/shard_map/slice | solution.py:510
  1.7 0.0 copy-start
  1.7 0.0 copy-start.1
  1.7 0.5 %collective-permute-start.1 = (f32[12,7,32,64]{3,2,1,0:T(8,128)}, f32[12,7,32,64]{3,2,1,0:T(8,128)S(1)}, u32[]{:S(2)}, u32[]{:S(2)}) collective-permute-start(f32[12,7,32,64]{3,2,1,0:T(8,128)} %own.1), channel_id=1, source_target_pairs={{0,1},{1,0},{2,3},{3,2},{4,5},{5,4},{6,7},{7,6},{8,9},{9,8},{10,11... | collective-permute-start | bytes 2064392 | tf_op jit(solution)/shard_map/ppermute | solution.py:527
  2.2 0.1 shard_map.41
  2.4 2.6 %collective-permute-start = (f32[96,256]{1,0:T(8,128)S(1)}, f32[96,256]{1,0:T(8,128)S(1)}, u32[]{:S(2)}, u32[]{:S(2)}) collective-permute-start(f32[96,256]{1,0:T(8,128)S(1)} %get-tuple-element.34), channel_id=1, source_target_pairs={{0,2},{2,4},{4,6},{6,8},{8,10},{10,12},{12,14},{14,0},{1,3},{3,5},... | collective-permute-start | bytes 294920 | tf_op jit(solution)/shard_map/ppermute | solution.py:531
  4.9 3.1 %collective-permute-start.3 = (f32[96,256]{1,0:T(8,128)S(1)}, f32[96,256]{1,0:T(8,128)S(1)}, u32[]{:S(2)}, u32[]{:S(2)}) collective-permute-start(f32[96,256]{1,0:T(8,128)S(1)} %get-tuple-element.38), channel_id=1, source_target_pairs={{2,0},{4,2},{6,4},{8,6},{10,8},{12,10},{14,12},{0,14},{3,1},{5,3},... | collective-permute-start | bytes 294920 | tf_op jit(solution)/shard_map/ppermute | solution.py:530
  8.0 0.0 collective-permute-done.1.other
  8.0 0.0 copy-done
  8.0 0.0 copy-done.1
  8.0 3.8 %shard_map.42 = (f32[12,7,32,64]{3,2,1,0:T(8,128)}, f32[12,7,32,64]{3,2,1,0:T(8,128)}, f32[3,7,32,64]{3,2,1,0:T(8,128)S(1)}, f32[3,7,32,64]{3,2,1,0:T(8,128)S(1)...) custom-call(f32[12,7,32,64]{3,2,1,0:T(8,128)S(1)} %copy-done, ...), custom_call_target="tpu_custom_call" | custom-call | flops 1610612736 | bytes 16777216 | tf_op jit(solution)/shard_map/pallas_call | solution.py:546
  11.8 0.0 collective-permute-done.low_own
  11.8 0.1 collective-permute-done.3.high_own
  11.9 0.2 %collective-permute-start.4 = (f32[96,256]{1,0:T(8,128)S(1)}, f32[96,256]{1,0:T(8,128)S(1)}, u32[]{:S(2)}, u32[]{:S(2)}) collective-permute-start(f32[96,256]{1,0:T(8,128)S(1)} %collective-permute-done.3.high_own), channel_id=1, source_target_pairs={{0,1},{1,0},{2,3},{3,2},{4,5},{5,4},{6,7},{7,6},{8,9},{9,8},{10,11... | collective-permute-start | bytes 294920 | tf_op jit(solution)/shard_map/ppermute | solution.py:567
  12.1 0.3 %collective-permute-start.2 = (f32[96,256]{1,0:T(8,128)S(1)}, f32[96,256]{1,0:T(8,128)S(1)}, u32[]{:S(2)}, u32[]{:S(2)}) collective-permute-start(f32[96,256]{1,0:T(8,128)S(1)} %collective-permute-done.low_own), channel_id=1, source_target_pairs={{0,1},{1,0},{2,3},{3,2},{4,5},{5,4},{6,7},{7,6},{8,9},{9,8},{10,11... | collective-permute-start | bytes 294920 | tf_op jit(solution)/shard_map/ppermute | solution.py:566
  12.4 0.4 %shard_map.43 = (f32[4,7,32,64]{3,2,1,0:T(8,128)S(1)}, f32[3,7,32,64]{3,2,1,0:T(8,128)S(1)}) custom-call(f32[12,7,32,64]{3,2,1,0:T(8,128)S(1)} %copy-done, f32[20,768]{1,0:T(8,128)S(1)} %get-tuple-element.41.lines, bf16[2,3,256,768]{3,2,1,0:T(8,128)(2,1)S(1)} %get-tuple-element.42.full, bf16[2,3,128,768]{3,2,1,0:T(8,128)(2,1)S(1)} %get-tuple-element.43.mine, ...), custom_call_target="tpu_custom_call" | custom-call | flops 402653184 | bytes 4194304 | tf_op jit(solution)/shard_map/pallas_call | solution.py:569
  12.9 0.3 %collective-permute-done.4.high_other = f32[96,256]{1,0:T(8,128)S(1)} collective-permute-done((f32[96,256]{1,0:T(8,128)S(1)}, f32[96,256]{1,0:T(8,128)S(1)}, u32[]{:S(2)}, u32[]{:S(2)}) %collective-permute-start.4) | collective-permute-done | bytes 98336 | tf_op jit(solution)/shard_map/ppermute | solution.py:567
  13.2 0.2 %collective-permute-done.2.low_other = f32[96,256]{1,0:T(8,128)S(1)} collective-permute-done((f32[96,256]{1,0:T(8,128)S(1)}, f32[96,256]{1,0:T(8,128)S(1)}, u32[]{:S(2)}, u32[]{:S(2)}) %collective-permute-start.2) | collective-permute-done | bytes 98336 | tf_op jit(solution)/shard_map/ppermute | solution.py:566
  13.4 2.2 %shard_map.44 = (f32[3,7,32,64]{3,2,1,0:T(8,128)S(1)}, f32[3,7,32,64]{3,2,1,0:T(8,128)S(1)}, f32[3,7,32,64]{3,2,1,0:T(8,128)S(1)}, f32[3,7,32,64]{3,2,1,0:T(8,12...) custom-call(f32[96,256]{1,0:T(8,128)S(1)} %collective-permute-done.l, ...), custom_call_target="tpu_custom_call", output_to_operand_aliasing={{0}: (14, {}), {1}: (15, {}), {2}: (16, {}), {3}: (17, {}),... | custom-call | flops 402653184 | bytes 2097152 | tf_op jit(solution)/shard_map/pallas_call | solution.py:581
Async XLA Ops:
  1.7 6.3 %copy-start = (f32[12,7,32,64]{3,2,1,0:T(8,128)S(1)}, f32[12,7,32,64]{3,2,1,0:T(8,128)}, u32[]{:S(2)}) copy-start(f32[12,7,32,64]{3,2,1,0:T(8,128)} %own.1) | copy-start | bytes 2064388
  1.7 6.3 %copy-start.1 = (s32[96,7]{0,1:T(8,128)S(1)}, s32[96,7]{0,1:T(8,128)}, u32[]{:S(2)}) copy-start(s32[96,7]{0,1:T(8,128)} %param.3) | copy-start | bytes 8068
  1.7 6.3 %collective-permute-start.1 = (f32[12,7,32,64]{3,2,1,0:T(8,128)}, f32[12,7,32,64]{3,2,1,0:T(8,128)S(1)}, u32[]{:S(2)}, u32[]{:S(2)}) collective-permute-start(f32[12,7,32,64]{3,2,1,0:T(8,128)} %own.1), channel_id=1, source_target_pairs={{0,1},{1,0},{2,3},{3,2},{4,5},{5,4},{6,7},{7,6},{8,9},{9,8},{10,11... | collective-permute-start | bytes 2064392 | tf_op jit(solution)/shard_map/ppermute | solution.py:527
  2.4 9.4 %collective-permute-start = (f32[96,256]{1,0:T(8,128)S(1)}, f32[96,256]{1,0:T(8,128)S(1)}, u32[]{:S(2)}, u32[]{:S(2)}) collective-permute-start(f32[96,256]{1,0:T(8,128)S(1)} %get-tuple-element.34), channel_id=1, source_target_pairs={{0,2},{2,4},{4,6},{6,8},{8,10},{10,12},{12,14},{14,0},{1,3},{3,5},... | collective-permute-start | bytes 294920 | tf_op jit(solution)/shard_map/ppermute | solution.py:531
  4.9 7.0 %collective-permute-start.3 = (f32[96,256]{1,0:T(8,128)S(1)}, f32[96,256]{1,0:T(8,128)S(1)}, u32[]{:S(2)}, u32[]{:S(2)}) collective-permute-start(f32[96,256]{1,0:T(8,128)S(1)} %get-tuple-element.38), channel_id=1, source_target_pairs={{2,0},{4,2},{6,4},{8,6},{10,8},{12,10},{14,12},{0,14},{3,1},{5,3},... | collective-permute-start | bytes 294920 | tf_op jit(solution)/shard_map/ppermute | solution.py:530
  11.9 1.3 %collective-permute-start.4 = (f32[96,256]{1,0:T(8,128)S(1)}, f32[96,256]{1,0:T(8,128)S(1)}, u32[]{:S(2)}, u32[]{:S(2)}) collective-permute-start(f32[96,256]{1,0:T(8,128)S(1)} %collective-permute-done.3.high_own), channel_id=1, source_target_pairs={{0,1},{1,0},{2,3},{3,2},{4,5},{5,4},{6,7},{7,6},{8,9},{9,8},{10,11... | collective-permute-start | bytes 294920 | tf_op jit(solution)/shard_map/ppermute | solution.py:567
  12.1 1.3 %collective-permute-start.2 = (f32[96,256]{1,0:T(8,128)S(1)}, f32[96,256]{1,0:T(8,128)S(1)}, u32[]{:S(2)}, u32[]{:S(2)}) collective-permute-start(f32[96,256]{1,0:T(8,128)S(1)} %collective-permute-done.low_own), channel_id=1, source_target_pairs={{0,1},{1,0},{2,3},{3,2},{4,5},{5,4},{6,7},{7,6},{8,9},{9,8},{10,11... | collective-permute-start | bytes 294920 | tf_op jit(solution)/shard_map/ppermute | solution.py:566

commit v21 on v15

--- a/solution.py
+++ b/solution.py
@@ -412,6 +412,7 @@
     across = padded(rows, side == 1)
     reach_out = [p_ref[q, 0] for q in range(2)]
     back = product([(reach_out, across)], True)
+    partly = product([([p_ref[q, 1] for q in range(2)], across)])
     for s in range(REACH):
         part = jnp.where(upper_half, rows[s][HALF:], rows[s][:HALF])
         for t in range(REACH):
@@ -425,8 +426,7 @@
         first[1, p * BS : (p + 1) * BS] * line_of(lines, outer_group, p + at, outer_group)
         for p in range(REACH)
     ]
-    inside = [p_ref[q, 1] for q in range(2)]
-    out = product([(reach_out, padded(rows, side == 0)), (inside, across)])
+    out = product([(reach_out, padded(rows, side == 0))])
     last[1] = back
     for s in range(REACH):
         close = last[1, s * HALF : (s + 1) * HALF] * (
@@ -436,7 +436,7 @@
             k = t - s + REACH
             sign[s, k] = sign[s, k] - close[:, (t + 1 - at) * BS : (t + 2 - at) * BS]
     yield
-    last[0] = out
+    last[0] = out + partly
     for s in range(REACH):
         far = last[0, s * HALF : (s + 1) * HALF] * (
             line_of(lines, edge_group, s + 1 - at, outer_group) * 0.5

time: 15.7 us -> 15.8 us (level)
  no operation moved by 1% of the time
where the time goes in v21:
time: 15.8 us; the launch traced here: 15.7 us
  starting transfers between devices  6.68 us (42%)
  Pallas kernels  6.62 us (42%)
  local copies, waits for them, and re-layouts  1.07 us (7%)
  between operations  0.69 us (4%)
  waiting for transfers between devices  0.63 us (4%)
    pallas_call x1, Pallas kernels, shards(): pl.pallas_call(functools.partial(first_kernel, axes=axes, half_axis=half_...  3.77 us
    ppermute x1, starting transfers between devices, shards(): high_own = lax.ppermute(to_left, axes, backward)  3.1 us
    ppermute x1, starting transfers between devices, shards(): low_own = lax.ppermute(to_right, axes, forward)  2.55 us
    pallas_call x1, Pallas kernels, shards(): pl.pallas_call(functools.partial(border_kernel, groups=groups, half_axis=...  2.29 us
    slice x1, local copies, waits for them, and re-layouts, shards(): top, bottom = (matrix[:REACH, REACH:], matrix[count - REACH:, :REACH + 1])  1.06 us
    ppermute x1, starting transfers between devices, shards(): other = lax.ppermute(matrix, half_axis, swap)  0.52 us
    pallas_call x1, Pallas kernels, shards(): pl.pallas_call(last_kernel, out_shape=[rows, edges], in_specs=[vmem] * 5,...  0.45 us
    ppermute x1, starting transfers between devices, shards(): low_other = lax.ppermute(low_own, half_axis, swap)  0.34 us
  transfers between devices with their start and end apart: 5, of which 3 were waited for; matrix products, arithmetic and copies ran while one was open for 0% of the time, Pallas kernels for 28%

profile of v21, /device:TPU:0, one launch (start us, length us, event | category | flops | bytes accessed | tf_op | source)
XLA Modules:
  0.0 15.7 jit_solution(12907685836425558212)
XLA Ops:
  0.6 1.1 %fusion = (f32[3,4,32,64]{3,2,1,0:T(8,128)S(1)}, f32[3,4,32,64]{3,2,1,0:T(8,128)S(1)}) fusion(f32[12,7,32,64]{3,2,1,0:T(8,128)} %own.1), kind=kLoop, calls=%fused_computation | loop fusion | bytes 393216 | tf_op jit(solution)/shard_map/slice | solution.py:503
  1.7 0.0 copy-start
  1.7 0.0 copy-start.1
  1.7 0.5 %collective-permute-start.1 = (f32[12,7,32,64]{3,2,1,0:T(8,128)}, f32[12,7,32,64]{3,2,1,0:T(8,128)S(1)}, u32[]{:S(2)}, u32[]{:S(2)}) collective-permute-start(f32[12,7,32,64]{3,2,1,0:T(8,128)} %own.1), channel_id=1, source_target_pairs={{0,1},{1,0},{2,3},{3,2},{4,5},{5,4},{6,7},{7,6},{8,9},{9,8},{10,11... | collective-permute-start | bytes 2064392 | tf_op jit(solution)/shard_map/ppermute | solution.py:520
  2.2 0.1 shard_map.41
  2.4 2.6 %collective-permute-start = (f32[96,256]{1,0:T(8,128)S(1)}, f32[96,256]{1,0:T(8,128)S(1)}, u32[]{:S(2)}, u32[]{:S(2)}) collective-permute-start(f32[96,256]{1,0:T(8,128)S(1)} %get-tuple-element.34), channel_id=1, source_target_pairs={{0,2},{2,4},{4,6},{6,8},{8,10},{10,12},{12,14},{14,0},{1,3},{3,5},... | collective-permute-start | bytes 294920 | tf_op jit(solution)/shard_map/ppermute | solution.py:524
  4.9 3.1 %collective-permute-start.3 = (f32[96,256]{1,0:T(8,128)S(1)}, f32[96,256]{1,0:T(8,128)S(1)}, u32[]{:S(2)}, u32[]{:S(2)}) collective-permute-start(f32[96,256]{1,0:T(8,128)S(1)} %get-tuple-element.38), channel_id=1, source_target_pairs={{2,0},{4,2},{6,4},{8,6},{10,8},{12,10},{14,12},{0,14},{3,1},{5,3},... | collective-permute-start | bytes 294920 | tf_op jit(solution)/shard_map/ppermute | solution.py:523
  8.0 0.0 collective-permute-done.1.other
  8.0 0.0 copy-done
  8.0 0.0 copy-done.1
  8.0 3.8 %shard_map.42 = (f32[12,7,32,64]{3,2,1,0:T(8,128)}, f32[12,7,32,64]{3,2,1,0:T(8,128)}, f32[3,7,32,64]{3,2,1,0:T(8,128)S(1)}, f32[3,7,32,64]{3,2,1,0:T(8,128)S(1)...) custom-call(f32[12,7,32,64]{3,2,1,0:T(8,128)S(1)} %copy-done, ...), custom_call_target="tpu_custom_call" | custom-call | flops 1610612736 | bytes 16777216 | tf_op jit(solution)/shard_map/pallas_call | solution.py:539
  11.8 0.0 collective-permute-done.low_own
  11.8 0.1 collective-permute-done.3.high_own
  11.9 0.2 %collective-permute-start.4 = (f32[96,256]{1,0:T(8,128)S(1)}, f32[96,256]{1,0:T(8,128)S(1)}, u32[]{:S(2)}, u32[]{:S(2)}) collective-permute-start(f32[96,256]{1,0:T(8,128)S(1)} %collective-permute-done.3.high_own), channel_id=1, source_target_pairs={{0,1},{1,0},{2,3},{3,2},{4,5},{5,4},{6,7},{7,6},{8,9},{9,8},{10,11... | collective-permute-start | bytes 294920 | tf_op jit(solution)/shard_map/ppermute | solution.py:560
  12.1 0.3 %collective-permute-start.2 = (f32[96,256]{1,0:T(8,128)S(1)}, f32[96,256]{1,0:T(8,128)S(1)}, u32[]{:S(2)}, u32[]{:S(2)}) collective-permute-start(f32[96,256]{1,0:T(8,128)S(1)} %collective-permute-done.low_own), channel_id=1, source_target_pairs={{0,1},{1,0},{2,3},{3,2},{4,5},{5,4},{6,7},{7,6},{8,9},{9,8},{10,11... | collective-permute-start | bytes 294920 | tf_op jit(solution)/shard_map/ppermute | solution.py:559
  12.4 0.4 %shard_map.43 = (f32[4,7,32,64]{3,2,1,0:T(8,128)S(1)}, f32[3,7,32,64]{3,2,1,0:T(8,128)S(1)}) custom-call(f32[12,7,32,64]{3,2,1,0:T(8,128)S(1)} %copy-done, f32[20,768]{1,0:T(8,128)S(1)} %get-tuple-element.41.lines, bf16[2,3,256,768]{3,2,1,0:T(8,128)(2,1)S(1)} %get-tuple-element.42.full, bf16[2,3,128,768]{3,2,1,0:T(8,128)(2,1)S(1)} %get-tuple-element.43.mine, ...), custom_call_target="tpu_custom_call" | custom-call | flops 402653184 | bytes 4194304 | tf_op jit(solution)/shard_map/pallas_call | solution.py:562
  12.9 0.3 %collective-permute-done.4.high_other = f32[96,256]{1,0:T(8,128)S(1)} collective-permute-done((f32[96,256]{1,0:T(8,128)S(1)}, f32[96,256]{1,0:T(8,128)S(1)}, u32[]{:S(2)}, u32[]{:S(2)}) %collective-permute-start.4) | collective-permute-done | bytes 98336 | tf_op jit(solution)/shard_map/ppermute | solution.py:560
  13.2 0.2 %collective-permute-done.2.low_other = f32[96,256]{1,0:T(8,128)S(1)} collective-permute-done((f32[96,256]{1,0:T(8,128)S(1)}, f32[96,256]{1,0:T(8,128)S(1)}, u32[]{:S(2)}, u32[]{:S(2)}) %collective-permute-start.2) | collective-permute-done | bytes 98336 | tf_op jit(solution)/shard_map/ppermute | solution.py:559
  13.4 2.3 %shard_map.44 = (f32[3,7,32,64]{3,2,1,0:T(8,128)S(1)}, f32[3,7,32,64]{3,2,1,0:T(8,128)S(1)}, f32[3,7,32,64]{3,2,1,0:T(8,128)S(1)}, f32[3,7,32,64]{3,2,1,0:T(8,12...) custom-call(f32[96,256]{1,0:T(8,128)S(1)} %collective-permute-done.l, ...), custom_call_target="tpu_custom_call", output_to_operand_aliasing={{0}: (14, {}), {1}: (15, {}), {2}: (16, {}), {3}: (17, {}),... | custom-call | flops 402653184 | bytes 2097152 | tf_op jit(solution)/shard_map/pallas_call | solution.py:574
Async XLA Ops:
  1.7 6.3 %copy-start = (f32[12,7,32,64]{3,2,1,0:T(8,128)S(1)}, f32[12,7,32,64]{3,2,1,0:T(8,128)}, u32[]{:S(2)}) copy-start(f32[12,7,32,64]{3,2,1,0:T(8,128)} %own.1) | copy-start | bytes 2064388
  1.7 6.3 %copy-start.1 = (s32[96,7]{0,1:T(8,128)S(1)}, s32[96,7]{0,1:T(8,128)}, u32[]{:S(2)}) copy-start(s32[96,7]{0,1:T(8,128)} %param.3) | copy-start | bytes 8068
  1.7 6.3 %collective-permute-start.1 = (f32[12,7,32,64]{3,2,1,0:T(8,128)}, f32[12,7,32,64]{3,2,1,0:T(8,128)S(1)}, u32[]{:S(2)}, u32[]{:S(2)}) collective-permute-start(f32[12,7,32,64]{3,2,1,0:T(8,128)} %own.1), channel_id=1, source_target_pairs={{0,1},{1,0},{2,3},{3,2},{4,5},{5,4},{6,7},{7,6},{8,9},{9,8},{10,11... | collective-permute-start | bytes 2064392 | tf_op jit(solution)/shard_map/ppermute | solution.py:520
  2.4 9.4 %collective-permute-start = (f32[96,256]{1,0:T(8,128)S(1)}, f32[96,256]{1,0:T(8,128)S(1)}, u32[]{:S(2)}, u32[]{:S(2)}) collective-permute-start(f32[96,256]{1,0:T(8,128)S(1)} %get-tuple-element.34), channel_id=1, source_target_pairs={{0,2},{2,4},{4,6},{6,8},{8,10},{10,12},{12,14},{14,0},{1,3},{3,5},... | collective-permute-start | bytes 294920 | tf_op jit(solution)/shard_map/ppermute | solution.py:524
  4.9 7.0 %collective-permute-start.3 = (f32[96,256]{1,0:T(8,128)S(1)}, f32[96,256]{1,0:T(8,128)S(1)}, u32[]{:S(2)}, u32[]{:S(2)}) collective-permute-start(f32[96,256]{1,0:T(8,128)S(1)} %get-tuple-element.38), channel_id=1, source_target_pairs={{2,0},{4,2},{6,4},{8,6},{10,8},{12,10},{14,12},{0,14},{3,1},{5,3},... | collective-permute-start | bytes 294920 | tf_op jit(solution)/shard_map/ppermute | solution.py:523
  11.9 1.3 %collective-permute-start.4 = (f32[96,256]{1,0:T(8,128)S(1)}, f32[96,256]{1,0:T(8,128)S(1)}, u32[]{:S(2)}, u32[]{:S(2)}) collective-permute-start(f32[96,256]{1,0:T(8,128)S(1)} %collective-permute-done.3.high_own), channel_id=1, source_target_pairs={{0,1},{1,0},{2,3},{3,2},{4,5},{5,4},{6,7},{7,6},{8,9},{9,8},{10,11... | collective-permute-start | bytes 294920 | tf_op jit(solution)/shard_map/ppermute | solution.py:560
  12.1 1.3 %collective-permute-start.2 = (f32[96,256]{1,0:T(8,128)S(1)}, f32[96,256]{1,0:T(8,128)S(1)}, u32[]{:S(2)}, u32[]{:S(2)}) collective-permute-start(f32[96,256]{1,0:T(8,128)S(1)} %collective-permute-done.low_own), channel_id=1, source_target_pairs={{0,1},{1,0},{2,3},{3,2},{4,5},{5,4},{6,7},{7,6},{8,9},{9,8},{10,11... | collective-permute-start | bytes 294920 | tf_op jit(solution)/shard_map/ppermute | solution.py:559

commit v22 on v20

--- a/solution.py
+++ b/solution.py
@@ -387,15 +387,19 @@
             return whole_rows[c][:, k * BS : (k + 1) * BS].T
         return jnp.zeros((BS, BS), F32)
 
-    base = -5 if side == 0 else 0
+    bases = (-1, -4) if side == 0 else (0, REACH)
     empty = slice(0, BS) if side == 0 else slice(REACH * BS, WIDE)
+
+    def place(p, part, e):
+        c = bases[part] + e
+        return block(p, c) if part == 1 or 0 <= c < REACH else jnp.zeros((BS, BS), F32)
 
     def build(part):
         for p in range(REACH):
             rows = slice((p + at) * BS, (p + at + 1) * BS)
             for t in (2 * part, 2 * part + 1):
                 value = jnp.concatenate(
-                    [block(p, base + 2 * t), block(p, base + 2 * t + 1)], axis=1
+                    [place(p, part, 2 * (t - 2 * part) + e) for e in range(2)], axis=1
                 )
                 for q, x in enumerate(split(value)):
                     halo[q, rows, t * 2 * BS : (t + 1) * 2 * BS] = x
@@ -404,14 +408,15 @@
         return [halo[q, :, part * WIDE : (part + 1) * WIDE] for q in range(2)]
 
     outer_rows = slice(at * BS, (at + REACH) * BS)
-    beyond = build(0 if side == 0 else 1)
+    beyond = build(1)
     further = product([([x[outer_rows] for x in beyond], beyond)], True)
     yield
-    tile = build(1 if side == 0 else 0)
-    to_edge = product([([m_ref[q] for q in range(2)], tile)])
-    among = product([([x[outer_rows] for x in tile], tile)], True)
+    tile = build(0)
+    both = product(
+        [([jnp.concatenate([m_ref[q], tile[q][outer_rows]], axis=0) for q in range(2)], tile)]
+    )
     yield
-    first[0] = to_edge + b_ref[...]
+    first[0] = both[: REACH * BS] + b_ref[...]
     rows = [
         first[0, s * BS : (s + 1) * BS] * line_of(lines, edge_group, s + 1 - at, outer_group)
         for s in range(REACH)
@@ -427,7 +432,7 @@
                 square[s, k] = part[:, (t + at) * BS : (t + at + 1) * BS]
     sent(0)
     yield
-    first[1] = among + (further + a_ref[...])
+    first[1] = both[REACH * BS :] + (further + a_ref[...])
     rows = [
         first[1, p * BS : (p + 1) * BS] * line_of(lines, outer_group, p + at, outer_group)
         for p in range(REACH)

time: 15.7 us -> 15.7 us (level)
  no operation moved by 1% of the time
where the time goes in v22:
time: 15.7 us; the launch traced here: 15.6 us
  starting transfers between devices  6.68 us (43%)
  Pallas kernels  6.48 us (41%)
  local copies, waits for them, and re-layouts  1.07 us (7%)
  between operations  0.69 us (4%)
  waiting for transfers between devices  0.63 us (4%)
    pallas_call x1, Pallas kernels, shards(): pl.pallas_call(functools.partial(first_kernel, axes=axes, half_axis=half_...  3.77 us
    ppermute x1, starting transfers between devices, shards(): high_own = lax.ppermute(to_left, axes, backward)  3.1 us
    ppermute x1, starting transfers between devices, shards(): low_own = lax.ppermute(to_right, axes, forward)  2.55 us
    pallas_call x1, Pallas kernels, shards(): pl.pallas_call(functools.partial(border_kernel, groups=groups, half_axis=...  2.16 us
    slice x1, local copies, waits for them, and re-layouts, shards(): top, bottom = (matrix[:REACH, REACH:], matrix[count - REACH:, :REACH + 1])  1.06 us
    ppermute x1, starting transfers between devices, shards(): other = lax.ppermute(matrix, half_axis, swap)  0.52 us
    pallas_call x1, Pallas kernels, shards(): pl.pallas_call(last_kernel, out_shape=[rows, edges], in_specs=[vmem] * 5,...  0.45 us
    ppermute x1, starting transfers between devices, shards(): low_other = lax.ppermute(low_own, half_axis, swap)  0.34 us
  transfers between devices with their start and end apart: 5, of which 3 were waited for; matrix products, arithmetic and copies ran while one was open for 0% of the time, Pallas kernels for 28%

profile of v22, /device:TPU:0, one launch (start us, length us, event | category | flops | bytes accessed | tf_op | source)
XLA Modules:
  0.0 15.6 jit_solution(12340915310814762369)
XLA Ops:
  0.6 1.1 %fusion = (f32[3,4,32,64]{3,2,1,0:T(8,128)S(1)}, f32[3,4,32,64]{3,2,1,0:T(8,128)S(1)}) fusion(f32[12,7,32,64]{3,2,1,0:T(8,128)} %own.1), kind=kLoop, calls=%fused_computation | loop fusion | bytes 393216 | tf_op jit(solution)/shard_map/slice | solution.py:515
  1.7 0.0 copy-start
  1.7 0.0 copy-start.1
  1.7 0.5 %collective-permute-start.1 = (f32[12,7,32,64]{3,2,1,0:T(8,128)}, f32[12,7,32,64]{3,2,1,0:T(8,128)S(1)}, u32[]{:S(2)}, u32[]{:S(2)}) collective-permute-start(f32[12,7,32,64]{3,2,1,0:T(8,128)} %own.1), channel_id=1, source_target_pairs={{0,1},{1,0},{2,3},{3,2},{4,5},{5,4},{6,7},{7,6},{8,9},{9,8},{10,11... | collective-permute-start | bytes 2064392 | tf_op jit(solution)/shard_map/ppermute | solution.py:532
  2.2 0.1 shard_map.41
  2.4 2.6 %collective-permute-start = (f32[96,256]{1,0:T(8,128)S(1)}, f32[96,256]{1,0:T(8,128)S(1)}, u32[]{:S(2)}, u32[]{:S(2)}) collective-permute-start(f32[96,256]{1,0:T(8,128)S(1)} %get-tuple-element.34), channel_id=1, source_target_pairs={{0,2},{2,4},{4,6},{6,8},{8,10},{10,12},{12,14},{14,0},{1,3},{3,5},... | collective-permute-start | bytes 294920 | tf_op jit(solution)/shard_map/ppermute | solution.py:536
  4.9 3.1 %collective-permute-start.3 = (f32[96,256]{1,0:T(8,128)S(1)}, f32[96,256]{1,0:T(8,128)S(1)}, u32[]{:S(2)}, u32[]{:S(2)}) collective-permute-start(f32[96,256]{1,0:T(8,128)S(1)} %get-tuple-element.38), channel_id=1, source_target_pairs={{2,0},{4,2},{6,4},{8,6},{10,8},{12,10},{14,12},{0,14},{3,1},{5,3},... | collective-permute-start | bytes 294920 | tf_op jit(solution)/shard_map/ppermute | solution.py:535
  8.0 0.0 collective-permute-done.1.other
  8.0 0.0 copy-done
  8.0 0.0 copy-done.1
  8.0 3.8 %shard_map.42 = (f32[12,7,32,64]{3,2,1,0:T(8,128)}, f32[12,7,32,64]{3,2,1,0:T(8,128)}, f32[3,7,32,64]{3,2,1,0:T(8,128)S(1)}, f32[3,7,32,64]{3,2,1,0:T(8,128)S(1)...) custom-call(f32[12,7,32,64]{3,2,1,0:T(8,128)S(1)} %copy-done, ...), custom_call_target="tpu_custom_call" | custom-call | flops 1610612736 | bytes 16777216 | tf_op jit(solution)/shard_map/pallas_call | solution.py:551
  11.8 0.0 collective-permute-done.low_own
  11.8 0.1 collective-permute-done.3.high_own
  11.9 0.2 %collective-permute-start.4 = (f32[96,256]{1,0:T(8,128)S(1)}, f32[96,256]{1,0:T(8,128)S(1)}, u32[]{:S(2)}, u32[]{:S(2)}) collective-permute-start(f32[96,256]{1,0:T(8,128)S(1)} %collective-permute-done.3.high_own), channel_id=1, source_target_pairs={{0,1},{1,0},{2,3},{3,2},{4,5},{5,4},{6,7},{7,6},{8,9},{9,8},{10,11... | collective-permute-start | bytes 294920 | tf_op jit(solution)/shard_map/ppermute | solution.py:572
  12.1 0.3 %collective-permute-start.2 = (f32[96,256]{1,0:T(8,128)S(1)}, f32[96,256]{1,0:T(8,128)S(1)}, u32[]{:S(2)}, u32[]{:S(2)}) collective-permute-start(f32[96,256]{1,0:T(8,128)S(1)} %collective-permute-done.low_own), channel_id=1, source_target_pairs={{0,1},{1,0},{2,3},{3,2},{4,5},{5,4},{6,7},{7,6},{8,9},{9,8},{10,11... | collective-permute-start | bytes 294920 | tf_op jit(solution)/shard_map/ppermute | solution.py:571
  12.4 0.4 %shard_map.43 = (f32[4,7,32,64]{3,2,1,0:T(8,128)S(1)}, f32[3,7,32,64]{3,2,1,0:T(8,128)S(1)}) custom-call(f32[12,7,32,64]{3,2,1,0:T(8,128)S(1)} %copy-done, f32[20,768]{1,0:T(8,128)S(1)} %get-tuple-element.41.lines, bf16[2,3,256,768]{3,2,1,0:T(8,128)(2,1)S(1)} %get-tuple-element.42.full, bf16[2,3,128,768]{3,2,1,0:T(8,128)(2,1)S(1)} %get-tuple-element.43.mine, ...), custom_call_target="tpu_custom_call" | custom-call | flops 402653184 | bytes 4194304 | tf_op jit(solution)/shard_map/pallas_call | solution.py:574
  12.9 0.3 %collective-permute-done.4.high_other = f32[96,256]{1,0:T(8,128)S(1)} collective-permute-done((f32[96,256]{1,0:T(8,128)S(1)}, f32[96,256]{1,0:T(8,128)S(1)}, u32[]{:S(2)}, u32[]{:S(2)}) %collective-permute-start.4) | collective-permute-done | bytes 98336 | tf_op jit(solution)/shard_map/ppermute | solution.py:572
  13.2 0.2 %collective-permute-done.2.low_other = f32[96,256]{1,0:T(8,128)S(1)} collective-permute-done((f32[96,256]{1,0:T(8,128)S(1)}, f32[96,256]{1,0:T(8,128)S(1)}, u32[]{:S(2)}, u32[]{:S(2)}) %collective-permute-start.2) | collective-permute-done | bytes 98336 | tf_op jit(solution)/shard_map/ppermute | solution.py:571
  13.4 2.2 %shard_map.44 = (f32[3,7,32,64]{3,2,1,0:T(8,128)S(1)}, f32[3,7,32,64]{3,2,1,0:T(8,128)S(1)}, f32[3,7,32,64]{3,2,1,0:T(8,128)S(1)}, f32[3,7,32,64]{3,2,1,0:T(8,12...) custom-call(f32[96,256]{1,0:T(8,128)S(1)} %collective-permute-done.l, ...), custom_call_target="tpu_custom_call", output_to_operand_aliasing={{0}: (14, {}), {1}: (15, {}), {2}: (16, {}), {3}: (17, {}),... | custom-call | flops 402653184 | bytes 2097152 | tf_op jit(solution)/shard_map/pallas_call | solution.py:586
Async XLA Ops:
  1.7 6.3 %copy-start = (f32[12,7,32,64]{3,2,1,0:T(8,128)S(1)}, f32[12,7,32,64]{3,2,1,0:T(8,128)}, u32[]{:S(2)}) copy-start(f32[12,7,32,64]{3,2,1,0:T(8,128)} %own.1) | copy-start | bytes 2064388
  1.7 6.3 %copy-start.1 = (s32[96,7]{0,1:T(8,128)S(1)}, s32[96,7]{0,1:T(8,128)}, u32[]{:S(2)}) copy-start(s32[96,7]{0,1:T(8,128)} %param.3) | copy-start | bytes 8068
  1.7 6.3 %collective-permute-start.1 = (f32[12,7,32,64]{3,2,1,0:T(8,128)}, f32[12,7,32,64]{3,2,1,0:T(8,128)S(1)}, u32[]{:S(2)}, u32[]{:S(2)}) collective-permute-start(f32[12,7,32,64]{3,2,1,0:T(8,128)} %own.1), channel_id=1, source_target_pairs={{0,1},{1,0},{2,3},{3,2},{4,5},{5,4},{6,7},{7,6},{8,9},{9,8},{10,11... | collective-permute-start | bytes 2064392 | tf_op jit(solution)/shard_map/ppermute | solution.py:532
  2.4 9.4 %collective-permute-start = (f32[96,256]{1,0:T(8,128)S(1)}, f32[96,256]{1,0:T(8,128)S(1)}, u32[]{:S(2)}, u32[]{:S(2)}) collective-permute-start(f32[96,256]{1,0:T(8,128)S(1)} %get-tuple-element.34), channel_id=1, source_target_pairs={{0,2},{2,4},{4,6},{6,8},{8,10},{10,12},{12,14},{14,0},{1,3},{3,5},... | collective-permute-start | bytes 294920 | tf_op jit(solution)/shard_map/ppermute | solution.py:536
  4.9 7.0 %collective-permute-start.3 = (f32[96,256]{1,0:T(8,128)S(1)}, f32[96,256]{1,0:T(8,128)S(1)}, u32[]{:S(2)}, u32[]{:S(2)}) collective-permute-start(f32[96,256]{1,0:T(8,128)S(1)} %get-tuple-element.38), channel_id=1, source_target_pairs={{2,0},{4,2},{6,4},{8,6},{10,8},{12,10},{14,12},{0,14},{3,1},{5,3},... | collective-permute-start | bytes 294920 | tf_op jit(solution)/shard_map/ppermute | solution.py:535
  11.9 1.3 %collective-permute-start.4 = (f32[96,256]{1,0:T(8,128)S(1)}, f32[96,256]{1,0:T(8,128)S(1)}, u32[]{:S(2)}, u32[]{:S(2)}) collective-permute-start(f32[96,256]{1,0:T(8,128)S(1)} %collective-permute-done.3.high_own), channel_id=1, source_target_pairs={{0,1},{1,0},{2,3},{3,2},{4,5},{5,4},{6,7},{7,6},{8,9},{9,8},{10,11... | collective-permute-start | bytes 294920 | tf_op jit(solution)/shard_map/ppermute | solution.py:572
  12.1 1.3 %collective-permute-start.2 = (f32[96,256]{1,0:T(8,128)S(1)}, f32[96,256]{1,0:T(8,128)S(1)}, u32[]{:S(2)}, u32[]{:S(2)}) collective-permute-start(f32[96,256]{1,0:T(8,128)S(1)} %collective-permute-done.low_own), channel_id=1, source_target_pairs={{0,1},{1,0},{2,3},{3,2},{4,5},{5,4},{6,7},{7,6},{8,9},{9,8},{10,11... | collective-permute-start | bytes 294920 | tf_op jit(solution)/shard_map/ppermute | solution.py:571

commit v23 on v18

--- a/solution.py
+++ b/solution.py
@@ -229,8 +229,8 @@
 
 
 def first_kernel(
-    own, other, pat, square_out, sign_out, low_square, high_square, low_sign, full, mine, keep, lines, low_a, low_b, low_m, low_p,
-    high_a, high_b, high_m, high_p, square, sign, results, sems, edge_sems, *, axes, half_axis
+    own, other, pat, square_out, sign_out, low_square, high_square, low_sign, full, mine, keep, lines,
+    square, sign, results, sems, edge_sems, *, axes, half_axis
 ):
     it = Interior(own, lines, full, mine, keep)
     groups = it.groups
@@ -337,17 +337,20 @@
         steps.append(functools.partial(it.send, g, 1, sign.at[g], sign_out, sems))
         if g == 0:
             steps.append(functools.partial(it.send_edge, 0, 1, low_sign, sign_out, edge_sems.at[2]))
-    steps.append(it.reaching(low_a, low_b, low_m, low_p, 0, -1, 0))
-    steps.append(it.reaching(high_a, high_b, high_m, high_p, groups - 1, groups, BS))
     staggered(steps)
     it.finish()
 
 
-def last_kernel(own, lines, full, mine, keep, sign, high_sign, results):
+def last_kernel(
+    own, lines, full, mine, keep, sign, high_sign, low_a, low_b, low_m, low_p, high_a, high_b, high_m,
+    high_p, results
+):
     it = Interior(own, lines, full, mine, keep)
     last = it.groups - 1
     steps = [it.second(last, h, sign, None, high_sign, results.at[i]) for i, h in enumerate(it.near(last))]
     steps.append(functools.partial(it.far_seed, last, high_sign))
+    steps.append(it.reaching(low_a, low_b, low_m, low_p, 0, -1, 0))
+    steps.append(it.reaching(high_a, high_b, high_m, high_p, last, it.groups, BS))
 
     staggered(steps)
 
@@ -537,11 +540,11 @@
         jax.ShapeDtypeStruct((2, 2, REACH * HALF, WIDE), BF),
     ]
     rows = jax.ShapeDtypeStruct((GROUP,) + matrix.shape[1:], F32)
-    square, sign, low_square, high_square, low_sign, full, mine, keep, lines, *ends = pl.pallas_call(
+    square, sign, low_square, high_square, low_sign, full, mine, keep, lines = pl.pallas_call(
         functools.partial(first_kernel, axes=axes, half_axis=half_axis),
-        out_shape=[band, band, edges, edges, edges, full, mine, keep, lines] + ends_out * 2,
+        out_shape=[band, band, edges, edges, edges, full, mine, keep, lines],
         in_specs=[vmem] * 3,
-        out_specs=[hbm] * 2 + [vmem] * 15,
+        out_specs=[hbm] * 2 + [vmem] * 7,
         scratch_shapes=[
             pltpu.VMEM((groups,) + rows.shape, F32),
             pltpu.VMEM((groups - 1,) + rows.shape, F32),
@@ -555,16 +558,16 @@
         ),
     )(matrix, other, flags)
 
+    high_own, low_sign = lax.optimization_barrier((high_own, low_sign))
+    high_other = lax.ppermute(high_own, half_axis, swap)
     low_own, low_sign = lax.optimization_barrier((low_own, low_sign))
-    high_own, low_sign = lax.optimization_barrier((high_own, low_sign))
     low_other = lax.ppermute(low_own, half_axis, swap)
-    high_other = lax.ppermute(high_own, half_axis, swap)
-
-    sign_last, high_sign = pl.pallas_call(
+
+    sign_last, high_sign, *ends = pl.pallas_call(
         last_kernel,
-        out_shape=[rows, edges],
+        out_shape=[rows, edges] + ends_out * 2,
         in_specs=[vmem] * 5,
-        out_specs=[vmem] * 2,
+        out_specs=[vmem] * 10,
         scratch_shapes=[pltpu.VMEM((2, GROUP * HALF, WIDE), F32)],
         compiler_params=params,
         cost_estimate=pl.CostEstimate(

time: 15.7 us -> 19.3 us (1.23)
  waiting for transfers between devices: 0.63 us -> 4.34 us
    ppermute x1, waiting for transfers between devices: 0.01 us -> 4.09 us  [shards(): low_own = lax.ppermute(to_right, axes, forward)]
    ppermute x1, starting transfers between devices: 2.56 us -> 0.01 us  [shards(): low_own = lax.ppermute(to_right, axes, forward)]
    ppermute x1, starting transfers between devices: 3.1 us -> 5.6 us  [shards(): high_own = lax.ppermute(to_left, axes, backward)]
    ppermute x1, starting transfers between devices: 0.17 us -> 0.51 us  [shards(): high_other = lax.ppermute(high_own, half_axis, swap)]
    ppermute x1, starting transfers between devices: 0.34 us -> 0.01 us  [shards(): low_other = lax.ppermute(low_own, half_axis, swap)]
    pallas_call x1, Pallas kernels: 3.77 us -> 3.48 us  [shards(): pl.pallas_call(functools.partial(first_kernel, axes=axes, half_axis=half_...]
    pallas_call x1, Pallas kernels: 0.44 us -> 0.69 us  [shards(): pl.pallas_call(last_kernel, out_shape=[rows, edges] + ends_out * 2, in_sp...]
  transfers between devices with their start and end apart: 5 -> 5, of which waited for: 3 -> 3; matrix products, arithmetic and copies ran while one was open for 7% -> 5% of each run, Pallas kernels for 28% -> 22%
where the time goes in v23:
time: 19.3 us; the launch traced here: 19.2 us
  starting transfers between devices  6.63 us (34%)
  Pallas kernels  6.46 us (33%)
  waiting for transfers between devices  4.34 us (22%)
  local copies, waits for them, and re-layouts  1.06 us (5%)
  between operations  0.7 us (4%)
    ppermute x1, starting transfers between devices, shards(): high_own = lax.ppermute(to_left, axes, backward)  5.6 us
    ppermute x1, waiting for transfers between devices, shards(): low_own = lax.ppermute(to_right, axes, forward)  4.09 us
    pallas_call x1, Pallas kernels, shards(): pl.pallas_call(functools.partial(first_kernel, axes=axes, half_axis=half_...  3.48 us
    pallas_call x1, Pallas kernels, shards(): pl.pallas_call(functools.partial(border_kernel, groups=groups, half_axis=...  2.18 us
    slice x1, local copies, waits for them, and re-layouts, shards(): top, bottom = (matrix[:REACH, REACH:], matrix[count - REACH:, :REACH + 1])  1.05 us
    pallas_call x1, Pallas kernels, shards(): pl.pallas_call(last_kernel, out_shape=[rows, edges] + ends_out * 2, in_sp...  0.69 us
    ppermute x1, starting transfers between devices, shards(): other = lax.ppermute(matrix, half_axis, swap)  0.52 us
    ppermute x1, starting transfers between devices, shards(): high_other = lax.ppermute(high_own, half_axis, swap)  0.51 us
  transfers between devices with their start and end apart: 5, of which 3 were waited for; matrix products, arithmetic and copies ran while one was open for 5% of the time, Pallas kernels for 22%

profile of v23, /device:TPU:0, one launch (start us, length us, event | category | flops | bytes accessed | tf_op | source)
XLA Modules:
  0.0 19.2 jit_solution(13314439839950750973)
XLA Ops:
  0.6 0.5 %collective-permute-start.2 = (f32[12,7,32,64]{3,2,1,0:T(8,128)}, f32[12,7,32,64]{3,2,1,0:T(8,128)S(1)}, u32[]{:S(2)}, u32[]{:S(2)}) collective-permute-start(f32[12,7,32,64]{3,2,1,0:T(8,128)} %own.3), channel_id=1, source_target_pairs={{0,1},{1,0},{2,3},{3,2},{4,5},{5,4},{6,7},{7,6},{8,9},{9,8},{10,11... | collective-permute-start | bytes 2064392 | tf_op jit(solution)/shard_map/ppermute | solution.py:524
  1.1 1.0 %fusion = (f32[3,4,32,64]{3,2,1,0:T(8,128)S(1)}, f32[3,4,32,64]{3,2,1,0:T(8,128)S(1)}) fusion(f32[12,7,32,64]{3,2,1,0:T(8,128)} %own.3), kind=kLoop, calls=%fused_computation | loop fusion | bytes 393216 | tf_op jit(solution)/shard_map/slice | solution.py:506
  2.2 0.0 copy-start
  2.2 0.0 copy-start.1
  2.2 0.1 shard_map.41
  2.3 5.6 %collective-permute-start.1 = (f32[96,256]{1,0:T(8,128)S(1)}, f32[96,256]{1,0:T(8,128)S(1)}, u32[]{:S(2)}, u32[]{:S(2)}) collective-permute-start(f32[96,256]{1,0:T(8,128)S(1)} %get-tuple-element.30), channel_id=1, source_target_pairs={{2,0},{4,2},{6,4},{8,6},{10,8},{12,10},{14,12},{0,14},{3,1},{5,3},... | collective-permute-start | bytes 294920 | tf_op jit(solution)/shard_map/ppermute | solution.py:527
  7.9 0.0 collective-permute-start
  7.9 0.0 collective-permute-done.2.other
  8.0 0.0 copy-done
  8.0 0.0 copy-done.1
  8.0 3.5 %shard_map.42 = (f32[12,7,32,64]{3,2,1,0:T(8,128)}, f32[12,7,32,64]{3,2,1,0:T(8,128)}, f32[3,7,32,64]{3,2,1,0:T(8,128)S(1)}, f32[3,7,32,64]{3,2,1,0:T(8,128)S(1)...) custom-call(f32[12,7,32,64]{3,2,1,0:T(8,128)S(1)} %copy-done, ...), custom_call_target="tpu_custom_call" | custom-call | flops 1610612736 | bytes 16777216 | tf_op jit(solution)/shard_map/pallas_call | solution.py:543
  11.5 0.0 collective-permute-done.1.high_own
  11.5 4.1 %collective-permute-done.low_own = f32[96,256]{1,0:T(8,128)S(1)} collective-permute-done((f32[96,256]{1,0:T(8,128)S(1)}, f32[96,256]{1,0:T(8,128)S(1)}, u32[]{:S(2)}, u32[]{:S(2)}) %collective-permute-start) | collective-permute-done | bytes 98336 | tf_op jit(solution)/shard_map/ppermute | solution.py:528
  15.6 0.0 collective-permute-start.3
  15.6 0.5 %collective-permute-start.4 = (f32[96,256]{1,0:T(8,128)S(1)}, f32[96,256]{1,0:T(8,128)S(1)}, u32[]{:S(2)}, u32[]{:S(2)}) collective-permute-start(f32[96,256]{1,0:T(8,128)S(1)} %collective-permute-done.1.high_own), channel_id=1, source_target_pairs={{0,1},{1,0},{2,3},{3,2},{4,5},{5,4},{6,7},{7,6},{8,9},{9,8},{10,11... | collective-permute-start | bytes 294920 | tf_op jit(solution)/shard_map/ppermute | solution.py:562
  16.1 0.7 %shard_map.43 = (f32[4,7,32,64]{3,2,1,0:T(8,128)S(1)}, f32[3,7,32,64]{3,2,1,0:T(8,128)S(1)}, f32[192,256]{1,0:T(8,128)S(1)}, f32[192,256]{1,0:T(8,128)S(1)}, bf1...) custom-call(f32[12,7,32,64]{3,2,1,0:T(8,128)S(1)} %copy-done, ...), custom_call_target="tpu_custom_call" | custom-call | flops 402653184 | bytes 4194304 | tf_op jit(solution)/shard_map/pallas_call | solution.py:566
  16.8 0.1 collective-permute-done.3.low_other
  16.9 0.2 collective-permute-done.4.high_other
  17.0 2.2 %shard_map.44 = (f32[3,7,32,64]{3,2,1,0:T(8,128)S(1)}, f32[3,7,32,64]{3,2,1,0:T(8,128)S(1)}, f32[3,7,32,64]{3,2,1,0:T(8,128)S(1)}, f32[3,7,32,64]{3,2,1,0:T(8,12...) custom-call(f32[96,256]{1,0:T(8,128)S(1)} %collective-permute-done.l, ...), custom_call_target="tpu_custom_call", output_to_operand_aliasing={{0}: (14, {}), {1}: (15, {}), {2}: (16, {}), {3}: (17, {}),... | custom-call | flops 402653184 | bytes 2097152 | tf_op jit(solution)/shard_map/pallas_call | solution.py:578
Async XLA Ops:
  0.6 7.3 %collective-permute-start.2 = (f32[12,7,32,64]{3,2,1,0:T(8,128)}, f32[12,7,32,64]{3,2,1,0:T(8,128)S(1)}, u32[]{:S(2)}, u32[]{:S(2)}) collective-permute-start(f32[12,7,32,64]{3,2,1,0:T(8,128)} %own.3), channel_id=1, source_target_pairs={{0,1},{1,0},{2,3},{3,2},{4,5},{5,4},{6,7},{7,6},{8,9},{9,8},{10,11... | collective-permute-start | bytes 2064392 | tf_op jit(solution)/shard_map/ppermute | solution.py:524
  2.2 5.8 %copy-start = (f32[12,7,32,64]{3,2,1,0:T(8,128)S(1)}, f32[12,7,32,64]{3,2,1,0:T(8,128)}, u32[]{:S(2)}) copy-start(f32[12,7,32,64]{3,2,1,0:T(8,128)} %own.3) | copy-start | bytes 2064388
  2.2 5.7 %copy-start.1 = (s32[96,7]{0,1:T(8,128)S(1)}, s32[96,7]{0,1:T(8,128)}, u32[]{:S(2)}) copy-start(s32[96,7]{0,1:T(8,128)} %param.3) | copy-start | bytes 8068
  2.3 9.1 %collective-permute-start.1 = (f32[96,256]{1,0:T(8,128)S(1)}, f32[96,256]{1,0:T(8,128)S(1)}, u32[]{:S(2)}, u32[]{:S(2)}) collective-permute-start(f32[96,256]{1,0:T(8,128)S(1)} %get-tuple-element.30), channel_id=1, source_target_pairs={{2,0},{4,2},{6,4},{8,6},{10,8},{12,10},{14,12},{0,14},{3,1},{5,3},... | collective-permute-start | bytes 294920 | tf_op jit(solution)/shard_map/ppermute | solution.py:527
  7.9 7.6 %collective-permute-start = (f32[96,256]{1,0:T(8,128)S(1)}, f32[96,256]{1,0:T(8,128)S(1)}, u32[]{:S(2)}, u32[]{:S(2)}) collective-permute-start(f32[96,256]{1,0:T(8,128)S(1)} %get-tuple-element.29), channel_id=1, source_target_pairs={{0,2},{2,4},{4,6},{6,8},{8,10},{10,12},{12,14},{14,0},{1,3},{3,5},... | collective-permute-start | bytes 294920 | tf_op jit(solution)/shard_map/ppermute | solution.py:528
  15.6 1.3 %collective-permute-start.3 = (f32[96,256]{1,0:T(8,128)S(1)}, f32[96,256]{1,0:T(8,128)S(1)}, u32[]{:S(2)}, u32[]{:S(2)}) collective-permute-start(f32[96,256]{1,0:T(8,128)S(1)} %collective-permute-done.low_own), channel_id=1, source_target_pairs={{0,1},{1,0},{2,3},{3,2},{4,5},{5,4},{6,7},{7,6},{8,9},{9,8},{10,11... | collective-permute-start | bytes 294920 | tf_op jit(solution)/shard_map/ppermute | solution.py:564
  15.6 1.5 %collective-permute-start.4 = (f32[96,256]{1,0:T(8,128)S(1)}, f32[96,256]{1,0:T(8,128)S(1)}, u32[]{:S(2)}, u32[]{:S(2)}) collective-permute-start(f32[96,256]{1,0:T(8,128)S(1)} %collective-permute-done.1.high_own), channel_id=1, source_target_pairs={{0,1},{1,0},{2,3},{3,2},{4,5},{5,4},{6,7},{7,6},{8,9},{9,8},{10,11... | collective-permute-start | bytes 294920 | tf_op jit(solution)/shard_map/ppermute | solution.py:562

commit v24 on v23

--- a/solution.py
+++ b/solution.py
@@ -558,10 +558,10 @@
         ),
     )(matrix, other, flags)
 
+    low_own, low_sign = lax.optimization_barrier((low_own, low_sign))
     high_own, low_sign = lax.optimization_barrier((high_own, low_sign))
+    low_other = lax.ppermute(low_own, half_axis, swap)
     high_other = lax.ppermute(high_own, half_axis, swap)
-    low_own, low_sign = lax.optimization_barrier((low_own, low_sign))
-    low_other = lax.ppermute(low_own, half_axis, swap)
 
     sign_last, high_sign, *ends = pl.pallas_call(
         last_kernel,

time: 19.3 us -> 15.7 us (0.81)
  waiting for transfers between devices: 4.34 us -> 0.65 us
    ppermute x1, waiting for transfers between devices: 4.09 us -> 0.01 us  [shards(): low_own = lax.ppermute(to_right, axes, forward)]
    ppermute x1, starting transfers between devices: 0.01 us -> 2.56 us  [shards(): low_own = lax.ppermute(to_right, axes, forward)]
    ppermute x1, starting transfers between devices: 5.6 us -> 3.1 us  [shards(): high_own = lax.ppermute(to_left, axes, backward)]
    ppermute x1, starting transfers between devices: 0.51 us -> 0.01 us  [shards(): high_other = lax.ppermute(high_own, half_axis, swap)]
    ppermute x1, starting transfers between devices: 0.01 us -> 0.51 us  [shards(): low_other = lax.ppermute(low_own, half_axis, swap)]
    ppermute x1, waiting for transfers between devices: 0.01 us -> 0.4 us  [shards(): high_own = lax.ppermute(to_left, axes, backward)]
  transfers between devices with their start and end apart: 5 -> 5, of which waited for: 3 -> 3; matrix products, arithmetic and copies ran while one was open for 5% -> 7% of each run, Pallas kernels for 22% -> 27%
where the time goes in v24:
time: 15.7 us; the launch traced here: 15.6 us
  starting transfers between devices  6.69 us (43%)
  Pallas kernels  6.47 us (41%)
  local copies, waits for them, and re-layouts  1.06 us (7%)
  between operations  0.69 us (4%)
  waiting for transfers between devices  0.65 us (4%)
    pallas_call x1, Pallas kernels, shards(): pl.pallas_call(functools.partial(first_kernel, axes=axes, half_axis=half_...  3.48 us
    ppermute x1, starting transfers between devices, shards(): high_own = lax.ppermute(to_left, axes, backward)  3.1 us
    ppermute x1, starting transfers between devices, shards(): low_own = lax.ppermute(to_right, axes, forward)  2.56 us
    pallas_call x1, Pallas kernels, shards(): pl.pallas_call(functools.partial(border_kernel, groups=groups, half_axis=...  2.18 us
    slice x1, local copies, waits for them, and re-layouts, shards(): top, bottom = (matrix[:REACH, REACH:], matrix[count - REACH:, :REACH + 1])  1.05 us
    pallas_call x1, Pallas kernels, shards(): pl.pallas_call(last_kernel, out_shape=[rows, edges] + ends_out * 2, in_sp...  0.7 us
    ppermute x1, starting transfers between devices, shards(): other = lax.ppermute(matrix, half_axis, swap)  0.52 us
    ppermute x1, starting transfers between devices, shards(): low_other = lax.ppermute(low_own, half_axis, swap)  0.51 us
  transfers between devices with their start and end apart: 5, of which 3 were waited for; matrix products, arithmetic and copies ran while one was open for 7% of the time, Pallas kernels for 27%

profile of v24, /device:TPU:0, one launch (start us, length us, event | category | flops | bytes accessed | tf_op | source)
XLA Modules:
  0.0 15.6 jit_solution(836791551482925431)
XLA Ops:
  0.6 0.5 %collective-permute-start.1 = (f32[12,7,32,64]{3,2,1,0:T(8,128)}, f32[12,7,32,64]{3,2,1,0:T(8,128)S(1)}, u32[]{:S(2)}, u32[]{:S(2)}) collective-permute-start(f32[12,7,32,64]{3,2,1,0:T(8,128)} %own.3), channel_id=1, source_target_pairs={{0,1},{1,0},{2,3},{3,2},{4,5},{5,4},{6,7},{7,6},{8,9},{9,8},{10,11... | collective-permute-start | bytes 2064392 | tf_op jit(solution)/shard_map/ppermute | solution.py:524
  1.1 1.0 %fusion = (f32[3,4,32,64]{3,2,1,0:T(8,128)S(1)}, f32[3,4,32,64]{3,2,1,0:T(8,128)S(1)}) fusion(f32[12,7,32,64]{3,2,1,0:T(8,128)} %own.3), kind=kLoop, calls=%fused_computation | loop fusion | bytes 393216 | tf_op jit(solution)/shard_map/slice | solution.py:506
  2.2 0.0 copy-start
  2.2 0.0 copy-start.1
  2.2 0.1 shard_map.41
  2.3 2.6 %collective-permute-start = (f32[96,256]{1,0:T(8,128)S(1)}, f32[96,256]{1,0:T(8,128)S(1)}, u32[]{:S(2)}, u32[]{:S(2)}) collective-permute-start(f32[96,256]{1,0:T(8,128)S(1)} %get-tuple-element.29), channel_id=1, source_target_pairs={{0,2},{2,4},{4,6},{6,8},{8,10},{10,12},{12,14},{14,0},{1,3},{3,5},... | collective-permute-start | bytes 294920 | tf_op jit(solution)/shard_map/ppermute | solution.py:528
  4.9 3.1 %collective-permute-start.3 = (f32[96,256]{1,0:T(8,128)S(1)}, f32[96,256]{1,0:T(8,128)S(1)}, u32[]{:S(2)}, u32[]{:S(2)}) collective-permute-start(f32[96,256]{1,0:T(8,128)S(1)} %get-tuple-element.32), channel_id=1, source_target_pairs={{2,0},{4,2},{6,4},{8,6},{10,8},{12,10},{14,12},{0,14},{3,1},{5,3},... | collective-permute-start | bytes 294920 | tf_op jit(solution)/shard_map/ppermute | solution.py:527
  8.0 0.0 collective-permute-done.1.other
  8.0 0.0 copy-done
  8.0 0.0 copy-done.1
  8.0 3.5 %shard_map.42 = (f32[12,7,32,64]{3,2,1,0:T(8,128)}, f32[12,7,32,64]{3,2,1,0:T(8,128)}, f32[3,7,32,64]{3,2,1,0:T(8,128)S(1)}, f32[3,7,32,64]{3,2,1,0:T(8,128)S(1)...) custom-call(f32[12,7,32,64]{3,2,1,0:T(8,128)S(1)} %copy-done, ...), custom_call_target="tpu_custom_call" | custom-call | flops 1610612736 | bytes 16777216 | tf_op jit(solution)/shard_map/pallas_call | solution.py:543
  11.5 0.0 collective-permute-done.low_own
  11.5 0.4 %collective-permute-done.3.high_own = f32[96,256]{1,0:T(8,128)S(1)} collective-permute-done((f32[96,256]{1,0:T(8,128)S(1)}, f32[96,256]{1,0:T(8,128)S(1)}, u32[]{:S(2)}, u32[]{:S(2)}) %collective-permute-start.3) | collective-permute-done | bytes 98336 | tf_op jit(solution)/shard_map/ppermute | solution.py:527
  11.9 0.0 collective-permute-start.4
  11.9 0.5 %collective-permute-start.2 = (f32[96,256]{1,0:T(8,128)S(1)}, f32[96,256]{1,0:T(8,128)S(1)}, u32[]{:S(2)}, u32[]{:S(2)}) collective-permute-start(f32[96,256]{1,0:T(8,128)S(1)} %collective-permute-done.low_own), channel_id=1, source_target_pairs={{0,1},{1,0},{2,3},{3,2},{4,5},{5,4},{6,7},{7,6},{8,9},{9,8},{10,11... | collective-permute-start | bytes 294920 | tf_op jit(solution)/shard_map/ppermute | solution.py:563
  12.4 0.7 %shard_map.43 = (f32[4,7,32,64]{3,2,1,0:T(8,128)S(1)}, f32[3,7,32,64]{3,2,1,0:T(8,128)S(1)}, f32[192,256]{1,0:T(8,128)S(1)}, f32[192,256]{1,0:T(8,128)S(1)}, bf1...) custom-call(f32[12,7,32,64]{3,2,1,0:T(8,128)S(1)} %copy-done, ...), custom_call_target="tpu_custom_call" | custom-call | flops 402653184 | bytes 4194304 | tf_op jit(solution)/shard_map/pallas_call | solution.py:566
  13.1 0.1 collective-permute-done.4.high_other
  13.2 0.2 collective-permute-done.2.low_other
  13.4 2.2 %shard_map.44 = (f32[3,7,32,64]{3,2,1,0:T(8,128)S(1)}, f32[3,7,32,64]{3,2,1,0:T(8,128)S(1)}, f32[3,7,32,64]{3,2,1,0:T(8,128)S(1)}, f32[3,7,32,64]{3,2,1,0:T(8,12...) custom-call(f32[96,256]{1,0:T(8,128)S(1)} %collective-permute-done.l, ...), custom_call_target="tpu_custom_call", output_to_operand_aliasing={{0}: (14, {}), {1}: (15, {}), {2}: (16, {}), {3}: (17, {}),... | custom-call | flops 402653184 | bytes 2097152 | tf_op jit(solution)/shard_map/pallas_call | solution.py:578
Async XLA Ops:
  0.6 7.4 %collective-permute-start.1 = (f32[12,7,32,64]{3,2,1,0:T(8,128)}, f32[12,7,32,64]{3,2,1,0:T(8,128)S(1)}, u32[]{:S(2)}, u32[]{:S(2)}) collective-permute-start(f32[12,7,32,64]{3,2,1,0:T(8,128)} %own.3), channel_id=1, source_target_pairs={{0,1},{1,0},{2,3},{3,2},{4,5},{5,4},{6,7},{7,6},{8,9},{9,8},{10,11... | collective-permute-start | bytes 2064392 | tf_op jit(solution)/shard_map/ppermute | solution.py:524
  2.2 5.8 %copy-start = (f32[12,7,32,64]{3,2,1,0:T(8,128)S(1)}, f32[12,7,32,64]{3,2,1,0:T(8,128)}, u32[]{:S(2)}) copy-start(f32[12,7,32,64]{3,2,1,0:T(8,128)} %own.3) | copy-start | bytes 2064388
  2.2 5.8 %copy-start.1 = (s32[96,7]{0,1:T(8,128)S(1)}, s32[96,7]{0,1:T(8,128)}, u32[]{:S(2)}) copy-start(s32[96,7]{0,1:T(8,128)} %param.3) | copy-start | bytes 8068
  2.3 9.2 %collective-permute-start = (f32[96,256]{1,0:T(8,128)S(1)}, f32[96,256]{1,0:T(8,128)S(1)}, u32[]{:S(2)}, u32[]{:S(2)}) collective-permute-start(f32[96,256]{1,0:T(8,128)S(1)} %get-tuple-element.29), channel_id=1, source_target_pairs={{0,2},{2,4},{4,6},{6,8},{8,10},{10,12},{12,14},{14,0},{1,3},{3,5},... | collective-permute-start | bytes 294920 | tf_op jit(solution)/shard_map/ppermute | solution.py:528
  4.9 7.0 %collective-permute-start.3 = (f32[96,256]{1,0:T(8,128)S(1)}, f32[96,256]{1,0:T(8,128)S(1)}, u32[]{:S(2)}, u32[]{:S(2)}) collective-permute-start(f32[96,256]{1,0:T(8,128)S(1)} %get-tuple-element.32), channel_id=1, source_target_pairs={{2,0},{4,2},{6,4},{8,6},{10,8},{12,10},{14,12},{0,14},{3,1},{5,3},... | collective-permute-start | bytes 294920 | tf_op jit(solution)/shard_map/ppermute | solution.py:527
  11.9 1.3 %collective-permute-start.4 = (f32[96,256]{1,0:T(8,128)S(1)}, f32[96,256]{1,0:T(8,128)S(1)}, u32[]{:S(2)}, u32[]{:S(2)}) collective-permute-start(f32[96,256]{1,0:T(8,128)S(1)} %collective-permute-done.3.high_own), channel_id=1, source_target_pairs={{0,1},{1,0},{2,3},{3,2},{4,5},{5,4},{6,7},{7,6},{8,9},{9,8},{10,11... | collective-permute-start | bytes 294920 | tf_op jit(solution)/shard_map/ppermute | solution.py:564
  11.9 1.5 %collective-permute-start.2 = (f32[96,256]{1,0:T(8,128)S(1)}, f32[96,256]{1,0:T(8,128)S(1)}, u32[]{:S(2)}, u32[]{:S(2)}) collective-permute-start(f32[96,256]{1,0:T(8,128)S(1)} %collective-permute-done.low_own), channel_id=1, source_target_pairs={{0,1},{1,0},{2,3},{3,2},{4,5},{5,4},{6,7},{7,6},{8,9},{9,8},{10,11... | collective-permute-start | bytes 294920 | tf_op jit(solution)/shard_map/ppermute | solution.py:563
